TPU v7x, 256 devices: a whole 4x4x8 slice. The times are simulated.
256 devices in a mesh: dp: 16 (over z, y_lo), ctx: 16 (over x, y_hi, core).
Axes of the slice: x: 4, y: 4 (y_hi: 2, y_lo: 2; y = y_hi * 2 + y_lo), z: 8, core: 2. Of those that a mesh axis runs over, the one named last changes fastest.
Arguments:
- layer_input: bfloat16 [16, 4096, 8192], P('dp', 'ctx'), may hold values from -0.078125 to 0.078125
- query_rows: bfloat16 [16, 4096, 1024], P('dp', 'ctx'), may hold values from -6 to 6
- key_rows: bfloat16 [16, 4096, 128], P('dp', 'ctx'), may hold values from -6 to 6
- value_rows: bfloat16 [16, 4096, 128], P('dp', 'ctx'), may hold values from -6 to 6
- attn_out: bfloat16 [16, 4096, 1024], P('dp', 'ctx'), may hold values from -6 to 6
- d_attn: bfloat16 [16, 4096, 1024], P('dp', 'ctx'), may hold values from -6 to 6
- log_sum_exp: float32 [16, 8, 4096], P('dp', None, 'ctx')
- block_order: int32 [32], replicated, may hold values from 0 to 31, as said below
Outputs:
- d_query: bfloat16 [16, 4096, 1024], P('dp', 'ctx')
- d_weight: float32 [8192, 256], P(('dp', 'ctx'))
Inputs may be any that keep to these rules, and one draw needn't show every extreme that they name: `block_order`: each value appears exactly once.
All inputs are finite; a program needn't handle non-finite values.
Results may differ from a plain program's by a relative error of at most 0.0051.
Values may be sent and summed in bfloat16 or wider, within the bound.
No kernel may reach another device: no remote copies, remote signals or barrier semaphores. Data moves between devices by JAX's collectives and lax.ppermute only.
A program may use at most 64 MiB of HBM per device.

v0:
```python
import jax
import jax.numpy as jnp
from jax import lax
from jax.sharding import PartitionSpec as P


def passed_along(value, axis, steps):
    count = lax.axis_size(axis)
    pairs = [(source, (source + steps) % count) for source in range(count)]
    return lax.ppermute(value, axis, pairs)


def slot_positions(block_order, owner, half):
    firsts = lax.dynamic_slice_in_dim(block_order, 2 * owner, 2)
    offsets = jnp.arange(half, dtype=jnp.int32)
    return (firsts[:, None] * half + offsets[None, :]).reshape(2 * half)


def body(layer_input, query_rows, key_rows, value_rows, attn_out, d_attn, log_sum_exp, block_order):
    rows = query_rows.shape[1]
    head_dim = key_rows.shape[2]
    heads = query_rows.shape[2] // head_dim
    half = rows // 2
    scale = head_dim ** (-0.5)
    width = lax.axis_size("ctx")
    mine = lax.axis_index("ctx")
    q_pos = slot_positions(block_order, mine, half)
    queries = query_rows[0].reshape(rows, heads, head_dim)
    grad_out = d_attn[0].reshape(rows, heads, head_dim)
    saved = attn_out[0].reshape(rows, heads, head_dim)
    delta = jnp.sum(grad_out.astype(jnp.float32) * saved.astype(jnp.float32), axis=2).T
    stats = log_sum_exp[0]

    def tile(pair, k_pos):
        keys = pair[0]
        values = pair[1]
        score = jnp.einsum("rhd,sd->hrs", queries, keys, preferred_element_type=jnp.float32) * scale
        visible = q_pos[:, None] >= k_pos[None, :]
        prob = jnp.where(visible[None], jnp.exp(score - stats[:, :, None]), 0.0)
        d_value = jnp.einsum(
            "hrs,rhd->sd", prob.astype(jnp.bfloat16), grad_out, preferred_element_type=jnp.float32
        )
        d_prob = jnp.einsum("rhd,sd->hrs", grad_out, values, preferred_element_type=jnp.float32)
        d_score = (prob * (d_prob - delta[:, :, None])).astype(jnp.bfloat16)
        d_query = (
            jnp.einsum("hrs,sd->rhd", d_score, keys, preferred_element_type=jnp.float32) * scale
        )
        d_key = (
            jnp.einsum("hrs,rhd->sd", d_score, queries, preferred_element_type=jnp.float32) * scale
        )
        return (d_query, jnp.stack([d_key, d_value]))

    pair = jnp.stack([key_rows[0], value_rows[0]])
    query_zero = jnp.zeros((rows, heads, head_dim), jnp.float32)

    def pass_grads(sums):
        return passed_along(sums, "ctx", 1)

    def cycle_step(step, carry):
        pair_now, sums, query_sum = carry
        owner = (mine - step) % width
        d_query, d_kv = tile(pair_now, slot_positions(block_order, owner, half))
        sums = pass_grads(sums + d_kv)
        pair_now = passed_along(pair_now, "ctx", 1)
        return (pair_now, sums, query_sum + d_query)

    start = (pair, jnp.zeros((2, rows, head_dim), jnp.float32), query_zero)
    pair_last, sums, query_sum = lax.fori_loop(0, width - 1, cycle_step, start)
    d_query, d_kv = tile(pair_last, slot_positions(block_order, (mine + 1) % width, half))
    kv_sums = pass_grads(sums + d_kv)
    query_sum = query_sum + d_query
    d_query_out = query_sum.reshape(1, rows, heads * head_dim).astype(jnp.bfloat16)
    grads_bf = jnp.concatenate([kv_sums[0], kv_sums[1]], axis=1).astype(jnp.bfloat16)
    inputs = layer_input[0]
    d_weight = lax.psum_scatter(
        lax.dot_general(
            inputs, grads_bf, (((0,), (0,)), ((), ())), preferred_element_type=jnp.float32
        ),
        ("dp", "ctx"),
        scatter_dimension=0,
        tiled=True,
    )
    return (d_query_out, d_weight)


def solution(mesh):
    return jax.shard_map(
        body,
        mesh=mesh,
        in_specs=(
            P("dp", "ctx", None),
            P("dp", "ctx", None),
            P("dp", "ctx", None),
            P("dp", "ctx", None),
            P("dp", "ctx", None),
            P("dp", "ctx", None),
            P("dp", None, "ctx"),
            P(),
        ),
        out_specs=(P("dp", "ctx", None), P(("dp", "ctx"), None)),
        check_vma=False,
    )
```

profile of v0, /device:TPU:4, one launch (start us, length us, event | category | flops | bytes accessed | tf_op | source)
XLA Modules:
  0.0 1514.0 jit_solution(11473081751703162344)
XLA Ops:
  7.2 1.3 copy.32
  9.1 1.3 copy.33
  12.4 198.0 %while.20 = (s32[]{:T(128)}, bf16[2,256,128]{2,1,0:T(8,128)(2,1)}, f32[2,256,128]{2,1,0:T(8,128)S(1)}, f32[256,8,128]{2,0,1:T(8,128)S(1)}, s32[]{:T(128)}, /*ind...) while((s32[]{:T(128)}, bf16[2,256,128]{2,1,0:T(8,128)(2,1)}, ...), condition=%wide.region_2.3_spmd.clone, body=%wide.region_1.2_spmd.clone.sunk | while | flops 675774976 | bytes 16863680 | solution.py:68
  17.0 3.3 collective-permute-start.1
  21.2 4.2 collective-permute-done.1
  26.7 1.3 fusion.75
  30.0 2.4 collective-permute-start.1
  33.4 5.1 collective-permute-done.1
  43.1 1.5 collective-permute-start.1
  46.3 5.2 collective-permute-done.1
  52.7 1.3 fusion.75
  57.6 1.7 collective-permute-done
  59.3 5.2 collective-permute-done.1
  70.0 2.3 collective-permute-done
  72.3 5.2 collective-permute-done.1
  78.7 1.3 fusion.75
  83.0 2.3 collective-permute-done
  85.3 5.2 collective-permute-done.1
  96.0 2.3 collective-permute-done
  98.3 5.2 collective-permute-done.1
  104.8 1.3 fusion.75
  109.0 2.3 collective-permute-done
  111.3 5.2 collective-permute-done.1
  122.0 2.3 collective-permute-done
  124.3 5.2 collective-permute-done.1
  130.8 1.3 fusion.75
  135.6 1.7 collective-permute-done
  137.3 5.2 collective-permute-done.1
  147.1 1.8 collective-permute-start.1
  150.3 5.2 collective-permute-done.1
  160.2 3.0 collective-permute-start.1
  164.1 4.5 collective-permute-done.1
  170.2 1.3 fusion.75
  173.5 3.9 collective-permute-start.1
  178.3 3.6 collective-permute-done.1
  184.4 1.3 fusion.75
  187.8 3.9 collective-permute-start.1
  192.5 3.6 collective-permute-done.1
  198.6 1.3 fusion.75
  202.0 3.9 collective-permute-start.1
  206.8 3.6 collective-permute-done.1
  210.4 1.7 fusion.21
  212.5 1.4 fusion.19
  214.4 1.3 collective-permute-start.2
  215.8 5.6 collective-permute-done.2
  221.3 4.5 convolution_bitcast_fusion.2
  225.9 9.0 copy.54
  237.4 1269.8 %reduce-scatter.4.cloned.1.call-done = f32[32,256]{1,0:T(8,128)} async-done(((f32[8192,256]{1,0:T(8,128)}), f32[32,256]{1,0:T(8,128)}) %reduce-scatter.4.cloned.1.call-update) | async-done | bytes 32784
  (224 shorter events, 82.6 us)
Async XLA Ops:
  7.2 1.7 copy-start.5
  7.2 1500.0 %reduce-scatter.4.cloned.1.call-start = ((), (), s32[]{:S(2)}) async-start(), calls=%async_computation.1 | async-start | bytes 8421376
  8.5 1.8 copy-start.2
  8.8 2.0 copy-start.8
  9.1 2.7 copy-start.6
  9.1 2.7 copy-start.7
  10.4 2.0 copy-start
  13.3 7.9 collective-permute-start
  17.0 8.4 collective-permute-start.1
  26.4 7.0 collective-permute-start
  30.0 8.4 collective-permute-start.1
  39.4 6.9 collective-permute-start
  43.1 8.4 collective-permute-start.1
  52.4 6.9 collective-permute-start
  56.1 8.4 collective-permute-start.1
  65.4 6.9 collective-permute-start
  69.1 8.4 collective-permute-start.1
  78.4 6.9 collective-permute-start
  82.1 8.4 collective-permute-start.1
  91.4 6.9 collective-permute-start
  95.1 8.4 collective-permute-start.1
  104.4 6.9 collective-permute-start
  108.1 8.4 collective-permute-start.1
  117.4 6.9 collective-permute-start
  121.1 8.4 collective-permute-start.1
  130.4 6.9 collective-permute-start
  134.1 8.4 collective-permute-start.1
  143.4 6.9 collective-permute-start
  147.1 8.4 collective-permute-start.1
  156.5 7.6 collective-permute-start
  160.2 8.4 collective-permute-start.1
  169.5 8.8 collective-permute-start
  173.5 8.4 collective-permute-start.1
  182.9 9.7 collective-permute-start
  187.8 8.4 collective-permute-start.1
  197.1 9.7 collective-permute-start
  202.0 8.4 collective-permute-start.1
  210.4 1.7 copy-start.1
  212.5 1.4 copy-start.3
  212.5 8.8 copy-start.4
  214.4 6.9 collective-permute-start.2
Sparse Core Ops, SparseCore 0:
  235.0 1272.1 reduce-scatter.3
where the time goes:
time: 1540 us; the launch traced here: 1510 us
  waiting for transfers between devices  1360 us (88%)
  matrix products  61.4 us (4%)
  starting transfers between devices  29.1 us (2%)
  local copies, waits for them, and re-layouts  27.3 us (2%)
  other arithmetic  17.8 us (1%)
    unnamed x2, waiting for transfers between devices  1270 us
    ppermute x31, waiting for transfers between devices, passed_along(): return lax.ppermute(value, axis, pairs)  93.5 us
  transfers between devices with their start and end apart: 32, of which 26 were waited for; matrix products, arithmetic and copies ran while one was open for 5% of the time, Pallas kernels for 0%

commit v1 on v0

v1 whole, which is shorter than its diff:
```python
import functools
import math

import jax
import jax.numpy as jnp
from jax import lax
from jax.experimental import pallas as pl
from jax.experimental.pallas import tpu as pltpu
from jax.sharding import PartitionSpec as P

F32 = jnp.float32
BF16 = jnp.bfloat16
BLK = 128
H = 8
Z, YL, X, YH, C = 8, 2, 4, 2, 2
CHUNK = 4
VMEM_LIMIT = 48 * 1024 * 1024


def coords(i):
    return (i // 32, i // 16 % 2, i // 4 % 4, i // 2 % 2, i % 2)


def index_of(z, yl, x, yh, c):
    return (((z * YL + yl) * X + x) * YH + yh) * C + c


def fetch(value, shift):
    pairs = [(index_of(*shift(*coords(i))), i) for i in range(Z * YL * X * YH * C)]
    return lax.ppermute(value, ("dp", "ctx"), pairs)


def swap_core(z, yl, x, yh, c):
    return (z, yl, x, yh, 1 - c)


def by_ctx(dx, dyh):
    return lambda z, yl, x, yh, c: (z, yl, (x + dx) % X, yh ^ dyh, c)


def by_x(k):
    return lambda z, yl, x, yh, c: (z, yl, (x + k) % X, yh, c)


def by_y(k):
    def shift(z, yl, x, yh, c):
        y = (2 * yh + yl + k) % 4
        return (z, y % 2, x, y // 2, c)

    return shift


def by_z(bit):
    return lambda z, yl, x, yh, c: (z ^ bit, yl, x, yh, c)


OFFSETS = [(dx, dyh) for dyh in range(YH) for dx in range(X)]


def vmem():
    return pl.BlockSpec(memory_space=pltpu.VMEM)


def smem():
    return pl.BlockSpec(memory_space=pltpu.SMEM)


def prep_kernel(me, x_ref, out_ref, grad_ref, lse_ref, mine_ref, other_ref, stats_ref):
    even = me[0] == 0
    for u in range(8):
        tile = x_ref[:, u * BLK : (u + 1) * BLK].T
        for yh in range(YH):
            first = tile[yh * 64 : yh * 64 + 32]
            second = tile[yh * 64 + 32 : yh * 64 + 64]
            at = slice(u * 64 + yh * 32, u * 64 + yh * 32 + 32)

            @pl.when(even)
            def _():
                mine_ref[at, :] = first
                other_ref[at, :] = second

            @pl.when(jnp.logical_not(even))
            def _():
                mine_ref[at, :] = second
                other_ref[at, :] = first

    @pl.when(pl.program_id(0) == 0)
    def _():
        stats_ref[...] = jnp.zeros_like(stats_ref)
        for h in range(H):
            cols = slice(h * BLK, (h + 1) * BLK)
            product = out_ref[:, cols].astype(F32) * grad_ref[:, cols].astype(F32)
            delta = jnp.sum(product.T, axis=0, keepdims=True)
            lse2 = lse_ref[h : h + 1, :] * math.log2(math.e)
            for i in range(2):
                rows = slice(i * BLK, (i + 1) * BLK)
                stats_ref[i : i + 1, cols] = lse2[:, rows]
                stats_ref[2 + i : 3 + i, cols] = delta[:, rows]


def prep(me, layer, saved, grad, lse):
    whole = lambda shape: pl.BlockSpec(shape, lambda z: (0,) * len(shape))
    return pl.pallas_call(
        prep_kernel,
        grid=(Z,),
        out_shape=(
            jax.ShapeDtypeStruct((4096, 256), BF16),
            jax.ShapeDtypeStruct((4096, 256), BF16),
            jax.ShapeDtypeStruct((8, H * BLK), F32),
        ),
        in_specs=[
            smem(),
            pl.BlockSpec((256, 1024), lambda z: (0, z)),
            whole((256, H * BLK)),
            whole((256, H * BLK)),
            whole((H, 256)),
        ],
        out_specs=(
            pl.BlockSpec((512, 256), lambda z: (z, 0)),
            pl.BlockSpec((512, 256), lambda z: (z, 0)),
            whole((8, H * BLK)),
        ),
        compiler_params=pltpu.CompilerParams(vmem_limit_bytes=VMEM_LIMIT),
        cost_estimate=pl.CostEstimate(flops=10**7, bytes_accessed=10 * 2**20, transcendentals=0),
        name="prep",
    )(me, layer, saved, grad, lse)


NQ, NK = 4, 16


def attn_kernel(meta, *refs):
    q_in, g_in, s_in = refs[0:2], refs[2:4], refs[4:6]
    kv_in = refs[6:14]
    dq_own, dq_other = refs[14:16]
    dkv_out = refs[16:24]
    q_all, g_all, qt, gt, kv, kt, dqt, dkv, stats = refs[24:]
    rows_all = H * BLK
    scale = BLK**-0.5
    factor = scale * math.log2(math.e)
    dkv[...] = jnp.zeros_like(dkv)
    for side in range(2):
        for i in range(2):
            n = 2 * side + i
            rows = slice(i * BLK, (i + 1) * BLK)
            q_all[n] = q_in[side][rows, :]
            g_all[n] = g_in[side][rows, :]
            stats[n : n + 1, :] = s_in[side][i : i + 1, :]
            stats[NQ + n : NQ + n + 1, :] = s_in[side][2 + i : 3 + i, :]

    def turn(n, carry):
        for h in range(H):
            cols = slice(h * BLK, (h + 1) * BLK)
            qt[n, :, cols] = q_all[n, :, cols].T
            gt[n, :, cols] = g_all[n, :, cols].T
        return carry

    lax.fori_loop(0, NQ, turn, 0)
    for b in range(8):
        for i in range(2):
            block = kv_in[b][i * BLK : (i + 1) * BLK, :]
            kv[2 * b + i] = block
            kt[2 * b + i] = block[:, :BLK].T

    keys = CHUNK * BLK

    def chunk(i, j, masked):
        at = [meta[j * CHUNK + n] for n in range(CHUNK)]
        kb = jnp.concatenate([kv[a, :, :BLK] for a in at], 0)
        vb = jnp.concatenate([kv[a, :, BLK:] for a in at], 0)
        ktb = jnp.concatenate([kt[a] for a in at], 1)
        if masked:
            q_pos = meta[2 * NK + i]
            u = lax.broadcasted_iota(jnp.int32, (BLK, 2 * BLK), 0)
            t = lax.broadcasted_iota(jnp.int32, (BLK, 2 * BLK), 1) % BLK
            ahead = t - u
            visible = [ahead >= (meta[NK + j * CHUNK + n] - q_pos) * BLK for n in range(CHUNK)]
        dv = jnp.zeros((keys, BLK), F32)
        dk = jnp.zeros((keys, BLK), F32)
        for pair in range(H // 2):
            cols = slice(pair * 2 * BLK, (pair + 1) * 2 * BLK)
            heads = [slice((2 * pair + g) * BLK, (2 * pair + g + 1) * BLK) for g in range(2)]
            score = jnp.dot(kb, qt[i, :, cols], preferred_element_type=F32)
            prob = jnp.exp2(score * factor - stats[pl.ds(i, 1), cols])
            if masked:
                prob = jnp.concatenate(
                    [
                        jnp.where(visible[n], prob[n * BLK : (n + 1) * BLK], 0.0)
                        for n in range(CHUNK)
                    ],
                    0,
                )
            d_prob = jnp.dot(vb, gt[i, :, cols], preferred_element_type=F32)
            d_score = (prob * (d_prob - stats[pl.ds(NQ + i, 1), cols])).astype(BF16)
            g_rows = jnp.concatenate([g_all[i, :, s] for s in heads], 0)
            q_rows = jnp.concatenate([q_all[i, :, s] for s in heads], 0)
            dv = dv + jnp.dot(prob.astype(BF16), g_rows, preferred_element_type=F32)
            dk = dk + jnp.dot(d_score, q_rows, preferred_element_type=F32)
            dqt[:, cols] += jnp.dot(ktb, d_score, preferred_element_type=F32)
        for n in range(CHUNK):
            dkv[at[n], :, :BLK] += dk[n * BLK : (n + 1) * BLK]
            dkv[at[n], :, BLK:] += dv[n * BLK : (n + 1) * BLK]

    def query_block(i, carry):
        dqt[...] = jnp.zeros_like(dqt)
        whole = meta[2 * NK + NQ + i]
        some = meta[2 * NK + 2 * NQ + i]

        def full_step(j, c):
            chunk(i, j, False)
            return c

        def masked_step(j, c):
            chunk(i, j, True)
            return c

        lax.fori_loop(0, whole, full_step, 0)
        lax.fori_loop(whole, some, masked_step, 0)
        rows = pl.ds(pl.multiple_of(i % 2 * BLK, BLK), BLK)

        def store(ref):
            for h in range(H):
                cols = slice(h * BLK, (h + 1) * BLK)
                ref[rows, cols] = (dqt[:, cols].T * scale).astype(ref.dtype)

        @pl.when(i < 2)
        def _():
            store(dq_own)

        @pl.when(i >= 2)
        def _():
            store(dq_other)

        return carry

    lax.fori_loop(0, NQ, query_block, 0)
    for b in range(8):
        for i in range(2):
            rows = slice(i * BLK, (i + 1) * BLK)
            ref = dkv_out[b]
            ref[rows, :BLK] = (dkv[2 * b + i, :, :BLK] * scale).astype(ref.dtype)
            ref[rows, BLK:] = dkv[2 * b + i, :, BLK:].astype(ref.dtype)


def attention(meta, queries, grads, stats, blocks):
    wide = H * BLK
    return pl.pallas_call(
        attn_kernel,
        out_shape=(
            jax.ShapeDtypeStruct((256, wide), F32),
            jax.ShapeDtypeStruct((256, wide), BF16),
            jax.ShapeDtypeStruct((256, 256), F32),
        )
        + (jax.ShapeDtypeStruct((256, 256), BF16),) * 7,
        in_specs=[smem()] + [vmem()] * 14,
        out_specs=(vmem(),) * 10,
        scratch_shapes=[
            pltpu.VMEM((NQ, BLK, wide), BF16),
            pltpu.VMEM((NQ, BLK, wide), BF16),
            pltpu.VMEM((NQ, BLK, wide), BF16),
            pltpu.VMEM((NQ, BLK, wide), BF16),
            pltpu.VMEM((NK, BLK, 2 * BLK), BF16),
            pltpu.VMEM((NK, BLK, BLK), BF16),
            pltpu.VMEM((BLK, wide), F32),
            pltpu.VMEM((NK, BLK, 2 * BLK), F32),
            pltpu.VMEM((2 * NQ, wide), F32),
        ],
        compiler_params=pltpu.CompilerParams(vmem_limit_bytes=VMEM_LIMIT),
        cost_estimate=pl.CostEstimate(
            flops=12 * 10**9, bytes_accessed=8 * 2**20, transcendentals=4 * 10**6
        ),
        name="attention",
    )(meta, *queries, *grads, *stats, *blocks)


def make_meta(k_pos, q_pos):
    order = jnp.argsort(k_pos).astype(jnp.int32)
    below = jnp.sum(k_pos[None, :] < q_pos[:, None], axis=1)
    reached = jnp.sum(k_pos[None, :] <= q_pos[:, None], axis=1)
    return jnp.concatenate(
        [order, k_pos[order], q_pos, below // CHUNK, (reached + CHUNK - 1) // CHUNK]
    ).astype(jnp.int32)


def project_kernel(place, mine_ref, other_ref, g_own, g_other, *refs):
    by_x_out, by_y_out = refs[0:4], refs[4:8]
    terms = refs[8]
    x, y = place[0], place[1]

    def step(z, carry):
        rows = pl.ds(pl.multiple_of(z * 512, 512), 512)
        terms[...] = jnp.dot(
            mine_ref[rows, :], g_own[...], preferred_element_type=F32
        ) + jnp.dot(other_ref[rows, :], g_other[...], preferred_element_type=F32)
        for k in range(4):
            x_to = (x + k) % 4
            for yl in range(YL):
                part = terms[pl.ds(pl.multiple_of(yl * 256 + x_to * 64, 64), 64), :BLK]
                at = pl.ds(pl.multiple_of(z * 128 + yl * 64, 64), 64)
                by_x_out[k][at, :] = part.astype(by_x_out[k].dtype)
            y_to = (y + k) % 4
            for xx in range(X):
                source = pl.multiple_of((y_to % 2) * 256 + xx * 64 + (y_to // 2) * 32, 32)
                part = terms[pl.ds(source, 32), BLK:]
                at = pl.ds(pl.multiple_of(z * 128 + xx * 32, 32), 32)
                by_y_out[k][at, :] = part.astype(by_y_out[k].dtype)
        return carry

    lax.fori_loop(0, Z, step, 0)


def project(place, mine, other, g_own, g_other):
    kept = jax.ShapeDtypeStruct((1024, BLK), F32)
    sent = jax.ShapeDtypeStruct((1024, BLK), BF16)
    return pl.pallas_call(
        project_kernel,
        out_shape=(kept, sent, sent, sent) * 2,
        in_specs=[smem()] + [vmem()] * 4,
        out_specs=(vmem(),) * 8,
        scratch_shapes=[pltpu.VMEM((512, 256), F32)],
        compiler_params=pltpu.CompilerParams(vmem_limit_bytes=VMEM_LIMIT),
        cost_estimate=pl.CostEstimate(
            flops=2 * 4096 * 512 * 256, bytes_accessed=8 * 2**20, transcendentals=0
        ),
        name="project",
    )(place, mine, other, g_own, g_other)


def second_kernel(place, *refs):
    a_in, b_in, a_out, b_out = refs[0:4], refs[4:8], refs[8:12], refs[12:16]
    a_sum, b_sum = refs[16:18]
    x, y = place[0], place[1]

    def total(parts):
        value = parts[0][...]
        for part in parts[1:]:
            value = value + part[...].astype(F32)
        return value

    a_sum[...] = total(a_in)
    b_sum[...] = total(b_in)
    for k in range(4):
        y_to = (y + k) % 4
        x_to = (x + k) % 4
        for z in range(Z):
            at = slice(z * 32, (z + 1) * 32)
            source = pl.multiple_of(z * 128 + (y_to % 2) * 64 + (y_to // 2) * 32, 32)
            a_out[k][at, :] = a_sum[pl.ds(source, 32), :].astype(a_out[k].dtype)
            source = pl.multiple_of(z * 128 + x_to * 32, 32)
            b_out[k][at, :] = b_sum[pl.ds(source, 32), :].astype(b_out[k].dtype)


def second(place, a_parts, b_parts):
    kept = jax.ShapeDtypeStruct((256, BLK), F32)
    sent = jax.ShapeDtypeStruct((256, BLK), BF16)
    return pl.pallas_call(
        second_kernel,
        out_shape=(kept, sent, sent, sent) * 2,
        in_specs=[smem()] + [vmem()] * 8,
        out_specs=(vmem(),) * 8,
        scratch_shapes=[pltpu.VMEM((1024, BLK), F32)] * 2,
        compiler_params=pltpu.CompilerParams(vmem_limit_bytes=VMEM_LIMIT),
        name="second",
    )(place, *a_parts, *b_parts)


def body(layer_input, query_rows, key_rows, value_rows, attn_out, d_attn, log_sum_exp, block_order):
    dp = lax.axis_index("dp")
    ctx = lax.axis_index("ctx")
    z, yl = dp // 2, dp % 2
    x, yh, c = ctx // 4, ctx // 2 % 2, ctx % 2
    y = 2 * yh + yl
    place = jnp.stack([x, y]).astype(jnp.int32)

    pair = jnp.concatenate([key_rows[0], value_rows[0]], axis=1)
    blocks = [pair] + [fetch(pair, by_ctx(*o)) for o in OFFSETS[1:]]
    q, g = query_rows[0], d_attn[0]
    q_other, g_other = fetch(q, swap_core), fetch(g, swap_core)
    mine, other, stats = prep(
        c.astype(jnp.int32)[None], layer_input[0], attn_out[0], g, log_sum_exp[0]
    )
    stats_other = fetch(stats, swap_core)
    mine_other = fetch(other, swap_core)

    owners = jnp.stack([(x + dx) % X * 4 + (yh ^ dyh) * 2 + c for dx, dyh in OFFSETS])
    slots = jnp.stack([2 * owners, 2 * owners + 1], axis=1).reshape(-1)
    q_slots = jnp.stack([2 * ctx, 2 * ctx + 1, 2 * (ctx ^ 1), 2 * (ctx ^ 1) + 1])
    meta = make_meta(block_order[slots], block_order[q_slots])
    dq_own, dq_sent, *dkv = attention(
        meta, (q, q_other), (g, g_other), (stats, stats_other), blocks
    )
    d_query = (dq_own + fetch(dq_sent, swap_core).astype(F32)).astype(BF16)[None]

    total = dkv[0]
    for (dx, dyh), part in zip(OFFSETS[1:], dkv[1:]):
        total = total + fetch(part, by_ctx(-dx, dyh)).astype(F32)
    grads = total.astype(BF16)
    grads_other = fetch(grads, swap_core)

    parts = project(place, mine, mine_other, grads, grads_other)
    a = [parts[0]] + [fetch(parts[k], by_x(-k)) for k in (1, 2, 3)]
    b = [parts[4]] + [fetch(parts[4 + k], by_y(-k)) for k in (1, 2, 3)]
    parts = second(place, a, b)
    a_sum, b_sum = parts[0], parts[4]
    for k in (1, 2, 3):
        a_sum = a_sum + fetch(parts[k], by_y(-k)).astype(F32)
        b_sum = b_sum + fetch(parts[4 + k], by_x(-k)).astype(F32)
    rest = jnp.concatenate([a_sum, b_sum], axis=1).reshape(4, 2, 32, 256)
    for bit in (1, 2, 4):
        own = (z // bit) % 2
        keep = lax.dynamic_index_in_dim(rest, own, 1, False)
        send = lax.dynamic_index_in_dim(rest, 1 - own, 1, False)
        rest = keep + fetch(send, by_z(bit))
        if bit < 4:
            rest = rest.reshape(rest.shape[0] // 2, 2, 32, 256)
    return (d_query, rest.reshape(32, 256))


def solution(mesh):
    return jax.shard_map(
        body,
        mesh=mesh,
        in_specs=(
            P("dp", "ctx", None),
            P("dp", "ctx", None),
            P("dp", "ctx", None),
            P("dp", "ctx", None),
            P("dp", "ctx", None),
            P("dp", "ctx", None),
            P("dp", None, "ctx"),
            P(),
        ),
        out_specs=(P("dp", "ctx", None), P(("dp", "ctx"), None)),
        check_vma=False,
    )
```

time: 1540 us -> 162 us (0.11); the launches traced: 1510 us -> 164 us
  waiting for transfers between devices: 1360 us -> 45.2 us
  matrix products: 61.4 us -> 0 us
  Pallas kernels: 0 us -> 34 us
  starting transfers between devices: 29.1 us -> 61.2 us
    unnamed x2 -> x0, waiting for transfers between devices: 1270 us -> none
    dot_general x81 -> x0, matrix products: 61.4 us -> none  [the longest x16 20.8 us: tile(): jnp.einsum('rhd,sd->hrs', queries, keys, preferred_element_type=jnp.float32)]
    ppermute x31 -> x35, waiting for transfers between devices: 93.5 us -> 45.2 us  [fetch(): return lax.ppermute(value, ('dp', 'ctx'), pairs)]
    pallas_call x0 -> x4, Pallas kernels: none -> 34 us  [the longest x1 20.4 us: attention(): pl.pallas_call(attn_kernel, out_shape=(jax.ShapeDtypeStruct((256, wide),...]
    ppermute x31 -> x35, starting transfers between devices: 29.1 us -> 61.2 us  [fetch(): return lax.ppermute(value, ('dp', 'ctx'), pairs)]
  transfers between devices with their start and end apart: 32 -> 35, of which waited for: 26 -> 20; matrix products, arithmetic and copies ran while one was open for 5% -> 3% of each run, Pallas kernels for 0% -> 18%
where the time goes in v1:
time: 162 us; the launch traced here: 164 us
  starting transfers between devices  61.2 us (38%)
  waiting for transfers between devices  45.2 us (28%)
  Pallas kernels  34 us (21%)
  local copies, waits for them, and re-layouts  18 us (11%)
  other arithmetic  4.34 us (3%)
    ppermute x35, starting transfers between devices, fetch(): return lax.ppermute(value, ('dp', 'ctx'), pairs)  61.2 us
    ppermute x35, waiting for transfers between devices, fetch(): return lax.ppermute(value, ('dp', 'ctx'), pairs)  45.2 us
    pallas_call x1, Pallas kernels, attention(): pl.pallas_call(attn_kernel, out_shape=(jax.ShapeDtypeStruct((256, wide),...  20.4 us
    unnamed x40, local copies, waits for them, and re-layouts  15.6 us
    pallas_call x1, Pallas kernels, prep(): pl.pallas_call(prep_kernel, grid=(Z,), out_shape=(jax.ShapeDtypeStruct((4...  8.41 us
    pallas_call x1, Pallas kernels, project(): pl.pallas_call(project_kernel, out_shape=(kept, sent, sent, sent) * 2, in...  4.24 us
  transfers between devices with their start and end apart: 35, of which 20 were waited for; matrix products, arithmetic and copies ran while one was open for 3% of the time, Pallas kernels for 18%

profile of v1, /device:TPU:4, one launch (start us, length us, event | category | flops | bytes accessed | tf_op | source)
XLA Modules:
  0.0 163.6 jit_solution(11646515024101224388)
XLA Ops:
  2.2 2.7 %collective-permute-start.4 = (bf16[256,256]{1,0:T(8,128)(2,1)S(1)}, bf16[256,256]{1,0:T(8,128)(2,1)S(1)}, u32[]{:S(2)}, u32[]{:S(2)}) collective-permute-start(bf16[256,256]{1,0:T(8,128)(2,1)S(1)} %pad_maximum_fusion.1.refs_6_), channel_id=1, source_target_pairs={{8,0},{9,1},{10,2},{11,3},{12,4},{13,5},{14,6},{15,7},{0,8},{1,9},... | collective-permute-start | bytes 393224 | tf_op jit(solution)/shard_map/ppermute | solution.py:30
  4.9 1.6 collective-permute-start.5
  6.5 1.0 copy-done.1
  7.5 1.0 copy-done.2
  9.3 8.4 %prep.1 = (bf16[4096,256]{1,0:T(8,128)(2,1)S(1)}, bf16[4096,256]{1,0:T(8,128)(2,1)S(1)}, f32[8,1024]{1,0:T(8,128)}) custom-call(s32[1]{0:T(128)} %bitcast.16.me, bf16[256,8192]{1,0:T(8,128)(2,1)} %bitcast.47, bf16[256,1024]{1,0:T(8,128)(2,1)S(1)} %bitcast.40, bf16[256,1024]{1,0:T(8,128)(2,1)S(1)} %bitcast.42, f32[8,256]{1,0:T(8,128)S(1)} %bitcast.44), custom_call_target="tpu_custom_call" | custom-call | flops 10000000 | bytes 10485760 | tf_op jit(solution)/shard_map/prep/pallas_call | solution.py:103
  17.7 1.3 copy-done.5
  20.5 1.3 sort.17
  22.5 1.6 collective-permute-start.6
  24.1 1.8 %collective-permute-start.7 = (bf16[256,256]{1,0:T(8,128)(2,1)S(1)}, bf16[256,256]{1,0:T(8,128)(2,1)S(1)}, u32[]{:S(2)}, u32[]{:S(2)}) collective-permute-start(bf16[256,256]{1,0:T(8,128)(2,1)S(1)} %pad_maximum_fusion.1.refs_6_), channel_id=1, source_target_pairs={{6,0},{7,1},{4,2},{5,3},{10,4},{11,5},{8,6},{9,7},{14,8},{15,9},{1... | collective-permute-start | bytes 393224 | tf_op jit(solution)/shard_map/ppermute | solution.py:30
  27.5 5.3 %collective-permute-done.6.refs_10_ = bf16[256,256]{1,0:T(8,128)(2,1)S(1)} collective-permute-done((bf16[256,256]{1,0:T(8,128)(2,1)S(1)}, bf16[256,256]{1,0:T(8,128)(2,1)S(1)}, u32[]{:S(2)}, u32[]{:S(2)}) %collective-permute-start.6) | collective-permute-done | bytes 131104 | tf_op jit(solution)/shard_map/ppermute | solution.py:30
  33.4 2.7 %collective-permute-start.8 = (bf16[256,256]{1,0:T(8,128)(2,1)S(1)}, bf16[256,256]{1,0:T(8,128)(2,1)S(1)}, u32[]{:S(2)}, u32[]{:S(2)}) collective-permute-start(bf16[256,256]{1,0:T(8,128)(2,1)S(1)} %pad_maximum_fusion.1.refs_6_), channel_id=1, source_target_pairs={{10,0},{11,1},{8,2},{9,3},{14,4},{15,5},{12,6},{13,7},{2,8},{3,9},... | collective-permute-start | bytes 393224 | tf_op jit(solution)/shard_map/ppermute | solution.py:30
  36.8 1.4 collective-permute-start.9
  38.3 4.3 %collective-permute-done.8.refs_12_ = bf16[256,256]{1,0:T(8,128)(2,1)S(1)} collective-permute-done((bf16[256,256]{1,0:T(8,128)(2,1)S(1)}, bf16[256,256]{1,0:T(8,128)(2,1)S(1)}, u32[]{:S(2)}, u32[]{:S(2)}) %collective-permute-start.8) | collective-permute-done | bytes 131104 | tf_op jit(solution)/shard_map/ppermute | solution.py:30
  43.2 2.1 %collective-permute-done.9.refs_13_ = bf16[256,256]{1,0:T(8,128)(2,1)S(1)} collective-permute-done((bf16[256,256]{1,0:T(8,128)(2,1)S(1)}, bf16[256,256]{1,0:T(8,128)(2,1)S(1)}, u32[]{:S(2)}, u32[]{:S(2)}) %collective-permute-start.9) | collective-permute-done | bytes 131104 | tf_op jit(solution)/shard_map/ppermute | solution.py:30
  46.7 1.0 copy-done.3
  47.8 1.0 copy-done.6
  48.8 1.0 copy-done.9
  54.2 20.4 %attention.1 = (f32[256,1024]{1,0:T(8,128)S(1)}, bf16[256,1024]{1,0:T(8,128)(2,1)S(1)}, f32[256,256]{1,0:T(8,128)S(1)}, bf16[256,256]{1,0:T(8,128)(2,1)S(1)}, bf...) custom-call(s32[44]{0:T(128)S(1)} %concatenate.39.meta, ...), custom_call_target="tpu_custom_call" | custom-call | flops 12000000000 | bytes 8388608 | tf_op jit(solution)/shard_map/attention/pallas_call | solution.py:247
  74.7 5.8 %collective-permute-start.17 = (bf16[256,256]{1,0:T(8,128)(2,1)S(1)}, bf16[256,256]{1,0:T(8,128)(2,1)S(1)}, u32[]{:S(2)}, u32[]{:S(2)}) collective-permute-start(bf16[256,256]{1,0:T(8,128)(2,1)S(1)} %get-tuple-element.44), channel_id=1, source_target_pairs={{10,0},{11,1},{8,2},{9,3},{14,4},{15,5},{12,6},{13,7},{2,8},{3,9},... | collective-permute-start | bytes 393224 | tf_op jit(solution)/shard_map/ppermute | solution.py:30
  80.5 1.1 collective-permute-start.15
  82.0 3.4 %collective-permute-start.14 = (bf16[256,256]{1,0:T(8,128)(2,1)S(1)}, bf16[256,256]{1,0:T(8,128)(2,1)S(1)}, u32[]{:S(2)}, u32[]{:S(2)}) collective-permute-start(bf16[256,256]{1,0:T(8,128)(2,1)S(1)} %get-tuple-element.41), channel_id=1, source_target_pairs={{4,0},{5,1},{6,2},{7,3},{8,4},{9,5},{10,6},{11,7},{12,8},{13,9},{1... | collective-permute-start | bytes 393224 | tf_op jit(solution)/shard_map/ppermute | solution.py:30
  85.5 7.8 %collective-permute-start.13 = (bf16[256,256]{1,0:T(8,128)(2,1)S(1)}, bf16[256,256]{1,0:T(8,128)(2,1)S(1)}, u32[]{:S(2)}, u32[]{:S(2)}) collective-permute-start(bf16[256,256]{1,0:T(8,128)(2,1)S(1)} %get-tuple-element.40), channel_id=1, source_target_pairs={{8,0},{9,1},{10,2},{11,3},{12,4},{13,5},{14,6},{15,7},{0,8},{1,9},... | collective-permute-start | bytes 393224 | tf_op jit(solution)/shard_map/ppermute | solution.py:30
  93.9 1.6 collective-permute-done.14
  95.5 2.0 %collective-permute-done.13 = bf16[256,256]{1,0:T(8,128)(2,1)S(1)} collective-permute-done((bf16[256,256]{1,0:T(8,128)(2,1)S(1)}, bf16[256,256]{1,0:T(8,128)(2,1)S(1)}, u32[]{:S(2)}, u32[]{:S(2)}) %collective-permute-start.13) | collective-permute-done | bytes 131104 | tf_op jit(solution)/shard_map/ppermute | solution.py:30
  97.5 2.3 %collective-permute-done.12 = bf16[256,256]{1,0:T(8,128)(2,1)S(1)} collective-permute-done((bf16[256,256]{1,0:T(8,128)(2,1)S(1)}, bf16[256,256]{1,0:T(8,128)(2,1)S(1)}, u32[]{:S(2)}, u32[]{:S(2)}) %collective-permute-start.12) | collective-permute-done | bytes 131104 | tf_op jit(solution)/shard_map/ppermute | solution.py:30
  100.1 1.2 collective-permute-done.19.g_other
  101.4 4.2 %project.1 = (f32[1024,128]{1,0:T(8,128)S(1)}, bf16[1024,128]{1,0:T(8,128)(2,1)S(1)}, bf16[1024,128]{1,0:T(8,128)(2,1)S(1)}, bf16[1024,128]{1,0:T(8,128)(2,1)S(1...) custom-call(s32[2]{0:T(128)S(1)} %pad_add_fusion.1.place, ...), custom_call_target="tpu_custom_call" | custom-call | flops 1073741824 | bytes 8388608 | tf_op jit(solution)/shard_map/project/pallas_call | solution.py:315
  105.6 1.9 %collective-permute-start.20 = (bf16[1024,128]{1,0:T(8,128)(2,1)S(1)}, bf16[1024,128]{1,0:T(8,128)(2,1)S(1)}, u32[]{:S(2)}, u32[]{:S(2)}) collective-permute-start(bf16[1024,128]{1,0:T(8,128)(2,1)S(1)} %get-tuple-element.47), channel_id=1, source_target_pairs={{12,0},{13,1},{14,2},{15,3},{0,4},{1,5},{2,6},{3,7},{4,8},{5,9},{6... | collective-permute-start | bytes 786440 | tf_op jit(solution)/shard_map/ppermute | solution.py:30
  107.5 1.3 collective-permute-start.21
  108.8 2.5 %collective-permute-start.22 = (bf16[1024,128]{1,0:T(8,128)(2,1)S(1)}, bf16[1024,128]{1,0:T(8,128)(2,1)S(1)}, u32[]{:S(2)}, u32[]{:S(2)}) collective-permute-start(bf16[1024,128]{1,0:T(8,128)(2,1)S(1)} %get-tuple-element.49), channel_id=1, source_target_pairs={{4,0},{5,1},{6,2},{7,3},{8,4},{9,5},{10,6},{11,7},{12,8},{13,9},{1... | collective-permute-start | bytes 786440 | tf_op jit(solution)/shard_map/ppermute | solution.py:30
  112.1 2.1 %collective-permute-done.20.refs_1_ = bf16[1024,128]{1,0:T(8,128)(2,1)S(1)} collective-permute-done((bf16[1024,128]{1,0:T(8,128)(2,1)S(1)}, bf16[1024,128]{1,0:T(8,128)(2,1)S(1)}, u32[]{:S(2)}, u32[]{:S(2)}) %collective-permute-start.20) | collective-permute-done | bytes 262176 | tf_op jit(solution)/shard_map/ppermute | solution.py:30
  114.7 6.2 %collective-permute-done.21.refs_2_ = bf16[1024,128]{1,0:T(8,128)(2,1)S(1)} collective-permute-done((bf16[1024,128]{1,0:T(8,128)(2,1)S(1)}, bf16[1024,128]{1,0:T(8,128)(2,1)S(1)}, u32[]{:S(2)}, u32[]{:S(2)}) %collective-permute-start.21) | collective-permute-done | bytes 262176 | tf_op jit(solution)/shard_map/ppermute | solution.py:30
  121.9 3.8 %collective-permute-done.23.refs_5_ = bf16[1024,128]{1,0:T(8,128)(2,1)S(1)} collective-permute-done((bf16[1024,128]{1,0:T(8,128)(2,1)S(1)}, bf16[1024,128]{1,0:T(8,128)(2,1)S(1)}, u32[]{:S(2)}, u32[]{:S(2)}) %collective-permute-start.23) | collective-permute-done | bytes 262176 | tf_op jit(solution)/shard_map/ppermute | solution.py:30
  126.3 0.9 second.1
  127.7 4.9 %collective-permute-start.30 = (bf16[256,128]{1,0:T(8,128)(2,1)S(1)}, bf16[256,128]{1,0:T(8,128)(2,1)S(1)}, u32[]{:S(2)}, u32[]{:S(2)}) collective-permute-start(bf16[256,128]{1,0:T(8,128)(2,1)S(1)} %get-tuple-element.60), channel_id=1, source_target_pairs={{8,0},{9,1},{10,2},{11,3},{12,4},{13,5},{14,6},{15,7},{0,8},{1,9},... | collective-permute-start | bytes 196616 | tf_op jit(solution)/shard_map/ppermute | solution.py:30
  132.6 2.5 %collective-permute-start.29 = (bf16[256,128]{1,0:T(8,128)(2,1)S(1)}, bf16[256,128]{1,0:T(8,128)(2,1)S(1)}, u32[]{:S(2)}, u32[]{:S(2)}) collective-permute-start(bf16[256,128]{1,0:T(8,128)(2,1)S(1)} %get-tuple-element.59), channel_id=1, source_target_pairs={{12,0},{13,1},{14,2},{15,3},{0,4},{1,5},{2,6},{3,7},{4,8},{5,9},{6... | collective-permute-start | bytes 196616 | tf_op jit(solution)/shard_map/ppermute | solution.py:30
  135.1 1.5 collective-permute-start.28
  136.6 1.2 collective-permute-start.27
  137.9 1.5 collective-permute-done.28
  139.4 3.0 %collective-permute-done.27 = bf16[256,128]{1,0:T(8,128)(2,1)S(1)} collective-permute-done((bf16[256,128]{1,0:T(8,128)(2,1)S(1)}, bf16[256,128]{1,0:T(8,128)(2,1)S(1)}, u32[]{:S(2)}, u32[]{:S(2)}) %collective-permute-start.27) | collective-permute-done | bytes 65568 | tf_op jit(solution)/shard_map/ppermute | solution.py:30
  142.4 1.0 collective-permute-done.26
  143.4 2.0 %collective-permute-start.32 = (f32[4,32,256]{2,1,0:T(8,128)S(1)}, f32[4,32,256]{2,1,0:T(8,128)S(1)}, u32[]{:S(2)}, u32[]{:S(2)}) collective-permute-start(f32[4,32,256]{2,1,0:T(8,128)S(1)} %dynamic-slice_bitcast_fusion), channel_id=1, source_target_pairs={{32,0},{33,1},{34,2},{35,3},{36,4},{37,5},{38,6},{39,7},{40,8},{41... | collective-permute-start | bytes 393224 | tf_op jit(solution)/shard_map/ppermute | solution.py:30
  145.4 3.0 %collective-permute-done.32 = f32[4,32,256]{2,1,0:T(8,128)S(1)} collective-permute-done((f32[4,32,256]{2,1,0:T(8,128)S(1)}, f32[4,32,256]{2,1,0:T(8,128)S(1)}, u32[]{:S(2)}, u32[]{:S(2)}) %collective-permute-start.32) | collective-permute-done | bytes 131104 | tf_op jit(solution)/shard_map/ppermute | solution.py:30
  148.5 4.1 %collective-permute-start.33 = (f32[2,32,256]{2,1,0:T(8,128)S(1)}, f32[2,32,256]{2,1,0:T(8,128)S(1)}, u32[]{:S(2)}, u32[]{:S(2)}) collective-permute-start(f32[2,32,256]{2,1,0:T(8,128)S(1)} %dynamic-slice_bitcast_fusion.1), channel_id=1, source_target_pairs={{64,0},{65,1},{66,2},{67,3},{68,4},{69,5},{70,6},{71,7},{72,8},{73... | collective-permute-start | bytes 196616 | tf_op jit(solution)/shard_map/ppermute | solution.py:30
  152.6 2.2 %collective-permute-done.33 = f32[2,32,256]{2,1,0:T(8,128)S(1)} collective-permute-done((f32[2,32,256]{2,1,0:T(8,128)S(1)}, f32[2,32,256]{2,1,0:T(8,128)S(1)}, u32[]{:S(2)}, u32[]{:S(2)}) %collective-permute-start.33) | collective-permute-done | bytes 65568 | tf_op jit(solution)/shard_map/ppermute | solution.py:30
  154.9 6.2 %collective-permute-start.34 = (f32[1,32,256]{2,1,0:T(8,128)S(1)}, f32[1,32,256]{2,1,0:T(8,128)S(1)}, u32[]{:S(2)}, u32[]{:S(2)}) collective-permute-start(f32[1,32,256]{2,1,0:T(8,128)S(1)} %constant_dynamic-slice_fusion), channel_id=1, source_target_pairs={{128,0},{129,1},{130,2},{131,3},{132,4},{133,5},{134,6},{135,7},{1... | collective-permute-start | bytes 98312 | tf_op jit(solution)/shard_map/ppermute | solution.py:30
  161.1 0.9 fusion
  162.1 0.9 collective-permute-done.34
  (98 shorter events, 19.2 us)
Async XLA Ops:
  0.6 19.2 %copy-start = (s32[32]{0:T(128)S(1)}, s32[32]{0:T(128)}, u32[]{:S(2)}) copy-start(s32[32]{0:T(128)} %param.15) | copy-start | bytes 388
  1.5 21.0 %collective-permute-start.3 = (bf16[256,256]{1,0:T(8,128)(2,1)S(1)}, bf16[256,256]{1,0:T(8,128)(2,1)S(1)}, u32[]{:S(2)}, u32[]{:S(2)}) collective-permute-start(bf16[256,256]{1,0:T(8,128)(2,1)S(1)} %pad_maximum_fusion.1.refs_6_), channel_id=1, source_target_pairs={{4,0},{5,1},{6,2},{7,3},{8,4},{9,5},{10,6},{11,7},{12,8},{13,9},{1... | collective-permute-start | bytes 393224 | tf_op jit(solution)/shard_map/ppermute | solution.py:30
  2.2 22.0 %collective-permute-start.4 = (bf16[256,256]{1,0:T(8,128)(2,1)S(1)}, bf16[256,256]{1,0:T(8,128)(2,1)S(1)}, u32[]{:S(2)}, u32[]{:S(2)}) collective-permute-start(bf16[256,256]{1,0:T(8,128)(2,1)S(1)} %pad_maximum_fusion.1.refs_6_), channel_id=1, source_target_pairs={{8,0},{9,1},{10,2},{11,3},{12,4},{13,5},{14,6},{15,7},{0,8},{1,9},... | collective-permute-start | bytes 393224 | tf_op jit(solution)/shard_map/ppermute | solution.py:30
  4.9 22.4 %collective-permute-start.5 = (bf16[256,256]{1,0:T(8,128)(2,1)S(1)}, bf16[256,256]{1,0:T(8,128)(2,1)}, u32[]{:S(2)}, u32[]{:S(2)}) collective-permute-start(bf16[256,256]{1,0:T(8,128)(2,1)S(1)} %pad_maximum_fusion.1.refs_6_), channel_id=1, source_target_pairs={{12,0},{13,1},{14,2},{15,3},{0,4},{1,5},{2,6},{3,7},{4,8},{5,9},{6... | collective-permute-start | bytes 393224 | tf_op jit(solution)/shard_map/ppermute | solution.py:30
  6.5 40.2 %collective-permute-start.1 = (bf16[256,1024]{1,0:T(8,128)(2,1)}, bf16[256,1024]{1,0:T(8,128)(2,1)}, u32[]{:S(2)}, u32[]{:S(2)}) collective-permute-start(bf16[256,1024]{1,0:T(8,128)(2,1)} %bitcast.41), channel_id=1, source_target_pairs={{1,0},{0,1},{3,2},{2,3},{5,4},{4,5},{7,6},{6,7},{9,8},{8,9},{11,10... | collective-permute-start | bytes 1572872 | tf_op jit(solution)/shard_map/ppermute | solution.py:30
  6.5 1.0 copy-start.1
  7.5 1.0 copy-start.2
  17.7 1.3 copy-start.5
  19.0 2.8 %collective-permute-start.2 = (f32[8,1024]{1,0:T(8,128)}, f32[8,1024]{1,0:T(8,128)S(1)}, u32[]{:S(2)}, u32[]{:S(2)}) collective-permute-start(f32[8,1024]{1,0:T(8,128)} %get-tuple-element.33.refs_4_), channel_id=1, source_target_pairs={{1,0},{0,1},{3,2},{2,3},{5,4},{4,5},{7,6},{6,7},{9,8},{8,9},{11,10... | collective-permute-start | bytes 98312 | tf_op jit(solution)/shard_map/ppermute | solution.py:30
  22.4 23.5 %collective-permute-start = (bf16[256,1024]{1,0:T(8,128)(2,1)}, bf16[256,1024]{1,0:T(8,128)(2,1)S(1)}, u32[]{:S(2)}, u32[]{:S(2)}) collective-permute-start(bf16[256,1024]{1,0:T(8,128)(2,1)} %bitcast.45), channel_id=1, source_target_pairs={{1,0},{0,1},{3,2},{2,3},{5,4},{4,5},{7,6},{6,7},{9,8},{8,9},{11,10... | collective-permute-start | bytes 1572872 | tf_op jit(solution)/shard_map/ppermute | solution.py:30
  22.5 10.3 %collective-permute-start.6 = (bf16[256,256]{1,0:T(8,128)(2,1)S(1)}, bf16[256,256]{1,0:T(8,128)(2,1)S(1)}, u32[]{:S(2)}, u32[]{:S(2)}) collective-permute-start(bf16[256,256]{1,0:T(8,128)(2,1)S(1)} %pad_maximum_fusion.1.refs_6_), channel_id=1, source_target_pairs={{2,0},{3,1},{0,2},{1,3},{6,4},{7,5},{4,6},{5,7},{10,8},{11,9},{8,1... | collective-permute-start | bytes 393224 | tf_op jit(solution)/shard_map/ppermute | solution.py:30
  24.1 12.0 %collective-permute-start.7 = (bf16[256,256]{1,0:T(8,128)(2,1)S(1)}, bf16[256,256]{1,0:T(8,128)(2,1)S(1)}, u32[]{:S(2)}, u32[]{:S(2)}) collective-permute-start(bf16[256,256]{1,0:T(8,128)(2,1)S(1)} %pad_maximum_fusion.1.refs_6_), channel_id=1, source_target_pairs={{6,0},{7,1},{4,2},{5,3},{10,4},{11,5},{8,6},{9,7},{14,8},{15,9},{1... | collective-permute-start | bytes 393224 | tf_op jit(solution)/shard_map/ppermute | solution.py:30
  27.2 74.1 %collective-permute-start.11 = (bf16[4096,256]{1,0:T(8,128)(2,1)}, bf16[4096,256]{1,0:T(8,128)(2,1)}, u32[]{:S(2)}, u32[]{:S(2)}) collective-permute-start(bf16[4096,256]{1,0:T(8,128)(2,1)} %copy-done.5), channel_id=1, source_target_pairs={{1,0},{0,1},{3,2},{2,3},{5,4},{4,5},{7,6},{6,7},{9,8},{8,9},{11,10... | collective-permute-start | bytes 6291464 | tf_op jit(solution)/shard_map/ppermute | solution.py:30
  33.4 9.1 %collective-permute-start.8 = (bf16[256,256]{1,0:T(8,128)(2,1)S(1)}, bf16[256,256]{1,0:T(8,128)(2,1)S(1)}, u32[]{:S(2)}, u32[]{:S(2)}) collective-permute-start(bf16[256,256]{1,0:T(8,128)(2,1)S(1)} %pad_maximum_fusion.1.refs_6_), channel_id=1, source_target_pairs={{10,0},{11,1},{8,2},{9,3},{14,4},{15,5},{12,6},{13,7},{2,8},{3,9},... | collective-permute-start | bytes 393224 | tf_op jit(solution)/shard_map/ppermute | solution.py:30
  36.8 8.5 %collective-permute-start.9 = (bf16[256,256]{1,0:T(8,128)(2,1)S(1)}, bf16[256,256]{1,0:T(8,128)(2,1)S(1)}, u32[]{:S(2)}, u32[]{:S(2)}) collective-permute-start(bf16[256,256]{1,0:T(8,128)(2,1)S(1)} %pad_maximum_fusion.1.refs_6_), channel_id=1, source_target_pairs={{14,0},{15,1},{12,2},{13,3},{2,4},{3,5},{0,6},{1,7},{6,8},{7,9},{4... | collective-permute-start | bytes 393224 | tf_op jit(solution)/shard_map/ppermute | solution.py:30
  45.9 0.8 copy-start.8
  46.7 1.0 copy-start.3
  47.8 1.0 copy-start.6
  48.8 1.0 copy-start.9
  49.8 0.9 copy-start.11
  50.7 0.9 copy-start.13
  51.6 0.9 copy-start.15
  52.6 0.9 copy-start.17
  74.6 25.4 %copy-start.7 = (bf16[256,1024]{1,0:T(8,128)(2,1)}, bf16[256,1024]{1,0:T(8,128)(2,1)S(1)}, u32[]{:S(2)}) copy-start(bf16[256,1024]{1,0:T(8,128)(2,1)S(1)} %get-tuple-element.35) | copy-start | bytes 1572868
  74.6 7.4 %collective-permute-start.18 = (bf16[256,256]{1,0:T(8,128)(2,1)S(1)}, bf16[256,256]{1,0:T(8,128)(2,1)S(1)}, u32[]{:S(2)}, u32[]{:S(2)}) collective-permute-start(bf16[256,256]{1,0:T(8,128)(2,1)S(1)} %get-tuple-element.45), channel_id=1, source_target_pairs={{6,0},{7,1},{4,2},{5,3},{10,4},{11,5},{8,6},{9,7},{14,8},{15,9},{1... | collective-permute-start | bytes 393224 | tf_op jit(solution)/shard_map/ppermute | solution.py:30
  74.7 10.8 %collective-permute-start.17 = (bf16[256,256]{1,0:T(8,128)(2,1)S(1)}, bf16[256,256]{1,0:T(8,128)(2,1)S(1)}, u32[]{:S(2)}, u32[]{:S(2)}) collective-permute-start(bf16[256,256]{1,0:T(8,128)(2,1)S(1)} %get-tuple-element.44), channel_id=1, source_target_pairs={{10,0},{11,1},{8,2},{9,3},{14,4},{15,5},{12,6},{13,7},{2,8},{3,9},... | collective-permute-start | bytes 393224 | tf_op jit(solution)/shard_map/ppermute | solution.py:30
  80.5 12.8 %collective-permute-start.16 = (bf16[256,256]{1,0:T(8,128)(2,1)S(1)}, bf16[256,256]{1,0:T(8,128)(2,1)S(1)}, u32[]{:S(2)}, u32[]{:S(2)}) collective-permute-start(bf16[256,256]{1,0:T(8,128)(2,1)S(1)} %get-tuple-element.43), channel_id=1, source_target_pairs={{14,0},{15,1},{12,2},{13,3},{2,4},{3,5},{0,6},{1,7},{6,8},{7,9},{4... | collective-permute-start | bytes 393224 | tf_op jit(solution)/shard_map/ppermute | solution.py:30
  80.5 13.4 %collective-permute-start.15 = (bf16[256,256]{1,0:T(8,128)(2,1)S(1)}, bf16[256,256]{1,0:T(8,128)(2,1)S(1)}, u32[]{:S(2)}, u32[]{:S(2)}) collective-permute-start(bf16[256,256]{1,0:T(8,128)(2,1)S(1)} %get-tuple-element.42), channel_id=1, source_target_pairs={{2,0},{3,1},{0,2},{1,3},{6,4},{7,5},{4,6},{5,7},{10,8},{11,9},{8,1... | collective-permute-start | bytes 393224 | tf_op jit(solution)/shard_map/ppermute | solution.py:30
  82.0 13.5 %collective-permute-start.14 = (bf16[256,256]{1,0:T(8,128)(2,1)S(1)}, bf16[256,256]{1,0:T(8,128)(2,1)S(1)}, u32[]{:S(2)}, u32[]{:S(2)}) collective-permute-start(bf16[256,256]{1,0:T(8,128)(2,1)S(1)} %get-tuple-element.41), channel_id=1, source_target_pairs={{4,0},{5,1},{6,2},{7,3},{8,4},{9,5},{10,6},{11,7},{12,8},{13,9},{1... | collective-permute-start | bytes 393224 | tf_op jit(solution)/shard_map/ppermute | solution.py:30
  85.5 12.1 %collective-permute-start.13 = (bf16[256,256]{1,0:T(8,128)(2,1)S(1)}, bf16[256,256]{1,0:T(8,128)(2,1)S(1)}, u32[]{:S(2)}, u32[]{:S(2)}) collective-permute-start(bf16[256,256]{1,0:T(8,128)(2,1)S(1)} %get-tuple-element.40), channel_id=1, source_target_pairs={{8,0},{9,1},{10,2},{11,3},{12,4},{13,5},{14,6},{15,7},{0,8},{1,9},... | collective-permute-start | bytes 393224 | tf_op jit(solution)/shard_map/ppermute | solution.py:30
  93.3 6.5 %collective-permute-start.12 = (bf16[256,256]{1,0:T(8,128)(2,1)S(1)}, bf16[256,256]{1,0:T(8,128)(2,1)S(1)}, u32[]{:S(2)}, u32[]{:S(2)}) collective-permute-start(bf16[256,256]{1,0:T(8,128)(2,1)S(1)} %get-tuple-element.39), channel_id=1, source_target_pairs={{12,0},{13,1},{14,2},{15,3},{0,4},{1,5},{2,6},{3,7},{4,8},{5,9},{6... | collective-permute-start | bytes 393224 | tf_op jit(solution)/shard_map/ppermute | solution.py:30
  99.9 1.4 collective-permute-start.19
  105.6 8.6 %collective-permute-start.20 = (bf16[1024,128]{1,0:T(8,128)(2,1)S(1)}, bf16[1024,128]{1,0:T(8,128)(2,1)S(1)}, u32[]{:S(2)}, u32[]{:S(2)}) collective-permute-start(bf16[1024,128]{1,0:T(8,128)(2,1)S(1)} %get-tuple-element.47), channel_id=1, source_target_pairs={{12,0},{13,1},{14,2},{15,3},{0,4},{1,5},{2,6},{3,7},{4,8},{5,9},{6... | collective-permute-start | bytes 786440 | tf_op jit(solution)/shard_map/ppermute | solution.py:30
  107.5 13.5 %collective-permute-start.21 = (bf16[1024,128]{1,0:T(8,128)(2,1)S(1)}, bf16[1024,128]{1,0:T(8,128)(2,1)S(1)}, u32[]{:S(2)}, u32[]{:S(2)}) collective-permute-start(bf16[1024,128]{1,0:T(8,128)(2,1)S(1)} %get-tuple-element.48), channel_id=1, source_target_pairs={{8,0},{9,1},{10,2},{11,3},{12,4},{13,5},{14,6},{15,7},{0,8},{1,9},... | collective-permute-start | bytes 786440 | tf_op jit(solution)/shard_map/ppermute | solution.py:30
  108.8 13.1 %collective-permute-start.22 = (bf16[1024,128]{1,0:T(8,128)(2,1)S(1)}, bf16[1024,128]{1,0:T(8,128)(2,1)S(1)}, u32[]{:S(2)}, u32[]{:S(2)}) collective-permute-start(bf16[1024,128]{1,0:T(8,128)(2,1)S(1)} %get-tuple-element.49), channel_id=1, source_target_pairs={{4,0},{5,1},{6,2},{7,3},{8,4},{9,5},{10,6},{11,7},{12,8},{13,9},{1... | collective-permute-start | bytes 786440 | tf_op jit(solution)/shard_map/ppermute | solution.py:30
  111.4 14.3 %collective-permute-start.23 = (bf16[1024,128]{1,0:T(8,128)(2,1)S(1)}, bf16[1024,128]{1,0:T(8,128)(2,1)S(1)}, u32[]{:S(2)}, u32[]{:S(2)}) collective-permute-start(bf16[1024,128]{1,0:T(8,128)(2,1)S(1)} %get-tuple-element.51), channel_id=1, source_target_pairs={{18,0},{19,1},{16,2},{17,3},{22,4},{23,5},{20,6},{21,7},{26,8},{27... | collective-permute-start | bytes 786440 | tf_op jit(solution)/shard_map/ppermute | solution.py:30
  112.1 13.7 %collective-permute-start.24 = (bf16[1024,128]{1,0:T(8,128)(2,1)S(1)}, bf16[1024,128]{1,0:T(8,128)(2,1)S(1)}, u32[]{:S(2)}, u32[]{:S(2)}) collective-permute-start(bf16[1024,128]{1,0:T(8,128)(2,1)S(1)} %get-tuple-element.52), channel_id=1, source_target_pairs={{2,0},{3,1},{0,2},{1,3},{6,4},{7,5},{4,6},{5,7},{10,8},{11,9},{8,1... | collective-permute-start | bytes 786440 | tf_op jit(solution)/shard_map/ppermute | solution.py:30
  114.2 12.2 %collective-permute-start.25 = (bf16[1024,128]{1,0:T(8,128)(2,1)S(1)}, bf16[1024,128]{1,0:T(8,128)(2,1)S(1)}, u32[]{:S(2)}, u32[]{:S(2)}) collective-permute-start(bf16[1024,128]{1,0:T(8,128)(2,1)S(1)} %get-tuple-element.53), channel_id=1, source_target_pairs={{16,0},{17,1},{18,2},{19,3},{20,4},{21,5},{22,6},{23,7},{24,8},{25... | collective-permute-start | bytes 786440 | tf_op jit(solution)/shard_map/ppermute | solution.py:30
  127.3 10.6 %collective-permute-start.31 = (bf16[256,128]{1,0:T(8,128)(2,1)S(1)}, bf16[256,128]{1,0:T(8,128)(2,1)S(1)}, u32[]{:S(2)}, u32[]{:S(2)}) collective-permute-start(bf16[256,128]{1,0:T(8,128)(2,1)S(1)} %get-tuple-element.61), channel_id=1, source_target_pairs={{4,0},{5,1},{6,2},{7,3},{8,4},{9,5},{10,6},{11,7},{12,8},{13,9},{1... | collective-permute-start | bytes 196616 | tf_op jit(solution)/shard_map/ppermute | solution.py:30
  127.7 10.2 %collective-permute-start.30 = (bf16[256,128]{1,0:T(8,128)(2,1)S(1)}, bf16[256,128]{1,0:T(8,128)(2,1)S(1)}, u32[]{:S(2)}, u32[]{:S(2)}) collective-permute-start(bf16[256,128]{1,0:T(8,128)(2,1)S(1)} %get-tuple-element.60), channel_id=1, source_target_pairs={{8,0},{9,1},{10,2},{11,3},{12,4},{13,5},{14,6},{15,7},{0,8},{1,9},... | collective-permute-start | bytes 196616 | tf_op jit(solution)/shard_map/ppermute | solution.py:30
  132.6 5.3 %collective-permute-start.29 = (bf16[256,128]{1,0:T(8,128)(2,1)S(1)}, bf16[256,128]{1,0:T(8,128)(2,1)S(1)}, u32[]{:S(2)}, u32[]{:S(2)}) collective-permute-start(bf16[256,128]{1,0:T(8,128)(2,1)S(1)} %get-tuple-element.59), channel_id=1, source_target_pairs={{12,0},{13,1},{14,2},{15,3},{0,4},{1,5},{2,6},{3,7},{4,8},{5,9},{6... | collective-permute-start | bytes 196616 | tf_op jit(solution)/shard_map/ppermute | solution.py:30
  135.1 4.3 %collective-permute-start.28 = (bf16[256,128]{1,0:T(8,128)(2,1)S(1)}, bf16[256,128]{1,0:T(8,128)(2,1)S(1)}, u32[]{:S(2)}, u32[]{:S(2)}) collective-permute-start(bf16[256,128]{1,0:T(8,128)(2,1)S(1)} %get-tuple-element.57), channel_id=1, source_target_pairs={{16,0},{17,1},{18,2},{19,3},{20,4},{21,5},{22,6},{23,7},{24,8},{25... | collective-permute-start | bytes 196616 | tf_op jit(solution)/shard_map/ppermute | solution.py:30
  136.6 5.8 %collective-permute-start.27 = (bf16[256,128]{1,0:T(8,128)(2,1)S(1)}, bf16[256,128]{1,0:T(8,128)(2,1)S(1)}, u32[]{:S(2)}, u32[]{:S(2)}) collective-permute-start(bf16[256,128]{1,0:T(8,128)(2,1)S(1)} %get-tuple-element.56), channel_id=1, source_target_pairs={{2,0},{3,1},{0,2},{1,3},{6,4},{7,5},{4,6},{5,7},{10,8},{11,9},{8,1... | collective-permute-start | bytes 196616 | tf_op jit(solution)/shard_map/ppermute | solution.py:30
  137.9 5.5 %collective-permute-start.26 = (bf16[256,128]{1,0:T(8,128)(2,1)S(1)}, bf16[256,128]{1,0:T(8,128)(2,1)S(1)}, u32[]{:S(2)}, u32[]{:S(2)}) collective-permute-start(bf16[256,128]{1,0:T(8,128)(2,1)S(1)} %get-tuple-element.55), channel_id=1, source_target_pairs={{18,0},{19,1},{16,2},{17,3},{22,4},{23,5},{20,6},{21,7},{26,8},{27... | collective-permute-start | bytes 196616 | tf_op jit(solution)/shard_map/ppermute | solution.py:30
  143.4 5.1 %collective-permute-start.32 = (f32[4,32,256]{2,1,0:T(8,128)S(1)}, f32[4,32,256]{2,1,0:T(8,128)S(1)}, u32[]{:S(2)}, u32[]{:S(2)}) collective-permute-start(f32[4,32,256]{2,1,0:T(8,128)S(1)} %dynamic-slice_bitcast_fusion), channel_id=1, source_target_pairs={{32,0},{33,1},{34,2},{35,3},{36,4},{37,5},{38,6},{39,7},{40,8},{41... | collective-permute-start | bytes 393224 | tf_op jit(solution)/shard_map/ppermute | solution.py:30
  145.4 15.7 %collective-permute-start.10 = (bf16[256,1024]{1,0:T(8,128)(2,1)}, bf16[256,1024]{1,0:T(8,128)(2,1)S(1)}, u32[]{:S(2)}, u32[]{:S(2)}) collective-permute-start(bf16[256,1024]{1,0:T(8,128)(2,1)} %copy-done.7), channel_id=1, source_target_pairs={{1,0},{0,1},{3,2},{2,3},{5,4},{4,5},{7,6},{6,7},{9,8},{8,9},{11,10... | collective-permute-start | bytes 1572872 | tf_op jit(solution)/shard_map/ppermute | solution.py:30
  148.5 6.3 %collective-permute-start.33 = (f32[2,32,256]{2,1,0:T(8,128)S(1)}, f32[2,32,256]{2,1,0:T(8,128)S(1)}, u32[]{:S(2)}, u32[]{:S(2)}) collective-permute-start(f32[2,32,256]{2,1,0:T(8,128)S(1)} %dynamic-slice_bitcast_fusion.1), channel_id=1, source_target_pairs={{64,0},{65,1},{66,2},{67,3},{68,4},{69,5},{70,6},{71,7},{72,8},{73... | collective-permute-start | bytes 196616 | tf_op jit(solution)/shard_map/ppermute | solution.py:30
  154.9 8.1 %collective-permute-start.34 = (f32[1,32,256]{2,1,0:T(8,128)S(1)}, f32[1,32,256]{2,1,0:T(8,128)S(1)}, u32[]{:S(2)}, u32[]{:S(2)}) collective-permute-start(f32[1,32,256]{2,1,0:T(8,128)S(1)} %constant_dynamic-slice_fusion), channel_id=1, source_target_pairs={{128,0},{129,1},{130,2},{131,3},{132,4},{133,5},{134,6},{135,7},{1... | collective-permute-start | bytes 98312 | tf_op jit(solution)/shard_map/ppermute | solution.py:30
  (7 other events, 4.7 us)

commit v2 on v0

v2 whole, which is shorter than its diff:
```python
import math

import jax
import jax.numpy as jnp
from jax import lax
from jax.experimental import pallas as pl
from jax.experimental.pallas import tpu as pltpu
from jax.sharding import PartitionSpec as P

F32 = jnp.float32
BF16 = jnp.bfloat16
BLK = 128
H = 8
Z, YL, X, YH, C = 8, 2, 4, 2, 2
AXES = ("z", "yl", "x", "yh", "c")
VMEM_LIMIT = 24 * 1024 * 1024


def coords(i):
    return (i // 32, i // 16 % 2, i // 4 % 4, i // 2 % 2, i % 2)


def index_of(z, yl, x, yh, c):
    return (((z * YL + yl) * X + x) * YH + yh) * C + c


def fetch(value, shift):
    pairs = [(index_of(*shift(*coords(i))), i) for i in range(Z * YL * X * YH * C)]
    return lax.ppermute(value, AXES, pairs)


def swap_core(z, yl, x, yh, c):
    return (z, yl, x, yh, 1 - c)


def by_ctx(dx, dyh):
    return lambda z, yl, x, yh, c: (z, yl, (x + dx) % X, yh ^ dyh, c)


def by_z(k):
    return lambda z, yl, x, yh, c: ((z + k) % Z, yl, x, yh, c)


FIRST = [(0, 0), (1, 0), (3, 0), (2, 0)]
SECOND = [(0, 1), (1, 1), (3, 1), (2, 1)]


def vmem():
    return pl.BlockSpec(memory_space=pltpu.VMEM)


def smem():
    return pl.BlockSpec(memory_space=pltpu.SMEM)


def anywhere():
    return pl.BlockSpec(memory_space=pl.ANY)


def stats_kernel(out_ref, grad_ref, lse_ref, stats_ref):
    for h in range(H):
        cols = slice(h * BLK, (h + 1) * BLK)
        product = out_ref[:, cols].astype(F32) * grad_ref[:, cols].astype(F32)
        delta = jnp.sum(product.T, axis=0, keepdims=True)
        lse2 = lse_ref[h : h + 1, :] * math.log2(math.e)
        for i in range(2):
            rows = slice(i * BLK, (i + 1) * BLK)
            stats_ref[i : i + 1, cols] = lse2[:, rows]
            stats_ref[2 + i : 3 + i, cols] = delta[:, rows]
    stats_ref[4:8, :] = jnp.zeros((4, H * BLK), F32)


def row_stats(saved, grad, lse):
    return pl.pallas_call(
        stats_kernel,
        out_shape=jax.ShapeDtypeStruct((8, H * BLK), F32),
        in_specs=[vmem()] * 3,
        out_specs=vmem(),
        compiler_params=pltpu.CompilerParams(vmem_limit_bytes=8 * 2**20),
        cost_estimate=pl.CostEstimate(flops=10**6, bytes_accessed=2**20, transcendentals=0),
        name="row_stats",
    )(saved, grad, lse)


def turn_kernel(me, x_ref, mine_ref, other_ref):
    even = me[0] == 0
    for u in range(8):
        tile = x_ref[:, u * BLK : (u + 1) * BLK].T
        for yh in range(YH):
            first = tile[yh * 64 : yh * 64 + 32]
            second = tile[yh * 64 + 32 : yh * 64 + 64]
            at = slice(u * 64 + yh * 32, u * 64 + yh * 32 + 32)

            @pl.when(even)
            def _():
                mine_ref[at, :] = first
                other_ref[at, :] = second

            @pl.when(jnp.logical_not(even))
            def _():
                mine_ref[at, :] = second
                other_ref[at, :] = first


def turn(me, layer):
    return pl.pallas_call(
        turn_kernel,
        grid=(Z,),
        out_shape=(jax.ShapeDtypeStruct((4096, 256), BF16),) * 2,
        in_specs=[smem(), pl.BlockSpec((256, 1024), lambda z: (0, z))],
        out_specs=(pl.BlockSpec((512, 256), lambda z: (z, 0)),) * 2,
        compiler_params=pltpu.CompilerParams(vmem_limit_bytes=8 * 2**20),
        cost_estimate=pl.CostEstimate(flops=10**7, bytes_accessed=8 * 2**20, transcendentals=0),
        name="turn",
    )(me, layer)


NQ, NK = 4, 8
SCALE = BLK**-0.5


def key_steps(meta, q_all, g_all, qt, gt, stats, kv, kt, dqt, dkv):
    factor = SCALE * math.log2(math.e)
    dkv[...] = jnp.zeros_like(dkv)

    def chunk(i, first, count, masked):
        keys = count * BLK
        at = [meta[first + n] for n in range(count)]
        rows = [pl.ds(pl.multiple_of(a * BLK, BLK), BLK) for a in at]
        kb = jnp.concatenate([kv[r, :BLK] for r in rows], 0)
        vb = jnp.concatenate([kv[r, BLK:] for r in rows], 0)
        ktb = jnp.concatenate([kt[a] for a in at], 1)
        if masked:
            q_pos = meta[2 * NK + i]
            u = lax.broadcasted_iota(jnp.int32, (BLK, 2 * BLK), 0)
            t = lax.broadcasted_iota(jnp.int32, (BLK, 2 * BLK), 1) % BLK
            ahead = t - u
            visible = [ahead >= (meta[NK + first + n] - q_pos) * BLK for n in range(count)]
        dv = jnp.zeros((keys, BLK), F32)
        dk = jnp.zeros((keys, BLK), F32)
        for pair in range(H // 2):
            cols = slice(pair * 2 * BLK, (pair + 1) * 2 * BLK)
            heads = [slice((2 * pair + g) * BLK, (2 * pair + g + 1) * BLK) for g in range(2)]
            score = jnp.dot(kb, qt[i, :, cols], preferred_element_type=F32)
            prob = jnp.exp2(score * factor - stats[pl.ds(i, 1), cols])
            if masked:
                prob = jnp.concatenate(
                    [
                        jnp.where(visible[n], prob[n * BLK : (n + 1) * BLK], 0.0)
                        for n in range(count)
                    ],
                    0,
                )
            d_prob = jnp.dot(vb, gt[i, :, cols], preferred_element_type=F32)
            d_score = (prob * (d_prob - stats[pl.ds(NQ + i, 1), cols])).astype(BF16)
            g_rows = jnp.concatenate([g_all[i, :, s] for s in heads], 0)
            q_rows = jnp.concatenate([q_all[i, :, s] for s in heads], 0)
            dv = dv + jnp.dot(prob.astype(BF16), g_rows, preferred_element_type=F32)
            dk = dk + jnp.dot(d_score, q_rows, preferred_element_type=F32)
            dqt[i, :, cols] += jnp.dot(ktb, d_score, preferred_element_type=F32)
        for n in range(count):
            dkv[at[n], :, :BLK] += dk[n * BLK : (n + 1) * BLK]
            dkv[at[n], :, BLK:] += dv[n * BLK : (n + 1) * BLK]

    def query_block(i, carry):
        whole = meta[2 * NK + NQ + i]
        pairs = meta[2 * NK + 2 * NQ + i]

        def full_step(j, c):
            chunk(i, 4 * j, 4, False)
            return c

        def pair_step(j, c):
            chunk(i, 4 * whole + 2 * j, 2, True)
            return c

        lax.fori_loop(0, whole, full_step, 0)
        lax.fori_loop(0, pairs, pair_step, 0)
        return carry

    lax.fori_loop(0, NQ, query_block, 0)


def store_keys(dkv, dkv_out):
    for b in range(4):
        for i in range(2):
            rows = slice(i * BLK, (i + 1) * BLK)
            ref = dkv_out[b]
            ref[rows, :BLK] = (dkv[2 * b + i, :, :BLK] * SCALE).astype(ref.dtype)
            ref[rows, BLK:] = dkv[2 * b + i, :, BLK:].astype(ref.dtype)


def first_kernel(meta, *refs):
    q_in, g_in, s_in, kv_in = refs[0:2], refs[2:4], refs[4:6], refs[6:10]
    q_all, g_all, qt, gt, stats, dqt = refs[10:16]
    dkv_out = refs[16:20]
    kv, kt, dkv, pieces, sems = refs[20:]
    copies = []
    for side in range(2):
        for i in range(2):
            rows = pl.ds(i * BLK, BLK)
            copies.append((q_in[side].at[rows], q_all.at[2 * side + i]))
            copies.append((g_in[side].at[rows], g_all.at[2 * side + i]))
        copies.append((s_in[side], pieces.at[side]))
    for b in range(4):
        copies.append((kv_in[b], kv.at[pl.ds(b * 2 * BLK, 2 * BLK)]))
    copies = [pltpu.make_async_copy(s, d, sems.at[n]) for n, (s, d) in enumerate(copies)]
    for copy in copies:
        copy.start()
    dqt[...] = jnp.zeros_like(dqt)
    for copy in copies:
        copy.wait()
    for side in range(2):
        stats[2 * side : 2 * side + 2, :] = pieces[side, 0:2, :]
        stats[NQ + 2 * side : NQ + 2 * side + 2, :] = pieces[side, 2:4, :]

    def transpose(n, carry):
        for h in range(H):
            cols = slice(h * BLK, (h + 1) * BLK)
            qt[n, :, cols] = q_all[n, :, cols].T
            gt[n, :, cols] = g_all[n, :, cols].T
        return carry

    lax.fori_loop(0, NQ, transpose, 0)
    for n in range(NK):
        kt[n] = kv[n * BLK : (n + 1) * BLK, :BLK].T
    key_steps(meta, q_all, g_all, qt, gt, stats, kv, kt, dqt, dkv)
    store_keys(dkv, dkv_out)


def second_kernel(meta, *refs):
    q_all, g_all, qt, gt, stats, dqt_in = refs[0:6]
    kv_in = refs[6:10]
    dq_own, dq_other = refs[10:12]
    dkv_out = refs[12:16]
    kv, kt, dkv, dqt, sems = refs[16:]
    copies = [
        pltpu.make_async_copy(kv_in[b], kv.at[pl.ds(b * 2 * BLK, 2 * BLK)], sems.at[b])
        for b in range(4)
    ]
    for copy in copies:
        copy.start()
    dqt[...] = dqt_in[...]
    for copy in copies:
        copy.wait()
    for n in range(NK):
        kt[n] = kv[n * BLK : (n + 1) * BLK, :BLK].T
    key_steps(meta, q_all, g_all, qt, gt, stats, kv, kt, dqt, dkv)
    store_keys(dkv, dkv_out)
    for n in range(NQ):
        ref = (dq_own, dq_own, dq_other, dq_other)[n]
        rows = slice(n % 2 * BLK, (n % 2 + 1) * BLK)
        for h in range(H):
            cols = slice(h * BLK, (h + 1) * BLK)
            ref[rows, cols] = (dqt[n, :, cols].T * SCALE).astype(ref.dtype)


WIDE = H * BLK
KEY_SCRATCH = [
    pltpu.VMEM((NK * BLK, 2 * BLK), BF16),
    pltpu.VMEM((NK, BLK, BLK), BF16),
    pltpu.VMEM((NK, BLK, 2 * BLK), F32),
]
COST = pl.CostEstimate(flops=6 * 10**10, bytes_accessed=2**20, transcendentals=2 * 10**6)


def dkv_shapes(own):
    return (jax.ShapeDtypeStruct((256, 256), own),) + (
        jax.ShapeDtypeStruct((256, 256), BF16),
    ) * 3


def first_call(meta, queries, grads, stats, blocks):
    rows = jax.ShapeDtypeStruct((NQ, BLK, WIDE), BF16)
    return pl.pallas_call(
        first_kernel,
        out_shape=(rows,) * 4
        + (
            jax.ShapeDtypeStruct((2 * NQ, WIDE), F32),
            jax.ShapeDtypeStruct((NQ, BLK, WIDE), F32),
        )
        + dkv_shapes(F32),
        in_specs=[smem()] + [anywhere()] * 10,
        out_specs=(vmem(),) * 10,
        scratch_shapes=KEY_SCRATCH
        + [pltpu.VMEM((2, 8, WIDE), F32), pltpu.SemaphoreType.DMA((14,))],
        compiler_params=pltpu.CompilerParams(vmem_limit_bytes=VMEM_LIMIT),
        cost_estimate=COST,
        name="attention_first",
    )(meta, *queries, *grads, *stats, *blocks)


def second_call(meta, carried, blocks):
    return pl.pallas_call(
        second_kernel,
        out_shape=(
            jax.ShapeDtypeStruct((256, WIDE), F32),
            jax.ShapeDtypeStruct((256, WIDE), BF16),
        )
        + dkv_shapes(BF16),
        in_specs=[smem()] + [vmem()] * 6 + [anywhere()] * 4,
        out_specs=(vmem(),) * 6,
        scratch_shapes=KEY_SCRATCH
        + [pltpu.VMEM((NQ, BLK, WIDE), F32), pltpu.SemaphoreType.DMA((4,))],
        compiler_params=pltpu.CompilerParams(vmem_limit_bytes=VMEM_LIMIT),
        cost_estimate=COST,
        name="attention_second",
    )(meta, *carried, *blocks)


def make_meta(k_pos, q_pos):
    rank = jnp.sum(k_pos[None, :] < k_pos[:, None], axis=1)
    hit = rank[None, :] == jnp.arange(NK)[:, None]
    order = jnp.sum(jnp.where(hit, jnp.arange(NK)[None, :], 0), axis=1)
    ordered = jnp.sum(jnp.where(hit, k_pos[None, :], 0), axis=1)
    below = jnp.sum(k_pos[None, :] < q_pos[:, None], axis=1)
    reached = jnp.sum(k_pos[None, :] <= q_pos[:, None], axis=1)
    whole = below // 4
    pairs = (reached - 4 * whole + 1) // 2
    return jnp.concatenate([order, ordered, q_pos, whole, pairs]).astype(jnp.int32)


def project_kernel(mine_ref, other_ref, g_own, g_other, out_ref):
    def step(z, carry):
        rows = pl.ds(pl.multiple_of(z * 512, 512), 512)
        terms = jnp.dot(mine_ref[rows, :], g_own[...], preferred_element_type=F32) + jnp.dot(
            other_ref[rows, :], g_other[...], preferred_element_type=F32
        )
        at = pl.ds(pl.multiple_of(z * 32, 32), 32)
        out_ref[:, at, :] = terms.astype(BF16).reshape(16, 32, 256)
        return carry

    lax.fori_loop(0, Z, step, 0)


def project(mine, other, g_own, g_other):
    return pl.pallas_call(
        project_kernel,
        out_shape=jax.ShapeDtypeStruct((16, 256, 256), BF16),
        in_specs=[vmem()] * 4,
        out_specs=vmem(),
        compiler_params=pltpu.CompilerParams(vmem_limit_bytes=16 * 2**20),
        cost_estimate=pl.CostEstimate(
            flops=2 * 4096 * 512 * 256, bytes_accessed=8 * 2**20, transcendentals=0
        ),
        name="project",
    )(mine, other, g_own, g_other)


def sum_kernel(place, in_ref, own_ref, *out_refs):
    for k in range(Z):
        at = pl.ds(pl.multiple_of((place[0] + k) % Z * 32, 32), 32)
        value = in_ref[0, at, :].astype(F32)
        for j in range(1, 16):
            value = value + in_ref[j, at, :].astype(F32)
        ref = own_ref if k == 0 else out_refs[k - 1]
        ref[...] = value.astype(ref.dtype)


def sum_terms(place, terms):
    return pl.pallas_call(
        sum_kernel,
        out_shape=(jax.ShapeDtypeStruct((32, 256), F32),)
        + (jax.ShapeDtypeStruct((32, 256), BF16),) * 7,
        in_specs=[smem(), vmem()],
        out_specs=(vmem(),) * 8,
        compiler_params=pltpu.CompilerParams(vmem_limit_bytes=8 * 2**20),
        name="sum_terms",
    )(place, terms)


def body(layer_input, query_rows, key_rows, value_rows, attn_out, d_attn, log_sum_exp, block_order):
    z, x, yh, c = (lax.axis_index(name) for name in ("z", "x", "yh", "c"))
    ctx = (x * YH + yh) * C + c

    q, g = query_rows[0], d_attn[0]
    pair = jnp.concatenate([key_rows[0], value_rows[0]], axis=1)
    blocks = [pair] + [fetch(pair, by_ctx(*o)) for o in FIRST[1:]]
    q_other, g_other = fetch(q, swap_core), fetch(g, swap_core)
    stats = row_stats(attn_out[0], g, log_sum_exp[0])
    stats_other = fetch(stats, swap_core)
    mine, other = turn(c.astype(jnp.int32)[None], layer_input[0])

    places = block_order.reshape(16, 2)
    q_pos = jnp.concatenate([places[ctx], places[ctx ^ 1]])

    def owners(group):
        return jnp.concatenate(
            [places[(x + dx) % X * 4 + (yh ^ dyh) * 2 + c] for dx, dyh in group]
        )

    pair_again, *blocks = lax.optimization_barrier((pair, *blocks))
    later = [fetch(pair_again, by_ctx(*o)) for o in SECOND]
    blocks, mine, other = lax.optimization_barrier((blocks, mine, other))
    outs = first_call(
        make_meta(owners(FIRST), q_pos), (q, q_other), (g, g_other), (stats, stats_other), blocks
    )
    outs, other = lax.optimization_barrier((outs, other))
    carried, dkv_first = outs[:6], outs[6:]
    mine_other = fetch(other, swap_core)
    dq_own, dq_sent, *dkv_second = second_call(make_meta(owners(SECOND), q_pos), carried, later)
    total = dkv_first[0]
    for (dx, dyh), part in zip(FIRST[1:], dkv_first[1:]):
        total = total + fetch(part, by_ctx(-dx, dyh)).astype(F32)
    total, dkv_second = lax.optimization_barrier((total, dkv_second))
    for (dx, dyh), part in zip(SECOND, dkv_second):
        total = total + fetch(part, by_ctx(-dx, dyh)).astype(F32)
    grads = total.astype(BF16)
    grads_other = fetch(grads, swap_core)
    d_query = (dq_own + fetch(dq_sent, swap_core).astype(F32)).astype(BF16)[None]

    terms = project(mine, mine_other, grads, grads_other)
    terms = lax.all_to_all(terms, ("yl", "x", "yh"), 0, 0)
    own, *sent = sum_terms(z.astype(jnp.int32)[None], terms)
    for k in range(1, Z):
        own = own + fetch(sent[k - 1], by_z(-k)).astype(F32)
    return (d_query, own)


def solution(mesh):
    fine = jax.sharding.Mesh(mesh.devices.reshape(Z, YL, X, YH, C), AXES)
    dp, ctx = ("z", "yl"), ("x", "yh", "c")
    rows = P(dp, ctx, None)
    return jax.shard_map(
        body,
        mesh=fine,
        in_specs=(rows, rows, rows, rows, rows, rows, P(dp, None, ctx), P()),
        out_specs=(rows, P(AXES, None)),
        check_vma=False,
    )
```

time: 1540 us -> 145 us (0.09); the launches traced: 1510 us -> 145 us
  waiting for transfers between devices: 1360 us -> 38.9 us
  matrix products: 61.4 us -> 0 us
  starting transfers between devices: 29.1 us -> 62.1 us
  Pallas kernels: 0 us -> 32.4 us
  local copies, waits for them, and re-layouts: 27.3 us -> 5.92 us
    unnamed x2 -> x0, waiting for transfers between devices: 1270 us -> none
    ppermute x31 -> x27, waiting for transfers between devices: 93.5 us -> 5.06 us  [fetch(): return lax.ppermute(value, AXES, pairs)]
    dot_general x81 -> x0, matrix products: 61.4 us -> none  [the longest x16 20.8 us: tile(): jnp.einsum('rhd,sd->hrs', queries, keys, preferred_element_type=jnp.float32)]
    all_to_all x0 -> x1, waiting for transfers between devices: none -> 33.8 us  [body(): terms = lax.all_to_all(terms, ('yl', 'x', 'yh'), 0, 0)]
    pallas_call x0 -> x6, Pallas kernels: none -> 32.4 us  [the longest x1 11.6 us: first_call(): pl.pallas_call(first_kernel, out_shape=(rows,) * 4 + (jax.ShapeDtypeStruc...]
    ppermute x31 -> x27, starting transfers between devices: 29.1 us -> 52.5 us  [fetch(): return lax.ppermute(value, AXES, pairs)]
  transfers between devices with their start and end apart: 32 -> 28, of which waited for: 26 -> 5; matrix products, arithmetic and copies ran while one was open for 5% -> 3% of each run, Pallas kernels for 0% -> 20%
where the time goes in v2:
time: 145 us
  starting transfers between devices  62.1 us (43%)
  waiting for transfers between devices  38.9 us (27%)
  Pallas kernels  32.4 us (22%)
  local copies, waits for them, and re-layouts  5.92 us (4%)
  other arithmetic  4.61 us (3%)
    ppermute x27, starting transfers between devices, fetch(): return lax.ppermute(value, AXES, pairs)  52.5 us
    all_to_all x1, waiting for transfers between devices, body(): terms = lax.all_to_all(terms, ('yl', 'x', 'yh'), 0, 0)  33.8 us
    pallas_call x1, Pallas kernels, first_call(): pl.pallas_call(first_kernel, out_shape=(rows,) * 4 + (jax.ShapeDtypeStruc...  11.6 us
    pallas_call x1, Pallas kernels, second_call(): pl.pallas_call(second_kernel, out_shape=(jax.ShapeDtypeStruct((256, WIDE)...  11.1 us
    all_to_all x1, starting transfers between devices, body(): terms = lax.all_to_all(terms, ('yl', 'x', 'yh'), 0, 0)  9.59 us
    pallas_call x1, Pallas kernels, turn(): pl.pallas_call(turn_kernel, grid=(Z,), out_shape=(jax.ShapeDtypeStruct((4...  5.33 us
    ppermute x27, waiting for transfers between devices, fetch(): return lax.ppermute(value, AXES, pairs)  5.06 us
    unnamed x14, local copies, waits for them, and re-layouts  4.99 us
  transfers between devices with their start and end apart: 28, of which 5 were waited for; matrix products, arithmetic and copies ran while one was open for 3% of the time, Pallas kernels for 20%

profile of v2, /device:TPU:4, one launch (start us, length us, event | category | flops | bytes accessed | tf_op | source)
XLA Modules:
  0.0 144.8 jit_solution(6292988150733518295)
XLA Ops:
  0.6 0.9 pad_maximum_fusion.refs_6_
  1.5 0.6 collective-permute-start.3
  2.1 1.5 %collective-permute-start.4 = (bf16[256,256]{1,0:T(8,128)(2,1)S(1)}, bf16[256,256]{1,0:T(8,128)(2,1)S(1)}, u32[]{:S(2)}, u32[]{:S(2)}) collective-permute-start(bf16[256,256]{1,0:T(8,128)(2,1)S(1)} %pad_maximum_fusion.refs_6_), channel_id=1, source_target_pairs={{12,0},{13,1},{14,2},{15,3},{0,4},{1,5},{2,6},{3,7},{4,8},{5,9},{6... | collective-permute-start | bytes 393224 | tf_op jit(solution)/shard_map/ppermute | solution.py:29
  3.6 2.2 %collective-permute-start.5 = (bf16[256,256]{1,0:T(8,128)(2,1)S(1)}, bf16[256,256]{1,0:T(8,128)(2,1)S(1)}, u32[]{:S(2)}, u32[]{:S(2)}) collective-permute-start(bf16[256,256]{1,0:T(8,128)(2,1)S(1)} %pad_maximum_fusion.refs_6_), channel_id=1, source_target_pairs={{8,0},{9,1},{10,2},{11,3},{12,4},{13,5},{14,6},{15,7},{0,8},{1,9},... | collective-permute-start | bytes 393224 | tf_op jit(solution)/shard_map/ppermute | solution.py:29
  5.9 0.5 collective-permute-start
  6.4 0.7 reshape.14
  7.4 0.2 convert_reduce_fusion.2
  7.6 0.2 convert_reduce_fusion.1
  7.8 0.2 convert_reduce_fusion
  8.0 1.0 copy-done.1
  9.1 1.0 copy-done.2
  10.1 0.7 copy-done.4
  10.8 0.3 row_stats.1.refs_4_
  11.2 0.1 collective-permute-start.2
  11.3 0.1 select_reduce_fusion
  11.4 0.1 concatenate.24.meta
  11.6 2.2 %copy-done = bf16[1,256,8192]{2,1,0:T(8,128)(2,1)S(1)} copy-done((bf16[1,256,8192]{2,1,0:T(8,128)(2,1)S(1)}, bf16[1,256,8192]{2,1,0:T(8,128)(2,1)}, u32[]{:S(2)}) %copy-start) | copy-done | bytes 4194328
  13.8 5.3 %turn.1 = (bf16[4096,256]{1,0:T(8,128)(2,1)S(1)}, bf16[4096,256]{1,0:T(8,128)(2,1)S(1)}) custom-call(s32[1]{0:T(128)} %bitcast.16.me, bf16[256,8192]{1,0:T(8,128)(2,1)S(1)} %bitcast.31), custom_call_target="tpu_custom_call" | custom-call | flops 10000000 | bytes 8388608 | tf_op jit(solution)/shard_map/turn/pallas_call | solution.py:106
  19.1 2.3 %collective-permute-start.6 = (bf16[256,256]{1,0:T(8,128)(2,1)S(1)}, bf16[256,256]{1,0:T(8,128)(2,1)S(1)}, u32[]{:S(2)}, u32[]{:S(2)}) collective-permute-start(bf16[256,256]{1,0:T(8,128)(2,1)S(1)} %pad_maximum_fusion.refs_6_), channel_id=1, source_target_pairs={{2,0},{3,1},{0,2},{1,3},{6,4},{7,5},{4,6},{5,7},{10,8},{11,9},{8,1... | collective-permute-start | bytes 393224 | tf_op jit(solution)/shard_map/ppermute | solution.py:29
  21.4 2.4 %collective-permute-start.7 = (bf16[256,256]{1,0:T(8,128)(2,1)S(1)}, bf16[256,256]{1,0:T(8,128)(2,1)S(1)}, u32[]{:S(2)}, u32[]{:S(2)}) collective-permute-start(bf16[256,256]{1,0:T(8,128)(2,1)S(1)} %pad_maximum_fusion.refs_6_), channel_id=1, source_target_pairs={{6,0},{7,1},{4,2},{5,3},{10,4},{11,5},{8,6},{9,7},{14,8},{15,9},{1... | collective-permute-start | bytes 393224 | tf_op jit(solution)/shard_map/ppermute | solution.py:29
  23.8 2.0 %collective-permute-start.8 = (bf16[256,256]{1,0:T(8,128)(2,1)S(1)}, bf16[256,256]{1,0:T(8,128)(2,1)S(1)}, u32[]{:S(2)}, u32[]{:S(2)}) collective-permute-start(bf16[256,256]{1,0:T(8,128)(2,1)S(1)} %pad_maximum_fusion.refs_6_), channel_id=1, source_target_pairs={{14,0},{15,1},{12,2},{13,3},{2,4},{3,5},{0,6},{1,7},{6,8},{7,9},{4... | collective-permute-start | bytes 393224 | tf_op jit(solution)/shard_map/ppermute | solution.py:29
  25.8 2.1 %collective-permute-start.9 = (bf16[256,256]{1,0:T(8,128)(2,1)S(1)}, bf16[256,256]{1,0:T(8,128)(2,1)S(1)}, u32[]{:S(2)}, u32[]{:S(2)}) collective-permute-start(bf16[256,256]{1,0:T(8,128)(2,1)S(1)} %pad_maximum_fusion.refs_6_), channel_id=1, source_target_pairs={{10,0},{11,1},{8,2},{9,3},{14,4},{15,5},{12,6},{13,7},{2,8},{3,9},... | collective-permute-start | bytes 393224 | tf_op jit(solution)/shard_map/ppermute | solution.py:29
  27.9 11.6 %attention_first.1 = (bf16[4,128,1024]{2,1,0:T(8,128)(2,1)S(1)}, bf16[4,128,1024]{2,1,0:T(8,128)(2,1)S(1)}, bf16[4,128,1024]{2,1,0:T(8,128)(2,1)S(1)}, bf16[4,12...) custom-call(s32[28]{0:T(128)S(1)} %concatenate.24.meta, ...), custom_call_target="tpu_custom_call" | custom-call | flops 60000002048 | bytes 1048576 | tf_op jit(solution)/shard_map/attention_first/pallas_call | solution.py:275
  39.6 4.3 %collective-permute-start.12 = (bf16[256,256]{1,0:T(8,128)(2,1)S(1)}, bf16[256,256]{1,0:T(8,128)(2,1)S(1)}, u32[]{:S(2)}, u32[]{:S(2)}) collective-permute-start(bf16[256,256]{1,0:T(8,128)(2,1)S(1)} %get-tuple-element.88), channel_id=1, source_target_pairs={{12,0},{13,1},{14,2},{15,3},{0,4},{1,5},{2,6},{3,7},{4,8},{5,9},{6... | collective-permute-start | bytes 393224 | tf_op jit(solution)/shard_map/ppermute | solution.py:29
  43.8 3.2 %collective-permute-start.14 = (bf16[256,256]{1,0:T(8,128)(2,1)S(1)}, bf16[256,256]{1,0:T(8,128)(2,1)S(1)}, u32[]{:S(2)}, u32[]{:S(2)}) collective-permute-start(bf16[256,256]{1,0:T(8,128)(2,1)S(1)} %get-tuple-element.90), channel_id=1, source_target_pairs={{8,0},{9,1},{10,2},{11,3},{12,4},{13,5},{14,6},{15,7},{0,8},{1,9},... | collective-permute-start | bytes 393224 | tf_op jit(solution)/shard_map/ppermute | solution.py:29
  47.0 11.1 %attention_second.1 = (f32[256,1024]{1,0:T(8,128)S(1)}, bf16[256,1024]{1,0:T(8,128)(2,1)S(1)}, bf16[256,256]{1,0:T(8,128)(2,1)S(1)}, bf16[256,256]{1,0:T(8,128)(...) custom-call(s32[28]{0:T(128)S(1)} %concatenate.22.meta, ...), custom_call_target="tpu_custom_call" | custom-call | flops 60000002048 | bytes 1048576 | tf_op jit(solution)/shard_map/attention_second/pallas_call | solution.py:294
  58.2 1.2 collective-permute-start.15
  59.4 3.1 %collective-permute-start.16 = (bf16[256,256]{1,0:T(8,128)(2,1)S(1)}, bf16[256,256]{1,0:T(8,128)(2,1)S(1)}, u32[]{:S(2)}, u32[]{:S(2)}) collective-permute-start(bf16[256,256]{1,0:T(8,128)(2,1)S(1)} %get-tuple-element.97), channel_id=1, source_target_pairs={{14,0},{15,1},{12,2},{13,3},{2,4},{3,5},{0,6},{1,7},{6,8},{7,9},{4... | collective-permute-start | bytes 393224 | tf_op jit(solution)/shard_map/ppermute | solution.py:29
  62.5 1.3 collective-permute-start.17
  63.8 7.2 %collective-permute-start.18 = (bf16[256,256]{1,0:T(8,128)(2,1)S(1)}, bf16[256,256]{1,0:T(8,128)(2,1)S(1)}, u32[]{:S(2)}, u32[]{:S(2)}) collective-permute-start(bf16[256,256]{1,0:T(8,128)(2,1)S(1)} %get-tuple-element.99), channel_id=1, source_target_pairs={{10,0},{11,1},{8,2},{9,3},{14,4},{15,5},{12,6},{13,7},{2,8},{3,9},... | collective-permute-start | bytes 393224 | tf_op jit(solution)/shard_map/ppermute | solution.py:29
  71.0 1.0 collective-permute-done.17
  72.0 1.9 %collective-permute-done.18 = bf16[256,256]{1,0:T(8,128)(2,1)S(1)} collective-permute-done((bf16[256,256]{1,0:T(8,128)(2,1)S(1)}, bf16[256,256]{1,0:T(8,128)(2,1)S(1)}, u32[]{:S(2)}, u32[]{:S(2)}) %collective-permute-start.18) | collective-permute-done | bytes 131104 | tf_op jit(solution)/shard_map/ppermute | solution.py:29
  74.1 0.1 collective-permute-start.19
  74.2 1.3 collective-permute-done.19.g_other
  75.5 3.7 %project.1 = bf16[16,256,256]{2,1,0:T(8,128)(2,1)} custom-call(bf16[4096,256]{1,0:T(8,128)(2,1)S(1)} %get-tuple-element.85.mine_ref, bf16[4096,256]{1,0:T(8,128)(2,1)S(1)} %collective-permute-done.11.other_ref, bf16[256,256]{1,0:T(8,128)(2,1)S(1)} %add_convert_fusion.1.g_own, bf16[256,256]{1,0:T(8,128)(2,1)S(1)} %collective-permute-done.19.g_other), custom_call_target="tpu_custom_call" | custom-call | flops 1073741824 | bytes 8388608 | tf_op jit(solution)/shard_map/project/pallas_call | solution.py:337
  79.2 9.6 %all-to-all-start = ((bf16[16,256,256]{2,1,0:T(8,128)(2,1)}), bf16[16,256,256]{2,1,0:T(8,128)(2,1)S(1)}, u32[]{:S(2)}, u32[]{:S(2)}) async-start(bf16[16,256,256]{2,1,0:T(8,128)(2,1)} %project.1), calls=%async_computation | async-start | bytes 4194304 | tf_op jit(solution)/shard_map/all_to_all | solution.py:413
  88.8 33.8 %all-to-all-done.in_ref = bf16[16,256,256]{2,1,0:T(8,128)(2,1)S(1)} async-done(((bf16[16,256,256]{2,1,0:T(8,128)(2,1)}), bf16[16,256,256]{2,1,0:T(8,128)(2,1)S(1)}, u32[]{:S(2)}, u32[]{:S(2)}) %all-to-all-start) | async-done | bytes 2097184 | tf_op jit(solution)/shard_map/all_to_all | solution.py:413
  122.7 0.3 sum_terms.1
  122.9 2.0 %collective-permute-start.20 = (bf16[32,256]{1,0:T(8,128)(2,1)S(1)}, bf16[32,256]{1,0:T(8,128)(2,1)S(1)}, u32[]{:S(2)}, u32[]{:S(2)}) collective-permute-start(bf16[32,256]{1,0:T(8,128)(2,1)S(1)} %get-tuple-element.101), channel_id=1, source_target_pairs={{224,0},{225,1},{226,2},{227,3},{228,4},{229,5},{230,6},{231,7},{2... | collective-permute-start | bytes 49160 | tf_op jit(solution)/shard_map/ppermute | solution.py:29
  124.9 3.3 %collective-permute-start.21 = (bf16[32,256]{1,0:T(8,128)(2,1)S(1)}, bf16[32,256]{1,0:T(8,128)(2,1)S(1)}, u32[]{:S(2)}, u32[]{:S(2)}) collective-permute-start(bf16[32,256]{1,0:T(8,128)(2,1)S(1)} %get-tuple-element.102), channel_id=1, source_target_pairs={{192,0},{193,1},{194,2},{195,3},{196,4},{197,5},{198,6},{199,7},{2... | collective-permute-start | bytes 49160 | tf_op jit(solution)/shard_map/ppermute | solution.py:29
  128.2 4.0 %collective-permute-start.22 = (bf16[32,256]{1,0:T(8,128)(2,1)S(1)}, bf16[32,256]{1,0:T(8,128)(2,1)S(1)}, u32[]{:S(2)}, u32[]{:S(2)}) collective-permute-start(bf16[32,256]{1,0:T(8,128)(2,1)S(1)} %get-tuple-element.103), channel_id=1, source_target_pairs={{160,0},{161,1},{162,2},{163,3},{164,4},{165,5},{166,6},{167,7},{1... | collective-permute-start | bytes 49160 | tf_op jit(solution)/shard_map/ppermute | solution.py:29
  132.2 0.5 collective-permute-start.23
  132.8 4.9 %collective-permute-start.24 = (bf16[32,256]{1,0:T(8,128)(2,1)S(1)}, bf16[32,256]{1,0:T(8,128)(2,1)S(1)}, u32[]{:S(2)}, u32[]{:S(2)}) collective-permute-start(bf16[32,256]{1,0:T(8,128)(2,1)S(1)} %get-tuple-element.105), channel_id=1, source_target_pairs={{96,0},{97,1},{98,2},{99,3},{100,4},{101,5},{102,6},{103,7},{104,8... | collective-permute-start | bytes 49160 | tf_op jit(solution)/shard_map/ppermute | solution.py:29
  137.7 2.7 %collective-permute-start.25 = (bf16[32,256]{1,0:T(8,128)(2,1)S(1)}, bf16[32,256]{1,0:T(8,128)(2,1)S(1)}, u32[]{:S(2)}, u32[]{:S(2)}) collective-permute-start(bf16[32,256]{1,0:T(8,128)(2,1)S(1)} %get-tuple-element.106), channel_id=1, source_target_pairs={{64,0},{65,1},{66,2},{67,3},{68,4},{69,5},{70,6},{71,7},{72,8},{73... | collective-permute-start | bytes 49160 | tf_op jit(solution)/shard_map/ppermute | solution.py:29
  140.4 1.0 collective-permute-start.26
  141.4 2.0 %fusion = bf16[1,256,1024]{2,1,0:T(8,128)(2,1)} fusion(f32[256,1024]{1,0:T(8,128)S(1)} %get-tuple-element.83, bf16[256,1024]{1,0:T(8,128)(2,1)} %collective-permute-done.10), kind=kLoop, calls=%fused_computation.1 | loop fusion | flops 786432 | bytes 2097152 | tf_op jit(solution)/shard_map/broadcast_in_dim | solution.py:410
  143.4 0.7 collective-permute-done.26
  144.1 0.6 convert_add_fusion.1
  (45 shorter events, 0.6 us)
Async XLA Ops:
  1.5 9.6 %collective-permute-start.3 = (bf16[256,256]{1,0:T(8,128)(2,1)S(1)}, bf16[256,256]{1,0:T(8,128)(2,1)S(1)}, u32[]{:S(2)}, u32[]{:S(2)}) collective-permute-start(bf16[256,256]{1,0:T(8,128)(2,1)S(1)} %pad_maximum_fusion.refs_6_), channel_id=1, source_target_pairs={{4,0},{5,1},{6,2},{7,3},{8,4},{9,5},{10,6},{11,7},{12,8},{13,9},{1... | collective-permute-start | bytes 393224 | tf_op jit(solution)/shard_map/ppermute | solution.py:29
  2.1 17.0 %collective-permute-start.4 = (bf16[256,256]{1,0:T(8,128)(2,1)S(1)}, bf16[256,256]{1,0:T(8,128)(2,1)S(1)}, u32[]{:S(2)}, u32[]{:S(2)}) collective-permute-start(bf16[256,256]{1,0:T(8,128)(2,1)S(1)} %pad_maximum_fusion.refs_6_), channel_id=1, source_target_pairs={{12,0},{13,1},{14,2},{15,3},{0,4},{1,5},{2,6},{3,7},{4,8},{5,9},{6... | collective-permute-start | bytes 393224 | tf_op jit(solution)/shard_map/ppermute | solution.py:29
  3.6 15.5 %collective-permute-start.5 = (bf16[256,256]{1,0:T(8,128)(2,1)S(1)}, bf16[256,256]{1,0:T(8,128)(2,1)S(1)}, u32[]{:S(2)}, u32[]{:S(2)}) collective-permute-start(bf16[256,256]{1,0:T(8,128)(2,1)S(1)} %pad_maximum_fusion.refs_6_), channel_id=1, source_target_pairs={{8,0},{9,1},{10,2},{11,3},{12,4},{13,5},{14,6},{15,7},{0,8},{1,9},... | collective-permute-start | bytes 393224 | tf_op jit(solution)/shard_map/ppermute | solution.py:29
  5.9 20.0 %collective-permute-start.1 = (bf16[256,1024]{1,0:T(8,128)(2,1)}, bf16[256,1024]{1,0:T(8,128)(2,1)S(1)}, u32[]{:S(2)}, u32[]{:S(2)}) collective-permute-start(bf16[256,1024]{1,0:T(8,128)(2,1)} %bitcast.33), channel_id=1, source_target_pairs={{1,0},{0,1},{3,2},{2,3},{5,4},{4,5},{7,6},{6,7},{9,8},{8,9},{11,10... | collective-permute-start | bytes 1572872 | tf_op jit(solution)/shard_map/ppermute | solution.py:29
  5.9 22.0 %collective-permute-start = (bf16[256,1024]{1,0:T(8,128)(2,1)}, bf16[256,1024]{1,0:T(8,128)(2,1)S(1)}, u32[]{:S(2)}, u32[]{:S(2)}) collective-permute-start(bf16[256,1024]{1,0:T(8,128)(2,1)} %bitcast.37), channel_id=1, source_target_pairs={{1,0},{0,1},{3,2},{2,3},{5,4},{4,5},{7,6},{6,7},{9,8},{8,9},{11,10... | collective-permute-start | bytes 1572872 | tf_op jit(solution)/shard_map/ppermute | solution.py:29
  8.0 1.0 copy-start.1
  9.1 1.0 copy-start.2
  10.1 0.7 copy-start.4
  11.2 12.7 %collective-permute-start.2 = (f32[8,1024]{1,0:T(8,128)S(1)}, f32[8,1024]{1,0:T(8,128)S(1)}, u32[]{:S(2)}, u32[]{:S(2)}) collective-permute-start(f32[8,1024]{1,0:T(8,128)S(1)} %row_stats.1.refs_4_), channel_id=1, source_target_pairs={{1,0},{0,1},{3,2},{2,3},{5,4},{4,5},{7,6},{6,7},{9,8},{8,9},{11,10... | collective-permute-start | bytes 98312 | tf_op jit(solution)/shard_map/ppermute | solution.py:29
  11.6 2.2 %copy-start = (bf16[1,256,8192]{2,1,0:T(8,128)(2,1)S(1)}, bf16[1,256,8192]{2,1,0:T(8,128)(2,1)}, u32[]{:S(2)}) copy-start(bf16[1,256,8192]{2,1,0:T(8,128)(2,1)} %param.8) | copy-start | bytes 12582916
  13.8 14.2 %copy-start.3 = (bf16[1,256,1024]{2,1,0:T(8,128)(2,1)S(1)}, bf16[1,256,1024]{2,1,0:T(8,128)(2,1)}, u32[]{:S(2)}) copy-start(bf16[1,256,1024]{2,1,0:T(8,128)(2,1)} %param.13) | copy-start | bytes 1572868
  13.8 14.2 %copy-start.5 = (bf16[1,256,1024]{2,1,0:T(8,128)(2,1)S(1)}, bf16[1,256,1024]{2,1,0:T(8,128)(2,1)}, u32[]{:S(2)}) copy-start(bf16[1,256,1024]{2,1,0:T(8,128)(2,1)} %param.9) | copy-start | bytes 1572868
  19.1 24.7 %collective-permute-start.6 = (bf16[256,256]{1,0:T(8,128)(2,1)S(1)}, bf16[256,256]{1,0:T(8,128)(2,1)S(1)}, u32[]{:S(2)}, u32[]{:S(2)}) collective-permute-start(bf16[256,256]{1,0:T(8,128)(2,1)S(1)} %pad_maximum_fusion.refs_6_), channel_id=1, source_target_pairs={{2,0},{3,1},{0,2},{1,3},{6,4},{7,5},{4,6},{5,7},{10,8},{11,9},{8,1... | collective-permute-start | bytes 393224 | tf_op jit(solution)/shard_map/ppermute | solution.py:29
  21.4 22.4 %collective-permute-start.7 = (bf16[256,256]{1,0:T(8,128)(2,1)S(1)}, bf16[256,256]{1,0:T(8,128)(2,1)S(1)}, u32[]{:S(2)}, u32[]{:S(2)}) collective-permute-start(bf16[256,256]{1,0:T(8,128)(2,1)S(1)} %pad_maximum_fusion.refs_6_), channel_id=1, source_target_pairs={{6,0},{7,1},{4,2},{5,3},{10,4},{11,5},{8,6},{9,7},{14,8},{15,9},{1... | collective-permute-start | bytes 393224 | tf_op jit(solution)/shard_map/ppermute | solution.py:29
  23.8 23.2 %collective-permute-start.8 = (bf16[256,256]{1,0:T(8,128)(2,1)S(1)}, bf16[256,256]{1,0:T(8,128)(2,1)S(1)}, u32[]{:S(2)}, u32[]{:S(2)}) collective-permute-start(bf16[256,256]{1,0:T(8,128)(2,1)S(1)} %pad_maximum_fusion.refs_6_), channel_id=1, source_target_pairs={{14,0},{15,1},{12,2},{13,3},{2,4},{3,5},{0,6},{1,7},{6,8},{7,9},{4... | collective-permute-start | bytes 393224 | tf_op jit(solution)/shard_map/ppermute | solution.py:29
  25.8 21.2 %collective-permute-start.9 = (bf16[256,256]{1,0:T(8,128)(2,1)S(1)}, bf16[256,256]{1,0:T(8,128)(2,1)S(1)}, u32[]{:S(2)}, u32[]{:S(2)}) collective-permute-start(bf16[256,256]{1,0:T(8,128)(2,1)S(1)} %pad_maximum_fusion.refs_6_), channel_id=1, source_target_pairs={{10,0},{11,1},{8,2},{9,3},{14,4},{15,5},{12,6},{13,7},{2,8},{3,9},... | collective-permute-start | bytes 393224 | tf_op jit(solution)/shard_map/ppermute | solution.py:29
  39.6 18.6 %collective-permute-start.12 = (bf16[256,256]{1,0:T(8,128)(2,1)S(1)}, bf16[256,256]{1,0:T(8,128)(2,1)S(1)}, u32[]{:S(2)}, u32[]{:S(2)}) collective-permute-start(bf16[256,256]{1,0:T(8,128)(2,1)S(1)} %get-tuple-element.88), channel_id=1, source_target_pairs={{12,0},{13,1},{14,2},{15,3},{0,4},{1,5},{2,6},{3,7},{4,8},{5,9},{6... | collective-permute-start | bytes 393224 | tf_op jit(solution)/shard_map/ppermute | solution.py:29
  43.8 14.3 %collective-permute-start.13 = (bf16[256,256]{1,0:T(8,128)(2,1)S(1)}, bf16[256,256]{1,0:T(8,128)(2,1)S(1)}, u32[]{:S(2)}, u32[]{:S(2)}) collective-permute-start(bf16[256,256]{1,0:T(8,128)(2,1)S(1)} %get-tuple-element.89), channel_id=1, source_target_pairs={{4,0},{5,1},{6,2},{7,3},{8,4},{9,5},{10,6},{11,7},{12,8},{13,9},{1... | collective-permute-start | bytes 393224 | tf_op jit(solution)/shard_map/ppermute | solution.py:29
  43.8 14.3 %collective-permute-start.14 = (bf16[256,256]{1,0:T(8,128)(2,1)S(1)}, bf16[256,256]{1,0:T(8,128)(2,1)S(1)}, u32[]{:S(2)}, u32[]{:S(2)}) collective-permute-start(bf16[256,256]{1,0:T(8,128)(2,1)S(1)} %get-tuple-element.90), channel_id=1, source_target_pairs={{8,0},{9,1},{10,2},{11,3},{12,4},{13,5},{14,6},{15,7},{0,8},{1,9},... | collective-permute-start | bytes 393224 | tf_op jit(solution)/shard_map/ppermute | solution.py:29
  47.0 28.5 %collective-permute-start.11 = (bf16[4096,256]{1,0:T(8,128)(2,1)S(1)}, bf16[4096,256]{1,0:T(8,128)(2,1)S(1)}, u32[]{:S(2)}, u32[]{:S(2)}) collective-permute-start(bf16[4096,256]{1,0:T(8,128)(2,1)S(1)} %get-tuple-element.86), channel_id=1, source_target_pairs={{1,0},{0,1},{3,2},{2,3},{5,4},{4,5},{7,6},{6,7},{9,8},{8,9},{11,10... | collective-permute-start | bytes 6291464 | tf_op jit(solution)/shard_map/ppermute | solution.py:29
  58.1 17.4 %copy-start.6 = (bf16[256,1024]{1,0:T(8,128)(2,1)}, bf16[256,1024]{1,0:T(8,128)(2,1)S(1)}, u32[]{:S(2)}) copy-start(bf16[256,1024]{1,0:T(8,128)(2,1)S(1)} %get-tuple-element.84) | copy-start | bytes 1572868
  58.2 12.8 %collective-permute-start.15 = (bf16[256,256]{1,0:T(8,128)(2,1)S(1)}, bf16[256,256]{1,0:T(8,128)(2,1)S(1)}, u32[]{:S(2)}, u32[]{:S(2)}) collective-permute-start(bf16[256,256]{1,0:T(8,128)(2,1)S(1)} %get-tuple-element.96), channel_id=1, source_target_pairs={{2,0},{3,1},{0,2},{1,3},{6,4},{7,5},{4,6},{5,7},{10,8},{11,9},{8,1... | collective-permute-start | bytes 393224 | tf_op jit(solution)/shard_map/ppermute | solution.py:29
  59.4 11.7 %collective-permute-start.16 = (bf16[256,256]{1,0:T(8,128)(2,1)S(1)}, bf16[256,256]{1,0:T(8,128)(2,1)S(1)}, u32[]{:S(2)}, u32[]{:S(2)}) collective-permute-start(bf16[256,256]{1,0:T(8,128)(2,1)S(1)} %get-tuple-element.97), channel_id=1, source_target_pairs={{14,0},{15,1},{12,2},{13,3},{2,4},{3,5},{0,6},{1,7},{6,8},{7,9},{4... | collective-permute-start | bytes 393224 | tf_op jit(solution)/shard_map/ppermute | solution.py:29
  62.5 9.6 %collective-permute-start.17 = (bf16[256,256]{1,0:T(8,128)(2,1)S(1)}, bf16[256,256]{1,0:T(8,128)(2,1)S(1)}, u32[]{:S(2)}, u32[]{:S(2)}) collective-permute-start(bf16[256,256]{1,0:T(8,128)(2,1)S(1)} %get-tuple-element.98), channel_id=1, source_target_pairs={{6,0},{7,1},{4,2},{5,3},{10,4},{11,5},{8,6},{9,7},{14,8},{15,9},{1... | collective-permute-start | bytes 393224 | tf_op jit(solution)/shard_map/ppermute | solution.py:29
  63.8 10.2 %collective-permute-start.18 = (bf16[256,256]{1,0:T(8,128)(2,1)S(1)}, bf16[256,256]{1,0:T(8,128)(2,1)S(1)}, u32[]{:S(2)}, u32[]{:S(2)}) collective-permute-start(bf16[256,256]{1,0:T(8,128)(2,1)S(1)} %get-tuple-element.99), channel_id=1, source_target_pairs={{10,0},{11,1},{8,2},{9,3},{14,4},{15,5},{12,6},{13,7},{2,8},{3,9},... | collective-permute-start | bytes 393224 | tf_op jit(solution)/shard_map/ppermute | solution.py:29
  74.1 1.4 collective-permute-start.19
  79.2 43.5 %all-to-all-start = ((bf16[16,256,256]{2,1,0:T(8,128)(2,1)}), bf16[16,256,256]{2,1,0:T(8,128)(2,1)S(1)}, u32[]{:S(2)}, u32[]{:S(2)}) async-start(bf16[16,256,256]{2,1,0:T(8,128)(2,1)} %project.1), calls=%async_computation | async-start | bytes 4194304 | tf_op jit(solution)/shard_map/all_to_all | solution.py:413
  88.8 44.0 %collective-permute-start.10 = (bf16[256,1024]{1,0:T(8,128)(2,1)}, bf16[256,1024]{1,0:T(8,128)(2,1)}, u32[]{:S(2)}, u32[]{:S(2)}) collective-permute-start(bf16[256,1024]{1,0:T(8,128)(2,1)} %copy-done.6), channel_id=1, source_target_pairs={{1,0},{0,1},{3,2},{2,3},{5,4},{4,5},{7,6},{6,7},{9,8},{8,9},{11,10... | collective-permute-start | bytes 1572872 | tf_op jit(solution)/shard_map/ppermute | solution.py:29
  122.9 14.8 %collective-permute-start.20 = (bf16[32,256]{1,0:T(8,128)(2,1)S(1)}, bf16[32,256]{1,0:T(8,128)(2,1)S(1)}, u32[]{:S(2)}, u32[]{:S(2)}) collective-permute-start(bf16[32,256]{1,0:T(8,128)(2,1)S(1)} %get-tuple-element.101), channel_id=1, source_target_pairs={{224,0},{225,1},{226,2},{227,3},{228,4},{229,5},{230,6},{231,7},{2... | collective-permute-start | bytes 49160 | tf_op jit(solution)/shard_map/ppermute | solution.py:29
  124.9 15.5 %collective-permute-start.21 = (bf16[32,256]{1,0:T(8,128)(2,1)S(1)}, bf16[32,256]{1,0:T(8,128)(2,1)S(1)}, u32[]{:S(2)}, u32[]{:S(2)}) collective-permute-start(bf16[32,256]{1,0:T(8,128)(2,1)S(1)} %get-tuple-element.102), channel_id=1, source_target_pairs={{192,0},{193,1},{194,2},{195,3},{196,4},{197,5},{198,6},{199,7},{2... | collective-permute-start | bytes 49160 | tf_op jit(solution)/shard_map/ppermute | solution.py:29
  128.2 15.2 %collective-permute-start.22 = (bf16[32,256]{1,0:T(8,128)(2,1)S(1)}, bf16[32,256]{1,0:T(8,128)(2,1)S(1)}, u32[]{:S(2)}, u32[]{:S(2)}) collective-permute-start(bf16[32,256]{1,0:T(8,128)(2,1)S(1)} %get-tuple-element.103), channel_id=1, source_target_pairs={{160,0},{161,1},{162,2},{163,3},{164,4},{165,5},{166,6},{167,7},{1... | collective-permute-start | bytes 49160 | tf_op jit(solution)/shard_map/ppermute | solution.py:29
  132.2 11.2 %collective-permute-start.23 = (bf16[32,256]{1,0:T(8,128)(2,1)S(1)}, bf16[32,256]{1,0:T(8,128)(2,1)S(1)}, u32[]{:S(2)}, u32[]{:S(2)}) collective-permute-start(bf16[32,256]{1,0:T(8,128)(2,1)S(1)} %get-tuple-element.104), channel_id=1, source_target_pairs={{128,0},{129,1},{130,2},{131,3},{132,4},{133,5},{134,6},{135,7},{1... | collective-permute-start | bytes 49160 | tf_op jit(solution)/shard_map/ppermute | solution.py:29
  132.8 10.6 %collective-permute-start.24 = (bf16[32,256]{1,0:T(8,128)(2,1)S(1)}, bf16[32,256]{1,0:T(8,128)(2,1)S(1)}, u32[]{:S(2)}, u32[]{:S(2)}) collective-permute-start(bf16[32,256]{1,0:T(8,128)(2,1)S(1)} %get-tuple-element.105), channel_id=1, source_target_pairs={{96,0},{97,1},{98,2},{99,3},{100,4},{101,5},{102,6},{103,7},{104,8... | collective-permute-start | bytes 49160 | tf_op jit(solution)/shard_map/ppermute | solution.py:29
  137.7 5.7 %collective-permute-start.25 = (bf16[32,256]{1,0:T(8,128)(2,1)S(1)}, bf16[32,256]{1,0:T(8,128)(2,1)S(1)}, u32[]{:S(2)}, u32[]{:S(2)}) collective-permute-start(bf16[32,256]{1,0:T(8,128)(2,1)S(1)} %get-tuple-element.106), channel_id=1, source_target_pairs={{64,0},{65,1},{66,2},{67,3},{68,4},{69,5},{70,6},{71,7},{72,8},{73... | collective-permute-start | bytes 49160 | tf_op jit(solution)/shard_map/ppermute | solution.py:29
  140.4 3.7 %collective-permute-start.26 = (bf16[32,256]{1,0:T(8,128)(2,1)S(1)}, bf16[32,256]{1,0:T(8,128)(2,1)S(1)}, u32[]{:S(2)}, u32[]{:S(2)}) collective-permute-start(bf16[32,256]{1,0:T(8,128)(2,1)S(1)} %get-tuple-element.107), channel_id=1, source_target_pairs={{32,0},{33,1},{34,2},{35,3},{36,4},{37,5},{38,6},{39,7},{40,8},{41... | collective-permute-start | bytes 49160 | tf_op jit(solution)/shard_map/ppermute | solution.py:29

commit v3 on v2

--- a/solution.py
+++ b/solution.py
@@ -1,3 +1,4 @@
+import functools
 import math
 
 import jax
@@ -41,8 +42,11 @@
     return lambda z, yl, x, yh, c: ((z + k) % Z, yl, x, yh, c)
 
 
-FIRST = [(0, 0), (1, 0), (3, 0), (2, 0)]
-SECOND = [(0, 1), (1, 1), (3, 1), (2, 1)]
+def swap_z(z, yl, x, yh, c):
+    return (z ^ 1, yl, x, yh, c)
+
+
+ALONG_X = (0, 1, 3, 2)
 
 
 def vmem():
@@ -57,7 +61,18 @@
     return pl.BlockSpec(memory_space=pl.ANY)
 
 
-def stats_kernel(out_ref, grad_ref, lse_ref, stats_ref):
+def hbm():
+    return pl.BlockSpec(memory_space=pltpu.HBM)
+
+
+def stats_kernel(out_hbm, grad_hbm, lse_hbm, stats_ref, out_ref, grad_ref, lse_ref, sems):
+    pairs = ((out_hbm, out_ref), (grad_hbm, grad_ref), (lse_hbm, lse_ref))
+    copies = [pltpu.make_async_copy(a, b, sems.at[n]) for n, (a, b) in enumerate(pairs)]
+    for copy in copies:
+        copy.start()
+    stats_ref[4:8, :] = jnp.zeros((4, H * BLK), F32)
+    for copy in copies:
+        copy.wait()
     for h in range(H):
         cols = slice(h * BLK, (h + 1) * BLK)
         product = out_ref[:, cols].astype(F32) * grad_ref[:, cols].astype(F32)
@@ -67,52 +82,111 @@
             rows = slice(i * BLK, (i + 1) * BLK)
             stats_ref[i : i + 1, cols] = lse2[:, rows]
             stats_ref[2 + i : 3 + i, cols] = delta[:, rows]
-    stats_ref[4:8, :] = jnp.zeros((4, H * BLK), F32)
 
 
 def row_stats(saved, grad, lse):
     return pl.pallas_call(
         stats_kernel,
         out_shape=jax.ShapeDtypeStruct((8, H * BLK), F32),
-        in_specs=[vmem()] * 3,
+        in_specs=[hbm()] * 3,
         out_specs=vmem(),
+        scratch_shapes=[
+            pltpu.VMEM((256, H * BLK), BF16),
+            pltpu.VMEM((256, H * BLK), BF16),
+            pltpu.VMEM((H, 256), F32),
+            pltpu.SemaphoreType.DMA((3,)),
+        ],
         compiler_params=pltpu.CompilerParams(vmem_limit_bytes=8 * 2**20),
         cost_estimate=pl.CostEstimate(flops=10**6, bytes_accessed=2**20, transcendentals=0),
         name="row_stats",
     )(saved, grad, lse)
 
 
-def turn_kernel(me, x_ref, mine_ref, other_ref):
-    even = me[0] == 0
-    for u in range(8):
-        tile = x_ref[:, u * BLK : (u + 1) * BLK].T
-        for yh in range(YH):
-            first = tile[yh * 64 : yh * 64 + 32]
-            second = tile[yh * 64 + 32 : yh * 64 + 64]
-            at = slice(u * 64 + yh * 32, u * 64 + yh * 32 + 32)
-
-            @pl.when(even)
-            def _():
-                mine_ref[at, :] = first
-                other_ref[at, :] = second
-
-            @pl.when(jnp.logical_not(even))
-            def _():
-                mine_ref[at, :] = second
-                other_ref[at, :] = first
-
-
-def turn(me, layer):
+SLABS = Z // 2
+
+
+def cut_kernel(place, x_ref, k_ref, v_ref, a_ref, b_ref, own_ref, pair_ref, sems):
+    moves = [
+        (k_ref, pair_ref.at[:, pl.ds(0, BLK)]),
+        (v_ref, pair_ref.at[:, pl.ds(BLK, BLK)]),
+    ]
+    for j in range(SLABS):
+        at = pl.ds(pl.multiple_of((2 * j + 1 - place[1]) * 1024, 1024), 1024)
+        moves.append((x_ref.at[:, at], (a_ref, b_ref)[j // 2].at[j % 2]))
+    for j in range(SLABS):
+        at = pl.ds(pl.multiple_of((2 * j + place[1]) * 1024, 1024), 1024)
+        moves.append((x_ref.at[:, at], own_ref.at[j]))
+    copies = [pltpu.make_async_copy(a, b, sems.at[n]) for n, (a, b) in enumerate(moves)]
+    for copy in copies:
+        copy.start()
+    for copy in copies:
+        copy.wait()
+
+
+def cut(place, layer, keys, values):
+    half = jax.ShapeDtypeStruct((SLABS // 2, 256, 1024), BF16)
+    return pl.pallas_call(
+        cut_kernel,
+        out_shape=(
+            half,
+            half,
+            jax.ShapeDtypeStruct((SLABS, 256, 1024), BF16),
+            jax.ShapeDtypeStruct((256, 2 * BLK), BF16),
+        ),
+        in_specs=[smem()] + [hbm()] * 3,
+        out_specs=(anywhere(),) * 4,
+        scratch_shapes=[pltpu.SemaphoreType.DMA((2 + 2 * SLABS,))],
+        compiler_params=pltpu.CompilerParams(vmem_limit_bytes=57 * 2**20),
+        name="cut",
+    )(place, layer, keys, values)
+
+
+def turn_kernel(place, *refs):
+    x_refs = refs[:-4]
+    mine_ref, other_ref, slabs, sems = refs[-4:]
+    copies = []
+    for j in range(SLABS):
+        each = SLABS // len(x_refs)
+        source = x_refs[j // each].at[j % each]
+        copies.append(pltpu.make_async_copy(source, slabs.at[j], sems.at[j]))
+    for copy in copies:
+        copy.start()
+    even = place[0] == 0
+    for j in range(SLABS):
+        copies[j].wait()
+        for u in range(8):
+            tile = slabs[j, :, u * BLK : (u + 1) * BLK].T
+            for yh in range(YH):
+                first = tile[yh * 64 : yh * 64 + 32]
+                second = tile[yh * 64 + 32 : yh * 64 + 64]
+                start = j * 512 + u * 64 + yh * 32
+                at = slice(start, start + 32)
+
+                @pl.when(even)
+                def _():
+                    mine_ref[at, :] = first
+                    other_ref[at, :] = second
+
+                @pl.when(jnp.logical_not(even))
+                def _():
+                    mine_ref[at, :] = second
+                    other_ref[at, :] = first
+
+
+def turn(place, *layers):
     return pl.pallas_call(
         turn_kernel,
-        grid=(Z,),
-        out_shape=(jax.ShapeDtypeStruct((4096, 256), BF16),) * 2,
-        in_specs=[smem(), pl.BlockSpec((256, 1024), lambda z: (0, z))],
-        out_specs=(pl.BlockSpec((512, 256), lambda z: (z, 0)),) * 2,
+        out_shape=(jax.ShapeDtypeStruct((2048, 256), BF16),) * 2,
+        in_specs=[smem()] + [anywhere()] * len(layers),
+        out_specs=(vmem(),) * 2,
+        scratch_shapes=[
+            pltpu.VMEM((SLABS, 256, 1024), BF16),
+            pltpu.SemaphoreType.DMA((SLABS,)),
+        ],
         compiler_params=pltpu.CompilerParams(vmem_limit_bytes=8 * 2**20),
-        cost_estimate=pl.CostEstimate(flops=10**7, bytes_accessed=8 * 2**20, transcendentals=0),
+        cost_estimate=pl.CostEstimate(flops=3 * 10**10, bytes_accessed=8 * 2**20, transcendentals=0),
         name="turn",
-    )(me, layer)
+    )(place, *layers)
 
 
 NQ, NK = 4, 8
@@ -181,20 +255,20 @@
     lax.fori_loop(0, NQ, query_block, 0)
 
 
-def store_keys(dkv, dkv_out):
-    for b in range(4):
-        for i in range(2):
-            rows = slice(i * BLK, (i + 1) * BLK)
-            ref = dkv_out[b]
-            ref[rows, :BLK] = (dkv[2 * b + i, :, :BLK] * SCALE).astype(ref.dtype)
-            ref[rows, BLK:] = dkv[2 * b + i, :, BLK:].astype(ref.dtype)
+def store_keys(dkv, refs):
+    for n in range(NK):
+        b, i = n // 2, n % 2
+        ref = refs[b]
+        rows = slice(i * BLK, (i + 1) * BLK)
+        ref[rows, :BLK] = (dkv[n, :, :BLK] * SCALE).astype(ref.dtype)
+        ref[rows, BLK:] = dkv[n, :, BLK:].astype(ref.dtype)
 
 
 def first_kernel(meta, *refs):
     q_in, g_in, s_in, kv_in = refs[0:2], refs[2:4], refs[4:6], refs[6:10]
     q_all, g_all, qt, gt, stats, dqt = refs[10:16]
-    dkv_out = refs[16:20]
-    kv, kt, dkv, pieces, sems = refs[20:]
+    dkv_out = refs[16]
+    kv, kt, dkv, pieces, sems = refs[17:]
     copies = []
     for side in range(2):
         for i in range(2):
@@ -203,7 +277,8 @@
             copies.append((g_in[side].at[rows], g_all.at[2 * side + i]))
         copies.append((s_in[side], pieces.at[side]))
     for b in range(4):
-        copies.append((kv_in[b], kv.at[pl.ds(b * 2 * BLK, 2 * BLK)]))
+        source = kv_in[b].at[pl.ds(2 * BLK, 2 * BLK)]
+        copies.append((source, kv.at[pl.ds(b * 2 * BLK, 2 * BLK)]))
     copies = [pltpu.make_async_copy(s, d, sems.at[n]) for n, (s, d) in enumerate(copies)]
     for copy in copies:
         copy.start()
@@ -225,7 +300,7 @@
     for n in range(NK):
         kt[n] = kv[n * BLK : (n + 1) * BLK, :BLK].T
     key_steps(meta, q_all, g_all, qt, gt, stats, kv, kt, dqt, dkv)
-    store_keys(dkv, dkv_out)
+    store_keys(dkv, [dkv_out.at[pl.ds(b * 2 * BLK, 2 * BLK)] for b in range(4)])
 
 
 def second_kernel(meta, *refs):
@@ -235,7 +310,9 @@
     dkv_out = refs[12:16]
     kv, kt, dkv, dqt, sems = refs[16:]
     copies = [
-        pltpu.make_async_copy(kv_in[b], kv.at[pl.ds(b * 2 * BLK, 2 * BLK)], sems.at[b])
+        pltpu.make_async_copy(
+            kv_in[b].at[pl.ds(0, 2 * BLK)], kv.at[pl.ds(b * 2 * BLK, 2 * BLK)], sems.at[b]
+        )
         for b in range(4)
     ]
     for copy in copies:
@@ -264,12 +341,6 @@
 COST = pl.CostEstimate(flops=6 * 10**10, bytes_accessed=2**20, transcendentals=2 * 10**6)
 
 
-def dkv_shapes(own):
-    return (jax.ShapeDtypeStruct((256, 256), own),) + (
-        jax.ShapeDtypeStruct((256, 256), BF16),
-    ) * 3
-
-
 def first_call(meta, queries, grads, stats, blocks):
     rows = jax.ShapeDtypeStruct((NQ, BLK, WIDE), BF16)
     return pl.pallas_call(
@@ -279,9 +350,9 @@
             jax.ShapeDtypeStruct((2 * NQ, WIDE), F32),
             jax.ShapeDtypeStruct((NQ, BLK, WIDE), F32),
         )
-        + dkv_shapes(F32),
-        in_specs=[smem()] + [anywhere()] * 10,
-        out_specs=(vmem(),) * 10,
+        + (jax.ShapeDtypeStruct((NK * BLK, 2 * BLK), BF16),),
+        in_specs=[smem()] + [hbm(), anywhere()] * 2 + [anywhere()] * 6,
+        out_specs=(vmem(),) * 7,
         scratch_shapes=KEY_SCRATCH
         + [pltpu.VMEM((2, 8, WIDE), F32), pltpu.SemaphoreType.DMA((14,))],
         compiler_params=pltpu.CompilerParams(vmem_limit_bytes=VMEM_LIMIT),
@@ -297,7 +368,7 @@
             jax.ShapeDtypeStruct((256, WIDE), F32),
             jax.ShapeDtypeStruct((256, WIDE), BF16),
         )
-        + dkv_shapes(BF16),
+        + (jax.ShapeDtypeStruct((2 * BLK, 2 * BLK), F32),) * 4,
         in_specs=[smem()] + [vmem()] * 6 + [anywhere()] * 4,
         out_specs=(vmem(),) * 6,
         scratch_shapes=KEY_SCRATCH
@@ -320,36 +391,38 @@
     return jnp.concatenate([order, ordered, q_pos, whole, pairs]).astype(jnp.int32)
 
 
-def project_kernel(mine_ref, other_ref, g_own, g_other, out_ref):
-    def step(z, carry):
-        rows = pl.ds(pl.multiple_of(z * 512, 512), 512)
-        terms = jnp.dot(mine_ref[rows, :], g_own[...], preferred_element_type=F32) + jnp.dot(
-            other_ref[rows, :], g_other[...], preferred_element_type=F32
-        )
-        at = pl.ds(pl.multiple_of(z * 32, 32), 32)
+def project_kernel(a_ref, b_ref, c_ref, d_ref, ga, gb, gc, gd, out_ref):
+    sides = ((a_ref, ga), (b_ref, gb), (c_ref, gc), (d_ref, gd))
+
+    def step(j, carry):
+        rows = pl.ds(pl.multiple_of(j * 512, 512), 512)
+        terms = jnp.zeros((512, 256), F32)
+        for turned, grads in sides:
+            terms = terms + jnp.dot(turned[rows, :], grads[...], preferred_element_type=F32)
+        at = pl.ds(pl.multiple_of(j * 32, 32), 32)
         out_ref[:, at, :] = terms.astype(BF16).reshape(16, 32, 256)
         return carry
 
-    lax.fori_loop(0, Z, step, 0)
-
-
-def project(mine, other, g_own, g_other):
+    lax.fori_loop(0, SLABS, step, 0)
+
+
+def project(turned, grads):
     return pl.pallas_call(
         project_kernel,
-        out_shape=jax.ShapeDtypeStruct((16, 256, 256), BF16),
-        in_specs=[vmem()] * 4,
+        out_shape=jax.ShapeDtypeStruct((16, SLABS * 32, 256), BF16),
+        in_specs=[vmem()] * 8,
         out_specs=vmem(),
-        compiler_params=pltpu.CompilerParams(vmem_limit_bytes=16 * 2**20),
+        compiler_params=pltpu.CompilerParams(vmem_limit_bytes=12 * 2**20),
         cost_estimate=pl.CostEstimate(
             flops=2 * 4096 * 512 * 256, bytes_accessed=8 * 2**20, transcendentals=0
         ),
         name="project",
-    )(mine, other, g_own, g_other)
+    )(*turned, *grads)
 
 
 def sum_kernel(place, in_ref, own_ref, *out_refs):
-    for k in range(Z):
-        at = pl.ds(pl.multiple_of((place[0] + k) % Z * 32, 32), 32)
+    for k in range(SLABS):
+        at = pl.ds(pl.multiple_of((place[2] + k) % SLABS * 32, 32), 32)
         value = in_ref[0, at, :].astype(F32)
         for j in range(1, 16):
             value = value + in_ref[j, at, :].astype(F32)
@@ -361,9 +434,9 @@
     return pl.pallas_call(
         sum_kernel,
         out_shape=(jax.ShapeDtypeStruct((32, 256), F32),)
-        + (jax.ShapeDtypeStruct((32, 256), BF16),) * 7,
+        + (jax.ShapeDtypeStruct((32, 256), BF16),) * (SLABS - 1),
         in_specs=[smem(), vmem()],
-        out_specs=(vmem(),) * 8,
+        out_specs=(vmem(),) * SLABS,
         compiler_params=pltpu.CompilerParams(vmem_limit_bytes=8 * 2**20),
         name="sum_terms",
     )(place, terms)
@@ -372,48 +445,56 @@
 def body(layer_input, query_rows, key_rows, value_rows, attn_out, d_attn, log_sum_exp, block_order):
     z, x, yh, c = (lax.axis_index(name) for name in ("z", "x", "yh", "c"))
     ctx = (x * YH + yh) * C + c
+    place = jnp.stack([c, z % 2, z // 2]).astype(jnp.int32)
 
     q, g = query_rows[0], d_attn[0]
-    pair = jnp.concatenate([key_rows[0], value_rows[0]], axis=1)
-    blocks = [pair] + [fetch(pair, by_ctx(*o)) for o in FIRST[1:]]
+    cut_a, cut_b, cut_own, pair = cut(place, layer_input[0], key_rows[0], value_rows[0])
+    pair_y = fetch(pair, by_ctx(0, 1))
     q_other, g_other = fetch(q, swap_core), fetch(g, swap_core)
+    slabs_a = fetch(cut_a, swap_z)
     stats = row_stats(attn_out[0], g, log_sum_exp[0])
     stats_other = fetch(stats, swap_core)
-    mine, other = turn(c.astype(jnp.int32)[None], layer_input[0])
+    both = jnp.concatenate([pair, pair_y], axis=0)
+    blocks = [both] + [fetch(both, by_ctx(k, 0)) for k in ALONG_X[1:]]
+    mine, other = turn(place, cut_own)
 
     places = block_order.reshape(16, 2)
     q_pos = jnp.concatenate([places[ctx], places[ctx ^ 1]])
 
-    def owners(group):
-        return jnp.concatenate(
-            [places[(x + dx) % X * 4 + (yh ^ dyh) * 2 + c] for dx, dyh in group]
-        )
-
-    pair_again, *blocks = lax.optimization_barrier((pair, *blocks))
-    later = [fetch(pair_again, by_ctx(*o)) for o in SECOND]
-    blocks, mine, other = lax.optimization_barrier((blocks, mine, other))
-    outs = first_call(
-        make_meta(owners(FIRST), q_pos), (q, q_other), (g, g_other), (stats, stats_other), blocks
+    def owners(row):
+        return jnp.concatenate([places[(x + k) % X * 4 + row * 2 + c] for k in ALONG_X])
+
+    blocks, mine, other, slabs_a = lax.optimization_barrier((blocks, mine, other, slabs_a))
+    slabs_b = fetch(cut_b, swap_z)
+    mine_core = fetch(other, swap_core)
+    *carried, dkv_y = first_call(
+        make_meta(owners(1 - yh), q_pos), (q, q_other), (g, g_other), (stats, stats_other), blocks
     )
-    outs, other = lax.optimization_barrier((outs, other))
-    carried, dkv_first = outs[:6], outs[6:]
-    mine_other = fetch(other, swap_core)
-    dq_own, dq_sent, *dkv_second = second_call(make_meta(owners(SECOND), q_pos), carried, later)
-    total = dkv_first[0]
-    for (dx, dyh), part in zip(FIRST[1:], dkv_first[1:]):
-        total = total + fetch(part, by_ctx(-dx, dyh)).astype(F32)
-    total, dkv_second = lax.optimization_barrier((total, dkv_second))
-    for (dx, dyh), part in zip(SECOND, dkv_second):
-        total = total + fetch(part, by_ctx(-dx, dyh)).astype(F32)
+    carried, mine_core = lax.optimization_barrier((carried, mine_core))
+    dq_own, dq_sent, *dkv = second_call(make_meta(owners(yh), q_pos), carried, blocks)
+    dkv_y = fetch(dkv_y, by_ctx(0, 1))
+    dkv = [part + dkv_y[256 * b : 256 * b + 256].astype(F32) for b, part in enumerate(dkv)]
+    parts = [fetch(part.astype(BF16), by_ctx(-k, 0)) for k, part in zip(ALONG_X[1:], dkv[1:])]
+    total = dkv[0]
+    for part in parts:
+        total = total + part.astype(F32)
     grads = total.astype(BF16)
-    grads_other = fetch(grads, swap_core)
+    grads_z = fetch(grads, swap_z)
+    grads_core = fetch(grads, swap_core)
+    slabs_a, slabs_b, grads_core = lax.optimization_barrier((slabs_a, slabs_b, grads_core))
+    grads_zc = fetch(grads_z, swap_core)
+    mine_z, other_z = turn(place, slabs_a, slabs_b)
+    mine_zc = fetch(other_z, swap_core)
+
+    terms = project(
+        (mine, mine_core, mine_z, mine_zc), (grads, grads_core, grads_z, grads_zc)
+    )
+    terms = lax.all_to_all(terms, ("yl", "x", "yh"), 0, 0)
+    terms, dq_sent = lax.optimization_barrier((terms, dq_sent))
+    own, *sent = sum_terms(place, terms)
     d_query = (dq_own + fetch(dq_sent, swap_core).astype(F32)).astype(BF16)[None]
-
-    terms = project(mine, mine_other, grads, grads_other)
-    terms = lax.all_to_all(terms, ("yl", "x", "yh"), 0, 0)
-    own, *sent = sum_terms(z.astype(jnp.int32)[None], terms)
-    for k in range(1, Z):
-        own = own + fetch(sent[k - 1], by_z(-k)).astype(F32)
+    for k in range(1, SLABS):
+        own = own + fetch(sent[k - 1], by_z(-2 * k)).astype(F32)
     return (d_query, own)
 
 

time: 145 us -> 259 us (1.79)
  Pallas kernels: 32.4 us -> 162 us
  starting transfers between devices: 62.1 us -> 26.7 us
  blocking collectives: 0 us -> 22 us
  waiting for transfers between devices: 38.9 us -> 32.1 us
  local copies, waits for them, and re-layouts: 5.92 us -> 9.07 us
    pallas_call x2 -> x4, Pallas kernels: 9.04 us -> 141 us  [the longest x1 133 us: cut(): pl.pallas_call(cut_kernel, out_shape=(half, half, jax.ShapeDtypeStruct((S...]
    all_to_all x1 -> x0, waiting for transfers between devices: 33.8 us -> none  [body(): terms = lax.all_to_all(terms, ('yl', 'x', 'yh'), 0, 0)]
    ppermute x27 -> x22, waiting for transfers between devices: 5.06 us -> 32.1 us  [fetch(): return lax.ppermute(value, AXES, pairs)]
    ppermute x27 -> x22, starting transfers between devices: 52.5 us -> 26.7 us  [fetch(): return lax.ppermute(value, AXES, pairs)]
    all_to_all x0 -> x1, blocking collectives: none -> 22 us  [body(): terms = lax.all_to_all(terms, ('yl', 'x', 'yh'), 0, 0)]
    all_to_all x1 -> x0, starting transfers between devices: 9.59 us -> none  [body(): terms = lax.all_to_all(terms, ('yl', 'x', 'yh'), 0, 0)]
    unnamed x14 -> x33, local copies, waits for them, and re-layouts: 4.99 us -> 6.59 us
  transfers between devices with their start and end apart: 28 -> 22, of which waited for: 5 -> 11; matrix products, arithmetic and copies ran while one was open for 3% -> 2% of each run, Pallas kernels for 20% -> 61%
where the time goes in v3:
time: 259 us; the launch traced here: 256 us
  Pallas kernels  162 us (63%)
  waiting for transfers between devices  32.1 us (12%)
  starting transfers between devices  26.7 us (10%)
  blocking collectives  22 us (8%)
  local copies, waits for them, and re-layouts  9.07 us (4%)
  other arithmetic  3.31 us (1%)
    pallas_call x1, Pallas kernels, cut(): pl.pallas_call(cut_kernel, out_shape=(half, half, jax.ShapeDtypeStruct((S...  133 us
    ppermute x22, waiting for transfers between devices, fetch(): return lax.ppermute(value, AXES, pairs)  32.1 us
    ppermute x22, starting transfers between devices, fetch(): return lax.ppermute(value, AXES, pairs)  26.7 us
    all_to_all x1, blocking collectives, body(): terms = lax.all_to_all(terms, ('yl', 'x', 'yh'), 0, 0)  22 us
    pallas_call x1, Pallas kernels, first_call(): pl.pallas_call(first_kernel, out_shape=(rows,) * 4 + (jax.ShapeDtypeStruc...  10.5 us
    pallas_call x1, Pallas kernels, second_call(): pl.pallas_call(second_kernel, out_shape=(jax.ShapeDtypeStruct((256, WIDE)...  9.49 us
    unnamed x33, local copies, waits for them, and re-layouts  6.59 us
    pallas_call x2, Pallas kernels, turn(): pl.pallas_call(turn_kernel, out_shape=(jax.ShapeDtypeStruct((2048, 256),...  6.37 us
  transfers between devices with their start and end apart: 22, of which 11 were waited for; matrix products, arithmetic and copies ran while one was open for 2% of the time, Pallas kernels for 61%

profile of v3, /device:TPU:4, one launch (start us, length us, event | category | flops | bytes accessed | tf_op | source)
XLA Modules:
  0.0 256.4 jit_solution(3662699051724899434)
XLA Ops:
  0.7 0.5 collective-permute-start.1
  1.2 0.6 pad_add_fusion.3.place
  1.8 133.0 %cut.1 = (bf16[2,256,1024]{2,1,0:T(8,128)(2,1)}, bf16[2,256,1024]{2,1,0:T(8,128)(2,1)}, bf16[4,256,1024]{2,1,0:T(8,128)(2,1)}, bf16[256,256]{1,0:T(8,128)(2,1)}) custom-call(s32[3]{0:T(128)} %pad_add_fusion.3.place, bf16[256,8192]{1,0:T(8,128)(2,1)} %bitcast.39, bf16[256,128]{1,0:T(8,128)(2,1)} %bitcast.40, bf16[256,128]{1,0:T(8,128)(2,1)} %bitcast.41), custom_call_target="tpu_custom_call" | custom-call | tf_op jit(solution)/shard_map/cut/pallas_call | solution.py:128
  134.8 3.3 %collective-permute-start.3 = (bf16[256,256]{1,0:T(8,128)(2,1)}, bf16[256,256]{1,0:T(8,128)(2,1)}, u32[]{:S(2)}, u32[]{:S(2)}) collective-permute-start(bf16[256,256]{1,0:T(8,128)(2,1)} %get-tuple-element.46), channel_id=1, source_target_pairs={{2,0},{3,1},{0,2},{1,3},{6,4},{7,5},{4,6},{5,7},{10,8},{11,9},{8,1... | collective-permute-start | bytes 393224 | tf_op jit(solution)/shard_map/ppermute | solution.py:30
  138.1 1.9 collective-permute-start.7
  140.1 1.6 copy-done.4
  141.7 3.2 %turn.2 = (bf16[2048,256]{1,0:T(8,128)(2,1)S(1)}, bf16[2048,256]{1,0:T(8,128)(2,1)S(1)}) custom-call(s32[3]{0:T(128)S(1)} %copy-done.3, bf16[4,256,1024]{2,1,0:T(8,128)(2,1)S(1)} %copy-done.4), custom_call_target="tpu_custom_call" | custom-call | flops 30000001024 | bytes 8388608 | tf_op jit(solution)/shard_map/turn/pallas_call | solution.py:177
  145.0 1.0 copy-done.5
  146.1 0.3 copy-done.14
  146.6 0.9 constant_dynamic-update-slice_fusion.refs_6_
  147.5 0.6 collective-permute-start.6
  148.1 0.2 convert_reduce_fusion.2
  148.3 2.2 collective-permute-start.5
  150.5 7.8 %collective-permute-done.6.refs_9_ = bf16[512,256]{1,0:T(8,128)(2,1)S(1)} collective-permute-done((bf16[512,256]{1,0:T(8,128)(2,1)S(1)}, bf16[512,256]{1,0:T(8,128)(2,1)S(1)}, u32[]{:S(2)}, u32[]{:S(2)}) %collective-permute-start.6) | collective-permute-done | bytes 262176 | tf_op jit(solution)/shard_map/ppermute | solution.py:30
  158.5 0.5 row_stats.1.refs_4_
  159.2 2.7 %collective-permute-done.5.refs_8_ = bf16[512,256]{1,0:T(8,128)(2,1)S(1)} collective-permute-done((bf16[512,256]{1,0:T(8,128)(2,1)S(1)}, bf16[512,256]{1,0:T(8,128)(2,1)S(1)}, u32[]{:S(2)}, u32[]{:S(2)}) %collective-permute-start.5) | collective-permute-done | bytes 262176 | tf_op jit(solution)/shard_map/ppermute | solution.py:30
  161.9 0.7 copy-done.10
  162.8 0.7 concatenate.22.meta
  163.5 0.7 concatenate.24.meta
  164.2 0.6 collective-permute-done.4.refs_7_
  164.9 1.0 copy-done.6
  166.0 0.9 copy-done.8
  166.9 0.9 copy-done.11
  167.9 10.5 %attention_first.1 = (bf16[4,128,1024]{2,1,0:T(8,128)(2,1)S(1)}, bf16[4,128,1024]{2,1,0:T(8,128)(2,1)S(1)}, bf16[4,128,1024]{2,1,0:T(8,128)(2,1)S(1)}, bf16[4,12...) custom-call(s32[28]{0:T(128)S(1)} %concatenate.24.meta, ...), custom_call_target="tpu_custom_call" | custom-call | flops 60000002048 | bytes 1048576 | tf_op jit(solution)/shard_map/attention_first/pallas_call | solution.py:346
  178.4 0.3 collective-permute-start.10
  178.7 9.5 %attention_second.1 = (f32[256,1024]{1,0:T(8,128)S(1)}, bf16[256,1024]{1,0:T(8,128)(2,1)S(1)}, f32[256,256]{1,0:T(8,128)S(1)}, f32[256,256]{1,0:T(8,128)S(1)}, f...) custom-call(s32[28]{0:T(128)S(1)} %concatenate.22.meta, bf16[4,128,1024]{2,1,0:T(8,128)(2,1)S(1)} %get-tuple-element.62.refs_0_, ...), custom_call_target="tpu_custom_call" | custom-call | flops 60000002048 | bytes 1048576 | tf_op jit(solution)/shard_map/attention_second/pallas_call | solution.py:365
  188.2 6.7 %collective-permute-done.10 = bf16[1024,256]{1,0:T(8,128)(2,1)S(1)} collective-permute-done((bf16[1024,256]{1,0:T(8,128)(2,1)S(1)}, bf16[1024,256]{1,0:T(8,128)(2,1)S(1)}, u32[]{:S(2)}, u32[]{:S(2)}) %collective-permute-start.10) | collective-permute-done | bytes 524320 | tf_op jit(solution)/shard_map/ppermute | solution.py:30
  195.0 1.4 collective-permute-start.11
  196.4 0.6 collective-permute-start.13
  197.0 2.5 collective-permute-start.12
  199.6 0.9 collective-permute-done.11
  200.5 3.6 %collective-permute-done.13 = bf16[256,256]{1,0:T(8,128)(2,1)S(1)} collective-permute-done((bf16[256,256]{1,0:T(8,128)(2,1)S(1)}, bf16[256,256]{1,0:T(8,128)(2,1)S(1)}, u32[]{:S(2)}, u32[]{:S(2)}) %collective-permute-start.13) | collective-permute-done | bytes 131104 | tf_op jit(solution)/shard_map/ppermute | solution.py:30
  204.1 1.1 collective-permute-done.12
  205.4 1.3 collective-permute-done.14.gb
  206.8 3.2 %turn.3 = (bf16[2048,256]{1,0:T(8,128)(2,1)S(1)}, bf16[2048,256]{1,0:T(8,128)(2,1)S(1)}) custom-call(s32[3]{0:T(128)S(1)} %copy-done.3, bf16[2,256,1024]{2,1,0:T(8,128)(2,1)S(1)} %collective-permute-done.7.refs_0_, bf16[2,256,1024]{2,1,0:T(8,128)(2,1)S(1)} %collective-permute-done.9.refs_1_), custom_call_target="tpu_custom_call" | custom-call | flops 30000001024 | bytes 8388608 | tf_op jit(solution)/shard_map/turn/pallas_call | solution.py:177
  210.0 0.3 collective-permute-start.15
  210.2 1.8 collective-permute-start.16
  212.0 4.0 %collective-permute-done.16.gc = bf16[256,256]{1,0:T(8,128)(2,1)S(1)} collective-permute-done((bf16[256,256]{1,0:T(8,128)(2,1)S(1)}, bf16[256,256]{1,0:T(8,128)(2,1)S(1)}, u32[]{:S(2)}, u32[]{:S(2)}) %collective-permute-start.16) | collective-permute-done | bytes 131104 | tf_op jit(solution)/shard_map/ppermute | solution.py:30
  216.0 1.3 collective-permute-done.17.gd
  217.4 1.8 project.1
  219.2 22.0 %all_to_all.5.in_ref = bf16[16,128,256]{2,1,0:T(8,128)(2,1)S(1)} all-to-all(bf16[16,128,256]{2,1,0:T(8,128)(2,1)S(1)} %project.1), channel_id=1, replica_groups=mesh['z'=8,'yl'=2,'x'=4,'yh'=2,'c'=2] {'yl','x','yh'}, dimensions={0} | all-to-all | bytes 2097152 | tf_op jit(solution)/shard_map/all_to_all | solution.py:492
  241.2 0.7 sum_terms.1
  241.9 3.3 %collective-permute-start.19 = (bf16[32,256]{1,0:T(8,128)(2,1)S(1)}, bf16[32,256]{1,0:T(8,128)(2,1)S(1)}, u32[]{:S(2)}, u32[]{:S(2)}) collective-permute-start(bf16[32,256]{1,0:T(8,128)(2,1)S(1)} %get-tuple-element.87), channel_id=1, source_target_pairs={{192,0},{193,1},{194,2},{195,3},{196,4},{197,5},{198,6},{199,7},{2... | collective-permute-start | bytes 49160 | tf_op jit(solution)/shard_map/ppermute | solution.py:30
  245.2 5.0 %collective-permute-start.20 = (bf16[32,256]{1,0:T(8,128)(2,1)S(1)}, bf16[32,256]{1,0:T(8,128)(2,1)S(1)}, u32[]{:S(2)}, u32[]{:S(2)}) collective-permute-start(bf16[32,256]{1,0:T(8,128)(2,1)S(1)} %get-tuple-element.88), channel_id=1, source_target_pairs={{128,0},{129,1},{130,2},{131,3},{132,4},{133,5},{134,6},{135,7},{1... | collective-permute-start | bytes 49160 | tf_op jit(solution)/shard_map/ppermute | solution.py:30
  250.2 2.7 %collective-permute-start.21 = (bf16[32,256]{1,0:T(8,128)(2,1)S(1)}, bf16[32,256]{1,0:T(8,128)(2,1)S(1)}, u32[]{:S(2)}, u32[]{:S(2)}) collective-permute-start(bf16[32,256]{1,0:T(8,128)(2,1)S(1)} %get-tuple-element.89), channel_id=1, source_target_pairs={{64,0},{65,1},{66,2},{67,3},{68,4},{69,5},{70,6},{71,7},{72,8},{73... | collective-permute-start | bytes 49160 | tf_op jit(solution)/shard_map/ppermute | solution.py:30
  252.9 1.9 collective-permute-done.21
  254.9 0.6 convert_add_fusion
  255.5 0.9 fusion
  (56 shorter events, 1.4 us)
Async XLA Ops:
  0.6 164.3 %collective-permute-start = (bf16[256,1024]{1,0:T(8,128)(2,1)}, bf16[256,1024]{1,0:T(8,128)(2,1)}, u32[]{:S(2)}, u32[]{:S(2)}) collective-permute-start(bf16[256,1024]{1,0:T(8,128)(2,1)} %bitcast.37), channel_id=1, source_target_pairs={{1,0},{0,1},{3,2},{2,3},{5,4},{4,5},{7,6},{6,7},{9,8},{8,9},{11,10... | collective-permute-start | bytes 1572872 | tf_op jit(solution)/shard_map/ppermute | solution.py:30
  0.7 164.2 %collective-permute-start.1 = (bf16[256,1024]{1,0:T(8,128)(2,1)}, bf16[256,1024]{1,0:T(8,128)(2,1)}, u32[]{:S(2)}, u32[]{:S(2)}) collective-permute-start(bf16[256,1024]{1,0:T(8,128)(2,1)} %bitcast.33), channel_id=1, source_target_pairs={{1,0},{0,1},{3,2},{2,3},{5,4},{4,5},{7,6},{6,7},{9,8},{8,9},{11,10... | collective-permute-start | bytes 1572872 | tf_op jit(solution)/shard_map/ppermute | solution.py:30
  1.8 138.2 %copy-start.15 = (s32[32]{0:T(128)S(1)}, s32[32]{0:T(128)}, u32[]{:S(2)}) copy-start(s32[32]{0:T(128)} %param.15) | copy-start | bytes 388
  1.8 138.3 %copy-start.3 = (s32[3]{0:T(128)S(1)}, s32[3]{0:T(128)}, u32[]{:S(2)}) copy-start(s32[3]{0:T(128)} %pad_add_fusion.3.place) | copy-start | bytes 40
  134.8 11.7 %collective-permute-start.3 = (bf16[256,256]{1,0:T(8,128)(2,1)}, bf16[256,256]{1,0:T(8,128)(2,1)}, u32[]{:S(2)}, u32[]{:S(2)}) collective-permute-start(bf16[256,256]{1,0:T(8,128)(2,1)} %get-tuple-element.46), channel_id=1, source_target_pairs={{2,0},{3,1},{0,2},{1,3},{6,4},{7,5},{4,6},{5,7},{10,8},{11,9},{8,1... | collective-permute-start | bytes 393224 | tf_op jit(solution)/shard_map/ppermute | solution.py:30
  138.1 26.7 %collective-permute-start.7 = (bf16[2,256,1024]{2,1,0:T(8,128)(2,1)}, bf16[2,256,1024]{2,1,0:T(8,128)(2,1)S(1)}, u32[]{:S(2)}, u32[]{:S(2)}) collective-permute-start(bf16[2,256,1024]{2,1,0:T(8,128)(2,1)} %get-tuple-element.50), channel_id=1, source_target_pairs={{32,0},{33,1},{34,2},{35,3},{36,4},{37,5},{38,6},{39,7},{40,8},{41... | collective-permute-start | bytes 3145736 | tf_op jit(solution)/shard_map/ppermute | solution.py:30
  140.1 1.6 copy-start.4
  141.7 4.8 %copy-start.13 = (bf16[256,256]{1,0:T(8,128)(2,1)S(1)}, bf16[256,256]{1,0:T(8,128)(2,1)}, u32[]{:S(2)}) copy-start(bf16[256,256]{1,0:T(8,128)(2,1)} %get-tuple-element.46) | copy-start | bytes 393220
  141.7 16.8 %copy-start = (bf16[1,256,1024]{2,1,0:T(8,128)(2,1)S(1)}, bf16[1,256,1024]{2,1,0:T(8,128)(2,1)}, u32[]{:S(2)}) copy-start(bf16[1,256,1024]{2,1,0:T(8,128)(2,1)} %param.12) | copy-start | bytes 1572868
  141.7 16.8 %copy-start.1 = (bf16[1,256,1024]{2,1,0:T(8,128)(2,1)S(1)}, bf16[1,256,1024]{2,1,0:T(8,128)(2,1)}, u32[]{:S(2)}) copy-start(bf16[1,256,1024]{2,1,0:T(8,128)(2,1)} %param.13) | copy-start | bytes 1572868
  141.7 16.8 %copy-start.2 = (f32[1,8,256]{2,1,0:T(8,128)S(1)}, f32[1,8,256]{2,1,0:T(8,128)}, u32[]{:S(2)}) copy-start(f32[1,8,256]{2,1,0:T(8,128)} %param.14) | copy-start | bytes 24580
  144.9 1.0 copy-start.5
  145.9 0.5 copy-start.14
  147.5 10.8 %collective-permute-start.6 = (bf16[512,256]{1,0:T(8,128)(2,1)S(1)}, bf16[512,256]{1,0:T(8,128)(2,1)S(1)}, u32[]{:S(2)}, u32[]{:S(2)}) collective-permute-start(bf16[512,256]{1,0:T(8,128)(2,1)S(1)} %constant_dynamic-update-slice_fusion.refs_6_), channel_id=1, source_target_pairs={{8,0},{9,1},{10,2},{11,3},{12,4},{13,5},{14,6},{15,7},{0,8},{1,9},... | collective-permute-start | bytes 786440 | tf_op jit(solution)/shard_map/ppermute | solution.py:30
  148.3 13.6 %collective-permute-start.5 = (bf16[512,256]{1,0:T(8,128)(2,1)S(1)}, bf16[512,256]{1,0:T(8,128)(2,1)S(1)}, u32[]{:S(2)}, u32[]{:S(2)}) collective-permute-start(bf16[512,256]{1,0:T(8,128)(2,1)S(1)} %constant_dynamic-update-slice_fusion.refs_6_), channel_id=1, source_target_pairs={{12,0},{13,1},{14,2},{15,3},{0,4},{1,5},{2,6},{3,7},{4,8},{5,9},{6... | collective-permute-start | bytes 786440 | tf_op jit(solution)/shard_map/ppermute | solution.py:30
  158.3 4.4 %copy-start.7 = (bf16[512,256]{1,0:T(8,128)(2,1)}, bf16[512,256]{1,0:T(8,128)(2,1)S(1)}, u32[]{:S(2)}) copy-start(bf16[512,256]{1,0:T(8,128)(2,1)S(1)} %collective-permute-done.6.refs_9_) | copy-start | bytes 786436
  158.3 6.5 %collective-permute-start.4 = (bf16[512,256]{1,0:T(8,128)(2,1)S(1)}, bf16[512,256]{1,0:T(8,128)(2,1)}, u32[]{:S(2)}, u32[]{:S(2)}) collective-permute-start(bf16[512,256]{1,0:T(8,128)(2,1)S(1)} %constant_dynamic-update-slice_fusion.refs_6_), channel_id=1, source_target_pairs={{4,0},{5,1},{6,2},{7,3},{8,4},{9,5},{10,6},{11,7},{12,8},{13,9},{1... | collective-permute-start | bytes 786440 | tf_op jit(solution)/shard_map/ppermute | solution.py:30
  161.9 0.7 copy-start.10
  162.6 2.3 collective-permute-start.2
  164.8 40.7 %collective-permute-start.9 = (bf16[2,256,1024]{2,1,0:T(8,128)(2,1)}, bf16[2,256,1024]{2,1,0:T(8,128)(2,1)S(1)}, u32[]{:S(2)}, u32[]{:S(2)}) collective-permute-start(bf16[2,256,1024]{2,1,0:T(8,128)(2,1)} %get-tuple-element.72), channel_id=1, source_target_pairs={{32,0},{33,1},{34,2},{35,3},{36,4},{37,5},{38,6},{39,7},{40,8},{41... | collective-permute-start | bytes 3145736 | tf_op jit(solution)/shard_map/ppermute | solution.py:30
  164.9 13.8 %collective-permute-start.8 = (bf16[2048,256]{1,0:T(8,128)(2,1)}, bf16[2048,256]{1,0:T(8,128)(2,1)S(1)}, u32[]{:S(2)}, u32[]{:S(2)}) collective-permute-start(bf16[2048,256]{1,0:T(8,128)(2,1)} %copy-done.5), channel_id=1, source_target_pairs={{1,0},{0,1},{3,2},{2,3},{5,4},{4,5},{7,6},{6,7},{9,8},{8,9},{11,10... | collective-permute-start | bytes 3145736 | tf_op jit(solution)/shard_map/ppermute | solution.py:30
  164.9 1.0 copy-start.6
  166.0 0.9 copy-start.8
  166.9 0.9 copy-start.11
  167.9 10.8 %copy-start.9 = (bf16[512,256]{1,0:T(8,128)(2,1)S(1)}, bf16[512,256]{1,0:T(8,128)(2,1)}, u32[]{:S(2)}) copy-start(bf16[512,256]{1,0:T(8,128)(2,1)} %copy-done.7) | copy-start | bytes 786436
  167.9 10.8 %copy-start.12 = (bf16[512,256]{1,0:T(8,128)(2,1)S(1)}, bf16[512,256]{1,0:T(8,128)(2,1)}, u32[]{:S(2)}) copy-start(bf16[512,256]{1,0:T(8,128)(2,1)} %copy-done.10) | copy-start | bytes 786436
  178.4 16.5 %collective-permute-start.10 = (bf16[1024,256]{1,0:T(8,128)(2,1)S(1)}, bf16[1024,256]{1,0:T(8,128)(2,1)S(1)}, u32[]{:S(2)}, u32[]{:S(2)}) collective-permute-start(bf16[1024,256]{1,0:T(8,128)(2,1)S(1)} %get-tuple-element.74), channel_id=1, source_target_pairs={{2,0},{3,1},{0,2},{1,3},{6,4},{7,5},{4,6},{5,7},{10,8},{11,9},{8,1... | collective-permute-start | bytes 1572872 | tf_op jit(solution)/shard_map/ppermute | solution.py:30
  195.0 5.5 %collective-permute-start.11 = (bf16[256,256]{1,0:T(8,128)(2,1)S(1)}, bf16[256,256]{1,0:T(8,128)(2,1)S(1)}, u32[]{:S(2)}, u32[]{:S(2)}) collective-permute-start(bf16[256,256]{1,0:T(8,128)(2,1)S(1)} %get-tuple-element.104), channel_id=1, source_target_pairs={{12,0},{13,1},{14,2},{15,3},{0,4},{1,5},{2,6},{3,7},{4,8},{5,9},{6... | collective-permute-start | bytes 393224 | tf_op jit(solution)/shard_map/ppermute | solution.py:30
  196.4 7.7 %collective-permute-start.13 = (bf16[256,256]{1,0:T(8,128)(2,1)S(1)}, bf16[256,256]{1,0:T(8,128)(2,1)S(1)}, u32[]{:S(2)}, u32[]{:S(2)}) collective-permute-start(bf16[256,256]{1,0:T(8,128)(2,1)S(1)} %get-tuple-element.105), channel_id=1, source_target_pairs={{8,0},{9,1},{10,2},{11,3},{12,4},{13,5},{14,6},{15,7},{0,8},{1,9},... | collective-permute-start | bytes 393224 | tf_op jit(solution)/shard_map/ppermute | solution.py:30
  197.0 8.2 %collective-permute-start.12 = (bf16[256,256]{1,0:T(8,128)(2,1)S(1)}, bf16[256,256]{1,0:T(8,128)(2,1)S(1)}, u32[]{:S(2)}, u32[]{:S(2)}) collective-permute-start(bf16[256,256]{1,0:T(8,128)(2,1)S(1)} %get-tuple-element.106), channel_id=1, source_target_pairs={{4,0},{5,1},{6,2},{7,3},{8,4},{9,5},{10,6},{11,7},{12,8},{13,9},{1... | collective-permute-start | bytes 393224 | tf_op jit(solution)/shard_map/ppermute | solution.py:30
  205.3 1.4 collective-permute-start.14
  210.0 7.4 %collective-permute-start.15 = (bf16[2048,256]{1,0:T(8,128)(2,1)S(1)}, bf16[2048,256]{1,0:T(8,128)(2,1)S(1)}, u32[]{:S(2)}, u32[]{:S(2)}) collective-permute-start(bf16[2048,256]{1,0:T(8,128)(2,1)S(1)} %get-tuple-element.81), channel_id=1, source_target_pairs={{1,0},{0,1},{3,2},{2,3},{5,4},{4,5},{7,6},{6,7},{9,8},{8,9},{11,10... | collective-permute-start | bytes 3145736 | tf_op jit(solution)/shard_map/ppermute | solution.py:30
  210.2 5.8 %collective-permute-start.16 = (bf16[256,256]{1,0:T(8,128)(2,1)S(1)}, bf16[256,256]{1,0:T(8,128)(2,1)S(1)}, u32[]{:S(2)}, u32[]{:S(2)}) collective-permute-start(bf16[256,256]{1,0:T(8,128)(2,1)S(1)} %add_convert_fusion.1.ga), channel_id=1, source_target_pairs={{32,0},{33,1},{34,2},{35,3},{36,4},{37,5},{38,6},{39,7},{40,8},{41... | collective-permute-start | bytes 393224 | tf_op jit(solution)/shard_map/ppermute | solution.py:30
  216.0 1.3 collective-permute-start.17
  241.2 14.3 %collective-permute-start.18 = (bf16[256,1024]{1,0:T(8,128)(2,1)S(1)}, bf16[256,1024]{1,0:T(8,128)(2,1)S(1)}, u32[]{:S(2)}, u32[]{:S(2)}) collective-permute-start(bf16[256,1024]{1,0:T(8,128)(2,1)S(1)} %get-tuple-element.84), channel_id=1, source_target_pairs={{1,0},{0,1},{3,2},{2,3},{5,4},{4,5},{7,6},{6,7},{9,8},{8,9},{11,10... | collective-permute-start | bytes 1572872 | tf_op jit(solution)/shard_map/ppermute | solution.py:30
  241.9 11.0 %collective-permute-start.19 = (bf16[32,256]{1,0:T(8,128)(2,1)S(1)}, bf16[32,256]{1,0:T(8,128)(2,1)S(1)}, u32[]{:S(2)}, u32[]{:S(2)}) collective-permute-start(bf16[32,256]{1,0:T(8,128)(2,1)S(1)} %get-tuple-element.87), channel_id=1, source_target_pairs={{192,0},{193,1},{194,2},{195,3},{196,4},{197,5},{198,6},{199,7},{2... | collective-permute-start | bytes 49160 | tf_op jit(solution)/shard_map/ppermute | solution.py:30
  245.2 7.7 %collective-permute-start.20 = (bf16[32,256]{1,0:T(8,128)(2,1)S(1)}, bf16[32,256]{1,0:T(8,128)(2,1)S(1)}, u32[]{:S(2)}, u32[]{:S(2)}) collective-permute-start(bf16[32,256]{1,0:T(8,128)(2,1)S(1)} %get-tuple-element.88), channel_id=1, source_target_pairs={{128,0},{129,1},{130,2},{131,3},{132,4},{133,5},{134,6},{135,7},{1... | collective-permute-start | bytes 49160 | tf_op jit(solution)/shard_map/ppermute | solution.py:30
  250.2 4.6 %collective-permute-start.21 = (bf16[32,256]{1,0:T(8,128)(2,1)S(1)}, bf16[32,256]{1,0:T(8,128)(2,1)S(1)}, u32[]{:S(2)}, u32[]{:S(2)}) collective-permute-start(bf16[32,256]{1,0:T(8,128)(2,1)S(1)} %get-tuple-element.89), channel_id=1, source_target_pairs={{64,0},{65,1},{66,2},{67,3},{68,4},{69,5},{70,6},{71,7},{72,8},{73... | collective-permute-start | bytes 49160 | tf_op jit(solution)/shard_map/ppermute | solution.py:30

commit v4 on v2

--- a/solution.py
+++ b/solution.py
@@ -41,8 +41,11 @@
     return lambda z, yl, x, yh, c: ((z + k) % Z, yl, x, yh, c)
 
 
-FIRST = [(0, 0), (1, 0), (3, 0), (2, 0)]
-SECOND = [(0, 1), (1, 1), (3, 1), (2, 1)]
+def swap_z(z, yl, x, yh, c):
+    return (z ^ 1, yl, x, yh, c)
+
+
+ALONG_X = (0, 1, 3, 2)
 
 
 def vmem():
@@ -57,7 +60,18 @@
     return pl.BlockSpec(memory_space=pl.ANY)
 
 
-def stats_kernel(out_ref, grad_ref, lse_ref, stats_ref):
+def hbm():
+    return pl.BlockSpec(memory_space=pltpu.HBM)
+
+
+def stats_kernel(out_hbm, grad_hbm, lse_hbm, stats_ref, out_ref, grad_ref, lse_ref, sems):
+    pairs = ((out_hbm, out_ref), (grad_hbm, grad_ref), (lse_hbm, lse_ref))
+    copies = [pltpu.make_async_copy(a, b, sems.at[n]) for n, (a, b) in enumerate(pairs)]
+    for copy in copies:
+        copy.start()
+    stats_ref[4:8, :] = jnp.zeros((4, H * BLK), F32)
+    for copy in copies:
+        copy.wait()
     for h in range(H):
         cols = slice(h * BLK, (h + 1) * BLK)
         product = out_ref[:, cols].astype(F32) * grad_ref[:, cols].astype(F32)
@@ -67,15 +81,20 @@
             rows = slice(i * BLK, (i + 1) * BLK)
             stats_ref[i : i + 1, cols] = lse2[:, rows]
             stats_ref[2 + i : 3 + i, cols] = delta[:, rows]
-    stats_ref[4:8, :] = jnp.zeros((4, H * BLK), F32)
 
 
 def row_stats(saved, grad, lse):
     return pl.pallas_call(
         stats_kernel,
         out_shape=jax.ShapeDtypeStruct((8, H * BLK), F32),
-        in_specs=[vmem()] * 3,
+        in_specs=[hbm()] * 3,
         out_specs=vmem(),
+        scratch_shapes=[
+            pltpu.VMEM((256, H * BLK), BF16),
+            pltpu.VMEM((256, H * BLK), BF16),
+            pltpu.VMEM((H, 256), F32),
+            pltpu.SemaphoreType.DMA((3,)),
+        ],
         compiler_params=pltpu.CompilerParams(vmem_limit_bytes=8 * 2**20),
         cost_estimate=pl.CostEstimate(flops=10**6, bytes_accessed=2**20, transcendentals=0),
         name="row_stats",
@@ -181,20 +200,20 @@
     lax.fori_loop(0, NQ, query_block, 0)
 
 
-def store_keys(dkv, dkv_out):
-    for b in range(4):
-        for i in range(2):
-            rows = slice(i * BLK, (i + 1) * BLK)
-            ref = dkv_out[b]
-            ref[rows, :BLK] = (dkv[2 * b + i, :, :BLK] * SCALE).astype(ref.dtype)
-            ref[rows, BLK:] = dkv[2 * b + i, :, BLK:].astype(ref.dtype)
+def store_keys(dkv, refs):
+    for n in range(NK):
+        b, i = n // 2, n % 2
+        ref = refs[b]
+        rows = slice(i * BLK, (i + 1) * BLK)
+        ref[rows, :BLK] = (dkv[n, :, :BLK] * SCALE).astype(ref.dtype)
+        ref[rows, BLK:] = dkv[n, :, BLK:].astype(ref.dtype)
 
 
 def first_kernel(meta, *refs):
     q_in, g_in, s_in, kv_in = refs[0:2], refs[2:4], refs[4:6], refs[6:10]
     q_all, g_all, qt, gt, stats, dqt = refs[10:16]
-    dkv_out = refs[16:20]
-    kv, kt, dkv, pieces, sems = refs[20:]
+    dkv_out = refs[16]
+    kv, kt, dkv, pieces, sems = refs[17:]
     copies = []
     for side in range(2):
         for i in range(2):
@@ -203,7 +222,8 @@
             copies.append((g_in[side].at[rows], g_all.at[2 * side + i]))
         copies.append((s_in[side], pieces.at[side]))
     for b in range(4):
-        copies.append((kv_in[b], kv.at[pl.ds(b * 2 * BLK, 2 * BLK)]))
+        source = kv_in[b].at[pl.ds(2 * BLK, 2 * BLK)]
+        copies.append((source, kv.at[pl.ds(b * 2 * BLK, 2 * BLK)]))
     copies = [pltpu.make_async_copy(s, d, sems.at[n]) for n, (s, d) in enumerate(copies)]
     for copy in copies:
         copy.start()
@@ -225,7 +245,7 @@
     for n in range(NK):
         kt[n] = kv[n * BLK : (n + 1) * BLK, :BLK].T
     key_steps(meta, q_all, g_all, qt, gt, stats, kv, kt, dqt, dkv)
-    store_keys(dkv, dkv_out)
+    store_keys(dkv, [dkv_out.at[pl.ds(b * 2 * BLK, 2 * BLK)] for b in range(4)])
 
 
 def second_kernel(meta, *refs):
@@ -235,7 +255,9 @@
     dkv_out = refs[12:16]
     kv, kt, dkv, dqt, sems = refs[16:]
     copies = [
-        pltpu.make_async_copy(kv_in[b], kv.at[pl.ds(b * 2 * BLK, 2 * BLK)], sems.at[b])
+        pltpu.make_async_copy(
+            kv_in[b].at[pl.ds(0, 2 * BLK)], kv.at[pl.ds(b * 2 * BLK, 2 * BLK)], sems.at[b]
+        )
         for b in range(4)
     ]
     for copy in copies:
@@ -264,12 +286,6 @@
 COST = pl.CostEstimate(flops=6 * 10**10, bytes_accessed=2**20, transcendentals=2 * 10**6)
 
 
-def dkv_shapes(own):
-    return (jax.ShapeDtypeStruct((256, 256), own),) + (
-        jax.ShapeDtypeStruct((256, 256), BF16),
-    ) * 3
-
-
 def first_call(meta, queries, grads, stats, blocks):
     rows = jax.ShapeDtypeStruct((NQ, BLK, WIDE), BF16)
     return pl.pallas_call(
@@ -279,9 +295,9 @@
             jax.ShapeDtypeStruct((2 * NQ, WIDE), F32),
             jax.ShapeDtypeStruct((NQ, BLK, WIDE), F32),
         )
-        + dkv_shapes(F32),
-        in_specs=[smem()] + [anywhere()] * 10,
-        out_specs=(vmem(),) * 10,
+        + (jax.ShapeDtypeStruct((NK * BLK, 2 * BLK), BF16),),
+        in_specs=[smem()] + [hbm(), anywhere()] * 2 + [anywhere()] * 6,
+        out_specs=(vmem(),) * 7,
         scratch_shapes=KEY_SCRATCH
         + [pltpu.VMEM((2, 8, WIDE), F32), pltpu.SemaphoreType.DMA((14,))],
         compiler_params=pltpu.CompilerParams(vmem_limit_bytes=VMEM_LIMIT),
@@ -297,7 +313,7 @@
             jax.ShapeDtypeStruct((256, WIDE), F32),
             jax.ShapeDtypeStruct((256, WIDE), BF16),
         )
-        + dkv_shapes(BF16),
+        + (jax.ShapeDtypeStruct((2 * BLK, 2 * BLK), F32),) * 4,
         in_specs=[smem()] + [vmem()] * 6 + [anywhere()] * 4,
         out_specs=(vmem(),) * 6,
         scratch_shapes=KEY_SCRATCH
@@ -347,73 +363,94 @@
     )(mine, other, g_own, g_other)
 
 
-def sum_kernel(place, in_ref, own_ref, *out_refs):
-    for k in range(Z):
-        at = pl.ds(pl.multiple_of((place[0] + k) % Z * 32, 32), 32)
-        value = in_ref[0, at, :].astype(F32)
-        for j in range(1, 16):
-            value = value + in_ref[j, at, :].astype(F32)
-        ref = own_ref if k == 0 else out_refs[k - 1]
-        ref[...] = value.astype(ref.dtype)
+def sum_kernel(place, in_ref, keep_ref, send_ref):
+    for j in range(Z // 2):
+        for ref, half in ((keep_ref, place[1]), (send_ref, 1 - place[1])):
+            at = pl.ds(pl.multiple_of((2 * j + half) * 32, 32), 32)
+            value = in_ref[0, at, :].astype(F32)
+            for n in range(1, 16):
+                value = value + in_ref[n, at, :].astype(F32)
+            ref[j * 32 : j * 32 + 32, :] = value.astype(ref.dtype)
 
 
 def sum_terms(place, terms):
     return pl.pallas_call(
         sum_kernel,
-        out_shape=(jax.ShapeDtypeStruct((32, 256), F32),)
-        + (jax.ShapeDtypeStruct((32, 256), BF16),) * 7,
+        out_shape=(
+            jax.ShapeDtypeStruct((128, 256), F32),
+            jax.ShapeDtypeStruct((128, 256), BF16),
+        ),
         in_specs=[smem(), vmem()],
-        out_specs=(vmem(),) * 8,
+        out_specs=(vmem(),) * 2,
         compiler_params=pltpu.CompilerParams(vmem_limit_bytes=8 * 2**20),
         name="sum_terms",
     )(place, terms)
 
 
+def split_kernel(place, keep_ref, got_ref, *out_refs):
+    for k in range(Z // 2):
+        at = pl.ds(pl.multiple_of((place[2] + k) % (Z // 2) * 32, 32), 32)
+        value = keep_ref[at, :] + got_ref[at, :].astype(F32)
+        out_refs[k][...] = value.astype(out_refs[k].dtype)
+
+
+def split_terms(place, keep, got):
+    return pl.pallas_call(
+        split_kernel,
+        out_shape=(jax.ShapeDtypeStruct((32, 256), F32),)
+        + (jax.ShapeDtypeStruct((32, 256), BF16),) * 3,
+        in_specs=[smem(), vmem(), vmem()],
+        out_specs=(vmem(),) * 4,
+        compiler_params=pltpu.CompilerParams(vmem_limit_bytes=4 * 2**20),
+        name="split_terms",
+    )(place, keep, got)
+
+
 def body(layer_input, query_rows, key_rows, value_rows, attn_out, d_attn, log_sum_exp, block_order):
     z, x, yh, c = (lax.axis_index(name) for name in ("z", "x", "yh", "c"))
     ctx = (x * YH + yh) * C + c
+    place = jnp.stack([c, z % 2, z // 2]).astype(jnp.int32)
 
     q, g = query_rows[0], d_attn[0]
     pair = jnp.concatenate([key_rows[0], value_rows[0]], axis=1)
-    blocks = [pair] + [fetch(pair, by_ctx(*o)) for o in FIRST[1:]]
+    pair_y = fetch(pair, by_ctx(0, 1))
     q_other, g_other = fetch(q, swap_core), fetch(g, swap_core)
     stats = row_stats(attn_out[0], g, log_sum_exp[0])
     stats_other = fetch(stats, swap_core)
-    mine, other = turn(c.astype(jnp.int32)[None], layer_input[0])
+    both = jnp.concatenate([pair, pair_y], axis=0)
+    blocks = [both] + [fetch(both, by_ctx(k, 0)) for k in ALONG_X[1:]]
+    mine, other = turn(place[:1], layer_input[0])
 
     places = block_order.reshape(16, 2)
     q_pos = jnp.concatenate([places[ctx], places[ctx ^ 1]])
 
-    def owners(group):
-        return jnp.concatenate(
-            [places[(x + dx) % X * 4 + (yh ^ dyh) * 2 + c] for dx, dyh in group]
-        )
-
-    pair_again, *blocks = lax.optimization_barrier((pair, *blocks))
-    later = [fetch(pair_again, by_ctx(*o)) for o in SECOND]
+    def owners(row):
+        return jnp.concatenate([places[(x + k) % X * 4 + row * 2 + c] for k in ALONG_X])
+
     blocks, mine, other = lax.optimization_barrier((blocks, mine, other))
-    outs = first_call(
-        make_meta(owners(FIRST), q_pos), (q, q_other), (g, g_other), (stats, stats_other), blocks
+    mine_core = fetch(other, swap_core)
+    *carried, dkv_y = first_call(
+        make_meta(owners(1 - yh), q_pos), (q, q_other), (g, g_other), (stats, stats_other), blocks
     )
-    outs, other = lax.optimization_barrier((outs, other))
-    carried, dkv_first = outs[:6], outs[6:]
-    mine_other = fetch(other, swap_core)
-    dq_own, dq_sent, *dkv_second = second_call(make_meta(owners(SECOND), q_pos), carried, later)
-    total = dkv_first[0]
-    for (dx, dyh), part in zip(FIRST[1:], dkv_first[1:]):
-        total = total + fetch(part, by_ctx(-dx, dyh)).astype(F32)
-    total, dkv_second = lax.optimization_barrier((total, dkv_second))
-    for (dx, dyh), part in zip(SECOND, dkv_second):
-        total = total + fetch(part, by_ctx(-dx, dyh)).astype(F32)
+    carried, mine_core = lax.optimization_barrier((carried, mine_core))
+    dq_own, dq_sent, *dkv = second_call(make_meta(owners(yh), q_pos), carried, blocks)
+    dkv_y = fetch(dkv_y, by_ctx(0, 1))
+    dkv = [part + dkv_y[256 * b : 256 * b + 256].astype(F32) for b, part in enumerate(dkv)]
+    parts = [fetch(part.astype(BF16), by_ctx(-k, 0)) for k, part in zip(ALONG_X[1:], dkv[1:])]
+    total = dkv[0]
+    for part in parts:
+        total = total + part.astype(F32)
     grads = total.astype(BF16)
-    grads_other = fetch(grads, swap_core)
+    grads_core = fetch(grads, swap_core)
+
+    terms = project(mine, mine_core, grads, grads_core)
+    terms = lax.all_to_all(terms, ("yl", "x", "yh"), 0, 0)
+    terms, dq_sent = lax.optimization_barrier((terms, dq_sent))
+    keep, sent = sum_terms(place, terms)
+    own, *sent = split_terms(place, keep, fetch(sent, swap_z))
     d_query = (dq_own + fetch(dq_sent, swap_core).astype(F32)).astype(BF16)[None]
-
-    terms = project(mine, mine_other, grads, grads_other)
-    terms = lax.all_to_all(terms, ("yl", "x", "yh"), 0, 0)
-    own, *sent = sum_terms(z.astype(jnp.int32)[None], terms)
-    for k in range(1, Z):
-        own = own + fetch(sent[k - 1], by_z(-k)).astype(F32)
+    for k in range(1, Z // 2):
+        own = own + fetch(sent[k - 1], by_z(-2 * k)).astype(F32)
     return (d_query, own)
 
 

time: 145 us -> 128 us (0.88)
  blocking collectives: 0 us -> 33.1 us
  starting transfers between devices: 62.1 us -> 32.8 us
  waiting for transfers between devices: 38.9 us -> 20 us
  Pallas kernels: 32.4 us -> 26.4 us
  local copies, waits for them, and re-layouts: 5.92 us -> 7.83 us
    all_to_all x1 -> x0, waiting for transfers between devices: 33.8 us -> none  [body(): terms = lax.all_to_all(terms, ('yl', 'x', 'yh'), 0, 0)]
    all_to_all x0 -> x1, blocking collectives: none -> 33.1 us  [body(): terms = lax.all_to_all(terms, ('yl', 'x', 'yh'), 0, 0)]
    ppermute x27 -> x18, starting transfers between devices: 52.5 us -> 32.8 us  [fetch(): return lax.ppermute(value, AXES, pairs)]
    ppermute x27 -> x18, waiting for transfers between devices: 5.06 us -> 20 us  [fetch(): return lax.ppermute(value, AXES, pairs)]
    all_to_all x1 -> x0, starting transfers between devices: 9.59 us -> none  [body(): terms = lax.all_to_all(terms, ('yl', 'x', 'yh'), 0, 0)]
    pallas_call x1, Pallas kernels: 11.6 us -> 7.97 us  [first_call(): pl.pallas_call(first_kernel, out_shape=(rows,) * 4 + (jax.ShapeDtypeStruc...]
    pallas_call x1, Pallas kernels: 11.1 us -> 8.87 us  [second_call(): pl.pallas_call(second_kernel, out_shape=(jax.ShapeDtypeStruct((256, WIDE)...]
    unnamed x14 -> x20, local copies, waits for them, and re-layouts: 4.99 us -> 6.89 us
  transfers between devices with their start and end apart: 28 -> 18, of which waited for: 5 -> 9; matrix products, arithmetic and copies ran while one was open for 3% -> 3% of each run, Pallas kernels for 20% -> 19%
where the time goes in v4:
time: 128 us; the launch traced here: 127 us
  blocking collectives  33.1 us (26%)
  starting transfers between devices  32.8 us (26%)
  Pallas kernels  26.4 us (21%)
  waiting for transfers between devices  20 us (16%)
  local copies, waits for them, and re-layouts  7.83 us (6%)
  other arithmetic  5.63 us (4%)
    all_to_all x1, blocking collectives, body(): terms = lax.all_to_all(terms, ('yl', 'x', 'yh'), 0, 0)  33.1 us
    ppermute x18, starting transfers between devices, fetch(): return lax.ppermute(value, AXES, pairs)  32.8 us
    ppermute x18, waiting for transfers between devices, fetch(): return lax.ppermute(value, AXES, pairs)  20 us
    pallas_call x1, Pallas kernels, second_call(): pl.pallas_call(second_kernel, out_shape=(jax.ShapeDtypeStruct((256, WIDE)...  8.87 us
    pallas_call x1, Pallas kernels, first_call(): pl.pallas_call(first_kernel, out_shape=(rows,) * 4 + (jax.ShapeDtypeStruc...  7.97 us
    unnamed x20, local copies, waits for them, and re-layouts  6.89 us
    pallas_call x1, Pallas kernels, turn(): pl.pallas_call(turn_kernel, grid=(Z,), out_shape=(jax.ShapeDtypeStruct((4...  5.33 us
  transfers between devices with their start and end apart: 18, of which 9 were waited for; matrix products, arithmetic and copies ran while one was open for 3% of the time, Pallas kernels for 19%

profile of v4, /device:TPU:4, one launch (start us, length us, event | category | flops | bytes accessed | tf_op | source)
XLA Modules:
  0.0 126.6 jit_solution(13703287163333444454)
XLA Ops:
  0.6 0.9 pad_maximum_fusion.1
  1.5 3.3 %collective-permute-start.3 = (bf16[256,256]{1,0:T(8,128)(2,1)S(1)}, bf16[256,256]{1,0:T(8,128)(2,1)S(1)}, u32[]{:S(2)}, u32[]{:S(2)}) collective-permute-start(bf16[256,256]{1,0:T(8,128)(2,1)S(1)} %pad_maximum_fusion.1), channel_id=1, source_target_pairs={{2,0},{3,1},{0,2},{1,3},{6,4},{7,5},{4,6},{5,7},{10,8},{11,9},{8,1... | collective-permute-start | bytes 393224 | tf_op jit(solution)/shard_map/ppermute | solution.py:29
  4.8 0.5 collective-permute-start.1
  5.3 0.7 reshape.14
  6.3 0.2 convert_reduce_fusion.2
  6.5 1.8 %collective-permute-done.3 = bf16[256,256]{1,0:T(8,128)(2,1)S(1)} collective-permute-done((bf16[256,256]{1,0:T(8,128)(2,1)S(1)}, bf16[256,256]{1,0:T(8,128)(2,1)S(1)}, u32[]{:S(2)}, u32[]{:S(2)}) %collective-permute-start.3) | collective-permute-done | bytes 131104 | tf_op jit(solution)/shard_map/ppermute | solution.py:29
  8.3 0.9 pad_maximum_fusion.refs_6_
  9.2 2.1 %collective-permute-start.6 = (bf16[512,256]{1,0:T(8,128)(2,1)S(1)}, bf16[512,256]{1,0:T(8,128)(2,1)S(1)}, u32[]{:S(2)}, u32[]{:S(2)}) collective-permute-start(bf16[512,256]{1,0:T(8,128)(2,1)S(1)} %pad_maximum_fusion.refs_6_), channel_id=1, source_target_pairs={{8,0},{9,1},{10,2},{11,3},{12,4},{13,5},{14,6},{15,7},{0,8},{1,9},... | collective-permute-start | bytes 786440 | tf_op jit(solution)/shard_map/ppermute | solution.py:29
  11.3 0.7 collective-permute-start.5
  12.0 1.4 %collective-permute-start.4 = (bf16[512,256]{1,0:T(8,128)(2,1)S(1)}, bf16[512,256]{1,0:T(8,128)(2,1)S(1)}, u32[]{:S(2)}, u32[]{:S(2)}) collective-permute-start(bf16[512,256]{1,0:T(8,128)(2,1)S(1)} %pad_maximum_fusion.refs_6_), channel_id=1, source_target_pairs={{4,0},{5,1},{6,2},{7,3},{8,4},{9,5},{10,6},{11,7},{12,8},{13,9},{1... | collective-permute-start | bytes 786440 | tf_op jit(solution)/shard_map/ppermute | solution.py:29
  13.4 0.2 convert_reduce_fusion.1
  13.6 1.0 copy-done.1
  14.7 1.0 copy-done.2
  15.7 0.7 copy-done.4
  16.4 0.5 row_stats.1.refs_4_
  16.9 0.2 convert_reduce_fusion
  17.1 3.0 %collective-permute-done.6.refs_9_ = bf16[512,256]{1,0:T(8,128)(2,1)S(1)} collective-permute-done((bf16[512,256]{1,0:T(8,128)(2,1)S(1)}, bf16[512,256]{1,0:T(8,128)(2,1)S(1)}, u32[]{:S(2)}, u32[]{:S(2)}) %collective-permute-start.6) | collective-permute-done | bytes 262176 | tf_op jit(solution)/shard_map/ppermute | solution.py:29
  20.1 0.1 select_reduce_fusion
  20.4 2.2 %copy-done = bf16[1,256,8192]{2,1,0:T(8,128)(2,1)S(1)} copy-done((bf16[1,256,8192]{2,1,0:T(8,128)(2,1)S(1)}, bf16[1,256,8192]{2,1,0:T(8,128)(2,1)}, u32[]{:S(2)}) %copy-start) | copy-done | bytes 4194328
  22.6 5.3 %turn.1 = (bf16[4096,256]{1,0:T(8,128)(2,1)S(1)}, bf16[4096,256]{1,0:T(8,128)(2,1)S(1)}) custom-call(s32[1]{0:T(128)} %bitcast.16.me, bf16[256,8192]{1,0:T(8,128)(2,1)S(1)} %bitcast.32), custom_call_target="tpu_custom_call" | custom-call | flops 10000000 | bytes 8388608 | tf_op jit(solution)/shard_map/turn/pallas_call | solution.py:125
  28.0 0.6 collective-permute-start.7
  28.6 8.0 %attention_first.1 = (bf16[4,128,1024]{2,1,0:T(8,128)(2,1)S(1)}, bf16[4,128,1024]{2,1,0:T(8,128)(2,1)S(1)}, bf16[4,128,1024]{2,1,0:T(8,128)(2,1)S(1)}, bf16[4,12...) custom-call(s32[28]{0:T(128)S(1)} %concatenate.27.meta, ...), custom_call_target="tpu_custom_call" | custom-call | flops 60000002048 | bytes 1048576 | tf_op jit(solution)/shard_map/attention_first/pallas_call | solution.py:291
  36.6 7.1 %collective-permute-start.8 = (bf16[1024,256]{1,0:T(8,128)(2,1)S(1)}, bf16[1024,256]{1,0:T(8,128)(2,1)S(1)}, u32[]{:S(2)}, u32[]{:S(2)}) collective-permute-start(bf16[1024,256]{1,0:T(8,128)(2,1)S(1)} %get-tuple-element.61), channel_id=1, source_target_pairs={{2,0},{3,1},{0,2},{1,3},{6,4},{7,5},{4,6},{5,7},{10,8},{11,9},{8,1... | collective-permute-start | bytes 1572872 | tf_op jit(solution)/shard_map/ppermute | solution.py:29
  43.8 0.9 copy-done.7
  44.7 0.9 copy-done.9
  45.7 8.9 %attention_second.1 = (f32[256,1024]{1,0:T(8,128)S(1)}, bf16[256,1024]{1,0:T(8,128)(2,1)}, f32[256,256]{1,0:T(8,128)S(1)}, f32[256,256]{1,0:T(8,128)S(1)}, f32[2...) custom-call(s32[28]{0:T(128)S(1)} %concatenate.25.meta, bf16[4,128,1024]{2,1,0:T(8,128)(2,1)S(1)} %get-tuple-element.51.refs_0_, ...), custom_call_target="tpu_custom_call" | custom-call | flops 60000002048 | bytes 1048576 | tf_op jit(solution)/shard_map/attention_second/pallas_call | solution.py:310
  54.5 1.7 %collective-permute-done.8 = bf16[1024,256]{1,0:T(8,128)(2,1)S(1)} collective-permute-done((bf16[1024,256]{1,0:T(8,128)(2,1)S(1)}, bf16[1024,256]{1,0:T(8,128)(2,1)S(1)}, u32[]{:S(2)}, u32[]{:S(2)}) %collective-permute-start.8) | collective-permute-done | bytes 524320 | tf_op jit(solution)/shard_map/ppermute | solution.py:29
  56.3 0.1 add_convert_fusion.4
  56.4 2.2 %collective-permute-start.9 = (bf16[256,256]{1,0:T(8,128)(2,1)S(1)}, bf16[256,256]{1,0:T(8,128)(2,1)S(1)}, u32[]{:S(2)}, u32[]{:S(2)}) collective-permute-start(bf16[256,256]{1,0:T(8,128)(2,1)S(1)} %get-tuple-element.88), channel_id=1, source_target_pairs={{12,0},{13,1},{14,2},{15,3},{0,4},{1,5},{2,6},{3,7},{4,8},{5,9},{6... | collective-permute-start | bytes 393224 | tf_op jit(solution)/shard_map/ppermute | solution.py:29
  58.6 1.6 %collective-permute-start.10 = (bf16[256,256]{1,0:T(8,128)(2,1)S(1)}, bf16[256,256]{1,0:T(8,128)(2,1)S(1)}, u32[]{:S(2)}, u32[]{:S(2)}) collective-permute-start(bf16[256,256]{1,0:T(8,128)(2,1)S(1)} %get-tuple-element.90), channel_id=1, source_target_pairs={{4,0},{5,1},{6,2},{7,3},{8,4},{9,5},{10,6},{11,7},{12,8},{13,9},{1... | collective-permute-start | bytes 393224 | tf_op jit(solution)/shard_map/ppermute | solution.py:29
  60.2 2.6 %collective-permute-done.9 = bf16[256,256]{1,0:T(8,128)(2,1)S(1)} collective-permute-done((bf16[256,256]{1,0:T(8,128)(2,1)S(1)}, bf16[256,256]{1,0:T(8,128)(2,1)S(1)}, u32[]{:S(2)}, u32[]{:S(2)}) %collective-permute-start.9) | collective-permute-done | bytes 131104 | tf_op jit(solution)/shard_map/ppermute | solution.py:29
  62.8 2.7 %collective-permute-done.11 = bf16[256,256]{1,0:T(8,128)(2,1)S(1)} collective-permute-done((bf16[256,256]{1,0:T(8,128)(2,1)S(1)}, bf16[256,256]{1,0:T(8,128)(2,1)S(1)}, u32[]{:S(2)}, u32[]{:S(2)}) %collective-permute-start.11) | collective-permute-done | bytes 131104 | tf_op jit(solution)/shard_map/ppermute | solution.py:29
  65.5 2.0 %collective-permute-done.10 = bf16[256,256]{1,0:T(8,128)(2,1)S(1)} collective-permute-done((bf16[256,256]{1,0:T(8,128)(2,1)S(1)}, bf16[256,256]{1,0:T(8,128)(2,1)S(1)}, u32[]{:S(2)}, u32[]{:S(2)}) %collective-permute-start.10) | collective-permute-done | bytes 131104 | tf_op jit(solution)/shard_map/ppermute | solution.py:29
  67.5 0.1 add_convert_fusion.1.g_own
  67.6 0.1 collective-permute-start.12
  67.7 1.3 %collective-permute-done.12.g_other = bf16[256,256]{1,0:T(8,128)(2,1)S(1)} collective-permute-done((bf16[256,256]{1,0:T(8,128)(2,1)S(1)}, bf16[256,256]{1,0:T(8,128)(2,1)S(1)}, u32[]{:S(2)}, u32[]{:S(2)}) %collective-permute-start.12) | collective-permute-done | bytes 131104 | tf_op jit(solution)/shard_map/ppermute | solution.py:29
  69.0 2.4 %project.1 = bf16[16,256,256]{2,1,0:T(8,128)(2,1)S(1)} custom-call(bf16[4096,256]{1,0:T(8,128)(2,1)S(1)} %get-tuple-element.58.mine_ref, bf16[4096,256]{1,0:T(8,128)(2,1)S(1)} %collective-permute-done.7.other_ref, bf16[256,256]{1,0:T(8,128)(2,1)S(1)} %add_convert_fusion.1.g_own, bf16[256,256]{1,0:T(8,128)(2,1)S(1)} %collective-permute-done.12.g_other), custom_call_target="tpu_custom_call" | custom-call | flops 1073741824 | bytes 8388608 | tf_op jit(solution)/shard_map/project/pallas_call | solution.py:353
  71.4 33.1 %all_to_all.5.in_ref = bf16[16,256,256]{2,1,0:T(8,128)(2,1)S(1)} all-to-all(bf16[16,256,256]{2,1,0:T(8,128)(2,1)S(1)} %project.1), channel_id=1, replica_groups=mesh['z'=8,'yl'=2,'x'=4,'yh'=2,'c'=2] {'yl','x','yh'}, dimensions={0} | all-to-all | bytes 4194304 | tf_op jit(solution)/shard_map/all_to_all | solution.py:447
  104.6 0.8 sum_terms.1
  105.4 2.0 %collective-permute-start.14 = (bf16[128,256]{1,0:T(8,128)(2,1)S(1)}, bf16[128,256]{1,0:T(8,128)(2,1)S(1)}, u32[]{:S(2)}, u32[]{:S(2)}) collective-permute-start(bf16[128,256]{1,0:T(8,128)(2,1)S(1)} %get-tuple-element.69), channel_id=1, source_target_pairs={{32,0},{33,1},{34,2},{35,3},{36,4},{37,5},{38,6},{39,7},{40,8},{41... | collective-permute-start | bytes 196616 | tf_op jit(solution)/shard_map/ppermute | solution.py:29
  107.4 2.8 %collective-permute-done.14.got_ref = bf16[128,256]{1,0:T(8,128)(2,1)S(1)} collective-permute-done((bf16[128,256]{1,0:T(8,128)(2,1)S(1)}, bf16[128,256]{1,0:T(8,128)(2,1)S(1)}, u32[]{:S(2)}, u32[]{:S(2)}) %collective-permute-start.14) | collective-permute-done | bytes 65568 | tf_op jit(solution)/shard_map/ppermute | solution.py:29
  110.2 0.6 split_terms.1
  110.7 3.4 %collective-permute-start.15 = (bf16[32,256]{1,0:T(8,128)(2,1)S(1)}, bf16[32,256]{1,0:T(8,128)(2,1)S(1)}, u32[]{:S(2)}, u32[]{:S(2)}) collective-permute-start(bf16[32,256]{1,0:T(8,128)(2,1)S(1)} %get-tuple-element.71), channel_id=1, source_target_pairs={{192,0},{193,1},{194,2},{195,3},{196,4},{197,5},{198,6},{199,7},{2... | collective-permute-start | bytes 49160 | tf_op jit(solution)/shard_map/ppermute | solution.py:29
  114.1 5.2 %collective-permute-start.16 = (bf16[32,256]{1,0:T(8,128)(2,1)S(1)}, bf16[32,256]{1,0:T(8,128)(2,1)S(1)}, u32[]{:S(2)}, u32[]{:S(2)}) collective-permute-start(bf16[32,256]{1,0:T(8,128)(2,1)S(1)} %get-tuple-element.72), channel_id=1, source_target_pairs={{128,0},{129,1},{130,2},{131,3},{132,4},{133,5},{134,6},{135,7},{1... | collective-permute-start | bytes 49160 | tf_op jit(solution)/shard_map/ppermute | solution.py:29
  119.3 2.7 %collective-permute-start.17 = (bf16[32,256]{1,0:T(8,128)(2,1)S(1)}, bf16[32,256]{1,0:T(8,128)(2,1)S(1)}, u32[]{:S(2)}, u32[]{:S(2)}) collective-permute-start(bf16[32,256]{1,0:T(8,128)(2,1)S(1)} %get-tuple-element.73), channel_id=1, source_target_pairs={{64,0},{65,1},{66,2},{67,3},{68,4},{69,5},{70,6},{71,7},{72,8},{73... | collective-permute-start | bytes 49160 | tf_op jit(solution)/shard_map/ppermute | solution.py:29
  122.0 2.0 %collective-permute-done.17 = bf16[32,256]{1,0:T(8,128)(2,1)S(1)} collective-permute-done((bf16[32,256]{1,0:T(8,128)(2,1)S(1)}, bf16[32,256]{1,0:T(8,128)(2,1)S(1)}, u32[]{:S(2)}, u32[]{:S(2)}) %collective-permute-start.17) | collective-permute-done | bytes 16416 | tf_op jit(solution)/shard_map/ppermute | solution.py:29
  124.0 0.6 convert_add_fusion
  124.6 2.0 %fusion = bf16[1,256,1024]{2,1,0:T(8,128)(2,1)} fusion(f32[256,1024]{1,0:T(8,128)S(1)} %get-tuple-element.57, bf16[256,1024]{1,0:T(8,128)(2,1)} %collective-permute-done.13), kind=kLoop, calls=%fused_computation.1 | loop fusion | flops 786432 | bytes 2097152 | tf_op jit(solution)/shard_map/broadcast_in_dim | solution.py:451
  (35 shorter events, 0.6 us)
Async XLA Ops:
  1.5 6.8 %collective-permute-start.3 = (bf16[256,256]{1,0:T(8,128)(2,1)S(1)}, bf16[256,256]{1,0:T(8,128)(2,1)S(1)}, u32[]{:S(2)}, u32[]{:S(2)}) collective-permute-start(bf16[256,256]{1,0:T(8,128)(2,1)S(1)} %pad_maximum_fusion.1), channel_id=1, source_target_pairs={{2,0},{3,1},{0,2},{1,3},{6,4},{7,5},{4,6},{5,7},{10,8},{11,9},{8,1... | collective-permute-start | bytes 393224 | tf_op jit(solution)/shard_map/ppermute | solution.py:29
  4.8 23.8 %collective-permute-start = (bf16[256,1024]{1,0:T(8,128)(2,1)}, bf16[256,1024]{1,0:T(8,128)(2,1)S(1)}, u32[]{:S(2)}, u32[]{:S(2)}) collective-permute-start(bf16[256,1024]{1,0:T(8,128)(2,1)} %bitcast.38), channel_id=1, source_target_pairs={{1,0},{0,1},{3,2},{2,3},{5,4},{4,5},{7,6},{6,7},{9,8},{8,9},{11,10... | collective-permute-start | bytes 1572872 | tf_op jit(solution)/shard_map/ppermute | solution.py:29
  4.8 23.8 %collective-permute-start.1 = (bf16[256,1024]{1,0:T(8,128)(2,1)}, bf16[256,1024]{1,0:T(8,128)(2,1)S(1)}, u32[]{:S(2)}, u32[]{:S(2)}) collective-permute-start(bf16[256,1024]{1,0:T(8,128)(2,1)} %bitcast.34), channel_id=1, source_target_pairs={{1,0},{0,1},{3,2},{2,3},{5,4},{4,5},{7,6},{6,7},{9,8},{8,9},{11,10... | collective-permute-start | bytes 1572872 | tf_op jit(solution)/shard_map/ppermute | solution.py:29
  9.2 10.8 %collective-permute-start.6 = (bf16[512,256]{1,0:T(8,128)(2,1)S(1)}, bf16[512,256]{1,0:T(8,128)(2,1)S(1)}, u32[]{:S(2)}, u32[]{:S(2)}) collective-permute-start(bf16[512,256]{1,0:T(8,128)(2,1)S(1)} %pad_maximum_fusion.refs_6_), channel_id=1, source_target_pairs={{8,0},{9,1},{10,2},{11,3},{12,4},{13,5},{14,6},{15,7},{0,8},{1,9},... | collective-permute-start | bytes 786440 | tf_op jit(solution)/shard_map/ppermute | solution.py:29
  11.3 16.6 %collective-permute-start.5 = (bf16[512,256]{1,0:T(8,128)(2,1)S(1)}, bf16[512,256]{1,0:T(8,128)(2,1)S(1)}, u32[]{:S(2)}, u32[]{:S(2)}) collective-permute-start(bf16[512,256]{1,0:T(8,128)(2,1)S(1)} %pad_maximum_fusion.refs_6_), channel_id=1, source_target_pairs={{12,0},{13,1},{14,2},{15,3},{0,4},{1,5},{2,6},{3,7},{4,8},{5,9},{6... | collective-permute-start | bytes 786440 | tf_op jit(solution)/shard_map/ppermute | solution.py:29
  12.0 15.9 %collective-permute-start.4 = (bf16[512,256]{1,0:T(8,128)(2,1)S(1)}, bf16[512,256]{1,0:T(8,128)(2,1)S(1)}, u32[]{:S(2)}, u32[]{:S(2)}) collective-permute-start(bf16[512,256]{1,0:T(8,128)(2,1)S(1)} %pad_maximum_fusion.refs_6_), channel_id=1, source_target_pairs={{4,0},{5,1},{6,2},{7,3},{8,4},{9,5},{10,6},{11,7},{12,8},{13,9},{1... | collective-permute-start | bytes 786440 | tf_op jit(solution)/shard_map/ppermute | solution.py:29
  13.6 1.0 copy-start.1
  14.7 1.0 copy-start.2
  15.7 0.7 copy-start.4
  20.1 8.5 %collective-permute-start.2 = (f32[8,1024]{1,0:T(8,128)S(1)}, f32[8,1024]{1,0:T(8,128)S(1)}, u32[]{:S(2)}, u32[]{:S(2)}) collective-permute-start(f32[8,1024]{1,0:T(8,128)S(1)} %row_stats.1.refs_4_), channel_id=1, source_target_pairs={{1,0},{0,1},{3,2},{2,3},{5,4},{4,5},{7,6},{6,7},{9,8},{8,9},{11,10... | collective-permute-start | bytes 98312 | tf_op jit(solution)/shard_map/ppermute | solution.py:29
  20.4 2.2 %copy-start = (bf16[1,256,8192]{2,1,0:T(8,128)(2,1)S(1)}, bf16[1,256,8192]{2,1,0:T(8,128)(2,1)}, u32[]{:S(2)}) copy-start(bf16[1,256,8192]{2,1,0:T(8,128)(2,1)} %param.8) | copy-start | bytes 12582916
  22.6 6.0 %copy-start.3 = (bf16[1,256,1024]{2,1,0:T(8,128)(2,1)S(1)}, bf16[1,256,1024]{2,1,0:T(8,128)(2,1)}, u32[]{:S(2)}) copy-start(bf16[1,256,1024]{2,1,0:T(8,128)(2,1)} %param.13) | copy-start | bytes 1572868
  22.6 6.0 %copy-start.5 = (bf16[1,256,1024]{2,1,0:T(8,128)(2,1)S(1)}, bf16[1,256,1024]{2,1,0:T(8,128)(2,1)}, u32[]{:S(2)}) copy-start(bf16[1,256,1024]{2,1,0:T(8,128)(2,1)} %param.9) | copy-start | bytes 1572868
  27.9 8.7 %copy-start.6 = (bf16[512,256]{1,0:T(8,128)(2,1)}, bf16[512,256]{1,0:T(8,128)(2,1)S(1)}, u32[]{:S(2)}) copy-start(bf16[512,256]{1,0:T(8,128)(2,1)S(1)} %collective-permute-done.5.refs_8_) | copy-start | bytes 786436
  28.0 8.6 %copy-start.8 = (bf16[512,256]{1,0:T(8,128)(2,1)}, bf16[512,256]{1,0:T(8,128)(2,1)S(1)}, u32[]{:S(2)}) copy-start(bf16[512,256]{1,0:T(8,128)(2,1)S(1)} %collective-permute-done.4.refs_7_) | copy-start | bytes 786436
  28.0 15.8 %collective-permute-start.7 = (bf16[4096,256]{1,0:T(8,128)(2,1)S(1)}, bf16[4096,256]{1,0:T(8,128)(2,1)S(1)}, u32[]{:S(2)}, u32[]{:S(2)}) collective-permute-start(bf16[4096,256]{1,0:T(8,128)(2,1)S(1)} %get-tuple-element.50), channel_id=1, source_target_pairs={{1,0},{0,1},{3,2},{2,3},{5,4},{4,5},{7,6},{6,7},{9,8},{8,9},{11,10... | collective-permute-start | bytes 6291464 | tf_op jit(solution)/shard_map/ppermute | solution.py:29
  36.6 19.7 %collective-permute-start.8 = (bf16[1024,256]{1,0:T(8,128)(2,1)S(1)}, bf16[1024,256]{1,0:T(8,128)(2,1)S(1)}, u32[]{:S(2)}, u32[]{:S(2)}) collective-permute-start(bf16[1024,256]{1,0:T(8,128)(2,1)S(1)} %get-tuple-element.61), channel_id=1, source_target_pairs={{2,0},{3,1},{0,2},{1,3},{6,4},{7,5},{4,6},{5,7},{10,8},{11,9},{8,1... | collective-permute-start | bytes 1572872 | tf_op jit(solution)/shard_map/ppermute | solution.py:29
  43.8 1.0 copy-start.7
  44.7 0.9 copy-start.9
  56.4 6.4 %collective-permute-start.9 = (bf16[256,256]{1,0:T(8,128)(2,1)S(1)}, bf16[256,256]{1,0:T(8,128)(2,1)S(1)}, u32[]{:S(2)}, u32[]{:S(2)}) collective-permute-start(bf16[256,256]{1,0:T(8,128)(2,1)S(1)} %get-tuple-element.88), channel_id=1, source_target_pairs={{12,0},{13,1},{14,2},{15,3},{0,4},{1,5},{2,6},{3,7},{4,8},{5,9},{6... | collective-permute-start | bytes 393224 | tf_op jit(solution)/shard_map/ppermute | solution.py:29
  58.6 6.9 %collective-permute-start.11 = (bf16[256,256]{1,0:T(8,128)(2,1)S(1)}, bf16[256,256]{1,0:T(8,128)(2,1)S(1)}, u32[]{:S(2)}, u32[]{:S(2)}) collective-permute-start(bf16[256,256]{1,0:T(8,128)(2,1)S(1)} %get-tuple-element.89), channel_id=1, source_target_pairs={{8,0},{9,1},{10,2},{11,3},{12,4},{13,5},{14,6},{15,7},{0,8},{1,9},... | collective-permute-start | bytes 393224 | tf_op jit(solution)/shard_map/ppermute | solution.py:29
  58.6 8.9 %collective-permute-start.10 = (bf16[256,256]{1,0:T(8,128)(2,1)S(1)}, bf16[256,256]{1,0:T(8,128)(2,1)S(1)}, u32[]{:S(2)}, u32[]{:S(2)}) collective-permute-start(bf16[256,256]{1,0:T(8,128)(2,1)S(1)} %get-tuple-element.90), channel_id=1, source_target_pairs={{4,0},{5,1},{6,2},{7,3},{8,4},{9,5},{10,6},{11,7},{12,8},{13,9},{1... | collective-permute-start | bytes 393224 | tf_op jit(solution)/shard_map/ppermute | solution.py:29
  67.6 1.4 %collective-permute-start.12 = (bf16[256,256]{1,0:T(8,128)(2,1)S(1)}, bf16[256,256]{1,0:T(8,128)(2,1)S(1)}, u32[]{:S(2)}, u32[]{:S(2)}) collective-permute-start(bf16[256,256]{1,0:T(8,128)(2,1)S(1)} %add_convert_fusion.1.g_own), channel_id=1, source_target_pairs={{1,0},{0,1},{3,2},{2,3},{5,4},{4,5},{7,6},{6,7},{9,8},{8,9},{11,10... | collective-permute-start | bytes 393224 | tf_op jit(solution)/shard_map/ppermute | solution.py:29
  104.5 20.1 %collective-permute-start.13 = (bf16[256,1024]{1,0:T(8,128)(2,1)}, bf16[256,1024]{1,0:T(8,128)(2,1)}, u32[]{:S(2)}, u32[]{:S(2)}) collective-permute-start(bf16[256,1024]{1,0:T(8,128)(2,1)} %get-tuple-element.66), channel_id=1, source_target_pairs={{1,0},{0,1},{3,2},{2,3},{5,4},{4,5},{7,6},{6,7},{9,8},{8,9},{11,10... | collective-permute-start | bytes 1572872 | tf_op jit(solution)/shard_map/ppermute | solution.py:29
  105.4 4.8 %collective-permute-start.14 = (bf16[128,256]{1,0:T(8,128)(2,1)S(1)}, bf16[128,256]{1,0:T(8,128)(2,1)S(1)}, u32[]{:S(2)}, u32[]{:S(2)}) collective-permute-start(bf16[128,256]{1,0:T(8,128)(2,1)S(1)} %get-tuple-element.69), channel_id=1, source_target_pairs={{32,0},{33,1},{34,2},{35,3},{36,4},{37,5},{38,6},{39,7},{40,8},{41... | collective-permute-start | bytes 196616 | tf_op jit(solution)/shard_map/ppermute | solution.py:29
  110.7 11.2 %collective-permute-start.15 = (bf16[32,256]{1,0:T(8,128)(2,1)S(1)}, bf16[32,256]{1,0:T(8,128)(2,1)S(1)}, u32[]{:S(2)}, u32[]{:S(2)}) collective-permute-start(bf16[32,256]{1,0:T(8,128)(2,1)S(1)} %get-tuple-element.71), channel_id=1, source_target_pairs={{192,0},{193,1},{194,2},{195,3},{196,4},{197,5},{198,6},{199,7},{2... | collective-permute-start | bytes 49160 | tf_op jit(solution)/shard_map/ppermute | solution.py:29
  114.1 7.9 %collective-permute-start.16 = (bf16[32,256]{1,0:T(8,128)(2,1)S(1)}, bf16[32,256]{1,0:T(8,128)(2,1)S(1)}, u32[]{:S(2)}, u32[]{:S(2)}) collective-permute-start(bf16[32,256]{1,0:T(8,128)(2,1)S(1)} %get-tuple-element.72), channel_id=1, source_target_pairs={{128,0},{129,1},{130,2},{131,3},{132,4},{133,5},{134,6},{135,7},{1... | collective-permute-start | bytes 49160 | tf_op jit(solution)/shard_map/ppermute | solution.py:29
  119.3 4.6 %collective-permute-start.17 = (bf16[32,256]{1,0:T(8,128)(2,1)S(1)}, bf16[32,256]{1,0:T(8,128)(2,1)S(1)}, u32[]{:S(2)}, u32[]{:S(2)}) collective-permute-start(bf16[32,256]{1,0:T(8,128)(2,1)S(1)} %get-tuple-element.73), channel_id=1, source_target_pairs={{64,0},{65,1},{66,2},{67,3},{68,4},{69,5},{70,6},{71,7},{72,8},{73... | collective-permute-start | bytes 49160 | tf_op jit(solution)/shard_map/ppermute | solution.py:29

commit v5 on v4

--- a/solution.py
+++ b/solution.py
@@ -101,37 +101,53 @@
     )(saved, grad, lse)
 
 
-def turn_kernel(me, x_ref, mine_ref, other_ref):
-    even = me[0] == 0
+def turn_kernel(place, x_ref, mine_ref, other_ref, away_ref):
+    even = place[0] == 0
+    here = lax.rem(pl.program_id(0), 2) == place[1]
+    half = pl.multiple_of(lax.div(pl.program_id(0), 2) * 512, 512)
     for u in range(8):
         tile = x_ref[:, u * BLK : (u + 1) * BLK].T
         for yh in range(YH):
             first = tile[yh * 64 : yh * 64 + 32]
             second = tile[yh * 64 + 32 : yh * 64 + 64]
-            at = slice(u * 64 + yh * 32, u * 64 + yh * 32 + 32)
+            at = pl.ds(half + (u * 64 + yh * 32), 32)
+
+            def store(a, b):
+                @pl.when(here)
+                def _():
+                    mine_ref[at, :] = a
+                    other_ref[at, :] = b
+
+                @pl.when(jnp.logical_not(here))
+                def _():
+                    away_ref[0, at, :] = a
+                    away_ref[1, at, :] = b
 
             @pl.when(even)
             def _():
-                mine_ref[at, :] = first
-                other_ref[at, :] = second
+                store(first, second)
 
             @pl.when(jnp.logical_not(even))
             def _():
-                mine_ref[at, :] = second
-                other_ref[at, :] = first
-
-
-def turn(me, layer):
+                store(second, first)
+
+
+def turn(place, layer):
+    half = jax.ShapeDtypeStruct((2048, 256), BF16)
     return pl.pallas_call(
         turn_kernel,
         grid=(Z,),
-        out_shape=(jax.ShapeDtypeStruct((4096, 256), BF16),) * 2,
+        out_shape=(half, half, jax.ShapeDtypeStruct((2, 2048, 256), BF16)),
         in_specs=[smem(), pl.BlockSpec((256, 1024), lambda z: (0, z))],
-        out_specs=(pl.BlockSpec((512, 256), lambda z: (z, 0)),) * 2,
-        compiler_params=pltpu.CompilerParams(vmem_limit_bytes=8 * 2**20),
-        cost_estimate=pl.CostEstimate(flops=10**7, bytes_accessed=8 * 2**20, transcendentals=0),
+        out_specs=(
+            pl.BlockSpec((2048, 256), lambda z: (0, 0)),
+            pl.BlockSpec((2048, 256), lambda z: (0, 0)),
+            pl.BlockSpec((2, 2048, 256), lambda z: (0, 0, 0)),
+        ),
+        compiler_params=pltpu.CompilerParams(vmem_limit_bytes=12 * 2**20),
+        cost_estimate=pl.CostEstimate(flops=3 * 10**10, bytes_accessed=8 * 2**20, transcendentals=0),
         name="turn",
-    )(me, layer)
+    )(place, layer)
 
 
 NQ, NK = 4, 8
@@ -143,7 +159,6 @@
     dkv[...] = jnp.zeros_like(dkv)
 
     def chunk(i, first, count, masked):
-        keys = count * BLK
         at = [meta[first + n] for n in range(count)]
         rows = [pl.ds(pl.multiple_of(a * BLK, BLK), BLK) for a in at]
         kb = jnp.concatenate([kv[r, :BLK] for r in rows], 0)
@@ -155,12 +170,16 @@
             t = lax.broadcasted_iota(jnp.int32, (BLK, 2 * BLK), 1) % BLK
             ahead = t - u
             visible = [ahead >= (meta[NK + first + n] - q_pos) * BLK for n in range(count)]
-        dv = jnp.zeros((keys, BLK), F32)
-        dk = jnp.zeros((keys, BLK), F32)
+        def ahead_of(pair):
+            cols = slice(pair * 2 * BLK, (pair + 1) * 2 * BLK)
+            score = jnp.dot(kb, qt[i, :, cols], preferred_element_type=F32)
+            return score, jnp.dot(vb, gt[i, :, cols], preferred_element_type=F32)
+
+        probs, d_scores = [], []
+        score, d_prob = ahead_of(0)
         for pair in range(H // 2):
+            following = ahead_of(pair + 1) if pair + 1 < H // 2 else (None, None)
             cols = slice(pair * 2 * BLK, (pair + 1) * 2 * BLK)
-            heads = [slice((2 * pair + g) * BLK, (2 * pair + g + 1) * BLK) for g in range(2)]
-            score = jnp.dot(kb, qt[i, :, cols], preferred_element_type=F32)
             prob = jnp.exp2(score * factor - stats[pl.ds(i, 1), cols])
             if masked:
                 prob = jnp.concatenate(
@@ -170,20 +189,25 @@
                     ],
                     0,
                 )
-            d_prob = jnp.dot(vb, gt[i, :, cols], preferred_element_type=F32)
-            d_score = (prob * (d_prob - stats[pl.ds(NQ + i, 1), cols])).astype(BF16)
-            g_rows = jnp.concatenate([g_all[i, :, s] for s in heads], 0)
-            q_rows = jnp.concatenate([q_all[i, :, s] for s in heads], 0)
-            dv = dv + jnp.dot(prob.astype(BF16), g_rows, preferred_element_type=F32)
-            dk = dk + jnp.dot(d_score, q_rows, preferred_element_type=F32)
-            dqt[i, :, cols] += jnp.dot(ktb, d_score, preferred_element_type=F32)
+            d_scores.append((prob * (d_prob - stats[pl.ds(NQ + i, 1), cols])).astype(BF16))
+            probs.append(prob.astype(BF16))
+            score, d_prob = following
+        prob = jnp.concatenate(probs, 1)
+        d_score = jnp.concatenate(d_scores, 1)
+        heads = [slice(h * BLK, (h + 1) * BLK) for h in range(H)]
+        g_rows = jnp.concatenate([g_all[i, :, s] for s in heads], 0)
+        q_rows = jnp.concatenate([q_all[i, :, s] for s in heads], 0)
+        dv = jnp.dot(prob, g_rows, preferred_element_type=F32)
+        dk = jnp.dot(d_score, q_rows, preferred_element_type=F32)
+        dqt[i] += jnp.dot(ktb, d_score, preferred_element_type=F32)
         for n in range(count):
             dkv[at[n], :, :BLK] += dk[n * BLK : (n + 1) * BLK]
             dkv[at[n], :, BLK:] += dv[n * BLK : (n + 1) * BLK]
 
     def query_block(i, carry):
         whole = meta[2 * NK + NQ + i]
-        pairs = meta[2 * NK + 2 * NQ + i]
+        reached = meta[2 * NK + 2 * NQ + i]
+        rest = reached - 4 * whole
 
         def full_step(j, c):
             chunk(i, 4 * j, 4, False)
@@ -194,7 +218,12 @@
             return c
 
         lax.fori_loop(0, whole, full_step, 0)
-        lax.fori_loop(0, pairs, pair_step, 0)
+        lax.fori_loop(0, lax.div(rest, 2), pair_step, 0)
+
+        @pl.when(lax.rem(rest, 2) == 1)
+        def _():
+            chunk(i, reached - 1, 1, True)
+
         return carry
 
     lax.fori_loop(0, NQ, query_block, 0)
@@ -332,78 +361,60 @@
     below = jnp.sum(k_pos[None, :] < q_pos[:, None], axis=1)
     reached = jnp.sum(k_pos[None, :] <= q_pos[:, None], axis=1)
     whole = below // 4
-    pairs = (reached - 4 * whole + 1) // 2
-    return jnp.concatenate([order, ordered, q_pos, whole, pairs]).astype(jnp.int32)
-
-
-def project_kernel(mine_ref, other_ref, g_own, g_other, out_ref):
-    def step(z, carry):
-        rows = pl.ds(pl.multiple_of(z * 512, 512), 512)
-        terms = jnp.dot(mine_ref[rows, :], g_own[...], preferred_element_type=F32) + jnp.dot(
-            other_ref[rows, :], g_other[...], preferred_element_type=F32
-        )
-        at = pl.ds(pl.multiple_of(z * 32, 32), 32)
+    return jnp.concatenate([order, ordered, q_pos, whole, reached]).astype(jnp.int32)
+
+
+HALF = Z // 2
+
+
+def project_kernel(a_ref, b_ref, c_ref, d_ref, ga, gb, gc, gd, out_ref):
+    def step(j, carry):
+        rows = pl.ds(pl.multiple_of(j * 512, 512), 512)
+        terms = jnp.dot(a_ref[rows, :], ga[...], preferred_element_type=F32)
+        terms = terms + jnp.dot(b_ref[rows, :], gb[...], preferred_element_type=F32)
+        terms = terms + jnp.dot(c_ref[0, rows, :], gc[...], preferred_element_type=F32)
+        terms = terms + jnp.dot(d_ref[rows, :], gd[...], preferred_element_type=F32)
+        at = pl.ds(pl.multiple_of(j * 32, 32), 32)
         out_ref[:, at, :] = terms.astype(BF16).reshape(16, 32, 256)
         return carry
 
-    lax.fori_loop(0, Z, step, 0)
-
-
-def project(mine, other, g_own, g_other):
+    lax.fori_loop(0, HALF, step, 0)
+
+
+def project(turned, grads):
     return pl.pallas_call(
         project_kernel,
-        out_shape=jax.ShapeDtypeStruct((16, 256, 256), BF16),
-        in_specs=[vmem()] * 4,
+        out_shape=jax.ShapeDtypeStruct((16, HALF * 32, 256), BF16),
+        in_specs=[vmem()] * 8,
         out_specs=vmem(),
-        compiler_params=pltpu.CompilerParams(vmem_limit_bytes=16 * 2**20),
+        compiler_params=pltpu.CompilerParams(vmem_limit_bytes=12 * 2**20),
         cost_estimate=pl.CostEstimate(
             flops=2 * 4096 * 512 * 256, bytes_accessed=8 * 2**20, transcendentals=0
         ),
         name="project",
-    )(mine, other, g_own, g_other)
-
-
-def sum_kernel(place, in_ref, keep_ref, send_ref):
-    for j in range(Z // 2):
-        for ref, half in ((keep_ref, place[1]), (send_ref, 1 - place[1])):
-            at = pl.ds(pl.multiple_of((2 * j + half) * 32, 32), 32)
-            value = in_ref[0, at, :].astype(F32)
-            for n in range(1, 16):
-                value = value + in_ref[n, at, :].astype(F32)
-            ref[j * 32 : j * 32 + 32, :] = value.astype(ref.dtype)
+    )(*turned, *grads)
+
+
+def sum_kernel(place, in_ref, own_ref, *out_refs):
+    for k in range(HALF):
+        at = pl.ds(pl.multiple_of((place[2] + k) % HALF * 32, 32), 32)
+        value = in_ref[0, at, :].astype(F32)
+        for j in range(1, 16):
+            value = value + in_ref[j, at, :].astype(F32)
+        ref = own_ref if k == 0 else out_refs[k - 1]
+        ref[...] = value.astype(ref.dtype)
 
 
 def sum_terms(place, terms):
     return pl.pallas_call(
         sum_kernel,
-        out_shape=(
-            jax.ShapeDtypeStruct((128, 256), F32),
-            jax.ShapeDtypeStruct((128, 256), BF16),
-        ),
+        out_shape=(jax.ShapeDtypeStruct((32, 256), F32),)
+        + (jax.ShapeDtypeStruct((32, 256), BF16),) * (HALF - 1),
         in_specs=[smem(), vmem()],
-        out_specs=(vmem(),) * 2,
+        out_specs=(vmem(),) * HALF,
         compiler_params=pltpu.CompilerParams(vmem_limit_bytes=8 * 2**20),
         name="sum_terms",
     )(place, terms)
-
-
-def split_kernel(place, keep_ref, got_ref, *out_refs):
-    for k in range(Z // 2):
-        at = pl.ds(pl.multiple_of((place[2] + k) % (Z // 2) * 32, 32), 32)
-        value = keep_ref[at, :] + got_ref[at, :].astype(F32)
-        out_refs[k][...] = value.astype(out_refs[k].dtype)
-
-
-def split_terms(place, keep, got):
-    return pl.pallas_call(
-        split_kernel,
-        out_shape=(jax.ShapeDtypeStruct((32, 256), F32),)
-        + (jax.ShapeDtypeStruct((32, 256), BF16),) * 3,
-        in_specs=[smem(), vmem(), vmem()],
-        out_specs=(vmem(),) * 4,
-        compiler_params=pltpu.CompilerParams(vmem_limit_bytes=4 * 2**20),
-        name="split_terms",
-    )(place, keep, got)
 
 
 def body(layer_input, query_rows, key_rows, value_rows, attn_out, d_attn, log_sum_exp, block_order):
@@ -419,7 +430,7 @@
     stats_other = fetch(stats, swap_core)
     both = jnp.concatenate([pair, pair_y], axis=0)
     blocks = [both] + [fetch(both, by_ctx(k, 0)) for k in ALONG_X[1:]]
-    mine, other = turn(place[:1], layer_input[0])
+    mine, other, away = turn(place, layer_input[0])
 
     places = block_order.reshape(16, 2)
     q_pos = jnp.concatenate([places[ctx], places[ctx ^ 1]])
@@ -427,11 +438,13 @@
     def owners(row):
         return jnp.concatenate([places[(x + k) % X * 4 + row * 2 + c] for k in ALONG_X])
 
-    blocks, mine, other = lax.optimization_barrier((blocks, mine, other))
+    blocks, mine, other, away = lax.optimization_barrier((blocks, mine, other, away))
+    away = fetch(away, swap_z)
     mine_core = fetch(other, swap_core)
     *carried, dkv_y = first_call(
         make_meta(owners(1 - yh), q_pos), (q, q_other), (g, g_other), (stats, stats_other), blocks
     )
+    carried, mine_core = lax.optimization_barrier((carried, mine_core))
     carried, mine_core = lax.optimization_barrier((carried, mine_core))
     dq_own, dq_sent, *dkv = second_call(make_meta(owners(yh), q_pos), carried, blocks)
     dkv_y = fetch(dkv_y, by_ctx(0, 1))
@@ -441,15 +454,17 @@
     for part in parts:
         total = total + part.astype(F32)
     grads = total.astype(BF16)
-    grads_core = fetch(grads, swap_core)
-
-    terms = project(mine, mine_core, grads, grads_core)
+    grads_z = fetch(grads, swap_z)
+    away, grads_core = lax.optimization_barrier((away, fetch(grads, swap_core)))
+    grads_zc = fetch(grads_z, swap_core)
+    mine_zc = fetch(away[1], swap_core)
+
+    terms = project((mine, mine_core, away, mine_zc), (grads, grads_core, grads_z, grads_zc))
     terms = lax.all_to_all(terms, ("yl", "x", "yh"), 0, 0)
     terms, dq_sent = lax.optimization_barrier((terms, dq_sent))
-    keep, sent = sum_terms(place, terms)
-    own, *sent = split_terms(place, keep, fetch(sent, swap_z))
+    own, *sent = sum_terms(place, terms)
     d_query = (dq_own + fetch(dq_sent, swap_core).astype(F32)).astype(BF16)[None]
-    for k in range(1, Z // 2):
+    for k in range(1, HALF):
         own = own + fetch(sent[k - 1], by_z(-2 * k)).astype(F32)
     return (d_query, own)
 

time: 128 us -> 128 us (level)
  waiting for transfers between devices: 20 us -> 33.9 us
  blocking collectives: 33.1 us -> 21.5 us
  Pallas kernels: 26.4 us -> 34 us
  starting transfers between devices: 32.8 us -> 25.7 us
  local copies, waits for them, and re-layouts: 7.83 us -> 6.19 us
    ppermute x18 -> x21, waiting for transfers between devices: 20 us -> 33.9 us  [fetch(): return lax.ppermute(value, AXES, pairs)]
    all_to_all x1, blocking collectives: 33.1 us -> 21.5 us  [body(): terms = lax.all_to_all(terms, ('yl', 'x', 'yh'), 0, 0)]
    ppermute x18 -> x21, starting transfers between devices: 32.8 us -> 25.7 us  [fetch(): return lax.ppermute(value, AXES, pairs)]
    pallas_call x1, Pallas kernels: 8.87 us -> 12.8 us  [second_call(): pl.pallas_call(second_kernel, out_shape=(jax.ShapeDtypeStruct((256, WIDE)...]
    pallas_call x1, Pallas kernels: 7.97 us -> 11.7 us  [first_call(): pl.pallas_call(first_kernel, out_shape=(rows,) * 4 + (jax.ShapeDtypeStruc...]
    unnamed x20, local copies, waits for them, and re-layouts: 6.89 us -> 5.2 us
    pallas_call x4 -> x3, Pallas kernels: 9.1 us -> 8.92 us  [the longest x1 6.47 us: turn(): pl.pallas_call(turn_kernel, grid=(Z,), out_shape=(half, half, jax.ShapeDt...]
  transfers between devices with their start and end apart: 18 -> 21, of which waited for: 9 -> 9; matrix products, arithmetic and copies ran while one was open for 3% -> 3% of each run, Pallas kernels for 19% -> 25%
where the time goes in v5:
time: 128 us; the launch traced here: 127 us
  Pallas kernels  34 us (27%)
  waiting for transfers between devices  33.9 us (26%)
  starting transfers between devices  25.7 us (20%)
  blocking collectives  21.5 us (17%)
  local copies, waits for them, and re-layouts  6.19 us (5%)
  other arithmetic  4.61 us (4%)
    ppermute x21, waiting for transfers between devices, fetch(): return lax.ppermute(value, AXES, pairs)  33.9 us
    ppermute x21, starting transfers between devices, fetch(): return lax.ppermute(value, AXES, pairs)  25.7 us
    all_to_all x1, blocking collectives, body(): terms = lax.all_to_all(terms, ('yl', 'x', 'yh'), 0, 0)  21.5 us
    pallas_call x1, Pallas kernels, second_call(): pl.pallas_call(second_kernel, out_shape=(jax.ShapeDtypeStruct((256, WIDE)...  12.8 us
    pallas_call x1, Pallas kernels, first_call(): pl.pallas_call(first_kernel, out_shape=(rows,) * 4 + (jax.ShapeDtypeStruc...  11.7 us
    pallas_call x1, Pallas kernels, turn(): pl.pallas_call(turn_kernel, grid=(Z,), out_shape=(half, half, jax.ShapeDt...  6.47 us
    unnamed x20, local copies, waits for them, and re-layouts  5.2 us
  transfers between devices with their start and end apart: 21, of which 9 were waited for; matrix products, arithmetic and copies ran while one was open for 3% of the time, Pallas kernels for 25%

profile of v5, /device:TPU:4, one launch (start us, length us, event | category | flops | bytes accessed | tf_op | source)
XLA Modules:
  0.0 126.8 jit_solution(13786275141687045649)
XLA Ops:
  0.6 0.9 pad_maximum_fusion.1
  1.5 3.3 %collective-permute-start.3 = (bf16[256,256]{1,0:T(8,128)(2,1)S(1)}, bf16[256,256]{1,0:T(8,128)(2,1)}, u32[]{:S(2)}, u32[]{:S(2)}) collective-permute-start(bf16[256,256]{1,0:T(8,128)(2,1)S(1)} %pad_maximum_fusion.1), channel_id=1, source_target_pairs={{2,0},{3,1},{0,2},{1,3},{6,4},{7,5},{4,6},{5,7},{10,8},{11,9},{8,1... | collective-permute-start | bytes 393224 | tf_op jit(solution)/shard_map/ppermute | solution.py:29
  4.8 0.5 collective-permute-start.1
  5.3 0.7 reshape.14
  6.3 2.2 %copy-done.3 = bf16[1,256,8192]{2,1,0:T(8,128)(2,1)S(1)} copy-done((bf16[1,256,8192]{2,1,0:T(8,128)(2,1)S(1)}, bf16[1,256,8192]{2,1,0:T(8,128)(2,1)}, u32[]{:S(2)}) %copy-start.3) | copy-done | bytes 4194328
  8.5 6.5 %turn.1 = (bf16[2048,256]{1,0:T(8,128)(2,1)S(1)}, bf16[2048,256]{1,0:T(8,128)(2,1)S(1)}, bf16[2,2048,256]{2,1,0:T(8,128)(2,1)S(1)}) custom-call(s32[3]{0:T(128)S(1)} %pad_add_fusion.3.place, bf16[256,8192]{1,0:T(8,128)(2,1)S(1)} %bitcast.39), custom_call_target="tpu_custom_call" | custom-call | flops 30000001024 | bytes 8388608 | tf_op jit(solution)/shard_map/turn/pallas_call | solution.py:137
  15.0 1.3 %copy-done.4 = bf16[2,2048,256]{2,1,0:T(8,128)(2,1)} copy-done((bf16[2,2048,256]{2,1,0:T(8,128)(2,1)}, bf16[2,2048,256]{2,1,0:T(8,128)(2,1)S(1)}, u32[]{:S(2)}) %copy-start.4) | copy-done | bytes 2097176
  16.5 0.2 convert_reduce_fusion.2
  16.7 0.9 pad_maximum_fusion.refs_6_
  17.7 0.6 collective-permute-start.6
  18.3 2.2 %collective-permute-start.5 = (bf16[512,256]{1,0:T(8,128)(2,1)S(1)}, bf16[512,256]{1,0:T(8,128)(2,1)}, u32[]{:S(2)}, u32[]{:S(2)}) collective-permute-start(bf16[512,256]{1,0:T(8,128)(2,1)S(1)} %pad_maximum_fusion.refs_6_), channel_id=1, source_target_pairs={{12,0},{13,1},{14,2},{15,3},{0,4},{1,5},{2,6},{3,7},{4,8},{5,9},{6... | collective-permute-start | bytes 786440 | tf_op jit(solution)/shard_map/ppermute | solution.py:29
  20.4 0.1 collective-permute-start.4
  20.6 0.2 convert_reduce_fusion.1
  20.8 0.5 row_stats.1.refs_4_
  21.3 0.2 convert_reduce_fusion
  21.5 7.0 %collective-permute-done.6.refs_9_ = bf16[512,256]{1,0:T(8,128)(2,1)S(1)} collective-permute-done((bf16[512,256]{1,0:T(8,128)(2,1)S(1)}, bf16[512,256]{1,0:T(8,128)(2,1)S(1)}, u32[]{:S(2)}, u32[]{:S(2)}) %collective-permute-start.6) | collective-permute-done | bytes 262176 | tf_op jit(solution)/shard_map/ppermute | solution.py:29
  28.5 0.7 copy-done.6
  29.2 0.1 select_reduce_fusion
  29.3 0.1 concatenate.27.meta
  29.5 2.6 %collective-permute-done.5.refs_8_ = bf16[512,256]{1,0:T(8,128)(2,1)} collective-permute-done((bf16[512,256]{1,0:T(8,128)(2,1)S(1)}, bf16[512,256]{1,0:T(8,128)(2,1)}, u32[]{:S(2)}, u32[]{:S(2)}) %collective-permute-start.5) | collective-permute-done | bytes 262176 | tf_op jit(solution)/shard_map/ppermute | solution.py:29
  32.1 1.9 %collective-permute-start.8 = (bf16[2,2048,256]{2,1,0:T(8,128)(2,1)}, bf16[2,2048,256]{2,1,0:T(8,128)(2,1)S(1)}, u32[]{:S(2)}, u32[]{:S(2)}) collective-permute-start(bf16[2,2048,256]{2,1,0:T(8,128)(2,1)} %copy-done.4), channel_id=1, source_target_pairs={{32,0},{33,1},{34,2},{35,3},{36,4},{37,5},{38,6},{39,7},{40,8},{41... | collective-permute-start | bytes 6291464 | tf_op jit(solution)/shard_map/ppermute | solution.py:29
  34.1 0.9 copy-done.7
  35.0 11.7 %attention_first.1 = (bf16[4,128,1024]{2,1,0:T(8,128)(2,1)S(1)}, bf16[4,128,1024]{2,1,0:T(8,128)(2,1)S(1)}, bf16[4,128,1024]{2,1,0:T(8,128)(2,1)S(1)}, bf16[4,12...) custom-call(s32[28]{0:T(128)S(1)} %concatenate.27.meta, ...), custom_call_target="tpu_custom_call" | custom-call | flops 60000002048 | bytes 1048576 | tf_op jit(solution)/shard_map/attention_first/pallas_call | solution.py:320
  46.8 1.8 %collective-permute-start.9 = (bf16[1024,256]{1,0:T(8,128)(2,1)S(1)}, bf16[1024,256]{1,0:T(8,128)(2,1)S(1)}, u32[]{:S(2)}, u32[]{:S(2)}) collective-permute-start(bf16[1024,256]{1,0:T(8,128)(2,1)S(1)} %get-tuple-element.65), channel_id=1, source_target_pairs={{2,0},{3,1},{0,2},{1,3},{6,4},{7,5},{4,6},{5,7},{10,8},{11,9},{8,1... | collective-permute-start | bytes 1572872 | tf_op jit(solution)/shard_map/ppermute | solution.py:29
  48.5 12.8 %attention_second.1 = (f32[256,1024]{1,0:T(8,128)S(1)}, bf16[256,1024]{1,0:T(8,128)(2,1)S(1)}, f32[256,256]{1,0:T(8,128)S(1)}, f32[256,256]{1,0:T(8,128)S(1)}, f...) custom-call(s32[28]{0:T(128)S(1)} %concatenate.25.meta, bf16[4,128,1024]{2,1,0:T(8,128)(2,1)S(1)} %get-tuple-element.54.refs_0_, ...), custom_call_target="tpu_custom_call" | custom-call | flops 60000002048 | bytes 1048576 | tf_op jit(solution)/shard_map/attention_second/pallas_call | solution.py:339
  61.4 0.1 add_convert_fusion.4
  61.5 0.1 collective-permute-start.10
  61.6 0.1 collective-permute-start.12
  61.7 1.9 %collective-permute-start.11 = (bf16[256,256]{1,0:T(8,128)(2,1)S(1)}, bf16[256,256]{1,0:T(8,128)(2,1)S(1)}, u32[]{:S(2)}, u32[]{:S(2)}) collective-permute-start(bf16[256,256]{1,0:T(8,128)(2,1)S(1)} %get-tuple-element.90), channel_id=1, source_target_pairs={{4,0},{5,1},{6,2},{7,3},{8,4},{9,5},{10,6},{11,7},{12,8},{13,9},{1... | collective-permute-start | bytes 393224 | tf_op jit(solution)/shard_map/ppermute | solution.py:29
  63.6 4.7 %collective-permute-done.10 = bf16[256,256]{1,0:T(8,128)(2,1)S(1)} collective-permute-done((bf16[256,256]{1,0:T(8,128)(2,1)S(1)}, bf16[256,256]{1,0:T(8,128)(2,1)S(1)}, u32[]{:S(2)}, u32[]{:S(2)}) %collective-permute-start.10) | collective-permute-done | bytes 131104 | tf_op jit(solution)/shard_map/ppermute | solution.py:29
  68.3 1.7 %collective-permute-done.11 = bf16[256,256]{1,0:T(8,128)(2,1)S(1)} collective-permute-done((bf16[256,256]{1,0:T(8,128)(2,1)S(1)}, bf16[256,256]{1,0:T(8,128)(2,1)S(1)}, u32[]{:S(2)}, u32[]{:S(2)}) %collective-permute-start.11) | collective-permute-done | bytes 131104 | tf_op jit(solution)/shard_map/ppermute | solution.py:29
  70.0 0.1 add_convert_fusion.1.ga
  70.1 0.1 collective-permute-start.13
  70.2 1.3 %collective-permute-done.13.gb = bf16[256,256]{1,0:T(8,128)(2,1)S(1)} collective-permute-done((bf16[256,256]{1,0:T(8,128)(2,1)S(1)}, bf16[256,256]{1,0:T(8,128)(2,1)S(1)}, u32[]{:S(2)}, u32[]{:S(2)}) %collective-permute-start.13) | collective-permute-done | bytes 131104 | tf_op jit(solution)/shard_map/ppermute | solution.py:29
  71.5 9.0 %collective-permute-done.8.c_ref = bf16[2,2048,256]{2,1,0:T(8,128)(2,1)S(1)} collective-permute-done((bf16[2,2048,256]{2,1,0:T(8,128)(2,1)}, bf16[2,2048,256]{2,1,0:T(8,128)(2,1)S(1)}, u32[]{:S(2)}, u32[]{:S(2)}) %collective-permute-start.8) | collective-permute-done | bytes 2097184 | tf_op jit(solution)/shard_map/ppermute | solution.py:29
  80.6 0.1 collective-permute-start.14
  80.7 1.8 %collective-permute-start.15 = (bf16[256,256]{1,0:T(8,128)(2,1)S(1)}, bf16[256,256]{1,0:T(8,128)(2,1)S(1)}, u32[]{:S(2)}, u32[]{:S(2)}) collective-permute-start(bf16[256,256]{1,0:T(8,128)(2,1)S(1)} %add_convert_fusion.1.ga), channel_id=1, source_target_pairs={{32,0},{33,1},{34,2},{35,3},{36,4},{37,5},{38,6},{39,7},{40,8},{41... | collective-permute-start | bytes 393224 | tf_op jit(solution)/shard_map/ppermute | solution.py:29
  82.6 4.1 %collective-permute-done.15.gc = bf16[256,256]{1,0:T(8,128)(2,1)S(1)} collective-permute-done((bf16[256,256]{1,0:T(8,128)(2,1)S(1)}, bf16[256,256]{1,0:T(8,128)(2,1)S(1)}, u32[]{:S(2)}, u32[]{:S(2)}) %collective-permute-start.15) | collective-permute-done | bytes 131104 | tf_op jit(solution)/shard_map/ppermute | solution.py:29
  86.7 1.3 %collective-permute-done.16.gd = bf16[256,256]{1,0:T(8,128)(2,1)S(1)} collective-permute-done((bf16[256,256]{1,0:T(8,128)(2,1)S(1)}, bf16[256,256]{1,0:T(8,128)(2,1)S(1)}, u32[]{:S(2)}, u32[]{:S(2)}) %collective-permute-start.16) | collective-permute-done | bytes 131104 | tf_op jit(solution)/shard_map/ppermute | solution.py:29
  88.0 1.8 %project.1 = bf16[16,128,256]{2,1,0:T(8,128)(2,1)S(1)} custom-call(bf16[2048,256]{1,0:T(8,128)(2,1)S(1)} %get-tuple-element.61.a_ref, bf16[2048,256]{1,0:T(8,128)(2,1)S(1)} %collective-permute-done.7.b_ref, bf16[2,2048,256]{2,1,0:T(8,128)(2,1)S(1)} %collective-permute-done.8.c_ref, bf16[2048,256]{1,0:T(8,128)(2,1)S(1)} %collective-permute-done.14.d_ref, ...), custom_call_target="tpu_custom_call" | custom-call | flops 1073741824 | bytes 8388608 | tf_op jit(solution)/shard_map/project/pallas_call | solution.py:385
  89.8 21.5 %all_to_all.5.in_ref = bf16[16,128,256]{2,1,0:T(8,128)(2,1)S(1)} all-to-all(bf16[16,128,256]{2,1,0:T(8,128)(2,1)S(1)} %project.1), channel_id=1, replica_groups=mesh['z'=8,'yl'=2,'x'=4,'yh'=2,'c'=2] {'yl','x','yh'}, dimensions={0} | all-to-all | bytes 2097152 | tf_op jit(solution)/shard_map/all_to_all | solution.py:463
  111.3 0.7 sum_terms.1
  112.0 3.3 %collective-permute-start.18 = (bf16[32,256]{1,0:T(8,128)(2,1)S(1)}, bf16[32,256]{1,0:T(8,128)(2,1)S(1)}, u32[]{:S(2)}, u32[]{:S(2)}) collective-permute-start(bf16[32,256]{1,0:T(8,128)(2,1)S(1)} %get-tuple-element.75), channel_id=1, source_target_pairs={{192,0},{193,1},{194,2},{195,3},{196,4},{197,5},{198,6},{199,7},{2... | collective-permute-start | bytes 49160 | tf_op jit(solution)/shard_map/ppermute | solution.py:29
  115.3 5.2 %collective-permute-start.19 = (bf16[32,256]{1,0:T(8,128)(2,1)S(1)}, bf16[32,256]{1,0:T(8,128)(2,1)S(1)}, u32[]{:S(2)}, u32[]{:S(2)}) collective-permute-start(bf16[32,256]{1,0:T(8,128)(2,1)S(1)} %get-tuple-element.76), channel_id=1, source_target_pairs={{128,0},{129,1},{130,2},{131,3},{132,4},{133,5},{134,6},{135,7},{1... | collective-permute-start | bytes 49160 | tf_op jit(solution)/shard_map/ppermute | solution.py:29
  120.6 2.7 %collective-permute-start.20 = (bf16[32,256]{1,0:T(8,128)(2,1)S(1)}, bf16[32,256]{1,0:T(8,128)(2,1)S(1)}, u32[]{:S(2)}, u32[]{:S(2)}) collective-permute-start(bf16[32,256]{1,0:T(8,128)(2,1)S(1)} %get-tuple-element.77), channel_id=1, source_target_pairs={{64,0},{65,1},{66,2},{67,3},{68,4},{69,5},{70,6},{71,7},{72,8},{73... | collective-permute-start | bytes 49160 | tf_op jit(solution)/shard_map/ppermute | solution.py:29
  123.2 2.0 %collective-permute-done.20 = bf16[32,256]{1,0:T(8,128)(2,1)S(1)} collective-permute-done((bf16[32,256]{1,0:T(8,128)(2,1)S(1)}, bf16[32,256]{1,0:T(8,128)(2,1)S(1)}, u32[]{:S(2)}, u32[]{:S(2)}) %collective-permute-start.20) | collective-permute-done | bytes 16416 | tf_op jit(solution)/shard_map/ppermute | solution.py:29
  125.2 0.6 convert_add_fusion
  125.8 0.9 fusion
  (42 shorter events, 0.6 us)
Async XLA Ops:
  1.5 15.2 %collective-permute-start.3 = (bf16[256,256]{1,0:T(8,128)(2,1)S(1)}, bf16[256,256]{1,0:T(8,128)(2,1)}, u32[]{:S(2)}, u32[]{:S(2)}) collective-permute-start(bf16[256,256]{1,0:T(8,128)(2,1)S(1)} %pad_maximum_fusion.1), channel_id=1, source_target_pairs={{2,0},{3,1},{0,2},{1,3},{6,4},{7,5},{4,6},{5,7},{10,8},{11,9},{8,1... | collective-permute-start | bytes 393224 | tf_op jit(solution)/shard_map/ppermute | solution.py:29
  4.8 29.3 %collective-permute-start = (bf16[256,1024]{1,0:T(8,128)(2,1)}, bf16[256,1024]{1,0:T(8,128)(2,1)}, u32[]{:S(2)}, u32[]{:S(2)}) collective-permute-start(bf16[256,1024]{1,0:T(8,128)(2,1)} %bitcast.40), channel_id=1, source_target_pairs={{1,0},{0,1},{3,2},{2,3},{5,4},{4,5},{7,6},{6,7},{9,8},{8,9},{11,10... | collective-permute-start | bytes 1572872 | tf_op jit(solution)/shard_map/ppermute | solution.py:29
  4.8 29.3 %collective-permute-start.1 = (bf16[256,1024]{1,0:T(8,128)(2,1)}, bf16[256,1024]{1,0:T(8,128)(2,1)}, u32[]{:S(2)}, u32[]{:S(2)}) collective-permute-start(bf16[256,1024]{1,0:T(8,128)(2,1)} %bitcast.35), channel_id=1, source_target_pairs={{1,0},{0,1},{3,2},{2,3},{5,4},{4,5},{7,6},{6,7},{9,8},{8,9},{11,10... | collective-permute-start | bytes 1572872 | tf_op jit(solution)/shard_map/ppermute | solution.py:29
  6.3 2.2 %copy-start.3 = (bf16[1,256,8192]{2,1,0:T(8,128)(2,1)S(1)}, bf16[1,256,8192]{2,1,0:T(8,128)(2,1)}, u32[]{:S(2)}) copy-start(bf16[1,256,8192]{2,1,0:T(8,128)(2,1)} %param.8) | copy-start | bytes 12582916
  8.5 8.2 %copy-start.8 = (bf16[1,256,128]{2,1,0:T(8,128)(2,1)S(1)}, bf16[1,256,128]{2,1,0:T(8,128)(2,1)}, u32[]{:S(2)}) copy-start(bf16[1,256,128]{2,1,0:T(8,128)(2,1)} %param.11) | copy-start | bytes 196612
  8.5 8.3 %copy-start.9 = (bf16[1,256,128]{2,1,0:T(8,128)(2,1)S(1)}, bf16[1,256,128]{2,1,0:T(8,128)(2,1)}, u32[]{:S(2)}) copy-start(bf16[1,256,128]{2,1,0:T(8,128)(2,1)} %param.10) | copy-start | bytes 196612
  8.5 12.3 %copy-start = (bf16[1,256,1024]{2,1,0:T(8,128)(2,1)S(1)}, bf16[1,256,1024]{2,1,0:T(8,128)(2,1)}, u32[]{:S(2)}) copy-start(bf16[1,256,1024]{2,1,0:T(8,128)(2,1)} %param.12) | copy-start | bytes 1572868
  8.5 12.3 %copy-start.1 = (bf16[1,256,1024]{2,1,0:T(8,128)(2,1)S(1)}, bf16[1,256,1024]{2,1,0:T(8,128)(2,1)}, u32[]{:S(2)}) copy-start(bf16[1,256,1024]{2,1,0:T(8,128)(2,1)} %param.13) | copy-start | bytes 1572868
  8.5 12.3 %copy-start.2 = (f32[1,8,256]{2,1,0:T(8,128)S(1)}, f32[1,8,256]{2,1,0:T(8,128)}, u32[]{:S(2)}) copy-start(f32[1,8,256]{2,1,0:T(8,128)} %param.14) | copy-start | bytes 24580
  8.5 25.6 %copy-start.5 = (bf16[1,256,1024]{2,1,0:T(8,128)(2,1)S(1)}, bf16[1,256,1024]{2,1,0:T(8,128)(2,1)}, u32[]{:S(2)}) copy-start(bf16[1,256,1024]{2,1,0:T(8,128)(2,1)} %param.9) | copy-start | bytes 1572868
  15.0 1.3 %copy-start.4 = (bf16[2,2048,256]{2,1,0:T(8,128)(2,1)}, bf16[2,2048,256]{2,1,0:T(8,128)(2,1)S(1)}, u32[]{:S(2)}) copy-start(bf16[2,2048,256]{2,1,0:T(8,128)(2,1)S(1)} %get-tuple-element.63) | copy-start | bytes 6291460
  17.7 10.8 %collective-permute-start.6 = (bf16[512,256]{1,0:T(8,128)(2,1)S(1)}, bf16[512,256]{1,0:T(8,128)(2,1)S(1)}, u32[]{:S(2)}, u32[]{:S(2)}) collective-permute-start(bf16[512,256]{1,0:T(8,128)(2,1)S(1)} %pad_maximum_fusion.refs_6_), channel_id=1, source_target_pairs={{8,0},{9,1},{10,2},{11,3},{12,4},{13,5},{14,6},{15,7},{0,8},{1,9},... | collective-permute-start | bytes 786440 | tf_op jit(solution)/shard_map/ppermute | solution.py:29
  18.3 13.9 %collective-permute-start.5 = (bf16[512,256]{1,0:T(8,128)(2,1)S(1)}, bf16[512,256]{1,0:T(8,128)(2,1)}, u32[]{:S(2)}, u32[]{:S(2)}) collective-permute-start(bf16[512,256]{1,0:T(8,128)(2,1)S(1)} %pad_maximum_fusion.refs_6_), channel_id=1, source_target_pairs={{12,0},{13,1},{14,2},{15,3},{0,4},{1,5},{2,6},{3,7},{4,8},{5,9},{6... | collective-permute-start | bytes 786440 | tf_op jit(solution)/shard_map/ppermute | solution.py:29
  20.4 11.7 %collective-permute-start.4 = (bf16[512,256]{1,0:T(8,128)(2,1)S(1)}, bf16[512,256]{1,0:T(8,128)(2,1)}, u32[]{:S(2)}, u32[]{:S(2)}) collective-permute-start(bf16[512,256]{1,0:T(8,128)(2,1)S(1)} %pad_maximum_fusion.refs_6_), channel_id=1, source_target_pairs={{4,0},{5,1},{6,2},{7,3},{8,4},{9,5},{10,6},{11,7},{12,8},{13,9},{1... | collective-permute-start | bytes 786440 | tf_op jit(solution)/shard_map/ppermute | solution.py:29
  28.5 0.7 copy-start.6
  29.2 4.9 %collective-permute-start.2 = (f32[8,1024]{1,0:T(8,128)S(1)}, f32[8,1024]{1,0:T(8,128)S(1)}, u32[]{:S(2)}, u32[]{:S(2)}) collective-permute-start(f32[8,1024]{1,0:T(8,128)S(1)} %row_stats.1.refs_4_), channel_id=1, source_target_pairs={{1,0},{0,1},{3,2},{2,3},{5,4},{4,5},{7,6},{6,7},{9,8},{8,9},{11,10... | collective-permute-start | bytes 98312 | tf_op jit(solution)/shard_map/ppermute | solution.py:29
  32.1 16.4 %collective-permute-start.7 = (bf16[2048,256]{1,0:T(8,128)(2,1)S(1)}, bf16[2048,256]{1,0:T(8,128)(2,1)S(1)}, u32[]{:S(2)}, u32[]{:S(2)}) collective-permute-start(bf16[2048,256]{1,0:T(8,128)(2,1)S(1)} %get-tuple-element.53), channel_id=1, source_target_pairs={{1,0},{0,1},{3,2},{2,3},{5,4},{4,5},{7,6},{6,7},{9,8},{8,9},{11,10... | collective-permute-start | bytes 3145736 | tf_op jit(solution)/shard_map/ppermute | solution.py:29
  32.1 48.4 %collective-permute-start.8 = (bf16[2,2048,256]{2,1,0:T(8,128)(2,1)}, bf16[2,2048,256]{2,1,0:T(8,128)(2,1)S(1)}, u32[]{:S(2)}, u32[]{:S(2)}) collective-permute-start(bf16[2,2048,256]{2,1,0:T(8,128)(2,1)} %copy-done.4), channel_id=1, source_target_pairs={{32,0},{33,1},{34,2},{35,3},{36,4},{37,5},{38,6},{39,7},{40,8},{41... | collective-permute-start | bytes 6291464 | tf_op jit(solution)/shard_map/ppermute | solution.py:29
  34.1 1.0 copy-start.7
  46.8 14.6 %collective-permute-start.9 = (bf16[1024,256]{1,0:T(8,128)(2,1)S(1)}, bf16[1024,256]{1,0:T(8,128)(2,1)S(1)}, u32[]{:S(2)}, u32[]{:S(2)}) collective-permute-start(bf16[1024,256]{1,0:T(8,128)(2,1)S(1)} %get-tuple-element.65), channel_id=1, source_target_pairs={{2,0},{3,1},{0,2},{1,3},{6,4},{7,5},{4,6},{5,7},{10,8},{11,9},{8,1... | collective-permute-start | bytes 1572872 | tf_op jit(solution)/shard_map/ppermute | solution.py:29
  61.5 6.8 %collective-permute-start.10 = (bf16[256,256]{1,0:T(8,128)(2,1)S(1)}, bf16[256,256]{1,0:T(8,128)(2,1)S(1)}, u32[]{:S(2)}, u32[]{:S(2)}) collective-permute-start(bf16[256,256]{1,0:T(8,128)(2,1)S(1)} %get-tuple-element.88), channel_id=1, source_target_pairs={{12,0},{13,1},{14,2},{15,3},{0,4},{1,5},{2,6},{3,7},{4,8},{5,9},{6... | collective-permute-start | bytes 393224 | tf_op jit(solution)/shard_map/ppermute | solution.py:29
  61.6 6.7 %collective-permute-start.12 = (bf16[256,256]{1,0:T(8,128)(2,1)S(1)}, bf16[256,256]{1,0:T(8,128)(2,1)S(1)}, u32[]{:S(2)}, u32[]{:S(2)}) collective-permute-start(bf16[256,256]{1,0:T(8,128)(2,1)S(1)} %get-tuple-element.89), channel_id=1, source_target_pairs={{8,0},{9,1},{10,2},{11,3},{12,4},{13,5},{14,6},{15,7},{0,8},{1,9},... | collective-permute-start | bytes 393224 | tf_op jit(solution)/shard_map/ppermute | solution.py:29
  61.7 8.3 %collective-permute-start.11 = (bf16[256,256]{1,0:T(8,128)(2,1)S(1)}, bf16[256,256]{1,0:T(8,128)(2,1)S(1)}, u32[]{:S(2)}, u32[]{:S(2)}) collective-permute-start(bf16[256,256]{1,0:T(8,128)(2,1)S(1)} %get-tuple-element.90), channel_id=1, source_target_pairs={{4,0},{5,1},{6,2},{7,3},{8,4},{9,5},{10,6},{11,7},{12,8},{13,9},{1... | collective-permute-start | bytes 393224 | tf_op jit(solution)/shard_map/ppermute | solution.py:29
  70.1 1.4 %collective-permute-start.13 = (bf16[256,256]{1,0:T(8,128)(2,1)S(1)}, bf16[256,256]{1,0:T(8,128)(2,1)S(1)}, u32[]{:S(2)}, u32[]{:S(2)}) collective-permute-start(bf16[256,256]{1,0:T(8,128)(2,1)S(1)} %add_convert_fusion.1.ga), channel_id=1, source_target_pairs={{1,0},{0,1},{3,2},{2,3},{5,4},{4,5},{7,6},{6,7},{9,8},{8,9},{11,10... | collective-permute-start | bytes 393224 | tf_op jit(solution)/shard_map/ppermute | solution.py:29
  80.6 7.4 %collective-permute-start.14 = (bf16[2048,256]{1,0:T(8,128)(2,1)S(1)}, bf16[2048,256]{1,0:T(8,128)(2,1)S(1)}, u32[]{:S(2)}, u32[]{:S(2)}) collective-permute-start(bf16[2048,256]{1,0:T(8,128)(2,1)S(1)} %slice_bitcast_fusion), channel_id=1, source_target_pairs={{1,0},{0,1},{3,2},{2,3},{5,4},{4,5},{7,6},{6,7},{9,8},{8,9},{11,10... | collective-permute-start | bytes 3145736 | tf_op jit(solution)/shard_map/ppermute | solution.py:29
  80.7 5.9 %collective-permute-start.15 = (bf16[256,256]{1,0:T(8,128)(2,1)S(1)}, bf16[256,256]{1,0:T(8,128)(2,1)S(1)}, u32[]{:S(2)}, u32[]{:S(2)}) collective-permute-start(bf16[256,256]{1,0:T(8,128)(2,1)S(1)} %add_convert_fusion.1.ga), channel_id=1, source_target_pairs={{32,0},{33,1},{34,2},{35,3},{36,4},{37,5},{38,6},{39,7},{40,8},{41... | collective-permute-start | bytes 393224 | tf_op jit(solution)/shard_map/ppermute | solution.py:29
  86.7 1.3 %collective-permute-start.16 = (bf16[256,256]{1,0:T(8,128)(2,1)S(1)}, bf16[256,256]{1,0:T(8,128)(2,1)S(1)}, u32[]{:S(2)}, u32[]{:S(2)}) collective-permute-start(bf16[256,256]{1,0:T(8,128)(2,1)S(1)} %collective-permute-done.15.gc), channel_id=1, source_target_pairs={{1,0},{0,1},{3,2},{2,3},{5,4},{4,5},{7,6},{6,7},{9,8},{8,9},{11,10... | collective-permute-start | bytes 393224 | tf_op jit(solution)/shard_map/ppermute | solution.py:29
  111.3 14.5 %collective-permute-start.17 = (bf16[256,1024]{1,0:T(8,128)(2,1)S(1)}, bf16[256,1024]{1,0:T(8,128)(2,1)S(1)}, u32[]{:S(2)}, u32[]{:S(2)}) collective-permute-start(bf16[256,1024]{1,0:T(8,128)(2,1)S(1)} %get-tuple-element.72), channel_id=1, source_target_pairs={{1,0},{0,1},{3,2},{2,3},{5,4},{4,5},{7,6},{6,7},{9,8},{8,9},{11,10... | collective-permute-start | bytes 1572872 | tf_op jit(solution)/shard_map/ppermute | solution.py:29
  112.0 11.2 %collective-permute-start.18 = (bf16[32,256]{1,0:T(8,128)(2,1)S(1)}, bf16[32,256]{1,0:T(8,128)(2,1)S(1)}, u32[]{:S(2)}, u32[]{:S(2)}) collective-permute-start(bf16[32,256]{1,0:T(8,128)(2,1)S(1)} %get-tuple-element.75), channel_id=1, source_target_pairs={{192,0},{193,1},{194,2},{195,3},{196,4},{197,5},{198,6},{199,7},{2... | collective-permute-start | bytes 49160 | tf_op jit(solution)/shard_map/ppermute | solution.py:29
  115.3 7.9 %collective-permute-start.19 = (bf16[32,256]{1,0:T(8,128)(2,1)S(1)}, bf16[32,256]{1,0:T(8,128)(2,1)S(1)}, u32[]{:S(2)}, u32[]{:S(2)}) collective-permute-start(bf16[32,256]{1,0:T(8,128)(2,1)S(1)} %get-tuple-element.76), channel_id=1, source_target_pairs={{128,0},{129,1},{130,2},{131,3},{132,4},{133,5},{134,6},{135,7},{1... | collective-permute-start | bytes 49160 | tf_op jit(solution)/shard_map/ppermute | solution.py:29
  120.6 4.6 %collective-permute-start.20 = (bf16[32,256]{1,0:T(8,128)(2,1)S(1)}, bf16[32,256]{1,0:T(8,128)(2,1)S(1)}, u32[]{:S(2)}, u32[]{:S(2)}) collective-permute-start(bf16[32,256]{1,0:T(8,128)(2,1)S(1)} %get-tuple-element.77), channel_id=1, source_target_pairs={{64,0},{65,1},{66,2},{67,3},{68,4},{69,5},{70,6},{71,7},{72,8},{73... | collective-permute-start | bytes 49160 | tf_op jit(solution)/shard_map/ppermute | solution.py:29

commit v6 on v5

--- a/solution.py
+++ b/solution.py
@@ -145,7 +145,7 @@
             pl.BlockSpec((2, 2048, 256), lambda z: (0, 0, 0)),
         ),
         compiler_params=pltpu.CompilerParams(vmem_limit_bytes=12 * 2**20),
-        cost_estimate=pl.CostEstimate(flops=3 * 10**10, bytes_accessed=8 * 2**20, transcendentals=0),
+        cost_estimate=pl.CostEstimate(flops=10**7, bytes_accessed=8 * 2**20, transcendentals=0),
         name="turn",
     )(place, layer)
 
@@ -312,7 +312,7 @@
     pltpu.VMEM((NK, BLK, BLK), BF16),
     pltpu.VMEM((NK, BLK, 2 * BLK), F32),
 ]
-COST = pl.CostEstimate(flops=6 * 10**10, bytes_accessed=2**20, transcendentals=2 * 10**6)
+COST = pl.CostEstimate(flops=6 * 10**9, bytes_accessed=2**20, transcendentals=2 * 10**6)
 
 
 def first_call(meta, queries, grads, stats, blocks):
@@ -428,6 +428,7 @@
     q_other, g_other = fetch(q, swap_core), fetch(g, swap_core)
     stats = row_stats(attn_out[0], g, log_sum_exp[0])
     stats_other = fetch(stats, swap_core)
+    pair_y, q_other, g_other = lax.optimization_barrier((pair_y, q_other, g_other))
     both = jnp.concatenate([pair, pair_y], axis=0)
     blocks = [both] + [fetch(both, by_ctx(k, 0)) for k in ALONG_X[1:]]
     mine, other, away = turn(place, layer_input[0])
@@ -438,9 +439,9 @@
     def owners(row):
         return jnp.concatenate([places[(x + k) % X * 4 + row * 2 + c] for k in ALONG_X])
 
-    blocks, mine, other, away = lax.optimization_barrier((blocks, mine, other, away))
     away = fetch(away, swap_z)
     mine_core = fetch(other, swap_core)
+    blocks, mine = lax.optimization_barrier((blocks, mine))
     *carried, dkv_y = first_call(
         make_meta(owners(1 - yh), q_pos), (q, q_other), (g, g_other), (stats, stats_other), blocks
     )

time: 128 us -> 125 us (0.977)
  waiting for transfers between devices: 33.9 us -> 25 us
  local copies, waits for them, and re-layouts: 6.19 us -> 9.68 us
  blocking collectives: 21.5 us -> 23.6 us
    ppermute x21, waiting for transfers between devices: 33.9 us -> 25 us  [fetch(): return lax.ppermute(value, AXES, pairs)]
    unnamed x20 -> x26, local copies, waits for them, and re-layouts: 5.2 us -> 8.02 us
    pallas_call x1, Pallas kernels: 12.8 us -> 10.6 us  [second_call(): pl.pallas_call(second_kernel, out_shape=(jax.ShapeDtypeStruct((256, WIDE)...]
    all_to_all x1, blocking collectives: 21.5 us -> 23.6 us  [body(): terms = lax.all_to_all(terms, ('yl', 'x', 'yh'), 0, 0)]
    pallas_call x1, Pallas kernels: 6.47 us -> 8.13 us  [turn(): pl.pallas_call(turn_kernel, grid=(Z,), out_shape=(half, half, jax.ShapeDt...]
    concatenate x2, local copies, waits for them, and re-layouts: 0.16 us -> 1.47 us  [make_meta(): jnp.concatenate([order, ordered, q_pos, whole, reached]).astype(jnp.int32)]
  transfers between devices with their start and end apart: 21 -> 21, of which waited for: 9 -> 11; matrix products, arithmetic and copies ran while one was open for 3% -> 4% of each run, Pallas kernels for 25% -> 25%
where the time goes in v6:
time: 125 us; the launch traced here: 124 us
  Pallas kernels  33.5 us (27%)
  starting transfers between devices  25.5 us (20%)
  waiting for transfers between devices  25 us (20%)
  blocking collectives  23.6 us (19%)
  local copies, waits for them, and re-layouts  9.68 us (8%)
  other arithmetic  5.67 us (5%)
    ppermute x21, starting transfers between devices, fetch(): return lax.ppermute(value, AXES, pairs)  25.5 us
    ppermute x21, waiting for transfers between devices, fetch(): return lax.ppermute(value, AXES, pairs)  25 us
    all_to_all x1, blocking collectives, body(): terms = lax.all_to_all(terms, ('yl', 'x', 'yh'), 0, 0)  23.6 us
    pallas_call x1, Pallas kernels, first_call(): pl.pallas_call(first_kernel, out_shape=(rows,) * 4 + (jax.ShapeDtypeStruc...  10.6 us
    pallas_call x1, Pallas kernels, second_call(): pl.pallas_call(second_kernel, out_shape=(jax.ShapeDtypeStruct((256, WIDE)...  10.6 us
    pallas_call x1, Pallas kernels, turn(): pl.pallas_call(turn_kernel, grid=(Z,), out_shape=(half, half, jax.ShapeDt...  8.13 us
    unnamed x26, local copies, waits for them, and re-layouts  8.02 us
    pallas_call x1, Pallas kernels, project(): pl.pallas_call(project_kernel, out_shape=jax.ShapeDtypeStruct((16, HALF *...  3.03 us
  transfers between devices with their start and end apart: 21, of which 11 were waited for; matrix products, arithmetic and copies ran while one was open for 4% of the time, Pallas kernels for 25%

profile of v6, /device:TPU:4, one launch (start us, length us, event | category | flops | bytes accessed | tf_op | source)
XLA Modules:
  0.0 123.8 jit_solution(5289146070754993530)
XLA Ops:
  0.6 0.9 pad_maximum_fusion.1
  1.5 3.3 %collective-permute-start = (bf16[256,256]{1,0:T(8,128)(2,1)S(1)}, bf16[256,256]{1,0:T(8,128)(2,1)}, u32[]{:S(2)}, u32[]{:S(2)}) collective-permute-start(bf16[256,256]{1,0:T(8,128)(2,1)S(1)} %pad_maximum_fusion.1), channel_id=1, source_target_pairs={{2,0},{3,1},{0,2},{1,3},{6,4},{7,5},{4,6},{5,7},{10,8},{11,9},{8,1... | collective-permute-start | bytes 393224 | tf_op jit(solution)/shard_map/ppermute | solution.py:29
  4.8 0.5 collective-permute-start.2
  5.4 2.2 %copy-done = bf16[1,256,8192]{2,1,0:T(8,128)(2,1)S(1)} copy-done((bf16[1,256,8192]{2,1,0:T(8,128)(2,1)S(1)}, bf16[1,256,8192]{2,1,0:T(8,128)(2,1)}, u32[]{:S(2)}) %copy-start) | copy-done | bytes 4194328
  7.6 8.1 %turn.1 = (bf16[2048,256]{1,0:T(8,128)(2,1)S(1)}, bf16[2048,256]{1,0:T(8,128)(2,1)}, bf16[2,2048,256]{2,1,0:T(8,128)(2,1)}) custom-call(s32[3]{0:T(128)S(1)} %pad_add_fusion.3.place, bf16[256,8192]{1,0:T(8,128)(2,1)S(1)} %bitcast.34), custom_call_target="tpu_custom_call" | custom-call | flops 10000000 | bytes 8388608 | tf_op jit(solution)/shard_map/turn/pallas_call | solution.py:137
  15.7 1.9 %collective-permute-start.8 = (bf16[2,2048,256]{2,1,0:T(8,128)(2,1)}, bf16[2,2048,256]{2,1,0:T(8,128)(2,1)S(1)}, u32[]{:S(2)}, u32[]{:S(2)}) collective-permute-start(bf16[2,2048,256]{2,1,0:T(8,128)(2,1)} %get-tuple-element.65), channel_id=1, source_target_pairs={{32,0},{33,1},{34,2},{35,3},{36,4},{37,5},{38,6},{39,7},{40,8},{41... | collective-permute-start | bytes 6291464 | tf_op jit(solution)/shard_map/ppermute | solution.py:29
  18.0 0.7 convert_reduce_fusion.2
  18.7 0.6 and_select_fusion
  19.3 0.9 pad_maximum_fusion.refs_6_
  20.2 0.6 collective-permute-start.6
  20.9 2.2 %collective-permute-start.5 = (bf16[512,256]{1,0:T(8,128)(2,1)S(1)}, bf16[512,256]{1,0:T(8,128)(2,1)}, u32[]{:S(2)}, u32[]{:S(2)}) collective-permute-start(bf16[512,256]{1,0:T(8,128)(2,1)S(1)} %pad_maximum_fusion.refs_6_), channel_id=1, source_target_pairs={{12,0},{13,1},{14,2},{15,3},{0,4},{1,5},{2,6},{3,7},{4,8},{5,9},{6... | collective-permute-start | bytes 786440 | tf_op jit(solution)/shard_map/ppermute | solution.py:29
  23.2 0.2 convert_reduce_fusion.1
  23.4 1.0 copy-done.1
  24.4 1.0 copy-done.2
  25.4 0.5 row_stats.1.refs_4_
  25.9 0.2 convert_reduce_fusion
  26.1 4.9 %collective-permute-done.6.refs_9_ = bf16[512,256]{1,0:T(8,128)(2,1)S(1)} collective-permute-done((bf16[512,256]{1,0:T(8,128)(2,1)S(1)}, bf16[512,256]{1,0:T(8,128)(2,1)S(1)}, u32[]{:S(2)}, u32[]{:S(2)}) %collective-permute-start.6) | collective-permute-done | bytes 262176 | tf_op jit(solution)/shard_map/ppermute | solution.py:29
  31.0 0.7 copy-done.6
  31.9 0.7 concatenate.27.meta
  32.6 0.7 concatenate.25.meta
  33.4 1.9 %collective-permute-done.5.refs_8_ = bf16[512,256]{1,0:T(8,128)(2,1)} collective-permute-done((bf16[512,256]{1,0:T(8,128)(2,1)S(1)}, bf16[512,256]{1,0:T(8,128)(2,1)}, u32[]{:S(2)}, u32[]{:S(2)}) %collective-permute-start.5) | collective-permute-done | bytes 262176 | tf_op jit(solution)/shard_map/ppermute | solution.py:29
  35.2 1.0 copy-done.3
  36.3 1.0 copy-done.5
  37.3 0.9 copy-done.7
  38.3 10.6 %attention_first.1 = (bf16[4,128,1024]{2,1,0:T(8,128)(2,1)S(1)}, bf16[4,128,1024]{2,1,0:T(8,128)(2,1)S(1)}, bf16[4,128,1024]{2,1,0:T(8,128)(2,1)S(1)}, bf16[4,12...) custom-call(s32[28]{0:T(128)S(1)} %concatenate.27.meta, ...), custom_call_target="tpu_custom_call" | custom-call | flops 6000000000 | bytes 1048576 | tf_op jit(solution)/shard_map/attention_first/pallas_call | solution.py:320
  48.9 0.3 collective-permute-start.9
  49.2 10.6 %attention_second.1 = (f32[256,1024]{1,0:T(8,128)S(1)}, bf16[256,1024]{1,0:T(8,128)(2,1)S(1)}, f32[256,256]{1,0:T(8,128)S(1)}, f32[256,256]{1,0:T(8,128)S(1)}, f...) custom-call(s32[28]{0:T(128)S(1)} %concatenate.25.meta, bf16[4,128,1024]{2,1,0:T(8,128)(2,1)S(1)} %get-tuple-element.56.refs_0_, ...), custom_call_target="tpu_custom_call" | custom-call | flops 6000000000 | bytes 1048576 | tf_op jit(solution)/shard_map/attention_second/pallas_call | solution.py:339
  59.8 1.8 %collective-permute-done.9 = bf16[1024,256]{1,0:T(8,128)(2,1)S(1)} collective-permute-done((bf16[1024,256]{1,0:T(8,128)(2,1)S(1)}, bf16[1024,256]{1,0:T(8,128)(2,1)S(1)}, u32[]{:S(2)}, u32[]{:S(2)}) %collective-permute-start.9) | collective-permute-done | bytes 524320 | tf_op jit(solution)/shard_map/ppermute | solution.py:29
  61.7 3.4 %collective-permute-start.10 = (bf16[256,256]{1,0:T(8,128)(2,1)S(1)}, bf16[256,256]{1,0:T(8,128)(2,1)S(1)}, u32[]{:S(2)}, u32[]{:S(2)}) collective-permute-start(bf16[256,256]{1,0:T(8,128)(2,1)S(1)} %get-tuple-element.90), channel_id=1, source_target_pairs={{12,0},{13,1},{14,2},{15,3},{0,4},{1,5},{2,6},{3,7},{4,8},{5,9},{6... | collective-permute-start | bytes 393224 | tf_op jit(solution)/shard_map/ppermute | solution.py:29
  65.1 2.0 %collective-permute-start.12 = (bf16[256,256]{1,0:T(8,128)(2,1)S(1)}, bf16[256,256]{1,0:T(8,128)(2,1)S(1)}, u32[]{:S(2)}, u32[]{:S(2)}) collective-permute-start(bf16[256,256]{1,0:T(8,128)(2,1)S(1)} %get-tuple-element.91), channel_id=1, source_target_pairs={{8,0},{9,1},{10,2},{11,3},{12,4},{13,5},{14,6},{15,7},{0,8},{1,9},... | collective-permute-start | bytes 393224 | tf_op jit(solution)/shard_map/ppermute | solution.py:29
  67.1 2.0 %collective-permute-done.10 = bf16[256,256]{1,0:T(8,128)(2,1)S(1)} collective-permute-done((bf16[256,256]{1,0:T(8,128)(2,1)S(1)}, bf16[256,256]{1,0:T(8,128)(2,1)S(1)}, u32[]{:S(2)}, u32[]{:S(2)}) %collective-permute-start.10) | collective-permute-done | bytes 131104 | tf_op jit(solution)/shard_map/ppermute | solution.py:29
  69.2 3.5 %collective-permute-done.12 = bf16[256,256]{1,0:T(8,128)(2,1)S(1)} collective-permute-done((bf16[256,256]{1,0:T(8,128)(2,1)S(1)}, bf16[256,256]{1,0:T(8,128)(2,1)S(1)}, u32[]{:S(2)}, u32[]{:S(2)}) %collective-permute-start.12) | collective-permute-done | bytes 131104 | tf_op jit(solution)/shard_map/ppermute | solution.py:29
  72.7 0.8 collective-permute-done.11
  73.7 1.3 %collective-permute-done.13.gb = bf16[256,256]{1,0:T(8,128)(2,1)S(1)} collective-permute-done((bf16[256,256]{1,0:T(8,128)(2,1)S(1)}, bf16[256,256]{1,0:T(8,128)(2,1)S(1)}, u32[]{:S(2)}, u32[]{:S(2)}) %collective-permute-start.13) | collective-permute-done | bytes 131104 | tf_op jit(solution)/shard_map/ppermute | solution.py:29
  75.1 0.2 collective-permute-start.14
  75.3 0.3 collective-permute-start.15
  75.6 5.4 %collective-permute-done.15.gc = bf16[256,256]{1,0:T(8,128)(2,1)S(1)} collective-permute-done((bf16[256,256]{1,0:T(8,128)(2,1)S(1)}, bf16[256,256]{1,0:T(8,128)(2,1)S(1)}, u32[]{:S(2)}, u32[]{:S(2)}) %collective-permute-start.15) | collective-permute-done | bytes 131104 | tf_op jit(solution)/shard_map/ppermute | solution.py:29
  81.1 1.3 %collective-permute-done.16.gd = bf16[256,256]{1,0:T(8,128)(2,1)S(1)} collective-permute-done((bf16[256,256]{1,0:T(8,128)(2,1)S(1)}, bf16[256,256]{1,0:T(8,128)(2,1)S(1)}, u32[]{:S(2)}, u32[]{:S(2)}) %collective-permute-start.16) | collective-permute-done | bytes 131104 | tf_op jit(solution)/shard_map/ppermute | solution.py:29
  82.4 3.0 %project.1 = bf16[16,128,256]{2,1,0:T(8,128)(2,1)S(1)} custom-call(bf16[2048,256]{1,0:T(8,128)(2,1)S(1)} %get-tuple-element.63.a_ref, bf16[2048,256]{1,0:T(8,128)(2,1)} %collective-permute-done.7.b_ref, bf16[2,2048,256]{2,1,0:T(8,128)(2,1)S(1)} %collective-permute-done.8.c_ref, bf16[2048,256]{1,0:T(8,128)(2,1)S(1)} %collective-permute-done.14.d_ref, ...), custom_call_target="tpu_custom_call" | custom-call | flops 1073741824 | bytes 8388608 | tf_op jit(solution)/shard_map/project/pallas_call | solution.py:385
  85.5 23.6 %all_to_all.5.in_ref = bf16[16,128,256]{2,1,0:T(8,128)(2,1)S(1)} all-to-all(bf16[16,128,256]{2,1,0:T(8,128)(2,1)S(1)} %project.1), channel_id=1, replica_groups=mesh['z'=8,'yl'=2,'x'=4,'yh'=2,'c'=2] {'yl','x','yh'}, dimensions={0} | all-to-all | bytes 2097152 | tf_op jit(solution)/shard_map/all_to_all | solution.py:464
  109.0 0.7 sum_terms.1
  109.7 3.4 %collective-permute-start.18 = (bf16[32,256]{1,0:T(8,128)(2,1)S(1)}, bf16[32,256]{1,0:T(8,128)(2,1)S(1)}, u32[]{:S(2)}, u32[]{:S(2)}) collective-permute-start(bf16[32,256]{1,0:T(8,128)(2,1)S(1)} %get-tuple-element.77), channel_id=1, source_target_pairs={{192,0},{193,1},{194,2},{195,3},{196,4},{197,5},{198,6},{199,7},{2... | collective-permute-start | bytes 49160 | tf_op jit(solution)/shard_map/ppermute | solution.py:29
  113.1 4.5 %collective-permute-start.19 = (bf16[32,256]{1,0:T(8,128)(2,1)S(1)}, bf16[32,256]{1,0:T(8,128)(2,1)S(1)}, u32[]{:S(2)}, u32[]{:S(2)}) collective-permute-start(bf16[32,256]{1,0:T(8,128)(2,1)S(1)} %get-tuple-element.78), channel_id=1, source_target_pairs={{128,0},{129,1},{130,2},{131,3},{132,4},{133,5},{134,6},{135,7},{1... | collective-permute-start | bytes 49160 | tf_op jit(solution)/shard_map/ppermute | solution.py:29
  117.6 2.7 %collective-permute-start.20 = (bf16[32,256]{1,0:T(8,128)(2,1)S(1)}, bf16[32,256]{1,0:T(8,128)(2,1)S(1)}, u32[]{:S(2)}, u32[]{:S(2)}) collective-permute-start(bf16[32,256]{1,0:T(8,128)(2,1)S(1)} %get-tuple-element.79), channel_id=1, source_target_pairs={{64,0},{65,1},{66,2},{67,3},{68,4},{69,5},{70,6},{71,7},{72,8},{73... | collective-permute-start | bytes 49160 | tf_op jit(solution)/shard_map/ppermute | solution.py:29
  120.3 0.5 collective-permute-done.19
  120.7 1.5 %collective-permute-done.20 = bf16[32,256]{1,0:T(8,128)(2,1)S(1)} collective-permute-done((bf16[32,256]{1,0:T(8,128)(2,1)S(1)}, bf16[32,256]{1,0:T(8,128)(2,1)S(1)}, u32[]{:S(2)}, u32[]{:S(2)}) %collective-permute-start.20) | collective-permute-done | bytes 16416 | tf_op jit(solution)/shard_map/ppermute | solution.py:29
  122.2 0.6 convert_add_fusion
  122.8 1.0 fusion
  (48 shorter events, 1.1 us)
Async XLA Ops:
  1.5 17.8 %collective-permute-start = (bf16[256,256]{1,0:T(8,128)(2,1)S(1)}, bf16[256,256]{1,0:T(8,128)(2,1)}, u32[]{:S(2)}, u32[]{:S(2)}) collective-permute-start(bf16[256,256]{1,0:T(8,128)(2,1)S(1)} %pad_maximum_fusion.1), channel_id=1, source_target_pairs={{2,0},{3,1},{0,2},{1,3},{6,4},{7,5},{4,6},{5,7},{10,8},{11,9},{8,1... | collective-permute-start | bytes 393224 | tf_op jit(solution)/shard_map/ppermute | solution.py:29
  4.8 14.5 %collective-permute-start.1 = (bf16[256,1024]{1,0:T(8,128)(2,1)}, bf16[256,1024]{1,0:T(8,128)(2,1)}, u32[]{:S(2)}, u32[]{:S(2)}) collective-permute-start(bf16[256,1024]{1,0:T(8,128)(2,1)} %bitcast.40), channel_id=1, source_target_pairs={{1,0},{0,1},{3,2},{2,3},{5,4},{4,5},{7,6},{6,7},{9,8},{8,9},{11,10... | collective-permute-start | bytes 1572872 | tf_op jit(solution)/shard_map/ppermute | solution.py:29
  4.8 14.5 %collective-permute-start.2 = (bf16[256,1024]{1,0:T(8,128)(2,1)}, bf16[256,1024]{1,0:T(8,128)(2,1)}, u32[]{:S(2)}, u32[]{:S(2)}) collective-permute-start(bf16[256,1024]{1,0:T(8,128)(2,1)} %bitcast.36), channel_id=1, source_target_pairs={{1,0},{0,1},{3,2},{2,3},{5,4},{4,5},{7,6},{6,7},{9,8},{8,9},{11,10... | collective-permute-start | bytes 1572872 | tf_op jit(solution)/shard_map/ppermute | solution.py:29
  5.4 2.2 %copy-start = (bf16[1,256,8192]{2,1,0:T(8,128)(2,1)S(1)}, bf16[1,256,8192]{2,1,0:T(8,128)(2,1)}, u32[]{:S(2)}) copy-start(bf16[1,256,8192]{2,1,0:T(8,128)(2,1)} %param.8) | copy-start | bytes 12582916
  7.6 10.1 %copy-start.12 = (s32[32]{0:T(128)S(1)}, s32[32]{0:T(128)}, u32[]{:S(2)}) copy-start(s32[32]{0:T(128)} %param.15) | copy-start | bytes 388
  7.6 11.7 %copy-start.9 = (bf16[1,256,128]{2,1,0:T(8,128)(2,1)S(1)}, bf16[1,256,128]{2,1,0:T(8,128)(2,1)}, u32[]{:S(2)}) copy-start(bf16[1,256,128]{2,1,0:T(8,128)(2,1)} %param.11) | copy-start | bytes 196612
  7.6 11.7 %copy-start.10 = (bf16[1,256,128]{2,1,0:T(8,128)(2,1)S(1)}, bf16[1,256,128]{2,1,0:T(8,128)(2,1)}, u32[]{:S(2)}) copy-start(bf16[1,256,128]{2,1,0:T(8,128)(2,1)} %param.10) | copy-start | bytes 196612
  7.6 15.8 %copy-start.4 = (f32[1,8,256]{2,1,0:T(8,128)S(1)}, f32[1,8,256]{2,1,0:T(8,128)}, u32[]{:S(2)}) copy-start(f32[1,8,256]{2,1,0:T(8,128)} %param.14) | copy-start | bytes 24580
  15.7 33.5 %collective-permute-start.7 = (bf16[2048,256]{1,0:T(8,128)(2,1)}, bf16[2048,256]{1,0:T(8,128)(2,1)}, u32[]{:S(2)}, u32[]{:S(2)}) collective-permute-start(bf16[2048,256]{1,0:T(8,128)(2,1)} %get-tuple-element.55), channel_id=1, source_target_pairs={{1,0},{0,1},{3,2},{2,3},{5,4},{4,5},{7,6},{6,7},{9,8},{8,9},{11,10... | collective-permute-start | bytes 3145736 | tf_op jit(solution)/shard_map/ppermute | solution.py:29
  15.7 59.3 %collective-permute-start.8 = (bf16[2,2048,256]{2,1,0:T(8,128)(2,1)}, bf16[2,2048,256]{2,1,0:T(8,128)(2,1)S(1)}, u32[]{:S(2)}, u32[]{:S(2)}) collective-permute-start(bf16[2,2048,256]{2,1,0:T(8,128)(2,1)} %get-tuple-element.65), channel_id=1, source_target_pairs={{32,0},{33,1},{34,2},{35,3},{36,4},{37,5},{38,6},{39,7},{40,8},{41... | collective-permute-start | bytes 6291464 | tf_op jit(solution)/shard_map/ppermute | solution.py:29
  17.8 1.5 %copy-start.11 = (s32[2]{0:T(128)}, s32[2]{0:T(128)S(1)}, u32[]{:S(2)}) copy-start(s32[2]{0:T(128)S(1)} %get-tuple-element.98) | copy-start | bytes 28
  20.2 10.8 %collective-permute-start.6 = (bf16[512,256]{1,0:T(8,128)(2,1)S(1)}, bf16[512,256]{1,0:T(8,128)(2,1)S(1)}, u32[]{:S(2)}, u32[]{:S(2)}) collective-permute-start(bf16[512,256]{1,0:T(8,128)(2,1)S(1)} %pad_maximum_fusion.refs_6_), channel_id=1, source_target_pairs={{8,0},{9,1},{10,2},{11,3},{12,4},{13,5},{14,6},{15,7},{0,8},{1,9},... | collective-permute-start | bytes 786440 | tf_op jit(solution)/shard_map/ppermute | solution.py:29
  20.9 14.4 %collective-permute-start.5 = (bf16[512,256]{1,0:T(8,128)(2,1)S(1)}, bf16[512,256]{1,0:T(8,128)(2,1)}, u32[]{:S(2)}, u32[]{:S(2)}) collective-permute-start(bf16[512,256]{1,0:T(8,128)(2,1)S(1)} %pad_maximum_fusion.refs_6_), channel_id=1, source_target_pairs={{12,0},{13,1},{14,2},{15,3},{0,4},{1,5},{2,6},{3,7},{4,8},{5,9},{6... | collective-permute-start | bytes 786440 | tf_op jit(solution)/shard_map/ppermute | solution.py:29
  23.0 12.2 %collective-permute-start.4 = (bf16[512,256]{1,0:T(8,128)(2,1)S(1)}, bf16[512,256]{1,0:T(8,128)(2,1)}, u32[]{:S(2)}, u32[]{:S(2)}) collective-permute-start(bf16[512,256]{1,0:T(8,128)(2,1)S(1)} %pad_maximum_fusion.refs_6_), channel_id=1, source_target_pairs={{4,0},{5,1},{6,2},{7,3},{8,4},{9,5},{10,6},{11,7},{12,8},{13,9},{1... | collective-permute-start | bytes 786440 | tf_op jit(solution)/shard_map/ppermute | solution.py:29
  23.4 1.0 copy-start.1
  24.4 1.0 copy-start.2
  31.0 0.7 copy-start.6
  31.7 3.5 %collective-permute-start.3 = (f32[8,1024]{1,0:T(8,128)S(1)}, f32[8,1024]{1,0:T(8,128)S(1)}, u32[]{:S(2)}, u32[]{:S(2)}) collective-permute-start(f32[8,1024]{1,0:T(8,128)S(1)} %row_stats.1.refs_4_), channel_id=1, source_target_pairs={{1,0},{0,1},{3,2},{2,3},{5,4},{4,5},{7,6},{6,7},{9,8},{8,9},{11,10... | collective-permute-start | bytes 98312 | tf_op jit(solution)/shard_map/ppermute | solution.py:29
  35.2 1.0 copy-start.3
  36.3 1.0 copy-start.5
  37.3 0.9 copy-start.7
  38.3 10.9 %copy-start.8 = (bf16[512,256]{1,0:T(8,128)(2,1)S(1)}, bf16[512,256]{1,0:T(8,128)(2,1)}, u32[]{:S(2)}) copy-start(bf16[512,256]{1,0:T(8,128)(2,1)} %copy-done.6) | copy-start | bytes 786436
  48.9 12.7 %collective-permute-start.9 = (bf16[1024,256]{1,0:T(8,128)(2,1)S(1)}, bf16[1024,256]{1,0:T(8,128)(2,1)S(1)}, u32[]{:S(2)}, u32[]{:S(2)}) collective-permute-start(bf16[1024,256]{1,0:T(8,128)(2,1)S(1)} %get-tuple-element.67), channel_id=1, source_target_pairs={{2,0},{3,1},{0,2},{1,3},{6,4},{7,5},{4,6},{5,7},{10,8},{11,9},{8,1... | collective-permute-start | bytes 1572872 | tf_op jit(solution)/shard_map/ppermute | solution.py:29
  61.7 7.4 %collective-permute-start.10 = (bf16[256,256]{1,0:T(8,128)(2,1)S(1)}, bf16[256,256]{1,0:T(8,128)(2,1)S(1)}, u32[]{:S(2)}, u32[]{:S(2)}) collective-permute-start(bf16[256,256]{1,0:T(8,128)(2,1)S(1)} %get-tuple-element.90), channel_id=1, source_target_pairs={{12,0},{13,1},{14,2},{15,3},{0,4},{1,5},{2,6},{3,7},{4,8},{5,9},{6... | collective-permute-start | bytes 393224 | tf_op jit(solution)/shard_map/ppermute | solution.py:29
  65.1 7.6 %collective-permute-start.12 = (bf16[256,256]{1,0:T(8,128)(2,1)S(1)}, bf16[256,256]{1,0:T(8,128)(2,1)S(1)}, u32[]{:S(2)}, u32[]{:S(2)}) collective-permute-start(bf16[256,256]{1,0:T(8,128)(2,1)S(1)} %get-tuple-element.91), channel_id=1, source_target_pairs={{8,0},{9,1},{10,2},{11,3},{12,4},{13,5},{14,6},{15,7},{0,8},{1,9},... | collective-permute-start | bytes 393224 | tf_op jit(solution)/shard_map/ppermute | solution.py:29
  67.1 6.3 %collective-permute-start.11 = (bf16[256,256]{1,0:T(8,128)(2,1)S(1)}, bf16[256,256]{1,0:T(8,128)(2,1)S(1)}, u32[]{:S(2)}, u32[]{:S(2)}) collective-permute-start(bf16[256,256]{1,0:T(8,128)(2,1)S(1)} %get-tuple-element.92), channel_id=1, source_target_pairs={{4,0},{5,1},{6,2},{7,3},{8,4},{9,5},{10,6},{11,7},{12,8},{13,9},{1... | collective-permute-start | bytes 393224 | tf_op jit(solution)/shard_map/ppermute | solution.py:29
  73.6 1.4 %collective-permute-start.13 = (bf16[256,256]{1,0:T(8,128)(2,1)S(1)}, bf16[256,256]{1,0:T(8,128)(2,1)S(1)}, u32[]{:S(2)}, u32[]{:S(2)}) collective-permute-start(bf16[256,256]{1,0:T(8,128)(2,1)S(1)} %add_convert_fusion.1.ga), channel_id=1, source_target_pairs={{1,0},{0,1},{3,2},{2,3},{5,4},{4,5},{7,6},{6,7},{9,8},{8,9},{11,10... | collective-permute-start | bytes 393224 | tf_op jit(solution)/shard_map/ppermute | solution.py:29
  75.1 7.4 %collective-permute-start.14 = (bf16[2048,256]{1,0:T(8,128)(2,1)S(1)}, bf16[2048,256]{1,0:T(8,128)(2,1)S(1)}, u32[]{:S(2)}, u32[]{:S(2)}) collective-permute-start(bf16[2048,256]{1,0:T(8,128)(2,1)S(1)} %slice_bitcast_fusion), channel_id=1, source_target_pairs={{1,0},{0,1},{3,2},{2,3},{5,4},{4,5},{7,6},{6,7},{9,8},{8,9},{11,10... | collective-permute-start | bytes 3145736 | tf_op jit(solution)/shard_map/ppermute | solution.py:29
  75.3 5.8 %collective-permute-start.15 = (bf16[256,256]{1,0:T(8,128)(2,1)S(1)}, bf16[256,256]{1,0:T(8,128)(2,1)S(1)}, u32[]{:S(2)}, u32[]{:S(2)}) collective-permute-start(bf16[256,256]{1,0:T(8,128)(2,1)S(1)} %add_convert_fusion.1.ga), channel_id=1, source_target_pairs={{32,0},{33,1},{34,2},{35,3},{36,4},{37,5},{38,6},{39,7},{40,8},{41... | collective-permute-start | bytes 393224 | tf_op jit(solution)/shard_map/ppermute | solution.py:29
  81.1 1.3 %collective-permute-start.16 = (bf16[256,256]{1,0:T(8,128)(2,1)S(1)}, bf16[256,256]{1,0:T(8,128)(2,1)S(1)}, u32[]{:S(2)}, u32[]{:S(2)}) collective-permute-start(bf16[256,256]{1,0:T(8,128)(2,1)S(1)} %collective-permute-done.15.gc), channel_id=1, source_target_pairs={{1,0},{0,1},{3,2},{2,3},{5,4},{4,5},{7,6},{6,7},{9,8},{8,9},{11,10... | collective-permute-start | bytes 393224 | tf_op jit(solution)/shard_map/ppermute | solution.py:29
  109.0 13.8 %collective-permute-start.17 = (bf16[256,1024]{1,0:T(8,128)(2,1)S(1)}, bf16[256,1024]{1,0:T(8,128)(2,1)S(1)}, u32[]{:S(2)}, u32[]{:S(2)}) collective-permute-start(bf16[256,1024]{1,0:T(8,128)(2,1)S(1)} %get-tuple-element.74), channel_id=1, source_target_pairs={{1,0},{0,1},{3,2},{2,3},{5,4},{4,5},{7,6},{6,7},{9,8},{8,9},{11,10... | collective-permute-start | bytes 1572872 | tf_op jit(solution)/shard_map/ppermute | solution.py:29
  109.7 10.5 %collective-permute-start.18 = (bf16[32,256]{1,0:T(8,128)(2,1)S(1)}, bf16[32,256]{1,0:T(8,128)(2,1)S(1)}, u32[]{:S(2)}, u32[]{:S(2)}) collective-permute-start(bf16[32,256]{1,0:T(8,128)(2,1)S(1)} %get-tuple-element.77), channel_id=1, source_target_pairs={{192,0},{193,1},{194,2},{195,3},{196,4},{197,5},{198,6},{199,7},{2... | collective-permute-start | bytes 49160 | tf_op jit(solution)/shard_map/ppermute | solution.py:29
  113.1 7.6 %collective-permute-start.19 = (bf16[32,256]{1,0:T(8,128)(2,1)S(1)}, bf16[32,256]{1,0:T(8,128)(2,1)S(1)}, u32[]{:S(2)}, u32[]{:S(2)}) collective-permute-start(bf16[32,256]{1,0:T(8,128)(2,1)S(1)} %get-tuple-element.78), channel_id=1, source_target_pairs={{128,0},{129,1},{130,2},{131,3},{132,4},{133,5},{134,6},{135,7},{1... | collective-permute-start | bytes 49160 | tf_op jit(solution)/shard_map/ppermute | solution.py:29
  117.6 4.6 %collective-permute-start.20 = (bf16[32,256]{1,0:T(8,128)(2,1)S(1)}, bf16[32,256]{1,0:T(8,128)(2,1)S(1)}, u32[]{:S(2)}, u32[]{:S(2)}) collective-permute-start(bf16[32,256]{1,0:T(8,128)(2,1)S(1)} %get-tuple-element.79), channel_id=1, source_target_pairs={{64,0},{65,1},{66,2},{67,3},{68,4},{69,5},{70,6},{71,7},{72,8},{73... | collective-permute-start | bytes 49160 | tf_op jit(solution)/shard_map/ppermute | solution.py:29

commit v7 on v6

--- a/solution.py
+++ b/solution.py
@@ -145,7 +145,7 @@
             pl.BlockSpec((2, 2048, 256), lambda z: (0, 0, 0)),
         ),
         compiler_params=pltpu.CompilerParams(vmem_limit_bytes=12 * 2**20),
-        cost_estimate=pl.CostEstimate(flops=10**7, bytes_accessed=8 * 2**20, transcendentals=0),
+        cost_estimate=pl.CostEstimate(flops=10**9, bytes_accessed=8 * 2**20, transcendentals=0),
         name="turn",
     )(place, layer)
 
@@ -312,7 +312,7 @@
     pltpu.VMEM((NK, BLK, BLK), BF16),
     pltpu.VMEM((NK, BLK, 2 * BLK), F32),
 ]
-COST = pl.CostEstimate(flops=6 * 10**9, bytes_accessed=2**20, transcendentals=2 * 10**6)
+COST = pl.CostEstimate(flops=10**10, bytes_accessed=2**20, transcendentals=2 * 10**6)
 
 
 def first_call(meta, queries, grads, stats, blocks):
@@ -428,7 +428,6 @@
     q_other, g_other = fetch(q, swap_core), fetch(g, swap_core)
     stats = row_stats(attn_out[0], g, log_sum_exp[0])
     stats_other = fetch(stats, swap_core)
-    pair_y, q_other, g_other = lax.optimization_barrier((pair_y, q_other, g_other))
     both = jnp.concatenate([pair, pair_y], axis=0)
     blocks = [both] + [fetch(both, by_ctx(k, 0)) for k in ALONG_X[1:]]
     mine, other, away = turn(place, layer_input[0])
@@ -456,8 +455,8 @@
         total = total + part.astype(F32)
     grads = total.astype(BF16)
     grads_z = fetch(grads, swap_z)
-    away, grads_core = lax.optimization_barrier((away, fetch(grads, swap_core)))
-    grads_zc = fetch(grads_z, swap_core)
+    grads_core = fetch(grads, swap_core)
+    away, grads_zc = lax.optimization_barrier((away, fetch(grads_z, swap_core)))
     mine_zc = fetch(away[1], swap_core)
 
     terms = project((mine, mine_core, away, mine_zc), (grads, grads_core, grads_z, grads_zc))

time: 125 us -> 124 us (level)
  starting transfers between devices: 25.5 us -> 32.2 us
  Pallas kernels: 33.5 us -> 28.8 us
  local copies, waits for them, and re-layouts: 9.68 us -> 7.85 us
    ppermute x21, starting transfers between devices: 25.5 us -> 32.2 us  [fetch(): return lax.ppermute(value, AXES, pairs)]
    pallas_call x1, Pallas kernels: 10.6 us -> 8.62 us  [second_call(): pl.pallas_call(second_kernel, out_shape=(jax.ShapeDtypeStruct((256, WIDE)...]
    concatenate x2, local copies, waits for them, and re-layouts: 1.47 us -> 0.16 us  [make_meta(): jnp.concatenate([order, ordered, q_pos, whole, reached]).astype(jnp.int32)]
    unnamed x26 -> x20, local copies, waits for them, and re-layouts: 8.02 us -> 6.85 us
  transfers between devices with their start and end apart: 21 -> 21, of which waited for: 11 -> 9; matrix products, arithmetic and copies ran while one was open for 4% -> 3% of each run, Pallas kernels for 25% -> 22%
where the time goes in v7:
time: 124 us; the launch traced here: 123 us
  starting transfers between devices  32.2 us (26%)
  Pallas kernels  28.8 us (23%)
  waiting for transfers between devices  25.5 us (21%)
  blocking collectives  23.1 us (19%)
  local copies, waits for them, and re-layouts  7.85 us (6%)
  other arithmetic  4.57 us (4%)
    ppermute x21, starting transfers between devices, fetch(): return lax.ppermute(value, AXES, pairs)  32.2 us
    ppermute x21, waiting for transfers between devices, fetch(): return lax.ppermute(value, AXES, pairs)  25.5 us
    all_to_all x1, blocking collectives, body(): terms = lax.all_to_all(terms, ('yl', 'x', 'yh'), 0, 0)  23.1 us
    pallas_call x1, Pallas kernels, first_call(): pl.pallas_call(first_kernel, out_shape=(rows,) * 4 + (jax.ShapeDtypeStruc...  9.75 us
    pallas_call x1, Pallas kernels, second_call(): pl.pallas_call(second_kernel, out_shape=(jax.ShapeDtypeStruct((256, WIDE)...  8.62 us
    pallas_call x1, Pallas kernels, turn(): pl.pallas_call(turn_kernel, grid=(Z,), out_shape=(half, half, jax.ShapeDt...  7.45 us
    unnamed x20, local copies, waits for them, and re-layouts  6.85 us
  transfers between devices with their start and end apart: 21, of which 9 were waited for; matrix products, arithmetic and copies ran while one was open for 3% of the time, Pallas kernels for 22%

profile of v7, /device:TPU:4, one launch (start us, length us, event | category | flops | bytes accessed | tf_op | source)
XLA Modules:
  0.0 122.7 jit_solution(14499825989177408073)
XLA Ops:
  0.6 0.9 pad_maximum_fusion.1
  1.5 3.3 %collective-permute-start.3 = (bf16[256,256]{1,0:T(8,128)(2,1)S(1)}, bf16[256,256]{1,0:T(8,128)(2,1)S(1)}, u32[]{:S(2)}, u32[]{:S(2)}) collective-permute-start(bf16[256,256]{1,0:T(8,128)(2,1)S(1)} %pad_maximum_fusion.1), channel_id=1, source_target_pairs={{2,0},{3,1},{0,2},{1,3},{6,4},{7,5},{4,6},{5,7},{10,8},{11,9},{8,1... | collective-permute-start | bytes 393224 | tf_op jit(solution)/shard_map/ppermute | solution.py:29
  4.8 0.5 collective-permute-start.1
  5.3 0.7 reshape.14
  6.3 0.2 convert_reduce_fusion.2
  6.6 0.2 convert_reduce_fusion.1
  6.8 1.6 %collective-permute-done.3 = bf16[256,256]{1,0:T(8,128)(2,1)S(1)} collective-permute-done((bf16[256,256]{1,0:T(8,128)(2,1)S(1)}, bf16[256,256]{1,0:T(8,128)(2,1)S(1)}, u32[]{:S(2)}, u32[]{:S(2)}) %collective-permute-start.3) | collective-permute-done | bytes 131104 | tf_op jit(solution)/shard_map/ppermute | solution.py:29
  8.3 0.9 pad_maximum_fusion.refs_6_
  9.2 2.1 %collective-permute-start.6 = (bf16[512,256]{1,0:T(8,128)(2,1)S(1)}, bf16[512,256]{1,0:T(8,128)(2,1)S(1)}, u32[]{:S(2)}, u32[]{:S(2)}) collective-permute-start(bf16[512,256]{1,0:T(8,128)(2,1)S(1)} %pad_maximum_fusion.refs_6_), channel_id=1, source_target_pairs={{8,0},{9,1},{10,2},{11,3},{12,4},{13,5},{14,6},{15,7},{0,8},{1,9},... | collective-permute-start | bytes 786440 | tf_op jit(solution)/shard_map/ppermute | solution.py:29
  11.3 0.6 collective-permute-start.5
  12.0 1.4 %collective-permute-start.4 = (bf16[512,256]{1,0:T(8,128)(2,1)S(1)}, bf16[512,256]{1,0:T(8,128)(2,1)}, u32[]{:S(2)}, u32[]{:S(2)}) collective-permute-start(bf16[512,256]{1,0:T(8,128)(2,1)S(1)} %pad_maximum_fusion.refs_6_), channel_id=1, source_target_pairs={{4,0},{5,1},{6,2},{7,3},{8,4},{9,5},{10,6},{11,7},{12,8},{13,9},{1... | collective-permute-start | bytes 786440 | tf_op jit(solution)/shard_map/ppermute | solution.py:29
  13.4 2.2 %copy-done = bf16[1,256,8192]{2,1,0:T(8,128)(2,1)S(1)} copy-done((bf16[1,256,8192]{2,1,0:T(8,128)(2,1)S(1)}, bf16[1,256,8192]{2,1,0:T(8,128)(2,1)}, u32[]{:S(2)}) %copy-start) | copy-done | bytes 4194328
  15.6 7.5 %turn.1 = (bf16[2048,256]{1,0:T(8,128)(2,1)S(1)}, bf16[2048,256]{1,0:T(8,128)(2,1)}, bf16[2,2048,256]{2,1,0:T(8,128)(2,1)S(1)}) custom-call(s32[3]{0:T(128)S(1)} %pad_add_fusion.3.place, bf16[256,8192]{1,0:T(8,128)(2,1)S(1)} %bitcast.34), custom_call_target="tpu_custom_call" | custom-call | flops 1000000000 | bytes 8388608 | tf_op jit(solution)/shard_map/turn/pallas_call | solution.py:137
  23.1 1.3 %copy-done.4 = bf16[2,2048,256]{2,1,0:T(8,128)(2,1)} copy-done((bf16[2,2048,256]{2,1,0:T(8,128)(2,1)}, bf16[2,2048,256]{2,1,0:T(8,128)(2,1)S(1)}, u32[]{:S(2)}) %copy-start.4) | copy-done | bytes 2097176
  24.4 0.5 row_stats.1.refs_4_
  24.9 0.2 convert_reduce_fusion
  25.1 0.7 copy-done.6
  25.8 0.7 copy-done.8
  26.5 0.5 collective-permute-start.7
  27.0 0.1 select_reduce_fusion
  27.3 0.6 collective-permute-start.8
  28.0 0.9 copy-done.7
  29.0 0.9 copy-done.9
  29.9 9.8 %attention_first.1 = (bf16[4,128,1024]{2,1,0:T(8,128)(2,1)S(1)}, bf16[4,128,1024]{2,1,0:T(8,128)(2,1)S(1)}, bf16[4,128,1024]{2,1,0:T(8,128)(2,1)S(1)}, bf16[4,12...) custom-call(s32[28]{0:T(128)S(1)} %concatenate.27.meta, ...), custom_call_target="tpu_custom_call" | custom-call | flops 10000000000 | bytes 1048576 | tf_op jit(solution)/shard_map/attention_first/pallas_call | solution.py:320
  39.7 3.8 %collective-permute-start.9 = (bf16[1024,256]{1,0:T(8,128)(2,1)S(1)}, bf16[1024,256]{1,0:T(8,128)(2,1)S(1)}, u32[]{:S(2)}, u32[]{:S(2)}) collective-permute-start(bf16[1024,256]{1,0:T(8,128)(2,1)S(1)} %get-tuple-element.61), channel_id=1, source_target_pairs={{2,0},{3,1},{0,2},{1,3},{6,4},{7,5},{4,6},{5,7},{10,8},{11,9},{8,1... | collective-permute-start | bytes 1572872 | tf_op jit(solution)/shard_map/ppermute | solution.py:29
  43.5 8.6 %attention_second.1 = (f32[256,1024]{1,0:T(8,128)S(1)}, bf16[256,1024]{1,0:T(8,128)(2,1)S(1)}, f32[256,256]{1,0:T(8,128)S(1)}, f32[256,256]{1,0:T(8,128)S(1)}, f...) custom-call(s32[28]{0:T(128)S(1)} %concatenate.25.meta, bf16[4,128,1024]{2,1,0:T(8,128)(2,1)S(1)} %get-tuple-element.50.refs_0_, ...), custom_call_target="tpu_custom_call" | custom-call | flops 10000000000 | bytes 1048576 | tf_op jit(solution)/shard_map/attention_second/pallas_call | solution.py:339
  52.1 3.2 %collective-permute-done.9 = bf16[1024,256]{1,0:T(8,128)(2,1)S(1)} collective-permute-done((bf16[1024,256]{1,0:T(8,128)(2,1)S(1)}, bf16[1024,256]{1,0:T(8,128)(2,1)S(1)}, u32[]{:S(2)}, u32[]{:S(2)}) %collective-permute-start.9) | collective-permute-done | bytes 524320 | tf_op jit(solution)/shard_map/ppermute | solution.py:29
  55.4 3.6 %collective-permute-start.10 = (bf16[256,256]{1,0:T(8,128)(2,1)S(1)}, bf16[256,256]{1,0:T(8,128)(2,1)S(1)}, u32[]{:S(2)}, u32[]{:S(2)}) collective-permute-start(bf16[256,256]{1,0:T(8,128)(2,1)S(1)} %get-tuple-element.84), channel_id=1, source_target_pairs={{12,0},{13,1},{14,2},{15,3},{0,4},{1,5},{2,6},{3,7},{4,8},{5,9},{6... | collective-permute-start | bytes 393224 | tf_op jit(solution)/shard_map/ppermute | solution.py:29
  58.9 0.8 collective-permute-start.12
  59.7 2.5 %collective-permute-start.11 = (bf16[256,256]{1,0:T(8,128)(2,1)S(1)}, bf16[256,256]{1,0:T(8,128)(2,1)S(1)}, u32[]{:S(2)}, u32[]{:S(2)}) collective-permute-start(bf16[256,256]{1,0:T(8,128)(2,1)S(1)} %get-tuple-element.86), channel_id=1, source_target_pairs={{4,0},{5,1},{6,2},{7,3},{8,4},{9,5},{10,6},{11,7},{12,8},{13,9},{1... | collective-permute-start | bytes 393224 | tf_op jit(solution)/shard_map/ppermute | solution.py:29
  62.2 0.5 collective-permute-done.10
  62.8 2.7 %collective-permute-done.12 = bf16[256,256]{1,0:T(8,128)(2,1)S(1)} collective-permute-done((bf16[256,256]{1,0:T(8,128)(2,1)S(1)}, bf16[256,256]{1,0:T(8,128)(2,1)S(1)}, u32[]{:S(2)}, u32[]{:S(2)}) %collective-permute-start.12) | collective-permute-done | bytes 131104 | tf_op jit(solution)/shard_map/ppermute | solution.py:29
  65.4 0.4 collective-permute-done.11
  65.9 0.6 collective-permute-start.13
  66.5 11.4 %collective-permute-done.13.gc = bf16[256,256]{1,0:T(8,128)(2,1)S(1)} collective-permute-done((bf16[256,256]{1,0:T(8,128)(2,1)S(1)}, bf16[256,256]{1,0:T(8,128)(2,1)S(1)}, u32[]{:S(2)}, u32[]{:S(2)}) %collective-permute-start.13) | collective-permute-done | bytes 131104 | tf_op jit(solution)/shard_map/ppermute | solution.py:29
  78.0 1.3 %collective-permute-done.14.gd = bf16[256,256]{1,0:T(8,128)(2,1)S(1)} collective-permute-done((bf16[256,256]{1,0:T(8,128)(2,1)S(1)}, bf16[256,256]{1,0:T(8,128)(2,1)S(1)}, u32[]{:S(2)}, u32[]{:S(2)}) %collective-permute-start.14) | collective-permute-done | bytes 131104 | tf_op jit(solution)/shard_map/ppermute | solution.py:29
  79.4 0.2 collective-permute-start.15
  79.6 0.4 collective-permute-start.16
  80.0 2.3 %collective-permute-done.16.gb = bf16[256,256]{1,0:T(8,128)(2,1)S(1)} collective-permute-done((bf16[256,256]{1,0:T(8,128)(2,1)S(1)}, bf16[256,256]{1,0:T(8,128)(2,1)S(1)}, u32[]{:S(2)}, u32[]{:S(2)}) %collective-permute-start.16) | collective-permute-done | bytes 131104 | tf_op jit(solution)/shard_map/ppermute | solution.py:29
  82.3 1.8 %project.1 = bf16[16,128,256]{2,1,0:T(8,128)(2,1)S(1)} custom-call(bf16[2048,256]{1,0:T(8,128)(2,1)S(1)} %get-tuple-element.57.a_ref, bf16[2048,256]{1,0:T(8,128)(2,1)S(1)} %collective-permute-done.7.b_ref, bf16[2,2048,256]{2,1,0:T(8,128)(2,1)S(1)} %collective-permute-done.8.c_ref, bf16[2048,256]{1,0:T(8,128)(2,1)S(1)} %collective-permute-done.15.d_ref, ...), custom_call_target="tpu_custom_call" | custom-call | flops 1073741824 | bytes 8388608 | tf_op jit(solution)/shard_map/project/pallas_call | solution.py:385
  84.1 23.1 %all_to_all.5.in_ref = bf16[16,128,256]{2,1,0:T(8,128)(2,1)S(1)} all-to-all(bf16[16,128,256]{2,1,0:T(8,128)(2,1)S(1)} %project.1), channel_id=1, replica_groups=mesh['z'=8,'yl'=2,'x'=4,'yh'=2,'c'=2] {'yl','x','yh'}, dimensions={0} | all-to-all | bytes 2097152 | tf_op jit(solution)/shard_map/all_to_all | solution.py:463
  107.2 0.7 sum_terms.1
  107.9 3.4 %collective-permute-start.18 = (bf16[32,256]{1,0:T(8,128)(2,1)S(1)}, bf16[32,256]{1,0:T(8,128)(2,1)S(1)}, u32[]{:S(2)}, u32[]{:S(2)}) collective-permute-start(bf16[32,256]{1,0:T(8,128)(2,1)S(1)} %get-tuple-element.71), channel_id=1, source_target_pairs={{192,0},{193,1},{194,2},{195,3},{196,4},{197,5},{198,6},{199,7},{2... | collective-permute-start | bytes 49160 | tf_op jit(solution)/shard_map/ppermute | solution.py:29
  111.3 5.2 %collective-permute-start.19 = (bf16[32,256]{1,0:T(8,128)(2,1)S(1)}, bf16[32,256]{1,0:T(8,128)(2,1)S(1)}, u32[]{:S(2)}, u32[]{:S(2)}) collective-permute-start(bf16[32,256]{1,0:T(8,128)(2,1)S(1)} %get-tuple-element.72), channel_id=1, source_target_pairs={{128,0},{129,1},{130,2},{131,3},{132,4},{133,5},{134,6},{135,7},{1... | collective-permute-start | bytes 49160 | tf_op jit(solution)/shard_map/ppermute | solution.py:29
  116.5 2.6 %collective-permute-start.20 = (bf16[32,256]{1,0:T(8,128)(2,1)S(1)}, bf16[32,256]{1,0:T(8,128)(2,1)S(1)}, u32[]{:S(2)}, u32[]{:S(2)}) collective-permute-start(bf16[32,256]{1,0:T(8,128)(2,1)S(1)} %get-tuple-element.73), channel_id=1, source_target_pairs={{64,0},{65,1},{66,2},{67,3},{68,4},{69,5},{70,6},{71,7},{72,8},{73... | collective-permute-start | bytes 49160 | tf_op jit(solution)/shard_map/ppermute | solution.py:29
  119.2 2.0 %collective-permute-done.20 = bf16[32,256]{1,0:T(8,128)(2,1)S(1)} collective-permute-done((bf16[32,256]{1,0:T(8,128)(2,1)S(1)}, bf16[32,256]{1,0:T(8,128)(2,1)S(1)}, u32[]{:S(2)}, u32[]{:S(2)}) %collective-permute-start.20) | collective-permute-done | bytes 16416 | tf_op jit(solution)/shard_map/ppermute | solution.py:29
  121.2 0.6 convert_add_fusion
  121.8 0.9 fusion
  (42 shorter events, 0.8 us)
Async XLA Ops:
  1.5 6.8 %collective-permute-start.3 = (bf16[256,256]{1,0:T(8,128)(2,1)S(1)}, bf16[256,256]{1,0:T(8,128)(2,1)S(1)}, u32[]{:S(2)}, u32[]{:S(2)}) collective-permute-start(bf16[256,256]{1,0:T(8,128)(2,1)S(1)} %pad_maximum_fusion.1), channel_id=1, source_target_pairs={{2,0},{3,1},{0,2},{1,3},{6,4},{7,5},{4,6},{5,7},{10,8},{11,9},{8,1... | collective-permute-start | bytes 393224 | tf_op jit(solution)/shard_map/ppermute | solution.py:29
  4.8 23.2 %collective-permute-start = (bf16[256,1024]{1,0:T(8,128)(2,1)}, bf16[256,1024]{1,0:T(8,128)(2,1)}, u32[]{:S(2)}, u32[]{:S(2)}) collective-permute-start(bf16[256,1024]{1,0:T(8,128)(2,1)} %bitcast.40), channel_id=1, source_target_pairs={{1,0},{0,1},{3,2},{2,3},{5,4},{4,5},{7,6},{6,7},{9,8},{8,9},{11,10... | collective-permute-start | bytes 1572872 | tf_op jit(solution)/shard_map/ppermute | solution.py:29
  4.8 23.2 %collective-permute-start.1 = (bf16[256,1024]{1,0:T(8,128)(2,1)}, bf16[256,1024]{1,0:T(8,128)(2,1)}, u32[]{:S(2)}, u32[]{:S(2)}) collective-permute-start(bf16[256,1024]{1,0:T(8,128)(2,1)} %bitcast.36), channel_id=1, source_target_pairs={{1,0},{0,1},{3,2},{2,3},{5,4},{4,5},{7,6},{6,7},{9,8},{8,9},{11,10... | collective-permute-start | bytes 1572872 | tf_op jit(solution)/shard_map/ppermute | solution.py:29
  9.2 15.8 %collective-permute-start.6 = (bf16[512,256]{1,0:T(8,128)(2,1)S(1)}, bf16[512,256]{1,0:T(8,128)(2,1)S(1)}, u32[]{:S(2)}, u32[]{:S(2)}) collective-permute-start(bf16[512,256]{1,0:T(8,128)(2,1)S(1)} %pad_maximum_fusion.refs_6_), channel_id=1, source_target_pairs={{8,0},{9,1},{10,2},{11,3},{12,4},{13,5},{14,6},{15,7},{0,8},{1,9},... | collective-permute-start | bytes 786440 | tf_op jit(solution)/shard_map/ppermute | solution.py:29
  11.3 14.5 %collective-permute-start.5 = (bf16[512,256]{1,0:T(8,128)(2,1)S(1)}, bf16[512,256]{1,0:T(8,128)(2,1)S(1)}, u32[]{:S(2)}, u32[]{:S(2)}) collective-permute-start(bf16[512,256]{1,0:T(8,128)(2,1)S(1)} %pad_maximum_fusion.refs_6_), channel_id=1, source_target_pairs={{12,0},{13,1},{14,2},{15,3},{0,4},{1,5},{2,6},{3,7},{4,8},{5,9},{6... | collective-permute-start | bytes 786440 | tf_op jit(solution)/shard_map/ppermute | solution.py:29
  12.0 15.3 %collective-permute-start.4 = (bf16[512,256]{1,0:T(8,128)(2,1)S(1)}, bf16[512,256]{1,0:T(8,128)(2,1)}, u32[]{:S(2)}, u32[]{:S(2)}) collective-permute-start(bf16[512,256]{1,0:T(8,128)(2,1)S(1)} %pad_maximum_fusion.refs_6_), channel_id=1, source_target_pairs={{4,0},{5,1},{6,2},{7,3},{8,4},{9,5},{10,6},{11,7},{12,8},{13,9},{1... | collective-permute-start | bytes 786440 | tf_op jit(solution)/shard_map/ppermute | solution.py:29
  13.4 2.2 %copy-start = (bf16[1,256,8192]{2,1,0:T(8,128)(2,1)S(1)}, bf16[1,256,8192]{2,1,0:T(8,128)(2,1)}, u32[]{:S(2)}) copy-start(bf16[1,256,8192]{2,1,0:T(8,128)(2,1)} %param.8) | copy-start | bytes 12582916
  15.6 8.8 %copy-start.1 = (bf16[1,256,1024]{2,1,0:T(8,128)(2,1)S(1)}, bf16[1,256,1024]{2,1,0:T(8,128)(2,1)}, u32[]{:S(2)}) copy-start(bf16[1,256,1024]{2,1,0:T(8,128)(2,1)} %param.12) | copy-start | bytes 1572868
  15.6 8.8 %copy-start.2 = (bf16[1,256,1024]{2,1,0:T(8,128)(2,1)S(1)}, bf16[1,256,1024]{2,1,0:T(8,128)(2,1)}, u32[]{:S(2)}) copy-start(bf16[1,256,1024]{2,1,0:T(8,128)(2,1)} %param.13) | copy-start | bytes 1572868
  15.6 8.8 %copy-start.3 = (f32[1,8,256]{2,1,0:T(8,128)S(1)}, f32[1,8,256]{2,1,0:T(8,128)}, u32[]{:S(2)}) copy-start(f32[1,8,256]{2,1,0:T(8,128)} %param.14) | copy-start | bytes 24580
  15.6 12.4 %copy-start.5 = (bf16[1,256,1024]{2,1,0:T(8,128)(2,1)S(1)}, bf16[1,256,1024]{2,1,0:T(8,128)(2,1)}, u32[]{:S(2)}) copy-start(bf16[1,256,1024]{2,1,0:T(8,128)(2,1)} %param.9) | copy-start | bytes 1572868
  23.1 1.3 %copy-start.4 = (bf16[2,2048,256]{2,1,0:T(8,128)(2,1)}, bf16[2,2048,256]{2,1,0:T(8,128)(2,1)S(1)}, u32[]{:S(2)}) copy-start(bf16[2,2048,256]{2,1,0:T(8,128)(2,1)S(1)} %get-tuple-element.59) | copy-start | bytes 6291460
  25.1 0.7 copy-start.6
  25.8 2.2 %collective-permute-start.2 = (f32[8,1024]{1,0:T(8,128)S(1)}, f32[8,1024]{1,0:T(8,128)S(1)}, u32[]{:S(2)}, u32[]{:S(2)}) collective-permute-start(f32[8,1024]{1,0:T(8,128)S(1)} %row_stats.1.refs_4_), channel_id=1, source_target_pairs={{1,0},{0,1},{3,2},{2,3},{5,4},{4,5},{7,6},{6,7},{9,8},{8,9},{11,10... | collective-permute-start | bytes 98312 | tf_op jit(solution)/shard_map/ppermute | solution.py:29
  25.8 0.7 copy-start.8
  26.5 16.9 %collective-permute-start.7 = (bf16[2048,256]{1,0:T(8,128)(2,1)}, bf16[2048,256]{1,0:T(8,128)(2,1)S(1)}, u32[]{:S(2)}, u32[]{:S(2)}) collective-permute-start(bf16[2048,256]{1,0:T(8,128)(2,1)} %get-tuple-element.49), channel_id=1, source_target_pairs={{1,0},{0,1},{3,2},{2,3},{5,4},{4,5},{7,6},{6,7},{9,8},{8,9},{11,10... | collective-permute-start | bytes 3145736 | tf_op jit(solution)/shard_map/ppermute | solution.py:29
  27.3 52.0 %collective-permute-start.8 = (bf16[2,2048,256]{2,1,0:T(8,128)(2,1)}, bf16[2,2048,256]{2,1,0:T(8,128)(2,1)S(1)}, u32[]{:S(2)}, u32[]{:S(2)}) collective-permute-start(bf16[2,2048,256]{2,1,0:T(8,128)(2,1)} %copy-done.4), channel_id=1, source_target_pairs={{32,0},{33,1},{34,2},{35,3},{36,4},{37,5},{38,6},{39,7},{40,8},{41... | collective-permute-start | bytes 6291464 | tf_op jit(solution)/shard_map/ppermute | solution.py:29
  28.0 1.0 copy-start.7
  29.0 0.9 copy-start.9
  39.7 15.6 %collective-permute-start.9 = (bf16[1024,256]{1,0:T(8,128)(2,1)S(1)}, bf16[1024,256]{1,0:T(8,128)(2,1)S(1)}, u32[]{:S(2)}, u32[]{:S(2)}) collective-permute-start(bf16[1024,256]{1,0:T(8,128)(2,1)S(1)} %get-tuple-element.61), channel_id=1, source_target_pairs={{2,0},{3,1},{0,2},{1,3},{6,4},{7,5},{4,6},{5,7},{10,8},{11,9},{8,1... | collective-permute-start | bytes 1572872 | tf_op jit(solution)/shard_map/ppermute | solution.py:29
  55.4 7.4 %collective-permute-start.10 = (bf16[256,256]{1,0:T(8,128)(2,1)S(1)}, bf16[256,256]{1,0:T(8,128)(2,1)S(1)}, u32[]{:S(2)}, u32[]{:S(2)}) collective-permute-start(bf16[256,256]{1,0:T(8,128)(2,1)S(1)} %get-tuple-element.84), channel_id=1, source_target_pairs={{12,0},{13,1},{14,2},{15,3},{0,4},{1,5},{2,6},{3,7},{4,8},{5,9},{6... | collective-permute-start | bytes 393224 | tf_op jit(solution)/shard_map/ppermute | solution.py:29
  58.9 6.5 %collective-permute-start.12 = (bf16[256,256]{1,0:T(8,128)(2,1)S(1)}, bf16[256,256]{1,0:T(8,128)(2,1)S(1)}, u32[]{:S(2)}, u32[]{:S(2)}) collective-permute-start(bf16[256,256]{1,0:T(8,128)(2,1)S(1)} %get-tuple-element.85), channel_id=1, source_target_pairs={{8,0},{9,1},{10,2},{11,3},{12,4},{13,5},{14,6},{15,7},{0,8},{1,9},... | collective-permute-start | bytes 393224 | tf_op jit(solution)/shard_map/ppermute | solution.py:29
  59.7 6.1 %collective-permute-start.11 = (bf16[256,256]{1,0:T(8,128)(2,1)S(1)}, bf16[256,256]{1,0:T(8,128)(2,1)S(1)}, u32[]{:S(2)}, u32[]{:S(2)}) collective-permute-start(bf16[256,256]{1,0:T(8,128)(2,1)S(1)} %get-tuple-element.86), channel_id=1, source_target_pairs={{4,0},{5,1},{6,2},{7,3},{8,4},{9,5},{10,6},{11,7},{12,8},{13,9},{1... | collective-permute-start | bytes 393224 | tf_op jit(solution)/shard_map/ppermute | solution.py:29
  65.9 12.1 %collective-permute-start.13 = (bf16[256,256]{1,0:T(8,128)(2,1)S(1)}, bf16[256,256]{1,0:T(8,128)(2,1)S(1)}, u32[]{:S(2)}, u32[]{:S(2)}) collective-permute-start(bf16[256,256]{1,0:T(8,128)(2,1)S(1)} %add_convert_fusion.1.ga), channel_id=1, source_target_pairs={{32,0},{33,1},{34,2},{35,3},{36,4},{37,5},{38,6},{39,7},{40,8},{41... | collective-permute-start | bytes 393224 | tf_op jit(solution)/shard_map/ppermute | solution.py:29
  78.0 1.3 %collective-permute-start.14 = (bf16[256,256]{1,0:T(8,128)(2,1)S(1)}, bf16[256,256]{1,0:T(8,128)(2,1)S(1)}, u32[]{:S(2)}, u32[]{:S(2)}) collective-permute-start(bf16[256,256]{1,0:T(8,128)(2,1)S(1)} %collective-permute-done.13.gc), channel_id=1, source_target_pairs={{1,0},{0,1},{3,2},{2,3},{5,4},{4,5},{7,6},{6,7},{9,8},{8,9},{11,10... | collective-permute-start | bytes 393224 | tf_op jit(solution)/shard_map/ppermute | solution.py:29
  79.4 2.9 %collective-permute-start.15 = (bf16[2048,256]{1,0:T(8,128)(2,1)S(1)}, bf16[2048,256]{1,0:T(8,128)(2,1)S(1)}, u32[]{:S(2)}, u32[]{:S(2)}) collective-permute-start(bf16[2048,256]{1,0:T(8,128)(2,1)S(1)} %slice_bitcast_fusion), channel_id=1, source_target_pairs={{1,0},{0,1},{3,2},{2,3},{5,4},{4,5},{7,6},{6,7},{9,8},{8,9},{11,10... | collective-permute-start | bytes 3145736 | tf_op jit(solution)/shard_map/ppermute | solution.py:29
  79.6 2.7 %collective-permute-start.16 = (bf16[256,256]{1,0:T(8,128)(2,1)S(1)}, bf16[256,256]{1,0:T(8,128)(2,1)S(1)}, u32[]{:S(2)}, u32[]{:S(2)}) collective-permute-start(bf16[256,256]{1,0:T(8,128)(2,1)S(1)} %add_convert_fusion.1.ga), channel_id=1, source_target_pairs={{1,0},{0,1},{3,2},{2,3},{5,4},{4,5},{7,6},{6,7},{9,8},{8,9},{11,10... | collective-permute-start | bytes 393224 | tf_op jit(solution)/shard_map/ppermute | solution.py:29
  107.2 14.6 %collective-permute-start.17 = (bf16[256,1024]{1,0:T(8,128)(2,1)S(1)}, bf16[256,1024]{1,0:T(8,128)(2,1)S(1)}, u32[]{:S(2)}, u32[]{:S(2)}) collective-permute-start(bf16[256,1024]{1,0:T(8,128)(2,1)S(1)} %get-tuple-element.68), channel_id=1, source_target_pairs={{1,0},{0,1},{3,2},{2,3},{5,4},{4,5},{7,6},{6,7},{9,8},{8,9},{11,10... | collective-permute-start | bytes 1572872 | tf_op jit(solution)/shard_map/ppermute | solution.py:29
  107.9 11.2 %collective-permute-start.18 = (bf16[32,256]{1,0:T(8,128)(2,1)S(1)}, bf16[32,256]{1,0:T(8,128)(2,1)S(1)}, u32[]{:S(2)}, u32[]{:S(2)}) collective-permute-start(bf16[32,256]{1,0:T(8,128)(2,1)S(1)} %get-tuple-element.71), channel_id=1, source_target_pairs={{192,0},{193,1},{194,2},{195,3},{196,4},{197,5},{198,6},{199,7},{2... | collective-permute-start | bytes 49160 | tf_op jit(solution)/shard_map/ppermute | solution.py:29
  111.3 7.9 %collective-permute-start.19 = (bf16[32,256]{1,0:T(8,128)(2,1)S(1)}, bf16[32,256]{1,0:T(8,128)(2,1)S(1)}, u32[]{:S(2)}, u32[]{:S(2)}) collective-permute-start(bf16[32,256]{1,0:T(8,128)(2,1)S(1)} %get-tuple-element.72), channel_id=1, source_target_pairs={{128,0},{129,1},{130,2},{131,3},{132,4},{133,5},{134,6},{135,7},{1... | collective-permute-start | bytes 49160 | tf_op jit(solution)/shard_map/ppermute | solution.py:29
  116.5 4.6 %collective-permute-start.20 = (bf16[32,256]{1,0:T(8,128)(2,1)S(1)}, bf16[32,256]{1,0:T(8,128)(2,1)S(1)}, u32[]{:S(2)}, u32[]{:S(2)}) collective-permute-start(bf16[32,256]{1,0:T(8,128)(2,1)S(1)} %get-tuple-element.73), channel_id=1, source_target_pairs={{64,0},{65,1},{66,2},{67,3},{68,4},{69,5},{70,6},{71,7},{72,8},{73... | collective-permute-start | bytes 49160 | tf_op jit(solution)/shard_map/ppermute | solution.py:29

commit v8 on v7

--- a/solution.py
+++ b/solution.py
@@ -105,31 +105,27 @@
     even = place[0] == 0
     here = lax.rem(pl.program_id(0), 2) == place[1]
     half = pl.multiple_of(lax.div(pl.program_id(0), 2) * 512, 512)
-    for u in range(8):
-        tile = x_ref[:, u * BLK : (u + 1) * BLK].T
-        for yh in range(YH):
-            first = tile[yh * 64 : yh * 64 + 32]
-            second = tile[yh * 64 + 32 : yh * 64 + 64]
-            at = pl.ds(half + (u * 64 + yh * 32), 32)
-
-            def store(a, b):
-                @pl.when(here)
-                def _():
-                    mine_ref[at, :] = a
-                    other_ref[at, :] = b
-
-                @pl.when(jnp.logical_not(here))
-                def _():
-                    away_ref[0, at, :] = a
-                    away_ref[1, at, :] = b
-
-            @pl.when(even)
-            def _():
-                store(first, second)
-
-            @pl.when(jnp.logical_not(even))
-            def _():
-                store(second, first)
+
+    def cut(even_ref, odd_ref):
+        for u in range(8):
+            tile = x_ref[:, u * BLK : (u + 1) * BLK].T
+            for yh in range(YH):
+                at = pl.ds(half + (u * 64 + yh * 32), 32)
+                even_ref[at, :] = tile[yh * 64 : yh * 64 + 32]
+                odd_ref[at, :] = tile[yh * 64 + 32 : yh * 64 + 64]
+
+    for holds, same, differs in (
+        (here, mine_ref, other_ref),
+        (jnp.logical_not(here), away_ref.at[0], away_ref.at[1]),
+    ):
+
+        @pl.when(jnp.logical_and(holds, even))
+        def _():
+            cut(same, differs)
+
+        @pl.when(jnp.logical_and(holds, jnp.logical_not(even)))
+        def _():
+            cut(differs, same)
 
 
 def turn(place, layer):
@@ -144,7 +140,7 @@
             pl.BlockSpec((2048, 256), lambda z: (0, 0)),
             pl.BlockSpec((2, 2048, 256), lambda z: (0, 0, 0)),
         ),
-        compiler_params=pltpu.CompilerParams(vmem_limit_bytes=12 * 2**20),
+        compiler_params=pltpu.CompilerParams(vmem_limit_bytes=54 * 2**20),
         cost_estimate=pl.CostEstimate(flops=10**9, bytes_accessed=8 * 2**20, transcendentals=0),
         name="turn",
     )(place, layer)

time: 124 us -> 121 us (0.976)
  Pallas kernels: 28.8 us -> 19.4 us
  starting transfers between devices: 32.2 us -> 40.5 us
  local copies, waits for them, and re-layouts: 7.85 us -> 4.32 us
    ppermute x21, starting transfers between devices: 32.2 us -> 40.5 us  [fetch(): return lax.ppermute(value, AXES, pairs)]
    pallas_call x1, Pallas kernels: 9.75 us -> 3.65 us  [first_call(): pl.pallas_call(first_kernel, out_shape=(rows,) * 4 + (jax.ShapeDtypeStruc...]
    unnamed x20 -> x24, local copies, waits for them, and re-layouts: 6.85 us -> 3.33 us
    pallas_call x1, Pallas kernels: 8.62 us -> 5.3 us  [second_call(): pl.pallas_call(second_kernel, out_shape=(jax.ShapeDtypeStruct((256, WIDE)...]
  transfers between devices with their start and end apart: 21 -> 21, of which waited for: 9 -> 8; matrix products, arithmetic and copies ran while one was open for 3% -> 3% of each run, Pallas kernels for 22% -> 15%
where the time goes in v8:
time: 121 us; the launch traced here: 120 us
  starting transfers between devices  40.5 us (33%)
  waiting for transfers between devices  26.5 us (22%)
  blocking collectives  23.2 us (19%)
  Pallas kernels  19.4 us (16%)
  other arithmetic  5.07 us (4%)
  local copies, waits for them, and re-layouts  4.32 us (4%)
    ppermute x21, starting transfers between devices, fetch(): return lax.ppermute(value, AXES, pairs)  40.5 us
    ppermute x21, waiting for transfers between devices, fetch(): return lax.ppermute(value, AXES, pairs)  26.5 us
    all_to_all x1, blocking collectives, body(): terms = lax.all_to_all(terms, ('yl', 'x', 'yh'), 0, 0)  23.2 us
    pallas_call x1, Pallas kernels, turn(): pl.pallas_call(turn_kernel, grid=(Z,), out_shape=(half, half, jax.ShapeDt...  7.53 us
    pallas_call x1, Pallas kernels, second_call(): pl.pallas_call(second_kernel, out_shape=(jax.ShapeDtypeStruct((256, WIDE)...  5.3 us
    pallas_call x1, Pallas kernels, first_call(): pl.pallas_call(first_kernel, out_shape=(rows,) * 4 + (jax.ShapeDtypeStruc...  3.65 us
    unnamed x24, local copies, waits for them, and re-layouts  3.33 us
  transfers between devices with their start and end apart: 21, of which 8 were waited for; matrix products, arithmetic and copies ran while one was open for 3% of the time, Pallas kernels for 15%

profile of v8, /device:TPU:4, one launch (start us, length us, event | category | flops | bytes accessed | tf_op | source)
XLA Modules:
  0.0 119.9 jit_solution(5070864834150475125)
XLA Ops:
  0.6 0.9 pad_maximum_fusion.1
  1.5 3.3 %collective-permute-start.3 = (bf16[256,256]{1,0:T(8,128)(2,1)S(1)}, bf16[256,256]{1,0:T(8,128)(2,1)S(1)}, u32[]{:S(2)}, u32[]{:S(2)}) collective-permute-start(bf16[256,256]{1,0:T(8,128)(2,1)S(1)} %pad_maximum_fusion.1), channel_id=1, source_target_pairs={{2,0},{3,1},{0,2},{1,3},{6,4},{7,5},{4,6},{5,7},{10,8},{11,9},{8,1... | collective-permute-start | bytes 393224 | tf_op jit(solution)/shard_map/ppermute | solution.py:29
  4.8 0.5 collective-permute-start.1
  5.3 0.7 reshape.14
  6.3 0.2 convert_reduce_fusion.2
  6.6 0.2 convert_reduce_fusion.1
  6.8 1.6 %collective-permute-done.3 = bf16[256,256]{1,0:T(8,128)(2,1)S(1)} collective-permute-done((bf16[256,256]{1,0:T(8,128)(2,1)S(1)}, bf16[256,256]{1,0:T(8,128)(2,1)S(1)}, u32[]{:S(2)}, u32[]{:S(2)}) %collective-permute-start.3) | collective-permute-done | bytes 131104 | tf_op jit(solution)/shard_map/ppermute | solution.py:29
  8.3 0.9 pad_maximum_fusion.refs_6_
  9.2 2.1 %collective-permute-start.6 = (bf16[512,256]{1,0:T(8,128)(2,1)S(1)}, bf16[512,256]{1,0:T(8,128)(2,1)S(1)}, u32[]{:S(2)}, u32[]{:S(2)}) collective-permute-start(bf16[512,256]{1,0:T(8,128)(2,1)S(1)} %pad_maximum_fusion.refs_6_), channel_id=1, source_target_pairs={{8,0},{9,1},{10,2},{11,3},{12,4},{13,5},{14,6},{15,7},{0,8},{1,9},... | collective-permute-start | bytes 786440 | tf_op jit(solution)/shard_map/ppermute | solution.py:29
  11.3 0.6 collective-permute-start.5
  11.9 0.6 pad_add_fusion.3.place
  12.5 1.4 %collective-permute-start.4 = (bf16[512,256]{1,0:T(8,128)(2,1)S(1)}, bf16[512,256]{1,0:T(8,128)(2,1)}, u32[]{:S(2)}, u32[]{:S(2)}) collective-permute-start(bf16[512,256]{1,0:T(8,128)(2,1)S(1)} %pad_maximum_fusion.refs_6_), channel_id=1, source_target_pairs={{4,0},{5,1},{6,2},{7,3},{8,4},{9,5},{10,6},{11,7},{12,8},{13,9},{1... | collective-permute-start | bytes 786440 | tf_op jit(solution)/shard_map/ppermute | solution.py:29
  13.9 7.5 %turn.1 = (bf16[2048,256]{1,0:T(8,128)(2,1)}, bf16[2048,256]{1,0:T(8,128)(2,1)}, bf16[2,2048,256]{2,1,0:T(8,128)(2,1)}) custom-call(s32[3]{0:T(128)} %pad_add_fusion.3.place, bf16[256,8192]{1,0:T(8,128)(2,1)} %bitcast.41), custom_call_target="tpu_custom_call" | custom-call | flops 1000000000 | bytes 8388608 | tf_op jit(solution)/shard_map/turn/pallas_call | solution.py:133
  21.4 0.5 row_stats.1.refs_4_
  21.9 0.2 convert_reduce_fusion
  22.1 0.7 copy-done.6
  22.8 0.7 copy-done.9
  23.5 0.5 collective-permute-start.7
  24.0 0.1 select_reduce_fusion
  24.4 1.4 %collective-permute-start.8 = (bf16[2,2048,256]{2,1,0:T(8,128)(2,1)}, bf16[2,2048,256]{2,1,0:T(8,128)(2,1)S(1)}, u32[]{:S(2)}, u32[]{:S(2)}) collective-permute-start(bf16[2,2048,256]{2,1,0:T(8,128)(2,1)} %get-tuple-element.59), channel_id=1, source_target_pairs={{32,0},{33,1},{34,2},{35,3},{36,4},{37,5},{38,6},{39,7},{40,8},{41... | collective-permute-start | bytes 6291464 | tf_op jit(solution)/shard_map/ppermute | solution.py:29
  25.8 0.9 copy-done.7
  26.7 0.9 copy-done.10
  27.7 3.7 %attention_first.1 = (bf16[4,128,1024]{2,1,0:T(8,128)(2,1)S(1)}, bf16[4,128,1024]{2,1,0:T(8,128)(2,1)S(1)}, bf16[4,128,1024]{2,1,0:T(8,128)(2,1)S(1)}, bf16[4,12...) custom-call(s32[28]{0:T(128)S(1)} %concatenate.27.meta, ...), custom_call_target="tpu_custom_call" | custom-call | flops 10000000000 | bytes 1048576 | tf_op jit(solution)/shard_map/attention_first/pallas_call | solution.py:316
  31.3 11.3 %collective-permute-start.9 = (bf16[1024,256]{1,0:T(8,128)(2,1)S(1)}, bf16[1024,256]{1,0:T(8,128)(2,1)S(1)}, u32[]{:S(2)}, u32[]{:S(2)}) collective-permute-start(bf16[1024,256]{1,0:T(8,128)(2,1)S(1)} %get-tuple-element.61), channel_id=1, source_target_pairs={{2,0},{3,1},{0,2},{1,3},{6,4},{7,5},{4,6},{5,7},{10,8},{11,9},{8,1... | collective-permute-start | bytes 1572872 | tf_op jit(solution)/shard_map/ppermute | solution.py:29
  42.6 5.3 %attention_second.1 = (f32[256,1024]{1,0:T(8,128)S(1)}, bf16[256,1024]{1,0:T(8,128)(2,1)S(1)}, f32[256,256]{1,0:T(8,128)S(1)}, f32[256,256]{1,0:T(8,128)S(1)}, f...) custom-call(s32[28]{0:T(128)S(1)} %concatenate.25.meta, bf16[4,128,1024]{2,1,0:T(8,128)(2,1)S(1)} %get-tuple-element.50.refs_0_, ...), custom_call_target="tpu_custom_call" | custom-call | flops 10000000000 | bytes 1048576 | tf_op jit(solution)/shard_map/attention_second/pallas_call | solution.py:335
  47.9 5.6 %collective-permute-done.9 = bf16[1024,256]{1,0:T(8,128)(2,1)S(1)} collective-permute-done((bf16[1024,256]{1,0:T(8,128)(2,1)S(1)}, bf16[1024,256]{1,0:T(8,128)(2,1)S(1)}, u32[]{:S(2)}, u32[]{:S(2)}) %collective-permute-start.9) | collective-permute-done | bytes 524320 | tf_op jit(solution)/shard_map/ppermute | solution.py:29
  53.5 0.1 add_convert_fusion.4
  53.6 0.6 collective-permute-start.10
  54.2 4.3 %collective-permute-start.12 = (bf16[256,256]{1,0:T(8,128)(2,1)S(1)}, bf16[256,256]{1,0:T(8,128)(2,1)S(1)}, u32[]{:S(2)}, u32[]{:S(2)}) collective-permute-start(bf16[256,256]{1,0:T(8,128)(2,1)S(1)} %get-tuple-element.85), channel_id=1, source_target_pairs={{8,0},{9,1},{10,2},{11,3},{12,4},{13,5},{14,6},{15,7},{0,8},{1,9},... | collective-permute-start | bytes 393224 | tf_op jit(solution)/shard_map/ppermute | solution.py:29
  58.6 2.5 %collective-permute-start.11 = (bf16[256,256]{1,0:T(8,128)(2,1)S(1)}, bf16[256,256]{1,0:T(8,128)(2,1)S(1)}, u32[]{:S(2)}, u32[]{:S(2)}) collective-permute-start(bf16[256,256]{1,0:T(8,128)(2,1)S(1)} %get-tuple-element.86), channel_id=1, source_target_pairs={{4,0},{5,1},{6,2},{7,3},{8,4},{9,5},{10,6},{11,7},{12,8},{13,9},{1... | collective-permute-start | bytes 393224 | tf_op jit(solution)/shard_map/ppermute | solution.py:29
  61.1 1.7 %collective-permute-done.12 = bf16[256,256]{1,0:T(8,128)(2,1)S(1)} collective-permute-done((bf16[256,256]{1,0:T(8,128)(2,1)S(1)}, bf16[256,256]{1,0:T(8,128)(2,1)S(1)}, u32[]{:S(2)}, u32[]{:S(2)}) %collective-permute-start.12) | collective-permute-done | bytes 131104 | tf_op jit(solution)/shard_map/ppermute | solution.py:29
  62.8 1.2 collective-permute-done.11
  64.0 0.1 add_convert_fusion.1.ga
  64.1 0.2 collective-permute-start.13
  64.3 10.8 %collective-permute-done.13.gc = bf16[256,256]{1,0:T(8,128)(2,1)S(1)} collective-permute-done((bf16[256,256]{1,0:T(8,128)(2,1)S(1)}, bf16[256,256]{1,0:T(8,128)(2,1)S(1)}, u32[]{:S(2)}, u32[]{:S(2)}) %collective-permute-start.13) | collective-permute-done | bytes 131104 | tf_op jit(solution)/shard_map/ppermute | solution.py:29
  75.1 1.3 %collective-permute-done.14.gd = bf16[256,256]{1,0:T(8,128)(2,1)S(1)} collective-permute-done((bf16[256,256]{1,0:T(8,128)(2,1)S(1)}, bf16[256,256]{1,0:T(8,128)(2,1)S(1)}, u32[]{:S(2)}, u32[]{:S(2)}) %collective-permute-start.14) | collective-permute-done | bytes 131104 | tf_op jit(solution)/shard_map/ppermute | solution.py:29
  76.5 0.2 collective-permute-start.15
  76.7 0.4 collective-permute-start.16
  77.1 2.3 %collective-permute-done.16.gb = bf16[256,256]{1,0:T(8,128)(2,1)S(1)} collective-permute-done((bf16[256,256]{1,0:T(8,128)(2,1)S(1)}, bf16[256,256]{1,0:T(8,128)(2,1)S(1)}, u32[]{:S(2)}, u32[]{:S(2)}) %collective-permute-start.16) | collective-permute-done | bytes 131104 | tf_op jit(solution)/shard_map/ppermute | solution.py:29
  79.4 1.8 %project.1 = bf16[16,128,256]{2,1,0:T(8,128)(2,1)S(1)} custom-call(bf16[2048,256]{1,0:T(8,128)(2,1)S(1)} %copy-done, bf16[2048,256]{1,0:T(8,128)(2,1)S(1)} %collective-permute-done.7.b_ref, bf16[2,2048,256]{2,1,0:T(8,128)(2,1)S(1)} %collective-permute-done.8.c_ref, bf16[2048,256]{1,0:T(8,128)(2,1)S(1)} %collective-permute-done.15.d_ref, ...), custom_call_target="tpu_custom_call" | custom-call | flops 1073741824 | bytes 8388608 | tf_op jit(solution)/shard_map/project/pallas_call | solution.py:381
  81.2 23.2 %all_to_all.5.in_ref = bf16[16,128,256]{2,1,0:T(8,128)(2,1)S(1)} all-to-all(bf16[16,128,256]{2,1,0:T(8,128)(2,1)S(1)} %project.1), channel_id=1, replica_groups=mesh['z'=8,'yl'=2,'x'=4,'yh'=2,'c'=2] {'yl','x','yh'}, dimensions={0} | all-to-all | bytes 2097152 | tf_op jit(solution)/shard_map/all_to_all | solution.py:459
  104.4 0.7 sum_terms.1
  105.1 3.3 %collective-permute-start.18 = (bf16[32,256]{1,0:T(8,128)(2,1)S(1)}, bf16[32,256]{1,0:T(8,128)(2,1)S(1)}, u32[]{:S(2)}, u32[]{:S(2)}) collective-permute-start(bf16[32,256]{1,0:T(8,128)(2,1)S(1)} %get-tuple-element.71), channel_id=1, source_target_pairs={{192,0},{193,1},{194,2},{195,3},{196,4},{197,5},{198,6},{199,7},{2... | collective-permute-start | bytes 49160 | tf_op jit(solution)/shard_map/ppermute | solution.py:29
  108.4 5.2 %collective-permute-start.19 = (bf16[32,256]{1,0:T(8,128)(2,1)S(1)}, bf16[32,256]{1,0:T(8,128)(2,1)S(1)}, u32[]{:S(2)}, u32[]{:S(2)}) collective-permute-start(bf16[32,256]{1,0:T(8,128)(2,1)S(1)} %get-tuple-element.72), channel_id=1, source_target_pairs={{128,0},{129,1},{130,2},{131,3},{132,4},{133,5},{134,6},{135,7},{1... | collective-permute-start | bytes 49160 | tf_op jit(solution)/shard_map/ppermute | solution.py:29
  113.7 2.7 %collective-permute-start.20 = (bf16[32,256]{1,0:T(8,128)(2,1)S(1)}, bf16[32,256]{1,0:T(8,128)(2,1)S(1)}, u32[]{:S(2)}, u32[]{:S(2)}) collective-permute-start(bf16[32,256]{1,0:T(8,128)(2,1)S(1)} %get-tuple-element.73), channel_id=1, source_target_pairs={{64,0},{65,1},{66,2},{67,3},{68,4},{69,5},{70,6},{71,7},{72,8},{73... | collective-permute-start | bytes 49160 | tf_op jit(solution)/shard_map/ppermute | solution.py:29
  116.3 2.0 %collective-permute-done.20 = bf16[32,256]{1,0:T(8,128)(2,1)S(1)} collective-permute-done((bf16[32,256]{1,0:T(8,128)(2,1)S(1)}, bf16[32,256]{1,0:T(8,128)(2,1)S(1)}, u32[]{:S(2)}, u32[]{:S(2)}) %collective-permute-start.20) | collective-permute-done | bytes 16416 | tf_op jit(solution)/shard_map/ppermute | solution.py:29
  118.3 0.6 convert_add_fusion
  118.9 1.0 fusion
  (46 shorter events, 0.6 us)
Async XLA Ops:
  1.5 6.8 %collective-permute-start.3 = (bf16[256,256]{1,0:T(8,128)(2,1)S(1)}, bf16[256,256]{1,0:T(8,128)(2,1)S(1)}, u32[]{:S(2)}, u32[]{:S(2)}) collective-permute-start(bf16[256,256]{1,0:T(8,128)(2,1)S(1)} %pad_maximum_fusion.1), channel_id=1, source_target_pairs={{2,0},{3,1},{0,2},{1,3},{6,4},{7,5},{4,6},{5,7},{10,8},{11,9},{8,1... | collective-permute-start | bytes 393224 | tf_op jit(solution)/shard_map/ppermute | solution.py:29
  4.8 21.0 %collective-permute-start = (bf16[256,1024]{1,0:T(8,128)(2,1)}, bf16[256,1024]{1,0:T(8,128)(2,1)S(1)}, u32[]{:S(2)}, u32[]{:S(2)}) collective-permute-start(bf16[256,1024]{1,0:T(8,128)(2,1)} %bitcast.39), channel_id=1, source_target_pairs={{1,0},{0,1},{3,2},{2,3},{5,4},{4,5},{7,6},{6,7},{9,8},{8,9},{11,10... | collective-permute-start | bytes 1572872 | tf_op jit(solution)/shard_map/ppermute | solution.py:29
  4.8 21.0 %collective-permute-start.1 = (bf16[256,1024]{1,0:T(8,128)(2,1)}, bf16[256,1024]{1,0:T(8,128)(2,1)S(1)}, u32[]{:S(2)}, u32[]{:S(2)}) collective-permute-start(bf16[256,1024]{1,0:T(8,128)(2,1)} %bitcast.35), channel_id=1, source_target_pairs={{1,0},{0,1},{3,2},{2,3},{5,4},{4,5},{7,6},{6,7},{9,8},{8,9},{11,10... | collective-permute-start | bytes 1572872 | tf_op jit(solution)/shard_map/ppermute | solution.py:29
  9.2 12.9 %collective-permute-start.6 = (bf16[512,256]{1,0:T(8,128)(2,1)S(1)}, bf16[512,256]{1,0:T(8,128)(2,1)S(1)}, u32[]{:S(2)}, u32[]{:S(2)}) collective-permute-start(bf16[512,256]{1,0:T(8,128)(2,1)S(1)} %pad_maximum_fusion.refs_6_), channel_id=1, source_target_pairs={{8,0},{9,1},{10,2},{11,3},{12,4},{13,5},{14,6},{15,7},{0,8},{1,9},... | collective-permute-start | bytes 786440 | tf_op jit(solution)/shard_map/ppermute | solution.py:29
  11.3 11.5 %collective-permute-start.5 = (bf16[512,256]{1,0:T(8,128)(2,1)S(1)}, bf16[512,256]{1,0:T(8,128)(2,1)S(1)}, u32[]{:S(2)}, u32[]{:S(2)}) collective-permute-start(bf16[512,256]{1,0:T(8,128)(2,1)S(1)} %pad_maximum_fusion.refs_6_), channel_id=1, source_target_pairs={{12,0},{13,1},{14,2},{15,3},{0,4},{1,5},{2,6},{3,7},{4,8},{5,9},{6... | collective-permute-start | bytes 786440 | tf_op jit(solution)/shard_map/ppermute | solution.py:29
  12.5 11.9 %collective-permute-start.4 = (bf16[512,256]{1,0:T(8,128)(2,1)S(1)}, bf16[512,256]{1,0:T(8,128)(2,1)}, u32[]{:S(2)}, u32[]{:S(2)}) collective-permute-start(bf16[512,256]{1,0:T(8,128)(2,1)S(1)} %pad_maximum_fusion.refs_6_), channel_id=1, source_target_pairs={{4,0},{5,1},{6,2},{7,3},{8,4},{9,5},{10,6},{11,7},{12,8},{13,9},{1... | collective-permute-start | bytes 786440 | tf_op jit(solution)/shard_map/ppermute | solution.py:29
  13.9 7.5 %copy-start.1 = (bf16[1,256,1024]{2,1,0:T(8,128)(2,1)S(1)}, bf16[1,256,1024]{2,1,0:T(8,128)(2,1)}, u32[]{:S(2)}) copy-start(bf16[1,256,1024]{2,1,0:T(8,128)(2,1)} %param.12) | copy-start | bytes 1572868
  13.9 7.5 %copy-start.2 = (bf16[1,256,1024]{2,1,0:T(8,128)(2,1)S(1)}, bf16[1,256,1024]{2,1,0:T(8,128)(2,1)}, u32[]{:S(2)}) copy-start(bf16[1,256,1024]{2,1,0:T(8,128)(2,1)} %param.13) | copy-start | bytes 1572868
  13.9 7.5 %copy-start.3 = (f32[1,8,256]{2,1,0:T(8,128)S(1)}, f32[1,8,256]{2,1,0:T(8,128)}, u32[]{:S(2)}) copy-start(f32[1,8,256]{2,1,0:T(8,128)} %param.14) | copy-start | bytes 24580
  13.9 11.9 %copy-start.5 = (bf16[1,256,1024]{2,1,0:T(8,128)(2,1)S(1)}, bf16[1,256,1024]{2,1,0:T(8,128)(2,1)}, u32[]{:S(2)}) copy-start(bf16[1,256,1024]{2,1,0:T(8,128)(2,1)} %param.9) | copy-start | bytes 1572868
  22.1 0.7 copy-start.6
  22.8 2.9 %collective-permute-start.2 = (f32[8,1024]{1,0:T(8,128)S(1)}, f32[8,1024]{1,0:T(8,128)S(1)}, u32[]{:S(2)}, u32[]{:S(2)}) collective-permute-start(f32[8,1024]{1,0:T(8,128)S(1)} %row_stats.1.refs_4_), channel_id=1, source_target_pairs={{1,0},{0,1},{3,2},{2,3},{5,4},{4,5},{7,6},{6,7},{9,8},{8,9},{11,10... | collective-permute-start | bytes 98312 | tf_op jit(solution)/shard_map/ppermute | solution.py:29
  22.8 0.7 copy-start.9
  23.5 19.1 %collective-permute-start.7 = (bf16[2048,256]{1,0:T(8,128)(2,1)}, bf16[2048,256]{1,0:T(8,128)(2,1)S(1)}, u32[]{:S(2)}, u32[]{:S(2)}) collective-permute-start(bf16[2048,256]{1,0:T(8,128)(2,1)} %get-tuple-element.49), channel_id=1, source_target_pairs={{1,0},{0,1},{3,2},{2,3},{5,4},{4,5},{7,6},{6,7},{9,8},{8,9},{11,10... | collective-permute-start | bytes 3145736 | tf_op jit(solution)/shard_map/ppermute | solution.py:29
  24.4 52.1 %collective-permute-start.8 = (bf16[2,2048,256]{2,1,0:T(8,128)(2,1)}, bf16[2,2048,256]{2,1,0:T(8,128)(2,1)S(1)}, u32[]{:S(2)}, u32[]{:S(2)}) collective-permute-start(bf16[2,2048,256]{2,1,0:T(8,128)(2,1)} %get-tuple-element.59), channel_id=1, source_target_pairs={{32,0},{33,1},{34,2},{35,3},{36,4},{37,5},{38,6},{39,7},{40,8},{41... | collective-permute-start | bytes 6291464 | tf_op jit(solution)/shard_map/ppermute | solution.py:29
  25.8 1.0 copy-start.7
  26.7 0.9 copy-start.10
  27.7 14.9 %copy-start.8 = (bf16[512,256]{1,0:T(8,128)(2,1)S(1)}, bf16[512,256]{1,0:T(8,128)(2,1)}, u32[]{:S(2)}) copy-start(bf16[512,256]{1,0:T(8,128)(2,1)} %copy-done.6) | copy-start | bytes 786436
  27.7 14.9 %copy-start.11 = (bf16[512,256]{1,0:T(8,128)(2,1)S(1)}, bf16[512,256]{1,0:T(8,128)(2,1)}, u32[]{:S(2)}) copy-start(bf16[512,256]{1,0:T(8,128)(2,1)} %copy-done.9) | copy-start | bytes 786436
  31.3 22.2 %collective-permute-start.9 = (bf16[1024,256]{1,0:T(8,128)(2,1)S(1)}, bf16[1024,256]{1,0:T(8,128)(2,1)S(1)}, u32[]{:S(2)}, u32[]{:S(2)}) collective-permute-start(bf16[1024,256]{1,0:T(8,128)(2,1)S(1)} %get-tuple-element.61), channel_id=1, source_target_pairs={{2,0},{3,1},{0,2},{1,3},{6,4},{7,5},{4,6},{5,7},{10,8},{11,9},{8,1... | collective-permute-start | bytes 1572872 | tf_op jit(solution)/shard_map/ppermute | solution.py:29
  53.5 25.9 %copy-start = (bf16[2048,256]{1,0:T(8,128)(2,1)S(1)}, bf16[2048,256]{1,0:T(8,128)(2,1)}, u32[]{:S(2)}) copy-start(bf16[2048,256]{1,0:T(8,128)(2,1)} %get-tuple-element.57.a_ref) | copy-start | bytes 3145732
  53.6 7.5 %collective-permute-start.10 = (bf16[256,256]{1,0:T(8,128)(2,1)S(1)}, bf16[256,256]{1,0:T(8,128)(2,1)S(1)}, u32[]{:S(2)}, u32[]{:S(2)}) collective-permute-start(bf16[256,256]{1,0:T(8,128)(2,1)S(1)} %get-tuple-element.84), channel_id=1, source_target_pairs={{12,0},{13,1},{14,2},{15,3},{0,4},{1,5},{2,6},{3,7},{4,8},{5,9},{6... | collective-permute-start | bytes 393224 | tf_op jit(solution)/shard_map/ppermute | solution.py:29
  54.2 8.6 %collective-permute-start.12 = (bf16[256,256]{1,0:T(8,128)(2,1)S(1)}, bf16[256,256]{1,0:T(8,128)(2,1)S(1)}, u32[]{:S(2)}, u32[]{:S(2)}) collective-permute-start(bf16[256,256]{1,0:T(8,128)(2,1)S(1)} %get-tuple-element.85), channel_id=1, source_target_pairs={{8,0},{9,1},{10,2},{11,3},{12,4},{13,5},{14,6},{15,7},{0,8},{1,9},... | collective-permute-start | bytes 393224 | tf_op jit(solution)/shard_map/ppermute | solution.py:29
  58.6 5.4 %collective-permute-start.11 = (bf16[256,256]{1,0:T(8,128)(2,1)S(1)}, bf16[256,256]{1,0:T(8,128)(2,1)S(1)}, u32[]{:S(2)}, u32[]{:S(2)}) collective-permute-start(bf16[256,256]{1,0:T(8,128)(2,1)S(1)} %get-tuple-element.86), channel_id=1, source_target_pairs={{4,0},{5,1},{6,2},{7,3},{8,4},{9,5},{10,6},{11,7},{12,8},{13,9},{1... | collective-permute-start | bytes 393224 | tf_op jit(solution)/shard_map/ppermute | solution.py:29
  64.1 11.0 %collective-permute-start.13 = (bf16[256,256]{1,0:T(8,128)(2,1)S(1)}, bf16[256,256]{1,0:T(8,128)(2,1)S(1)}, u32[]{:S(2)}, u32[]{:S(2)}) collective-permute-start(bf16[256,256]{1,0:T(8,128)(2,1)S(1)} %add_convert_fusion.1.ga), channel_id=1, source_target_pairs={{32,0},{33,1},{34,2},{35,3},{36,4},{37,5},{38,6},{39,7},{40,8},{41... | collective-permute-start | bytes 393224 | tf_op jit(solution)/shard_map/ppermute | solution.py:29
  75.1 1.3 %collective-permute-start.14 = (bf16[256,256]{1,0:T(8,128)(2,1)S(1)}, bf16[256,256]{1,0:T(8,128)(2,1)S(1)}, u32[]{:S(2)}, u32[]{:S(2)}) collective-permute-start(bf16[256,256]{1,0:T(8,128)(2,1)S(1)} %collective-permute-done.13.gc), channel_id=1, source_target_pairs={{1,0},{0,1},{3,2},{2,3},{5,4},{4,5},{7,6},{6,7},{9,8},{8,9},{11,10... | collective-permute-start | bytes 393224 | tf_op jit(solution)/shard_map/ppermute | solution.py:29
  76.5 2.9 %collective-permute-start.15 = (bf16[2048,256]{1,0:T(8,128)(2,1)S(1)}, bf16[2048,256]{1,0:T(8,128)(2,1)S(1)}, u32[]{:S(2)}, u32[]{:S(2)}) collective-permute-start(bf16[2048,256]{1,0:T(8,128)(2,1)S(1)} %slice_bitcast_fusion), channel_id=1, source_target_pairs={{1,0},{0,1},{3,2},{2,3},{5,4},{4,5},{7,6},{6,7},{9,8},{8,9},{11,10... | collective-permute-start | bytes 3145736 | tf_op jit(solution)/shard_map/ppermute | solution.py:29
  76.7 2.7 %collective-permute-start.16 = (bf16[256,256]{1,0:T(8,128)(2,1)S(1)}, bf16[256,256]{1,0:T(8,128)(2,1)S(1)}, u32[]{:S(2)}, u32[]{:S(2)}) collective-permute-start(bf16[256,256]{1,0:T(8,128)(2,1)S(1)} %add_convert_fusion.1.ga), channel_id=1, source_target_pairs={{1,0},{0,1},{3,2},{2,3},{5,4},{4,5},{7,6},{6,7},{9,8},{8,9},{11,10... | collective-permute-start | bytes 393224 | tf_op jit(solution)/shard_map/ppermute | solution.py:29
  81.2 23.2 %copy-start.4 = (s32[3]{0:T(128)S(1)}, s32[3]{0:T(128)}, u32[]{:S(2)}) copy-start(s32[3]{0:T(128)} %pad_add_fusion.3.place) | copy-start | bytes 40
  104.4 14.5 %collective-permute-start.17 = (bf16[256,1024]{1,0:T(8,128)(2,1)S(1)}, bf16[256,1024]{1,0:T(8,128)(2,1)S(1)}, u32[]{:S(2)}, u32[]{:S(2)}) collective-permute-start(bf16[256,1024]{1,0:T(8,128)(2,1)S(1)} %get-tuple-element.68), channel_id=1, source_target_pairs={{1,0},{0,1},{3,2},{2,3},{5,4},{4,5},{7,6},{6,7},{9,8},{8,9},{11,10... | collective-permute-start | bytes 1572872 | tf_op jit(solution)/shard_map/ppermute | solution.py:29
  105.1 11.2 %collective-permute-start.18 = (bf16[32,256]{1,0:T(8,128)(2,1)S(1)}, bf16[32,256]{1,0:T(8,128)(2,1)S(1)}, u32[]{:S(2)}, u32[]{:S(2)}) collective-permute-start(bf16[32,256]{1,0:T(8,128)(2,1)S(1)} %get-tuple-element.71), channel_id=1, source_target_pairs={{192,0},{193,1},{194,2},{195,3},{196,4},{197,5},{198,6},{199,7},{2... | collective-permute-start | bytes 49160 | tf_op jit(solution)/shard_map/ppermute | solution.py:29
  108.4 7.9 %collective-permute-start.19 = (bf16[32,256]{1,0:T(8,128)(2,1)S(1)}, bf16[32,256]{1,0:T(8,128)(2,1)S(1)}, u32[]{:S(2)}, u32[]{:S(2)}) collective-permute-start(bf16[32,256]{1,0:T(8,128)(2,1)S(1)} %get-tuple-element.72), channel_id=1, source_target_pairs={{128,0},{129,1},{130,2},{131,3},{132,4},{133,5},{134,6},{135,7},{1... | collective-permute-start | bytes 49160 | tf_op jit(solution)/shard_map/ppermute | solution.py:29
  113.7 4.6 %collective-permute-start.20 = (bf16[32,256]{1,0:T(8,128)(2,1)S(1)}, bf16[32,256]{1,0:T(8,128)(2,1)S(1)}, u32[]{:S(2)}, u32[]{:S(2)}) collective-permute-start(bf16[32,256]{1,0:T(8,128)(2,1)S(1)} %get-tuple-element.73), channel_id=1, source_target_pairs={{64,0},{65,1},{66,2},{67,3},{68,4},{69,5},{70,6},{71,7},{72,8},{73... | collective-permute-start | bytes 49160 | tf_op jit(solution)/shard_map/ppermute | solution.py:29

commit v9 on v8

--- a/solution.py
+++ b/solution.py
@@ -435,8 +435,8 @@
         return jnp.concatenate([places[(x + k) % X * 4 + row * 2 + c] for k in ALONG_X])
 
     away = fetch(away, swap_z)
+    blocks, mine, other = lax.optimization_barrier((blocks, mine, other))
     mine_core = fetch(other, swap_core)
-    blocks, mine = lax.optimization_barrier((blocks, mine))
     *carried, dkv_y = first_call(
         make_meta(owners(1 - yh), q_pos), (q, q_other), (g, g_other), (stats, stats_other), blocks
     )

time: 121 us -> 120 us (level)
  starting transfers between devices: 40.5 us -> 29.4 us
  Pallas kernels: 19.4 us -> 28.7 us
  local copies, waits for them, and re-layouts: 4.32 us -> 8.08 us
  waiting for transfers between devices: 26.5 us -> 23.2 us
    ppermute x21, starting transfers between devices: 40.5 us -> 29.4 us  [fetch(): return lax.ppermute(value, AXES, pairs)]
    pallas_call x1, Pallas kernels: 3.65 us -> 8.67 us  [first_call(): pl.pallas_call(first_kernel, out_shape=(rows,) * 4 + (jax.ShapeDtypeStruc...]
    pallas_call x1, Pallas kernels: 5.3 us -> 9.59 us  [second_call(): pl.pallas_call(second_kernel, out_shape=(jax.ShapeDtypeStruct((256, WIDE)...]
    unnamed x24 -> x32, local copies, waits for them, and re-layouts: 3.33 us -> 7.08 us
    ppermute x21, waiting for transfers between devices: 26.5 us -> 23.2 us  [fetch(): return lax.ppermute(value, AXES, pairs)]
  transfers between devices with their start and end apart: 21 -> 21, of which waited for: 8 -> 10; matrix products, arithmetic and copies ran while one was open for 3% -> 4% of each run, Pallas kernels for 15% -> 23%
where the time goes in v9:
time: 120 us; the launch traced here: 119 us
  starting transfers between devices  29.4 us (24%)
  Pallas kernels  28.7 us (24%)
  blocking collectives  23.4 us (20%)
  waiting for transfers between devices  23.2 us (19%)
  local copies, waits for them, and re-layouts  8.08 us (7%)
  other arithmetic  5.12 us (4%)
    ppermute x21, starting transfers between devices, fetch(): return lax.ppermute(value, AXES, pairs)  29.4 us
    all_to_all x1, blocking collectives, body(): terms = lax.all_to_all(terms, ('yl', 'x', 'yh'), 0, 0)  23.4 us
    ppermute x21, waiting for transfers between devices, fetch(): return lax.ppermute(value, AXES, pairs)  23.2 us
    pallas_call x1, Pallas kernels, second_call(): pl.pallas_call(second_kernel, out_shape=(jax.ShapeDtypeStruct((256, WIDE)...  9.59 us
    pallas_call x1, Pallas kernels, first_call(): pl.pallas_call(first_kernel, out_shape=(rows,) * 4 + (jax.ShapeDtypeStruc...  8.67 us
    pallas_call x1, Pallas kernels, turn(): pl.pallas_call(turn_kernel, grid=(Z,), out_shape=(half, half, jax.ShapeDt...  7.5 us
    unnamed x32, local copies, waits for them, and re-layouts  7.08 us
  transfers between devices with their start and end apart: 21, of which 10 were waited for; matrix products, arithmetic and copies ran while one was open for 4% of the time, Pallas kernels for 23%

profile of v9, /device:TPU:4, one launch (start us, length us, event | category | flops | bytes accessed | tf_op | source)
XLA Modules:
  0.0 118.8 jit_solution(3590528448033862410)
XLA Ops:
  0.6 0.9 pad_maximum_fusion.1
  1.5 3.3 %collective-permute-start.3 = (bf16[256,256]{1,0:T(8,128)(2,1)S(1)}, bf16[256,256]{1,0:T(8,128)(2,1)S(1)}, u32[]{:S(2)}, u32[]{:S(2)}) collective-permute-start(bf16[256,256]{1,0:T(8,128)(2,1)S(1)} %pad_maximum_fusion.1), channel_id=1, source_target_pairs={{2,0},{3,1},{0,2},{1,3},{6,4},{7,5},{4,6},{5,7},{10,8},{11,9},{8,1... | collective-permute-start | bytes 393224 | tf_op jit(solution)/shard_map/ppermute | solution.py:29
  4.8 0.5 collective-permute-start.1
  5.3 0.7 reshape.14
  6.2 0.2 convert_reduce_fusion.1
  6.5 0.2 convert_reduce_fusion.2
  6.8 0.6 pad_add_fusion.3.place
  7.5 0.8 collective-permute-done.3
  8.3 0.9 pad_maximum_fusion.refs_6_
  9.2 2.1 %collective-permute-start.6 = (bf16[512,256]{1,0:T(8,128)(2,1)S(1)}, bf16[512,256]{1,0:T(8,128)(2,1)S(1)}, u32[]{:S(2)}, u32[]{:S(2)}) collective-permute-start(bf16[512,256]{1,0:T(8,128)(2,1)S(1)} %pad_maximum_fusion.refs_6_), channel_id=1, source_target_pairs={{8,0},{9,1},{10,2},{11,3},{12,4},{13,5},{14,6},{15,7},{0,8},{1,9},... | collective-permute-start | bytes 786440 | tf_op jit(solution)/shard_map/ppermute | solution.py:29
  11.3 0.6 collective-permute-start.5
  11.9 1.4 %collective-permute-start.4 = (bf16[512,256]{1,0:T(8,128)(2,1)S(1)}, bf16[512,256]{1,0:T(8,128)(2,1)S(1)}, u32[]{:S(2)}, u32[]{:S(2)}) collective-permute-start(bf16[512,256]{1,0:T(8,128)(2,1)S(1)} %pad_maximum_fusion.refs_6_), channel_id=1, source_target_pairs={{4,0},{5,1},{6,2},{7,3},{8,4},{9,5},{10,6},{11,7},{12,8},{13,9},{1... | collective-permute-start | bytes 786440 | tf_op jit(solution)/shard_map/ppermute | solution.py:29
  13.3 7.5 %turn.1 = (bf16[2048,256]{1,0:T(8,128)(2,1)}, bf16[2048,256]{1,0:T(8,128)(2,1)}, bf16[2,2048,256]{2,1,0:T(8,128)(2,1)}) custom-call(s32[3]{0:T(128)} %pad_add_fusion.3.place, bf16[256,8192]{1,0:T(8,128)(2,1)} %bitcast.41), custom_call_target="tpu_custom_call" | custom-call | flops 1000000000 | bytes 8388608 | tf_op jit(solution)/shard_map/turn/pallas_call | solution.py:133
  20.9 0.5 row_stats.1.refs_4_
  21.4 0.7 copy-done.7
  22.1 0.9 collective-permute-done.5.refs_8_
  23.0 0.7 copy-done.10
  23.7 1.9 %collective-permute-start.8 = (bf16[2,2048,256]{2,1,0:T(8,128)(2,1)}, bf16[2,2048,256]{2,1,0:T(8,128)(2,1)S(1)}, u32[]{:S(2)}, u32[]{:S(2)}) collective-permute-start(bf16[2,2048,256]{2,1,0:T(8,128)(2,1)} %get-tuple-element.61), channel_id=1, source_target_pairs={{32,0},{33,1},{34,2},{35,3},{36,4},{37,5},{38,6},{39,7},{40,8},{41... | collective-permute-start | bytes 6291464 | tf_op jit(solution)/shard_map/ppermute | solution.py:29
  25.7 0.7 copy-done.13
  26.7 1.0 copy-done.3
  27.7 1.0 copy-done.6
  28.8 0.9 copy-done.8
  29.7 0.9 copy-done.11
  30.7 0.9 copy-done.14
  31.6 8.7 %attention_first.1 = (bf16[4,128,1024]{2,1,0:T(8,128)(2,1)S(1)}, bf16[4,128,1024]{2,1,0:T(8,128)(2,1)S(1)}, bf16[4,128,1024]{2,1,0:T(8,128)(2,1)S(1)}, bf16[4,12...) custom-call(s32[28]{0:T(128)S(1)} %concatenate.27.meta, ...), custom_call_target="tpu_custom_call" | custom-call | flops 10000000000 | bytes 1048576 | tf_op jit(solution)/shard_map/attention_first/pallas_call | solution.py:316
  40.3 6.1 %collective-permute-start.9 = (bf16[1024,256]{1,0:T(8,128)(2,1)S(1)}, bf16[1024,256]{1,0:T(8,128)(2,1)S(1)}, u32[]{:S(2)}, u32[]{:S(2)}) collective-permute-start(bf16[1024,256]{1,0:T(8,128)(2,1)S(1)} %get-tuple-element.63), channel_id=1, source_target_pairs={{2,0},{3,1},{0,2},{1,3},{6,4},{7,5},{4,6},{5,7},{10,8},{11,9},{8,1... | collective-permute-start | bytes 1572872 | tf_op jit(solution)/shard_map/ppermute | solution.py:29
  46.4 9.6 %attention_second.1 = (f32[256,1024]{1,0:T(8,128)S(1)}, bf16[256,1024]{1,0:T(8,128)(2,1)S(1)}, f32[256,256]{1,0:T(8,128)S(1)}, f32[256,256]{1,0:T(8,128)S(1)}, f...) custom-call(s32[28]{0:T(128)S(1)} %concatenate.25.meta, bf16[4,128,1024]{2,1,0:T(8,128)(2,1)S(1)} %get-tuple-element.52.refs_0_, ...), custom_call_target="tpu_custom_call" | custom-call | flops 10000000000 | bytes 1048576 | tf_op jit(solution)/shard_map/attention_second/pallas_call | solution.py:335
  56.0 2.3 %collective-permute-done.9 = bf16[1024,256]{1,0:T(8,128)(2,1)S(1)} collective-permute-done((bf16[1024,256]{1,0:T(8,128)(2,1)S(1)}, bf16[1024,256]{1,0:T(8,128)(2,1)S(1)}, u32[]{:S(2)}, u32[]{:S(2)}) %collective-permute-start.9) | collective-permute-done | bytes 524320 | tf_op jit(solution)/shard_map/ppermute | solution.py:29
  58.3 0.2 collective-permute-start.10
  58.6 2.0 %collective-permute-start.11 = (bf16[256,256]{1,0:T(8,128)(2,1)S(1)}, bf16[256,256]{1,0:T(8,128)(2,1)S(1)}, u32[]{:S(2)}, u32[]{:S(2)}) collective-permute-start(bf16[256,256]{1,0:T(8,128)(2,1)S(1)} %get-tuple-element.88), channel_id=1, source_target_pairs={{4,0},{5,1},{6,2},{7,3},{8,4},{9,5},{10,6},{11,7},{12,8},{13,9},{1... | collective-permute-start | bytes 393224 | tf_op jit(solution)/shard_map/ppermute | solution.py:29
  60.6 6.8 %collective-permute-done.10 = bf16[256,256]{1,0:T(8,128)(2,1)S(1)} collective-permute-done((bf16[256,256]{1,0:T(8,128)(2,1)S(1)}, bf16[256,256]{1,0:T(8,128)(2,1)S(1)}, u32[]{:S(2)}, u32[]{:S(2)}) %collective-permute-start.10) | collective-permute-done | bytes 131104 | tf_op jit(solution)/shard_map/ppermute | solution.py:29
  67.4 1.8 %collective-permute-done.11 = bf16[256,256]{1,0:T(8,128)(2,1)S(1)} collective-permute-done((bf16[256,256]{1,0:T(8,128)(2,1)S(1)}, bf16[256,256]{1,0:T(8,128)(2,1)S(1)}, u32[]{:S(2)}, u32[]{:S(2)}) %collective-permute-start.11) | collective-permute-done | bytes 131104 | tf_op jit(solution)/shard_map/ppermute | solution.py:29
  69.3 0.2 collective-permute-start.13
  69.5 5.0 %collective-permute-done.13.gc = bf16[256,256]{1,0:T(8,128)(2,1)S(1)} collective-permute-done((bf16[256,256]{1,0:T(8,128)(2,1)S(1)}, bf16[256,256]{1,0:T(8,128)(2,1)S(1)}, u32[]{:S(2)}, u32[]{:S(2)}) %collective-permute-start.13) | collective-permute-done | bytes 131104 | tf_op jit(solution)/shard_map/ppermute | solution.py:29
  74.4 1.3 %collective-permute-done.14.gd = bf16[256,256]{1,0:T(8,128)(2,1)S(1)} collective-permute-done((bf16[256,256]{1,0:T(8,128)(2,1)S(1)}, bf16[256,256]{1,0:T(8,128)(2,1)S(1)}, u32[]{:S(2)}, u32[]{:S(2)}) %collective-permute-start.14) | collective-permute-done | bytes 131104 | tf_op jit(solution)/shard_map/ppermute | solution.py:29
  75.9 0.2 collective-permute-start.15
  76.1 0.4 collective-permute-start.16
  76.5 2.3 %collective-permute-done.16.gb = bf16[256,256]{1,0:T(8,128)(2,1)S(1)} collective-permute-done((bf16[256,256]{1,0:T(8,128)(2,1)S(1)}, bf16[256,256]{1,0:T(8,128)(2,1)S(1)}, u32[]{:S(2)}, u32[]{:S(2)}) %collective-permute-start.16) | collective-permute-done | bytes 131104 | tf_op jit(solution)/shard_map/ppermute | solution.py:29
  78.8 1.8 %project.1 = bf16[16,128,256]{2,1,0:T(8,128)(2,1)S(1)} custom-call(bf16[2048,256]{1,0:T(8,128)(2,1)S(1)} %copy-done, bf16[2048,256]{1,0:T(8,128)(2,1)S(1)} %collective-permute-done.7.b_ref, bf16[2,2048,256]{2,1,0:T(8,128)(2,1)S(1)} %collective-permute-done.8.c_ref, bf16[2048,256]{1,0:T(8,128)(2,1)S(1)} %collective-permute-done.15.d_ref, ...), custom_call_target="tpu_custom_call" | custom-call | flops 1073741824 | bytes 8388608 | tf_op jit(solution)/shard_map/project/pallas_call | solution.py:381
  80.6 23.4 %all_to_all.5.in_ref = bf16[16,128,256]{2,1,0:T(8,128)(2,1)S(1)} all-to-all(bf16[16,128,256]{2,1,0:T(8,128)(2,1)S(1)} %project.1), channel_id=1, replica_groups=mesh['z'=8,'yl'=2,'x'=4,'yh'=2,'c'=2] {'yl','x','yh'}, dimensions={0} | all-to-all | bytes 2097152 | tf_op jit(solution)/shard_map/all_to_all | solution.py:459
  104.0 0.7 sum_terms.1
  104.7 3.4 %collective-permute-start.18 = (bf16[32,256]{1,0:T(8,128)(2,1)S(1)}, bf16[32,256]{1,0:T(8,128)(2,1)S(1)}, u32[]{:S(2)}, u32[]{:S(2)}) collective-permute-start(bf16[32,256]{1,0:T(8,128)(2,1)S(1)} %get-tuple-element.73), channel_id=1, source_target_pairs={{192,0},{193,1},{194,2},{195,3},{196,4},{197,5},{198,6},{199,7},{2... | collective-permute-start | bytes 49160 | tf_op jit(solution)/shard_map/ppermute | solution.py:29
  108.0 4.5 %collective-permute-start.19 = (bf16[32,256]{1,0:T(8,128)(2,1)S(1)}, bf16[32,256]{1,0:T(8,128)(2,1)S(1)}, u32[]{:S(2)}, u32[]{:S(2)}) collective-permute-start(bf16[32,256]{1,0:T(8,128)(2,1)S(1)} %get-tuple-element.74), channel_id=1, source_target_pairs={{128,0},{129,1},{130,2},{131,3},{132,4},{133,5},{134,6},{135,7},{1... | collective-permute-start | bytes 49160 | tf_op jit(solution)/shard_map/ppermute | solution.py:29
  112.5 2.7 %collective-permute-start.20 = (bf16[32,256]{1,0:T(8,128)(2,1)S(1)}, bf16[32,256]{1,0:T(8,128)(2,1)S(1)}, u32[]{:S(2)}, u32[]{:S(2)}) collective-permute-start(bf16[32,256]{1,0:T(8,128)(2,1)S(1)} %get-tuple-element.75), channel_id=1, source_target_pairs={{64,0},{65,1},{66,2},{67,3},{68,4},{69,5},{70,6},{71,7},{72,8},{73... | collective-permute-start | bytes 49160 | tf_op jit(solution)/shard_map/ppermute | solution.py:29
  115.2 0.5 collective-permute-done.19
  115.7 1.5 %collective-permute-done.20 = bf16[32,256]{1,0:T(8,128)(2,1)S(1)} collective-permute-done((bf16[32,256]{1,0:T(8,128)(2,1)S(1)}, bf16[32,256]{1,0:T(8,128)(2,1)S(1)}, u32[]{:S(2)}, u32[]{:S(2)}) %collective-permute-start.20) | collective-permute-done | bytes 16416 | tf_op jit(solution)/shard_map/ppermute | solution.py:29
  117.2 0.6 convert_add_fusion
  117.8 1.0 fusion
  (54 shorter events, 1.1 us)
Async XLA Ops:
  1.5 6.8 %collective-permute-start.3 = (bf16[256,256]{1,0:T(8,128)(2,1)S(1)}, bf16[256,256]{1,0:T(8,128)(2,1)S(1)}, u32[]{:S(2)}, u32[]{:S(2)}) collective-permute-start(bf16[256,256]{1,0:T(8,128)(2,1)S(1)} %pad_maximum_fusion.1), channel_id=1, source_target_pairs={{2,0},{3,1},{0,2},{1,3},{6,4},{7,5},{4,6},{5,7},{10,8},{11,9},{8,1... | collective-permute-start | bytes 393224 | tf_op jit(solution)/shard_map/ppermute | solution.py:29
  4.8 21.9 %collective-permute-start = (bf16[256,1024]{1,0:T(8,128)(2,1)}, bf16[256,1024]{1,0:T(8,128)(2,1)}, u32[]{:S(2)}, u32[]{:S(2)}) collective-permute-start(bf16[256,1024]{1,0:T(8,128)(2,1)} %bitcast.39), channel_id=1, source_target_pairs={{1,0},{0,1},{3,2},{2,3},{5,4},{4,5},{7,6},{6,7},{9,8},{8,9},{11,10... | collective-permute-start | bytes 1572872 | tf_op jit(solution)/shard_map/ppermute | solution.py:29
  4.8 21.9 %collective-permute-start.1 = (bf16[256,1024]{1,0:T(8,128)(2,1)}, bf16[256,1024]{1,0:T(8,128)(2,1)}, u32[]{:S(2)}, u32[]{:S(2)}) collective-permute-start(bf16[256,1024]{1,0:T(8,128)(2,1)} %bitcast.35), channel_id=1, source_target_pairs={{1,0},{0,1},{3,2},{2,3},{5,4},{4,5},{7,6},{6,7},{9,8},{8,9},{11,10... | collective-permute-start | bytes 1572872 | tf_op jit(solution)/shard_map/ppermute | solution.py:29
  9.2 12.1 %collective-permute-start.6 = (bf16[512,256]{1,0:T(8,128)(2,1)S(1)}, bf16[512,256]{1,0:T(8,128)(2,1)S(1)}, u32[]{:S(2)}, u32[]{:S(2)}) collective-permute-start(bf16[512,256]{1,0:T(8,128)(2,1)S(1)} %pad_maximum_fusion.refs_6_), channel_id=1, source_target_pairs={{8,0},{9,1},{10,2},{11,3},{12,4},{13,5},{14,6},{15,7},{0,8},{1,9},... | collective-permute-start | bytes 786440 | tf_op jit(solution)/shard_map/ppermute | solution.py:29
  11.3 11.7 %collective-permute-start.5 = (bf16[512,256]{1,0:T(8,128)(2,1)S(1)}, bf16[512,256]{1,0:T(8,128)(2,1)S(1)}, u32[]{:S(2)}, u32[]{:S(2)}) collective-permute-start(bf16[512,256]{1,0:T(8,128)(2,1)S(1)} %pad_maximum_fusion.refs_6_), channel_id=1, source_target_pairs={{12,0},{13,1},{14,2},{15,3},{0,4},{1,5},{2,6},{3,7},{4,8},{5,9},{6... | collective-permute-start | bytes 786440 | tf_op jit(solution)/shard_map/ppermute | solution.py:29
  11.9 13.7 %collective-permute-start.4 = (bf16[512,256]{1,0:T(8,128)(2,1)S(1)}, bf16[512,256]{1,0:T(8,128)(2,1)S(1)}, u32[]{:S(2)}, u32[]{:S(2)}) collective-permute-start(bf16[512,256]{1,0:T(8,128)(2,1)S(1)} %pad_maximum_fusion.refs_6_), channel_id=1, source_target_pairs={{4,0},{5,1},{6,2},{7,3},{8,4},{9,5},{10,6},{11,7},{12,8},{13,9},{1... | collective-permute-start | bytes 786440 | tf_op jit(solution)/shard_map/ppermute | solution.py:29
  13.3 7.5 %copy-start.1 = (bf16[1,256,1024]{2,1,0:T(8,128)(2,1)S(1)}, bf16[1,256,1024]{2,1,0:T(8,128)(2,1)}, u32[]{:S(2)}) copy-start(bf16[1,256,1024]{2,1,0:T(8,128)(2,1)} %param.12) | copy-start | bytes 1572868
  13.3 7.5 %copy-start.2 = (bf16[1,256,1024]{2,1,0:T(8,128)(2,1)S(1)}, bf16[1,256,1024]{2,1,0:T(8,128)(2,1)}, u32[]{:S(2)}) copy-start(bf16[1,256,1024]{2,1,0:T(8,128)(2,1)} %param.13) | copy-start | bytes 1572868
  13.3 7.5 %copy-start.4 = (f32[1,8,256]{2,1,0:T(8,128)S(1)}, f32[1,8,256]{2,1,0:T(8,128)}, u32[]{:S(2)}) copy-start(f32[1,8,256]{2,1,0:T(8,128)} %param.14) | copy-start | bytes 24580
  21.4 0.7 copy-start.7
  22.1 4.6 %collective-permute-start.2 = (f32[8,1024]{1,0:T(8,128)S(1)}, f32[8,1024]{1,0:T(8,128)S(1)}, u32[]{:S(2)}, u32[]{:S(2)}) collective-permute-start(f32[8,1024]{1,0:T(8,128)S(1)} %row_stats.1.refs_4_), channel_id=1, source_target_pairs={{1,0},{0,1},{3,2},{2,3},{5,4},{4,5},{7,6},{6,7},{9,8},{8,9},{11,10... | collective-permute-start | bytes 98312 | tf_op jit(solution)/shard_map/ppermute | solution.py:29
  23.0 0.7 copy-start.10
  23.7 52.1 %collective-permute-start.8 = (bf16[2,2048,256]{2,1,0:T(8,128)(2,1)}, bf16[2,2048,256]{2,1,0:T(8,128)(2,1)S(1)}, u32[]{:S(2)}, u32[]{:S(2)}) collective-permute-start(bf16[2,2048,256]{2,1,0:T(8,128)(2,1)} %get-tuple-element.61), channel_id=1, source_target_pairs={{32,0},{33,1},{34,2},{35,3},{36,4},{37,5},{38,6},{39,7},{40,8},{41... | collective-permute-start | bytes 6291464 | tf_op jit(solution)/shard_map/ppermute | solution.py:29
  25.7 0.7 copy-start.13
  26.4 20.0 %collective-permute-start.7 = (bf16[2048,256]{1,0:T(8,128)(2,1)}, bf16[2048,256]{1,0:T(8,128)(2,1)S(1)}, u32[]{:S(2)}, u32[]{:S(2)}) collective-permute-start(bf16[2048,256]{1,0:T(8,128)(2,1)} %get-tuple-element.51), channel_id=1, source_target_pairs={{1,0},{0,1},{3,2},{2,3},{5,4},{4,5},{7,6},{6,7},{9,8},{8,9},{11,10... | collective-permute-start | bytes 3145736 | tf_op jit(solution)/shard_map/ppermute | solution.py:29
  26.7 1.0 copy-start.3
  27.7 1.0 copy-start.6
  28.8 0.9 copy-start.8
  29.7 0.9 copy-start.11
  30.7 0.9 copy-start.14
  31.6 14.7 %copy-start.9 = (bf16[512,256]{1,0:T(8,128)(2,1)S(1)}, bf16[512,256]{1,0:T(8,128)(2,1)}, u32[]{:S(2)}) copy-start(bf16[512,256]{1,0:T(8,128)(2,1)} %copy-done.7) | copy-start | bytes 786436
  31.6 14.7 %copy-start.12 = (bf16[512,256]{1,0:T(8,128)(2,1)S(1)}, bf16[512,256]{1,0:T(8,128)(2,1)}, u32[]{:S(2)}) copy-start(bf16[512,256]{1,0:T(8,128)(2,1)} %copy-done.10) | copy-start | bytes 786436
  31.6 14.7 %copy-start.15 = (bf16[512,256]{1,0:T(8,128)(2,1)S(1)}, bf16[512,256]{1,0:T(8,128)(2,1)}, u32[]{:S(2)}) copy-start(bf16[512,256]{1,0:T(8,128)(2,1)} %copy-done.13) | copy-start | bytes 786436
  40.3 17.9 %collective-permute-start.9 = (bf16[1024,256]{1,0:T(8,128)(2,1)S(1)}, bf16[1024,256]{1,0:T(8,128)(2,1)S(1)}, u32[]{:S(2)}, u32[]{:S(2)}) collective-permute-start(bf16[1024,256]{1,0:T(8,128)(2,1)S(1)} %get-tuple-element.63), channel_id=1, source_target_pairs={{2,0},{3,1},{0,2},{1,3},{6,4},{7,5},{4,6},{5,7},{10,8},{11,9},{8,1... | collective-permute-start | bytes 1572872 | tf_op jit(solution)/shard_map/ppermute | solution.py:29
  58.2 20.6 %copy-start = (bf16[2048,256]{1,0:T(8,128)(2,1)S(1)}, bf16[2048,256]{1,0:T(8,128)(2,1)}, u32[]{:S(2)}) copy-start(bf16[2048,256]{1,0:T(8,128)(2,1)} %get-tuple-element.59.a_ref) | copy-start | bytes 3145732
  58.3 9.0 %collective-permute-start.10 = (bf16[256,256]{1,0:T(8,128)(2,1)S(1)}, bf16[256,256]{1,0:T(8,128)(2,1)S(1)}, u32[]{:S(2)}, u32[]{:S(2)}) collective-permute-start(bf16[256,256]{1,0:T(8,128)(2,1)S(1)} %get-tuple-element.86), channel_id=1, source_target_pairs={{12,0},{13,1},{14,2},{15,3},{0,4},{1,5},{2,6},{3,7},{4,8},{5,9},{6... | collective-permute-start | bytes 393224 | tf_op jit(solution)/shard_map/ppermute | solution.py:29
  58.6 8.8 %collective-permute-start.12 = (bf16[256,256]{1,0:T(8,128)(2,1)S(1)}, bf16[256,256]{1,0:T(8,128)(2,1)S(1)}, u32[]{:S(2)}, u32[]{:S(2)}) collective-permute-start(bf16[256,256]{1,0:T(8,128)(2,1)S(1)} %get-tuple-element.87), channel_id=1, source_target_pairs={{8,0},{9,1},{10,2},{11,3},{12,4},{13,5},{14,6},{15,7},{0,8},{1,9},... | collective-permute-start | bytes 393224 | tf_op jit(solution)/shard_map/ppermute | solution.py:29
  58.6 10.6 %collective-permute-start.11 = (bf16[256,256]{1,0:T(8,128)(2,1)S(1)}, bf16[256,256]{1,0:T(8,128)(2,1)S(1)}, u32[]{:S(2)}, u32[]{:S(2)}) collective-permute-start(bf16[256,256]{1,0:T(8,128)(2,1)S(1)} %get-tuple-element.88), channel_id=1, source_target_pairs={{4,0},{5,1},{6,2},{7,3},{8,4},{9,5},{10,6},{11,7},{12,8},{13,9},{1... | collective-permute-start | bytes 393224 | tf_op jit(solution)/shard_map/ppermute | solution.py:29
  69.3 5.2 %collective-permute-start.13 = (bf16[256,256]{1,0:T(8,128)(2,1)S(1)}, bf16[256,256]{1,0:T(8,128)(2,1)S(1)}, u32[]{:S(2)}, u32[]{:S(2)}) collective-permute-start(bf16[256,256]{1,0:T(8,128)(2,1)S(1)} %add_convert_fusion.1.ga), channel_id=1, source_target_pairs={{32,0},{33,1},{34,2},{35,3},{36,4},{37,5},{38,6},{39,7},{40,8},{41... | collective-permute-start | bytes 393224 | tf_op jit(solution)/shard_map/ppermute | solution.py:29
  74.4 1.3 %collective-permute-start.14 = (bf16[256,256]{1,0:T(8,128)(2,1)S(1)}, bf16[256,256]{1,0:T(8,128)(2,1)S(1)}, u32[]{:S(2)}, u32[]{:S(2)}) collective-permute-start(bf16[256,256]{1,0:T(8,128)(2,1)S(1)} %collective-permute-done.13.gc), channel_id=1, source_target_pairs={{1,0},{0,1},{3,2},{2,3},{5,4},{4,5},{7,6},{6,7},{9,8},{8,9},{11,10... | collective-permute-start | bytes 393224 | tf_op jit(solution)/shard_map/ppermute | solution.py:29
  75.9 2.9 %collective-permute-start.15 = (bf16[2048,256]{1,0:T(8,128)(2,1)S(1)}, bf16[2048,256]{1,0:T(8,128)(2,1)S(1)}, u32[]{:S(2)}, u32[]{:S(2)}) collective-permute-start(bf16[2048,256]{1,0:T(8,128)(2,1)S(1)} %slice_bitcast_fusion), channel_id=1, source_target_pairs={{1,0},{0,1},{3,2},{2,3},{5,4},{4,5},{7,6},{6,7},{9,8},{8,9},{11,10... | collective-permute-start | bytes 3145736 | tf_op jit(solution)/shard_map/ppermute | solution.py:29
  76.1 2.7 %collective-permute-start.16 = (bf16[256,256]{1,0:T(8,128)(2,1)S(1)}, bf16[256,256]{1,0:T(8,128)(2,1)S(1)}, u32[]{:S(2)}, u32[]{:S(2)}) collective-permute-start(bf16[256,256]{1,0:T(8,128)(2,1)S(1)} %add_convert_fusion.1.ga), channel_id=1, source_target_pairs={{1,0},{0,1},{3,2},{2,3},{5,4},{4,5},{7,6},{6,7},{9,8},{8,9},{11,10... | collective-permute-start | bytes 393224 | tf_op jit(solution)/shard_map/ppermute | solution.py:29
  80.6 23.4 %copy-start.5 = (s32[3]{0:T(128)S(1)}, s32[3]{0:T(128)}, u32[]{:S(2)}) copy-start(s32[3]{0:T(128)} %pad_add_fusion.3.place) | copy-start | bytes 40
  104.0 13.8 %collective-permute-start.17 = (bf16[256,1024]{1,0:T(8,128)(2,1)S(1)}, bf16[256,1024]{1,0:T(8,128)(2,1)S(1)}, u32[]{:S(2)}, u32[]{:S(2)}) collective-permute-start(bf16[256,1024]{1,0:T(8,128)(2,1)S(1)} %get-tuple-element.70), channel_id=1, source_target_pairs={{1,0},{0,1},{3,2},{2,3},{5,4},{4,5},{7,6},{6,7},{9,8},{8,9},{11,10... | collective-permute-start | bytes 1572872 | tf_op jit(solution)/shard_map/ppermute | solution.py:29
  104.7 10.5 %collective-permute-start.18 = (bf16[32,256]{1,0:T(8,128)(2,1)S(1)}, bf16[32,256]{1,0:T(8,128)(2,1)S(1)}, u32[]{:S(2)}, u32[]{:S(2)}) collective-permute-start(bf16[32,256]{1,0:T(8,128)(2,1)S(1)} %get-tuple-element.73), channel_id=1, source_target_pairs={{192,0},{193,1},{194,2},{195,3},{196,4},{197,5},{198,6},{199,7},{2... | collective-permute-start | bytes 49160 | tf_op jit(solution)/shard_map/ppermute | solution.py:29
  108.0 7.6 %collective-permute-start.19 = (bf16[32,256]{1,0:T(8,128)(2,1)S(1)}, bf16[32,256]{1,0:T(8,128)(2,1)S(1)}, u32[]{:S(2)}, u32[]{:S(2)}) collective-permute-start(bf16[32,256]{1,0:T(8,128)(2,1)S(1)} %get-tuple-element.74), channel_id=1, source_target_pairs={{128,0},{129,1},{130,2},{131,3},{132,4},{133,5},{134,6},{135,7},{1... | collective-permute-start | bytes 49160 | tf_op jit(solution)/shard_map/ppermute | solution.py:29
  112.5 4.6 %collective-permute-start.20 = (bf16[32,256]{1,0:T(8,128)(2,1)S(1)}, bf16[32,256]{1,0:T(8,128)(2,1)S(1)}, u32[]{:S(2)}, u32[]{:S(2)}) collective-permute-start(bf16[32,256]{1,0:T(8,128)(2,1)S(1)} %get-tuple-element.75), channel_id=1, source_target_pairs={{64,0},{65,1},{66,2},{67,3},{68,4},{69,5},{70,6},{71,7},{72,8},{73... | collective-permute-start | bytes 49160 | tf_op jit(solution)/shard_map/ppermute | solution.py:29
